TPU v7x, 32 devices: a whole 2x2x4 slice. The times are simulated.
32 devices in a mesh: segment: 4 (over x, core), ctx: 8 (over z, y).
Axes of the slice: x: 2, y: 2, z: 4, core: 2. Of those that a mesh axis runs over, the one named last changes fastest.
Arguments:
- query_stream: bfloat16 [4, 4096, 512], P('segment', 'ctx'), may hold values from -6 to 6
- key_stream: bfloat16 [4, 4096, 512], P('segment', 'ctx'), may hold values from -6 to 6
- value_stream: bfloat16 [4, 4096, 512], P('segment', 'ctx'), may hold values from -6 to 6
- filter_taps: bfloat16 [4, 4096, 512], P('segment', 'ctx'), may hold values from -1 to 1
- skip_weight: float32 [4, 512], P('segment'), may hold values from -3 to 3
Outputs:
- handed_on: bfloat16 [4, 4096, 512], P('segment', 'ctx')
All inputs are finite; a program needn't handle non-finite values.
Results may differ from a plain program's by a relative error of at most 0.001.
Values may be sent and summed in bfloat16 or wider, within the bound.
No kernel may reach another device: no remote copies, remote signals or barrier semaphores. Data moves between devices by JAX's collectives and lax.ppermute only.
A program may use at most 128 MiB of HBM per device.

v0:
```python
import math

import jax
import jax.numpy as jnp
from jax import lax
from jax.sharding import PartitionSpec as P

HIGHEST = lax.Precision.HIGHEST


def from_behind(value, axis, steps):
    count = lax.axis_size(axis)
    pairs = [(source, (source + steps) % count) for source in range(count)]
    return lax.ppermute(value, axis, pairs)


def angles(modulus, left, right):
    phase = left[:, None] * right[None, :] % modulus
    theta = phase.astype(jnp.float32) * (2.0 * math.pi / modulus)
    return (jnp.cos(theta), jnp.sin(theta))


def frequency_order(width):
    rows = jnp.arange(2 * width, dtype=jnp.int32)
    halves = rows // 2
    return jnp.where(rows % 2 == 0, halves, jnp.where(halves == 0, width, 2 * width - halves))


def across(table, data):
    return jnp.einsum("rd,dsc->rsc", table, data, precision=HIGHEST)


def along(table, data):
    return jnp.einsum("kb,rbc->rkc", table, data, precision=HIGHEST)


def rotate(real_part, imag_part, cosine, sine):
    return (real_part * cosine + imag_part * sine, imag_part * cosine - real_part * sine)


def on_device(query_stream, key_stream, value_stream, filter_taps, skip_weight):
    parts = lax.axis_size("ctx")
    device = lax.axis_index("ctx")
    length = query_stream.shape[1]
    channels = query_stream.shape[2]
    share = length // parts
    total = 2 * parts * length
    product = key_stream[0].astype(jnp.float32) * value_stream[0].astype(jnp.float32)
    taps = filter_taps[0].astype(jnp.float32)
    block_prod, block_taps = (
        lax.all_to_all(
            product.reshape(1, length, channels), "ctx", split_axis=1, concat_axis=0, tiled=True
        ),
        lax.all_to_all(
            taps.reshape(1, length, channels), "ctx", split_axis=1, concat_axis=0, tiled=True
        ),
    )
    order = frequency_order(parts)
    cos_cross, sin_cross = angles(2 * parts, order, jnp.arange(parts, dtype=jnp.int32))
    positions = device * share + jnp.arange(share, dtype=jnp.int32)
    cos_twist, sin_twist = angles(total, order, positions)
    cos_twist = cos_twist[:, :, None]
    sin_twist = sin_twist[:, :, None]
    span = jnp.arange(length, dtype=jnp.int32)
    cos_along, sin_along = angles(length, span, span)
    local_rows = lax.dynamic_slice(order, (2 * device,), (2,))
    cos_back, sin_back = angles(total, local_rows, span)
    cos_back = cos_back[:, :, None]
    sin_back = sin_back[:, :, None]

    def forward_along(real_part, imag_part):
        return (
            along(cos_along, real_part) + along(sin_along, imag_part),
            along(cos_along, imag_part) - along(sin_along, real_part),
        )

    prod_real, prod_imag = rotate(
        across(cos_cross, block_prod), -across(sin_cross, block_prod), cos_twist, sin_twist
    )
    taps_real, taps_imag = rotate(
        across(cos_cross, block_taps), -across(sin_cross, block_taps), cos_twist, sin_twist
    )
    first_real, first_imag = forward_along(
        lax.all_to_all(prod_real, "ctx", split_axis=0, concat_axis=1, tiled=True),
        lax.all_to_all(prod_imag, "ctx", split_axis=0, concat_axis=1, tiled=True),
    )
    second_real, second_imag = forward_along(
        lax.all_to_all(taps_real, "ctx", split_axis=0, concat_axis=1, tiled=True),
        lax.all_to_all(taps_imag, "ctx", split_axis=0, concat_axis=1, tiled=True),
    )
    result_real = first_real * second_real - first_imag * second_imag
    result_imag = first_real * second_imag + first_imag * second_real
    back_real = along(cos_along, result_real) - along(sin_along, result_imag)
    back_imag = along(cos_along, result_imag) + along(sin_along, result_real)
    spec_real, spec_imag = rotate(back_real, back_imag, cos_back, -sin_back)
    rows_real, rows_imag = (
        lax.all_to_all(spec_real, "ctx", split_axis=1, concat_axis=0, tiled=True),
        lax.all_to_all(spec_imag, "ctx", split_axis=1, concat_axis=0, tiled=True),
    )
    cos_final, sin_final = angles(2 * parts, jnp.arange(parts, dtype=jnp.int32), order)
    by_block = jnp.einsum("dr,rsc->dsc", cos_final, rows_real, precision=HIGHEST) - jnp.einsum(
        "dr,rsc->dsc", sin_final, rows_imag, precision=HIGHEST
    )
    by_block = by_block * (1.0 / total)
    convolved = lax.all_to_all(by_block, "ctx", split_axis=0, concat_axis=1, tiled=True)[0]
    gated = query_stream[0].astype(jnp.float32) * (convolved + skip_weight[0][None, :] * product)
    gated = gated.astype(jnp.bfloat16)[None]
    return from_behind(gated, "segment", 1)


def solution(mesh):
    placed = (
        P("segment", "ctx", None),
        P("segment", "ctx", None),
        P("segment", "ctx", None),
        P("segment", "ctx", None),
        P("segment", None),
    )
    return jax.shard_map(
        on_device, mesh=mesh, in_specs=placed, out_specs=P("segment", "ctx", None), check_vma=False
    )
```

profile of v0, /device:TPU:0, one launch (start us, length us, event | category | flops | bytes accessed | tf_op | source)
XLA Modules:
  0.0 532.6 jit_solution(4702733881749412872)
XLA Ops:
  3.4 7.3 %all-to-all-start = ((f32[1,512,512]{2,0,1:T(1,128)}), f32[1,512,512]{2,0,1:T(1,128)S(1)}, u32[]{:S(2)}, u32[]{:S(2)}) async-start(f32[1,512,512]{2,0,1:T(1,128)} %copy.87), calls=%async_computation | async-start | bytes 2097152 | tf_op jit(solution)/shard_map/all_to_all | solution.py:51
  12.5 23.9 %all-to-all-done = f32[1,512,512]{2,0,1:T(1,128)S(1)} async-done(((f32[1,512,512]{2,0,1:T(1,128)}), f32[1,512,512]{2,0,1:T(1,128)S(1)}, u32[]{:S(2)}, u32[]{:S(2)}) %all-to-all-start) | async-done | bytes 1048608 | tf_op jit(solution)/shard_map/all_to_all | solution.py:51
  47.7 18.4 %all-to-all-done.3 = f32[1,512,512]{2,0,1:T(1,128)S(1)} async-done(((f32[1,512,512]{2,0,1:T(1,128)}), f32[1,512,512]{2,0,1:T(1,128)S(1)}, u32[]{:S(2)}, u32[]{:S(2)}) %all-to-all-start.3) | async-done | bytes 1048608 | tf_op jit(solution)/shard_map/all_to_all | solution.py:54
  68.5 6.4 %multiply_subtract_fusion.1 = (f32[16,64,512]{2,0,1:T(8,128)S(1)}, f32[16,64,512]{2,0,1:T(8,128)}, f32[16,64,512]{2,0,1:T(8,128)}, f32[16,64,512]{2,0,1:T(8,128)S(1)}) fusion(f32[16,64,512]{2,0,1:T(8,128)S(1)} %fusion.39, f32[16,64]{0,1:T(8,128)S(1)} %get-tuple-element.16, f32[16,64]{0,1:T(8,128)S(1)} %get-tuple-element.15, ...), kind=kOutput, calls=%fused_computation.12 | convolution fusion | flops 57673472 | bytes 15736896 | tf_op jit(solution)/shard_map/rd,dsc->rsc/dot_general | solution.py:30
  77.5 4.3 all-to-all-start.5
  81.8 4.2 copy.99
  86.0 43.6 %all-to-all-done.5 = f32[16,64,512]{2,1,0:T(8,128)} async-done(((f32[16,64,512]{2,1,0:T(8,128)}), f32[16,64,512]{2,1,0:T(8,128)}, u32[]{:S(2)}, u32[]{:S(2)}) %all-to-all-start.5) | async-done | bytes 2097184 | tf_op jit(solution)/shard_map/all_to_all | solution.py:89
  129.7 4.8 all-to-all-start.4
  134.4 4.2 copy.93
  138.6 43.2 %all-to-all-done.4 = f32[16,64,512]{2,1,0:T(8,128)} async-done(((f32[16,64,512]{2,1,0:T(8,128)}), f32[16,64,512]{2,1,0:T(8,128)}, u32[]{:S(2)}, u32[]{:S(2)}) %all-to-all-start.4) | async-done | bytes 2097184 | tf_op jit(solution)/shard_map/all_to_all | solution.py:88
  181.8 4.4 all-to-all-start.2
  188.8 45.1 %all-to-all-done.2 = f32[16,64,512]{2,1,0:T(8,128)} async-done(((f32[16,64,512]{2,1,0:T(8,128)}), f32[16,64,512]{2,1,0:T(8,128)}, u32[]{:S(2)}, u32[]{:S(2)}) %all-to-all-start.2) | async-done | bytes 2097184 | tf_op jit(solution)/shard_map/all_to_all | solution.py:85
  233.9 4.4 all-to-all-start.1
  244.0 10.9 %fusion.28 = f32[2,512,512]{2,1,0:T(8,128)S(1)} fusion(f32[2,512,512]{2,1,0:T(8,128)S(1)} %bitcast.120), kind=kOutput, calls=%fused_computation.41 | convolution fusion | flops 3224895488 | bytes 4194304 | tf_op jit(solution)/shard_map/kb,rbc->rkc/dot_general | solution.py:34
  254.9 10.9 %fusion.32 = f32[2,512,512]{2,1,0:T(8,128)S(1)} fusion(f32[2,512,512]{2,1,0:T(8,128)S(1)} %bitcast.124), kind=kOutput, calls=%fused_computation.45 | convolution fusion | flops 3224895488 | bytes 4194304 | tf_op jit(solution)/shard_map/kb,rbc->rkc/dot_general | solution.py:34
  265.9 11.8 %fusion.30 = f32[2,512,512]{2,1,0:T(8,128)} fusion(f32[2,512,512]{2,1,0:T(8,128)S(1)} %bitcast.118), kind=kOutput, calls=%fused_computation.43 | convolution fusion | flops 3224895488 | bytes 4194304 | tf_op jit(solution)/shard_map/kb,rbc->rkc/dot_general | solution.py:34
  277.6 11.2 %convolution_subtract_fusion = f32[2,512,512]{2,1,0:T(8,128)S(1)} fusion(f32[2,512,512]{2,1,0:T(8,128)S(1)} %fusion.28, f32[2,512,512]{2,1,0:T(8,128)S(1)} %bitcast.125), kind=kOutput, calls=%fused_computation.18 | convolution fusion | flops 3225419776 | bytes 6291456 | tf_op jit(solution)/shard_map/kb,rbc->rkc/dot_general | solution.py:34
  288.9 11.8 %convolution_add_fusion = f32[2,512,512]{2,1,0:T(8,128)} fusion(f32[2,512,512]{2,1,0:T(8,128)S(1)} %fusion.32, f32[2,512,512]{2,1,0:T(8,128)S(1)} %bitcast.121), kind=kOutput, calls=%fused_computation.20 | convolution fusion | flops 3225419776 | bytes 6291456 | tf_op jit(solution)/shard_map/kb,rbc->rkc/dot_general | solution.py:34
  302.5 10.9 %fusion.34 = f32[2,512,512]{2,1,0:T(8,128)S(1)} fusion(f32[2,512,512]{2,1,0:T(8,128)S(1)} %bitcast.122), kind=kOutput, calls=%fused_computation.47 | convolution fusion | flops 3224895488 | bytes 4194304 | tf_op jit(solution)/shard_map/kb,rbc->rkc/dot_general | solution.py:34
  313.4 11.6 %convolution_add_fusion.1 = f32[2,512,512]{2,1,0:T(8,128)S(1)} fusion(f32[2,512,512]{2,1,0:T(8,128)S(1)} %fusion.34, f32[2,512,512]{2,1,0:T(8,128)S(1)} %bitcast.119), kind=kOutput, calls=%fused_computation.21 | convolution fusion | flops 3225419776 | bytes 6291456 | tf_op jit(solution)/shard_map/kb,rbc->rkc/dot_general | solution.py:34
  325.1 11.6 %multiply_subtract_fusion = (f32[2,512,512]{2,1,0:T(8,128)S(1)}, f32[2,512,512]{2,1,0:T(8,128)S(1)}) fusion(f32[2,512,512]{2,1,0:T(8,128)S(1)} %convolution_subtract_fusion, f32[2,512,512]{2,1,0:T(8,128)S(1)} %convolution_add_fusion.1, f32[2,512,512]{2,1,0:T(8,128)S(1)} %copy-done, f32[2,512,512]{2,1,0:T(8,128)S(1)} %copy-done.5, ...), kind=kOutput, calls=%fused_computation.11 | convolution fusion | flops 3228565504 | bytes 14680064 | tf_op jit(solution)/shard_map/kb,rbc->rkc/dot_general | solution.py:34
  336.7 8.6 %fusion = f32[2,512,512]{2,1,0:T(8,128)S(1)} fusion(f32[2,512,512]{2,1,0:T(8,128)S(1)} %get-tuple-element.6), kind=kOutput, calls=%fused_computation | convolution fusion | flops 3224895488 | bytes 4194304 | tf_op jit(solution)/shard_map/kb,rbc->rkc/dot_general | solution.py:34
  345.3 8.4 %fusion.2 = f32[2,512,512]{2,1,0:T(8,128)S(1)} fusion(f32[2,512,512]{2,1,0:T(8,128)S(1)} %get-tuple-element.6), kind=kOutput, calls=%fused_computation.2 | convolution fusion | flops 3224895488 | bytes 4194304 | tf_op jit(solution)/shard_map/kb,rbc->rkc/dot_general | solution.py:34
  353.7 8.7 %fusion.8 = f32[2,512,512]{2,1,0:T(8,128)S(1)} fusion(f32[2,512,512]{2,1,0:T(8,128)S(1)} %fusion.2, f32[2,512,512]{2,1,0:T(8,128)S(1)} %get-tuple-element.5), kind=kOutput, calls=%fused_computation.16 | convolution fusion | flops 3225419776 | bytes 6291456 | tf_op jit(solution)/shard_map/kb,rbc->rkc/dot_general | solution.py:34
  362.4 9.7 %subtract_bitcast_fusion = (f32[2,512,512]{1,2,0:T(8,128)S(1)}, f32[2,512,512]{1,2,0:T(8,128)}) fusion(f32[2,512,512]{2,1,0:T(8,128)S(1)} %fusion.8, f32[2,512]{1,0:T(2,128)S(1)} %get-tuple-element.18, f32[2,512]{1,0:T(2,128)S(1)} %get-tuple-element.17, f32[2,512,512]{2,1,0:T(8,128)S(1)} %fusion, f32[2,512,512]{2,1,0:T(8,128)S(1)} %get-tuple-element.5), kind=kOutput, calls=%fused_computation.8 | convolution fusion | flops 3228565504 | bytes 10493952 | tf_op jit(solution)/shard_map/kb,rbc->rkc/dot_general | solution.py:34
  374.5 5.9 %all-to-all-start.7 = ((f32[2,512,512]{2,0,1:T(2,128)}), f32[2,512,512]{2,0,1:T(2,128)S(1)}, u32[]{:S(2)}, u32[]{:S(2)}) async-start(f32[2,512,512]{2,0,1:T(2,128)} %copy.112), calls=%async_computation.7 | async-start | bytes 4194304 | tf_op jit(solution)/shard_map/all_to_all | solution.py:98
  380.4 4.1 copy.109
  384.6 43.1 %all-to-all-done.7 = f32[2,512,512]{2,0,1:T(2,128)S(1)} async-done(((f32[2,512,512]{2,0,1:T(2,128)}), f32[2,512,512]{2,0,1:T(2,128)S(1)}, u32[]{:S(2)}, u32[]{:S(2)}) %all-to-all-start.7) | async-done | bytes 2097184 | tf_op jit(solution)/shard_map/all_to_all | solution.py:98
  427.6 4.6 all-to-all-start.6
  438.3 41.7 %all-to-all-done.6 = f32[2,512,512]{2,0,1:T(2,128)} async-done(((f32[2,512,512]{2,0,1:T(2,128)}), f32[2,512,512]{2,0,1:T(2,128)}, u32[]{:S(2)}, u32[]{:S(2)}) %all-to-all-start.6) | async-done | bytes 2097184 | tf_op jit(solution)/shard_map/all_to_all | solution.py:97
  493.2 29.3 %all_to_all.141 = f32[8,64,512]{2,1,0:T(8,128)S(1)} all-to-all(f32[8,64,512]{2,1,0:T(8,128)S(1)} %copy.115), channel_id=1, replica_groups=mesh['segment'=4,'ctx'=8] {'ctx'}, dimensions={0} | all-to-all | bytes 2097152 | tf_op jit(solution)/shard_map/all_to_all | solution.py:105
  523.0 8.6 %collective-permute-done = bf16[1,512,512]{2,1,0:T(8,128)(2,1)S(1)} collective-permute-done((bf16[1,512,512]{2,1,0:T(8,128)(2,1)S(1)}, bf16[1,512,512]{2,1,0:T(8,128)(2,1)S(1)}, u32[]{:S(2)}, u32[]{:S(2)}) %collective-permute-start) | collective-permute-done | bytes 524320 | tf_op jit(solution)/shard_map/ppermute | solution.py:14
  (56 shorter events, 54.2 us)
Async XLA Ops:
  1.4 9.4 %copy-start.8 = (bf16[1,512,512]{2,1,0:T(8,128)(2,1)S(1)}, bf16[1,512,512]{2,1,0:T(8,128)(2,1)}, u32[]{:S(2)}) copy-start(bf16[1,512,512]{2,1,0:T(8,128)(2,1)} %param.8) | copy-start | bytes 1572868
  3.4 33.0 %all-to-all-start = ((f32[1,512,512]{2,0,1:T(1,128)}), f32[1,512,512]{2,0,1:T(1,128)S(1)}, u32[]{:S(2)}, u32[]{:S(2)}) async-start(f32[1,512,512]{2,0,1:T(1,128)} %copy.87), calls=%async_computation | async-start | bytes 2097152 | tf_op jit(solution)/shard_map/all_to_all | solution.py:51
  36.5 29.7 %all-to-all-start.3 = ((f32[1,512,512]{2,0,1:T(1,128)}), f32[1,512,512]{2,0,1:T(1,128)S(1)}, u32[]{:S(2)}, u32[]{:S(2)}) async-start(f32[1,512,512]{2,0,1:T(1,128)} %copy.96), calls=%async_computation.3 | async-start | bytes 2097152 | tf_op jit(solution)/shard_map/all_to_all | solution.py:54
  66.2 2.3 copy-start.4
  66.2 2.2 copy-start.3
  77.5 52.2 %all-to-all-start.5 = ((f32[16,64,512]{2,1,0:T(8,128)}), f32[16,64,512]{2,1,0:T(8,128)}, u32[]{:S(2)}, u32[]{:S(2)}) async-start(f32[16,64,512]{2,1,0:T(8,128)} %copy.102), calls=%async_computation.5 | async-start | bytes 4194304 | tf_op jit(solution)/shard_map/all_to_all | solution.py:89
  129.7 52.2 %all-to-all-start.4 = ((f32[16,64,512]{2,1,0:T(8,128)}), f32[16,64,512]{2,1,0:T(8,128)}, u32[]{:S(2)}, u32[]{:S(2)}) async-start(f32[16,64,512]{2,1,0:T(8,128)} %copy.99), calls=%async_computation.4 | async-start | bytes 4194304 | tf_op jit(solution)/shard_map/all_to_all | solution.py:88
  181.8 52.1 %all-to-all-start.2 = ((f32[16,64,512]{2,1,0:T(8,128)}), f32[16,64,512]{2,1,0:T(8,128)}, u32[]{:S(2)}, u32[]{:S(2)}) async-start(f32[16,64,512]{2,1,0:T(8,128)} %copy.93), calls=%async_computation.2 | async-start | bytes 4194304 | tf_op jit(solution)/shard_map/all_to_all | solution.py:85
  233.9 66.8 %all-to-all-start.1 = ((f32[16,64,512]{2,1,0:T(8,128)}), f32[16,64,512]{2,1,0:T(8,128)}, u32[]{:S(2)}, u32[]{:S(2)}) async-start(f32[16,64,512]{2,1,0:T(8,128)} %copy.90), calls=%async_computation.1 | async-start | bytes 4194304 | tf_op jit(solution)/shard_map/all_to_all | solution.py:84
  244.0 21.9 %copy-start.1 = (f32[2,8,64,512]{3,2,1,0:T(8,128)}, f32[2,8,64,512]{3,2,1,0:T(8,128)S(1)}, u32[]{:S(2)}) copy-start(f32[2,8,64,512]{3,2,1,0:T(8,128)S(1)} %copy.94) | copy-start | bytes 6291460
  302.5 10.9 %copy-start.2 = (f32[2,8,64,512]{3,2,1,0:T(8,128)S(1)}, f32[2,8,64,512]{3,2,1,0:T(8,128)}, u32[]{:S(2)}) copy-start(f32[2,8,64,512]{3,2,1,0:T(8,128)} %copy-done.1) | copy-start | bytes 6291460
  313.4 11.7 %copy-start = (f32[2,512,512]{2,1,0:T(8,128)S(1)}, f32[2,512,512]{2,1,0:T(8,128)}, u32[]{:S(2)}) copy-start(f32[2,512,512]{2,1,0:T(8,128)} %convolution_add_fusion) | copy-start | bytes 6291460
  313.4 11.7 %copy-start.5 = (f32[2,512,512]{2,1,0:T(8,128)S(1)}, f32[2,512,512]{2,1,0:T(8,128)}, u32[]{:S(2)}) copy-start(f32[2,512,512]{2,1,0:T(8,128)} %fusion.30) | copy-start | bytes 6291460
  374.5 53.1 %all-to-all-start.7 = ((f32[2,512,512]{2,0,1:T(2,128)}), f32[2,512,512]{2,0,1:T(2,128)S(1)}, u32[]{:S(2)}, u32[]{:S(2)}) async-start(f32[2,512,512]{2,0,1:T(2,128)} %copy.112), calls=%async_computation.7 | async-start | bytes 4194304 | tf_op jit(solution)/shard_map/all_to_all | solution.py:98
  427.6 52.4 %all-to-all-start.6 = ((f32[2,512,512]{2,0,1:T(2,128)}), f32[2,512,512]{2,0,1:T(2,128)}, u32[]{:S(2)}, u32[]{:S(2)}) async-start(f32[2,512,512]{2,0,1:T(2,128)} %copy.109), calls=%async_computation.6 | async-start | bytes 4194304 | tf_op jit(solution)/shard_map/all_to_all | solution.py:97
  492.6 30.0 %copy-start.6 = (bf16[1,512,512]{2,1,0:T(8,128)(2,1)S(1)}, bf16[1,512,512]{2,1,0:T(8,128)(2,1)}, u32[]{:S(2)}) copy-start(bf16[1,512,512]{2,1,0:T(8,128)(2,1)} %param.7) | copy-start | bytes 1572868
  492.6 30.0 %copy-start.7 = (bf16[1,512,512]{2,1,0:T(8,128)(2,1)S(1)}, bf16[1,512,512]{2,1,0:T(8,128)(2,1)}, u32[]{:S(2)}) copy-start(bf16[1,512,512]{2,1,0:T(8,128)(2,1)} %param.6) | copy-start | bytes 1572868
  492.6 30.0 %copy-start.9 = (bf16[1,512,512]{2,1,0:T(8,128)(2,1)S(1)}, bf16[1,512,512]{2,1,0:T(8,128)(2,1)}, u32[]{:S(2)}) copy-start(bf16[1,512,512]{2,1,0:T(8,128)(2,1)} %param.5) | copy-start | bytes 1572868
  492.6 30.0 %copy-start.10 = (f32[1,512]{1,0:T(1,128)S(1)}, f32[1,512]{1,0:T(1,128)}, u32[]{:S(2)}) copy-start(f32[1,512]{1,0:T(1,128)} %param.9) | copy-start | bytes 6148
  522.9 8.7 %collective-permute-start = (bf16[1,512,512]{2,1,0:T(8,128)(2,1)S(1)}, bf16[1,512,512]{2,1,0:T(8,128)(2,1)S(1)}, u32[]{:S(2)}, u32[]{:S(2)}) collective-permute-start(bf16[1,512,512]{2,1,0:T(8,128)(2,1)S(1)} %fusion.19), channel_id=1, source_target_pairs={{0,8},{8,16},{16,24},{24,0},{1,9},{9,17},{17,25},{25,1},{2,10},{10... | collective-permute-start | bytes 1572872 | tf_op jit(solution)/shard_map/ppermute | solution.py:14
where the time goes:
time: 536 us; the launch traced here: 533 us
  waiting for transfers between devices  268 us (50%)
  matrix products  146 us (27%)
  local copies, waits for them, and re-layouts  47.6 us (9%)
  starting transfers between devices  39.5 us (7%)
  blocking collectives  29.3 us (5%)
    dot_general x12, matrix products, along(): return jnp.einsum('kb,rbc->rkc', table, data, precision=HIGHEST)  126 us
    all_to_all x1, waiting for transfers between devices, on_device(): lax.all_to_all(prod_imag, 'ctx', split_axis=0, concat_axis=1, tiled=True)  45.1 us
    all_to_all x1, waiting for transfers between devices, on_device(): lax.all_to_all(taps_imag, 'ctx', split_axis=0, concat_axis=1, tiled=True)  43.6 us
    all_to_all x1, waiting for transfers between devices, on_device(): lax.all_to_all(taps_real, 'ctx', split_axis=0, concat_axis=1, tiled=True)  43.2 us
    all_to_all x1, waiting for transfers between devices, on_device(): lax.all_to_all(spec_imag, 'ctx', split_axis=1, concat_axis=0, tiled=True)  43.1 us
    all_to_all x1, waiting for transfers between devices, on_device(): lax.all_to_all(spec_real, 'ctx', split_axis=1, concat_axis=0, tiled=True)  41.7 us
    all_to_all x1, blocking collectives, on_device(): lax.all_to_all(by_block, 'ctx', split_axis=0, concat_axis=1, tiled=True)[0]  29.3 us
    all_to_all x1, waiting for transfers between devices, on_device(): lax.all_to_all(product.reshape(1, length, channels), 'ctx', split_axis=1,...  23.9 us
  transfers between devices with their start and end apart: 9, of which 8 were waited for; matrix products, arithmetic and copies ran while one was open for 17% of the time, Pallas kernels for 0%

commit v1 on v0

--- a/solution.py
+++ b/solution.py
@@ -1,11 +1,21 @@
+import functools
 import math
 
 import jax
 import jax.numpy as jnp
+import numpy as np
 from jax import lax
+from jax.experimental import pallas as pl
+from jax.experimental.pallas import tpu as pltpu
 from jax.sharding import PartitionSpec as P
 
 HIGHEST = lax.Precision.HIGHEST
+LANES = 128
+HALF = 64
+INNER = 64
+STEP = 8
+F32 = jnp.float32
+BF16 = jnp.bfloat16
 
 
 def from_behind(value, axis, steps):
@@ -38,7 +48,7 @@
     return (real_part * cosine + imag_part * sine, imag_part * cosine - real_part * sine)
 
 
-def on_device(query_stream, key_stream, value_stream, filter_taps, skip_weight):
+def general_on_device(query_stream, key_stream, value_stream, filter_taps, skip_weight):
     parts = lax.axis_size("ctx")
     device = lax.axis_index("ctx")
     length = query_stream.shape[1]
@@ -108,6 +118,250 @@
     return from_behind(gated, "segment", 1)
 
 
+def split_two(value):
+    high = value.astype(BF16)
+    return high, (value - high.astype(F32)).astype(BF16)
+
+
+def split_table(table):
+    table = table.astype(np.float32)
+    high = table.astype(jnp.bfloat16)
+    low = (table - high.astype(np.float32)).astype(jnp.bfloat16)
+    return np.concatenate([high, high, low], axis=1)
+
+
+def stacked(value):
+    high, low = split_two(value)
+    return jnp.concatenate([high, low, high], axis=0)
+
+
+def lower_half(shape):
+    return lax.broadcasted_iota(jnp.int32, shape, len(shape) - 1) < HALF
+
+
+def swap_halves(value):
+    return pltpu.roll(value, HALF, value.ndim - 1)
+
+
+def tables(outer):
+    total = outer * INNER
+    a = np.arange(outer)
+    b = np.arange(INNER)
+    c = np.arange(outer) + 0.25
+    first = 2.0 * np.pi * np.outer(c, a) / outer
+    second = 2.0 * np.pi * np.outer(b, b) / INNER
+    forward_a = split_table(np.concatenate([np.cos(first), -np.sin(first)], axis=0))
+    forward_b = split_table(
+        np.block([[np.cos(second), np.sin(second)], [-np.sin(second), np.cos(second)]])
+    )
+    back_b = split_table(np.concatenate([np.cos(second), np.sin(second)], axis=0))
+    back_a = split_table(np.concatenate([np.cos(first).T, -np.sin(first).T], axis=0) / total)
+
+    def turns(steps):
+        theta = 2.0 * np.pi * np.outer(steps, c) / total
+        wide = np.stack([np.cos(theta), np.sin(theta)], axis=1).astype(np.float32)
+        return np.ascontiguousarray(np.broadcast_to(wide[..., None], wide.shape + (LANES,)))
+
+    coarse = turns(np.arange(0, INNER, STEP))
+    fine = turns(np.arange(STEP))
+    return forward_a, forward_b, back_b, back_a, coarse, fine
+
+
+def pack_kernel(parts, k_ref, v_ref, h_ref, q_ref, kvh_ref, q_out_ref):
+    length = k_ref.shape[0]
+    rows = length // 2
+    low = lower_half((rows, LANES))
+
+    def pack(source, place):
+        for e in range(parts // 2):
+            tile = source[:, LANES * e : LANES * (e + 1)].astype(F32)
+            early, late = tile[:rows], tile[rows:]
+            place(2 * e, jnp.where(low, early, swap_halves(late)).astype(BF16))
+            place(2 * e + 1, jnp.where(low, swap_halves(early), late).astype(BF16))
+
+    for n, source in enumerate((k_ref, v_ref, h_ref)):
+
+        def place(d, value, n=n):
+            kvh_ref[d, n * rows : (n + 1) * rows, :] = value
+
+        pack(source, place)
+
+    def place_q(d, value):
+        q_out_ref[d] = value
+
+    pack(q_ref, place_q)
+
+
+def unpack_kernel(parts, g_ref, out_ref):
+    rows = g_ref.shape[1]
+    low = lower_half((rows, LANES))
+    for e in range(parts // 2):
+        even, odd = g_ref[2 * e].astype(F32), g_ref[2 * e + 1].astype(F32)
+        out_ref[:rows, LANES * e : LANES * (e + 1)] = jnp.where(low, even, swap_halves(odd)).astype(BF16)
+        out_ref[rows:, LANES * e : LANES * (e + 1)] = jnp.where(low, swap_halves(even), odd).astype(BF16)
+
+
+def convolve_kernel(
+    parts, outer, kvh_ref, fa_ref, fb_ref, bb_ref, ba_ref, coarse_ref, fine_ref, y_ref, x_s, z_s, w_s
+):
+    rows = kvh_ref.shape[1] // 3
+    per = rows // INNER
+    low = lower_half((INNER, LANES))
+    lowc = lower_half((outer, LANES))
+
+    def load(part, carry):
+        for m in range(per):
+            at = m * INNER
+            k = kvh_ref[part, at : at + INNER, :].astype(F32)
+            v = kvh_ref[part, rows + at : rows + at + INNER, :].astype(F32)
+            h = kvh_ref[part, 2 * rows + at : 2 * rows + at + INNER, :].astype(F32)
+            p = k * v
+            a = part * (2 * per) + m
+            x_s[pl.ds(a, INNER, stride=outer), :] = jnp.where(low, p, swap_halves(h))
+            x_s[pl.ds(a + per, INNER, stride=outer), :] = jnp.where(low, swap_halves(p), h)
+        return carry
+
+    lax.fori_loop(0, parts, load, 0)
+
+    def turn(group, n):
+        cos_1, sin_1 = coarse_ref[group, 0], coarse_ref[group, 1]
+        if n == 0:
+            return cos_1, sin_1
+        cos_2, sin_2 = fine_ref[n, 0], fine_ref[n, 1]
+        return cos_1 * cos_2 - sin_1 * sin_2, sin_1 * cos_2 + cos_1 * sin_2
+
+    def forward_outer(group, carry):
+        for n in range(0, STEP, 2):
+            b = group * STEP + n
+            data = jnp.concatenate(
+                [
+                    stacked(x_s[pl.ds(pl.multiple_of((b + j) * outer, outer), outer), :])
+                    for j in range(2)
+                ],
+                axis=1,
+            )
+            both = jnp.dot(fa_ref[...], data, preferred_element_type=F32)
+            for j in range(2):
+                re = both[:outer, LANES * j : LANES * (j + 1)]
+                im = both[outer:, LANES * j : LANES * (j + 1)]
+                cos, sin = turn(group, n + j)
+                z_s[pl.ds(b + j, outer, stride=2 * INNER), :] = re * cos + im * sin
+                z_s[pl.ds(b + j + INNER, outer, stride=2 * INNER), :] = im * cos - re * sin
+        return carry
+
+    lax.fori_loop(0, INNER // STEP, forward_outer, 0)
+
+    def middle(group, carry):
+        for n in range(0, STEP, 2):
+            c = group * STEP + n
+            data = jnp.concatenate(
+                [
+                    stacked(z_s[pl.ds(pl.multiple_of((c + j) * 2 * INNER, 2 * INNER), 2 * INNER), :])
+                    for j in range(2)
+                ],
+                axis=1,
+            )
+            both = jnp.dot(fb_ref[...], data, preferred_element_type=F32)
+            mixed = []
+            for j in range(2):
+                re = both[:INNER, LANES * j : LANES * (j + 1)]
+                im = both[INNER:, LANES * j : LANES * (j + 1)]
+                re_2, im_2 = swap_halves(re), swap_halves(im)
+                mixed.append(
+                    stacked(jnp.where(low, re * re_2 - im * im_2, re * im_2 + im * re_2))
+                )
+            both = jnp.dot(bb_ref[...], jnp.concatenate(mixed, axis=1), preferred_element_type=F32)
+            for j in range(2):
+                straight = both[:INNER, LANES * j : LANES * (j + 1)]
+                crossed = swap_halves(both[INNER:, LANES * j : LANES * (j + 1)])
+                w_s[pl.ds(c + j, INNER, stride=outer), :] = jnp.where(
+                    low, straight - crossed, straight + crossed
+                )
+        return carry
+
+    lax.fori_loop(0, outer // STEP, middle, 0)
+
+    def back_outer(group, carry):
+        for n in range(0, STEP, 2):
+            b = group * STEP + n
+            data = []
+            for j in range(2):
+                value = w_s[pl.ds(pl.multiple_of((b + j) * outer, outer), outer), :]
+                cos, sin = turn(group, n + j)
+                other = swap_halves(value) * sin
+                straight = value * cos
+                data.append(stacked(jnp.where(lowc, straight - other, straight + other)))
+            both = jnp.dot(ba_ref[...], jnp.concatenate(data, axis=1), preferred_element_type=F32)
+            for j in range(2):
+                re = both[:outer, LANES * j : LANES * (j + 1)]
+                im = both[outer:, LANES * j : LANES * (j + 1)]
+                y_ref[pl.ds(b + j, outer, stride=INNER), :] = re + swap_halves(im)
+        return carry
+
+    lax.fori_loop(0, INNER // STEP, back_outer, 0)
+
+
+def gate_kernel(parts, y_ref, kvh_ref, q_ref, skip_ref, g_ref):
+    rows = q_ref.shape[1]
+    low = lower_half((rows, LANES))
+
+    def one(part, carry):
+        at = pl.multiple_of(part * 2 * rows, 2 * rows)
+        early = y_ref[pl.ds(at, rows), :]
+        late = y_ref[pl.ds(at + rows, rows), :]
+        y = jnp.where(low, early, swap_halves(late))
+        p = kvh_ref[part, :rows, :].astype(F32) * kvh_ref[part, rows : 2 * rows, :].astype(F32)
+        g_ref[part] = (q_ref[part].astype(F32) * (y + skip_ref[...] * p)).astype(BF16)
+        return carry
+
+    lax.fori_loop(0, parts, one, 0)
+
+
+def fast_on_device(query_stream, key_stream, value_stream, filter_taps, skip_weight):
+    parts = lax.axis_size("ctx")
+    device = lax.axis_index("ctx")
+    length, channels = query_stream.shape[1:]
+    rows = length // 2
+    outer = parts * length // INNER
+    kvh, q = pl.pallas_call(
+        functools.partial(pack_kernel, parts),
+        out_shape=(
+            jax.ShapeDtypeStruct((parts, 3 * rows, LANES), BF16),
+            jax.ShapeDtypeStruct((parts, rows, LANES), BF16),
+        ),
+    )(key_stream[0], value_stream[0], filter_taps[0], query_stream[0])
+
+    def spread(value):
+        return lax.all_to_all(value, "ctx", split_axis=0, concat_axis=0, tiled=True)
+
+    kvh = spread(kvh)
+    q = spread(q)
+    consts = [jnp.asarray(t) for t in tables(outer)]
+    y = pl.pallas_call(
+        functools.partial(convolve_kernel, parts, outer),
+        out_shape=jax.ShapeDtypeStruct((parts * length, LANES), F32),
+        scratch_shapes=[
+            pltpu.VMEM((outer * INNER, LANES), F32),
+            pltpu.VMEM((2 * outer * INNER, LANES), F32),
+            pltpu.VMEM((outer * INNER, LANES), F32),
+        ],
+        compiler_params=pltpu.CompilerParams(vmem_limit_bytes=40 * 2**20),
+    )(kvh, *consts)
+    skip = lax.dynamic_slice(skip_weight, (0, device * HALF), (1, HALF))
+    g = pl.pallas_call(
+        functools.partial(gate_kernel, parts),
+        out_shape=jax.ShapeDtypeStruct((parts, rows, LANES), BF16),
+        compiler_params=pltpu.CompilerParams(vmem_limit_bytes=40 * 2**20),
+    )(y, kvh, q, jnp.concatenate([skip, skip], axis=1))
+    g = spread(g)
+    g = from_behind(g, "segment", 1)
+    out = pl.pallas_call(
+        functools.partial(unpack_kernel, parts),
+        out_shape=jax.ShapeDtypeStruct((length, channels), BF16),
+    )(g)
+    return out[None]
+
+
 def solution(mesh):
     placed = (
         P("segment", "ctx", None),
@@ -116,6 +370,14 @@
         P("segment", "ctx", None),
         P("segment", None),
     )
+
+    def on_device(*arrays):
+        parts = lax.axis_size("ctx")
+        length, channels = arrays[0].shape[1:]
+        small = parts * length <= 4096 and length % (2 * INNER) == 0 and parts % 2 == 0
+        run = fast_on_device if small and channels == parts * HALF else general_on_device
+        return run(*arrays)
+
     return jax.shard_map(
         on_device, mesh=mesh, in_specs=placed, out_specs=P("segment", "ctx", None), check_vma=False
     )

time: 536 us -> 110 us (0.21)
  waiting for transfers between devices: 268 us -> 8.61 us
  matrix products: 146 us -> 0 us
  local copies, waits for them, and re-layouts: 47.6 us -> 3.82 us
  starting transfers between devices: 39.5 us -> 3.59 us
  blocking collectives: 29.3 us -> 63.8 us
  Pallas kernels: 0 us -> 29.5 us
    all_to_all x8 -> x1, waiting for transfers between devices: 259 us -> 0.01 us  [spread(): return lax.all_to_all(value, 'ctx', split_axis=0, concat_axis=0, tiled=True)]
    dot_general x18 -> x0, matrix products: 146 us -> none  [the longest x12 126 us: along(): return jnp.einsum('kb,rbc->rkc', table, data, precision=HIGHEST)]
    all_to_all x8 -> x1, starting transfers between devices: 39.4 us -> 3.59 us  [spread(): return lax.all_to_all(value, 'ctx', split_axis=0, concat_axis=0, tiled=True)]
    all_to_all x1 -> x2, blocking collectives: 29.3 us -> 63.8 us  [spread(): return lax.all_to_all(value, 'ctx', split_axis=0, concat_axis=0, tiled=True)]
    pallas_call x0 -> x4, Pallas kernels: none -> 29.5 us  [the longest x1 23.2 us: fast_on_device(): pl.pallas_call(functools.partial(convolve_kernel, parts, outer), out_shap...]
    all_to_all x10 -> x0, local copies, waits for them, and re-layouts: 22 us -> none  [the longest x3 8.62 us: on_device(): lax.all_to_all(spec_real, 'ctx', split_axis=1, concat_axis=0, tiled=True)]
    add x3 -> x0, local copies, waits for them, and re-layouts: 10.9 us -> none  [rotate(): real_part * cosine + imag_part * sine]
    sub x3 -> x0, local copies, waits for them, and re-layouts: 9.2 us -> none  [rotate(): imag_part * cosine - real_part * sine]
  transfers between devices with their start and end apart: 9 -> 2, of which waited for: 8 -> 1; matrix products, arithmetic and copies ran while one was open for 17% -> 0% of each run, Pallas kernels for 0% -> 21%
where the time goes in v1:
time: 110 us; the launch traced here: 109 us
  blocking collectives  63.8 us (58%)
  Pallas kernels  29.5 us (27%)
  waiting for transfers between devices  8.61 us (8%)
  local copies, waits for them, and re-layouts  3.82 us (3%)
  starting transfers between devices  3.59 us (3%)
    all_to_all x2, blocking collectives, spread(): return lax.all_to_all(value, 'ctx', split_axis=0, concat_axis=0, tiled=True)  63.8 us
    pallas_call x1, Pallas kernels, fast_on_device(): pl.pallas_call(functools.partial(convolve_kernel, parts, outer), out_shap...  23.2 us
    ppermute x1, waiting for transfers between devices, from_behind(): return lax.ppermute(value, axis, pairs)  8.6 us
    unnamed x20, local copies, waits for them, and re-layouts  3.74 us
    all_to_all x1, starting transfers between devices, spread(): return lax.all_to_all(value, 'ctx', split_axis=0, concat_axis=0, tiled=True)  3.59 us
    pallas_call x1, Pallas kernels, fast_on_device(): pl.pallas_call(functools.partial(pack_kernel, parts), out_shape=(jax.Shap...  3.44 us
  transfers between devices with their start and end apart: 2, of which 1 were waited for; matrix products, arithmetic and copies ran while one was open for 0% of the time, Pallas kernels for 21%

profile of v1, /device:TPU:0, one launch (start us, length us, event | category | flops | bytes accessed | tf_op | source)
XLA Modules:
  0.0 109.5 jit_solution(14770279207377572135)
XLA Ops:
  0.0 0.0 copy-start
  0.0 3.4 %shard_map.109 = (bf16[8,768,128]{2,1,0:T(8,128)(2,1)}, bf16[8,256,128]{2,1,0:T(8,128)(2,1)}) custom-call(bf16[512,512]{1,0:T(8,128)(2,1)} %bitcast.5, bf16[512,512]{1,0:T(8,128)(2,1)} %bitcast.6, bf16[512,512]{1,0:T(8,128)(2,1)} %bitcast.7, bf16[512,512]{1,0:T(8,128)(2,1)} %bitcast.8), custom_call_target="tpu_custom_call" | custom-call | tf_op jit(solution)/shard_map/pallas_call | solution.py:326
  3.4 0.0 copy-start.3
  3.4 0.0 copy-start.4
  3.4 0.0 copy-start.5
  3.5 0.0 copy-start.6
  3.5 0.0 copy-start.7
  3.5 0.0 copy-start.8
  3.5 44.4 %all_to_all.15.kvh_ref = bf16[8,768,128]{2,1,0:T(8,128)(2,1)S(1)} all-to-all(bf16[8,768,128]{2,1,0:T(8,128)(2,1)} %get-tuple-element.7), channel_id=1, replica_groups=mesh['segment'=4,'ctx'=8] {'ctx'}, dimensions={0} | all-to-all | bytes 3145728 | tf_op jit(solution)/shard_map/all_to_all | solution.py:335
  47.9 3.6 %all-to-all-start.1 = ((bf16[8,256,128]{2,1,0:T(8,128)(2,1)}), bf16[8,256,128]{2,1,0:T(8,128)(2,1)S(1)}, u32[]{:S(2)}, u32[]{:S(2)}) async-start(bf16[8,256,128]{2,1,0:T(8,128)(2,1)} %get-tuple-element.8), calls=%async_computation.1 | async-start | bytes 1048576 | tf_op jit(solution)/shard_map/all_to_all | solution.py:335
  51.5 0.0 copy-done
  51.5 0.1 constant_dynamic-slice_fusion
  51.6 0.1 pad_maximum_fusion.skip_ref
  51.7 0.0 copy-done.3
  51.7 0.0 copy-done.4
  51.7 0.0 copy-done.5
  51.7 0.0 copy-done.6
  51.7 0.0 copy-done.7
  51.7 0.0 copy-done.8
  51.7 23.2 %shard_map.110.y_ref = f32[4096,128]{1,0:T(8,128)S(1)} custom-call(bf16[8,768,128]{2,1,0:T(8,128)(2,1)S(1)} %all_to_all.15.kvh_ref, bf16[128,192]{1,0:T(8,128)(2,1)S(1)} %copy-done.8, bf16[128,384]{1,0:T(8,128)(2,1)S(1)} %copy-done.5, bf16[128,192]{1,0:T(8,128)(2,1)S(1)} %copy-done.7, bf16[128,192]{1,0:T(8,128)(2,1)S(1)} %copy-done.6, ...), custom_call_target="tpu_custom_call" | custom-call | tf_op jit(solution)/shard_map/pallas_call | solution.py:340
  74.9 0.0 copy-start.1
  74.9 1.3 %copy-done.1 = f32[4096,128]{1,0:T(8,128)} copy-done((f32[4096,128]{1,0:T(8,128)}, f32[4096,128]{1,0:T(8,128)S(1)}, u32[]{:S(2)}) %copy-start.1) | copy-done | bytes 2097176
  76.2 0.0 all-to-all-done.1.q_ref
  76.2 0.0 copy-start.2
  76.2 1.6 %copy-done.2 = f32[4096,128]{1,0:T(8,128)S(1)} copy-done((f32[4096,128]{1,0:T(8,128)S(1)}, f32[4096,128]{1,0:T(8,128)}, u32[]{:S(2)}) %copy-start.2) | copy-done | bytes 2097176
  77.8 0.8 shard_map.111
  78.7 19.4 %all_to_all.16 = bf16[8,256,128]{2,1,0:T(8,128)(2,1)S(1)} all-to-all(bf16[8,256,128]{2,1,0:T(8,128)(2,1)S(1)} %shard_map.111), channel_id=1, replica_groups=mesh['segment'=4,'ctx'=8] {'ctx'}, dimensions={0} | all-to-all | bytes 1048576 | tf_op jit(solution)/shard_map/all_to_all | solution.py:335
  98.0 0.0 collective-permute-start
  98.0 8.6 %collective-permute-done.g_ref = bf16[8,256,128]{2,1,0:T(8,128)(2,1)S(1)} collective-permute-done((bf16[8,256,128]{2,1,0:T(8,128)(2,1)S(1)}, bf16[8,256,128]{2,1,0:T(8,128)(2,1)S(1)}, u32[]{:S(2)}, u32[]{:S(2)}) %collective-permute-start) | collective-permute-done | bytes 524320 | tf_op jit(solution)/shard_map/ppermute | solution.py:24
  106.6 0.0 copy-start.9
  106.6 0.8 copy-done.9
  107.4 2.1 %shard_map.112 = bf16[512,512]{1,0:T(8,128)(2,1)} custom-call(bf16[8,256,128]{2,1,0:T(8,128)(2,1)} %copy-done.9), custom_call_target="tpu_custom_call" | custom-call | tf_op jit(solution)/shard_map/pallas_call | solution.py:358
Async XLA Ops:
  0.0 51.5 %copy-start = (f32[1,512]{1,0:T(1,128)S(1)}, f32[1,512]{1,0:T(1,128)}, u32[]{:S(2)}) copy-start(f32[1,512]{1,0:T(1,128)} %param.15) | copy-start | bytes 6148
  3.4 48.2 %copy-start.3 = (f32[8,2,64,128]{3,2,1,0:T(8,128)S(1)}, f32[8,2,64,128]{3,2,1,0:T(8,128)}, u32[]{:S(2)}) copy-start(f32[8,2,64,128]{3,2,1,0:T(8,128)} %constant.27.clone.fine_ref) | copy-start | bytes 1572868
  3.4 48.2 %copy-start.4 = (f32[8,2,64,128]{3,2,1,0:T(8,128)S(1)}, f32[8,2,64,128]{3,2,1,0:T(8,128)}, u32[]{:S(2)}) copy-start(f32[8,2,64,128]{3,2,1,0:T(8,128)} %constant.26.clone.coarse_ref) | copy-start | bytes 1572868
  3.4 48.2 %copy-start.5 = (bf16[128,384]{1,0:T(8,128)(2,1)S(1)}, bf16[128,384]{1,0:T(8,128)(2,1)}, u32[]{:S(2)}) copy-start(bf16[128,384]{1,0:T(8,128)(2,1)} %constant.23.clone.fb_ref) | copy-start | bytes 294916
  3.5 48.2 %copy-start.6 = (bf16[128,192]{1,0:T(8,128)(2,1)S(1)}, bf16[128,192]{1,0:T(8,128)(2,1)}, u32[]{:S(2)}) copy-start(bf16[128,192]{1,0:T(8,128)(2,1)} %constant.25.clone.ba_ref) | copy-start | bytes 147460
  3.5 48.2 %copy-start.7 = (bf16[128,192]{1,0:T(8,128)(2,1)S(1)}, bf16[128,192]{1,0:T(8,128)(2,1)}, u32[]{:S(2)}) copy-start(bf16[128,192]{1,0:T(8,128)(2,1)} %constant.24.clone.bb_ref) | copy-start | bytes 147460
  3.5 48.2 %copy-start.8 = (bf16[128,192]{1,0:T(8,128)(2,1)S(1)}, bf16[128,192]{1,0:T(8,128)(2,1)}, u32[]{:S(2)}) copy-start(bf16[128,192]{1,0:T(8,128)(2,1)} %constant.22.clone.fa_ref) | copy-start | bytes 147460
  47.9 28.3 %all-to-all-start.1 = ((bf16[8,256,128]{2,1,0:T(8,128)(2,1)}), bf16[8,256,128]{2,1,0:T(8,128)(2,1)S(1)}, u32[]{:S(2)}, u32[]{:S(2)}) async-start(bf16[8,256,128]{2,1,0:T(8,128)(2,1)} %get-tuple-element.8), calls=%async_computation.1 | async-start | bytes 1048576 | tf_op jit(solution)/shard_map/all_to_all | solution.py:335
  74.9 1.3 %copy-start.1 = (f32[4096,128]{1,0:T(8,128)}, f32[4096,128]{1,0:T(8,128)S(1)}, u32[]{:S(2)}) copy-start(f32[4096,128]{1,0:T(8,128)S(1)} %shard_map.110.y_ref) | copy-start | bytes 6291460
  76.2 1.6 %copy-start.2 = (f32[4096,128]{1,0:T(8,128)S(1)}, f32[4096,128]{1,0:T(8,128)}, u32[]{:S(2)}) copy-start(f32[4096,128]{1,0:T(8,128)} %copy-done.1) | copy-start | bytes 6291460
  98.0 8.6 %collective-permute-start = (bf16[8,256,128]{2,1,0:T(8,128)(2,1)S(1)}, bf16[8,256,128]{2,1,0:T(8,128)(2,1)S(1)}, u32[]{:S(2)}, u32[]{:S(2)}) collective-permute-start(bf16[8,256,128]{2,1,0:T(8,128)(2,1)S(1)} %all_to_all.16), channel_id=1, source_target_pairs={{0,8},{8,16},{16,24},{24,0},{1,9},{9,17},{17,25},{25,1},{2,10},{10... | collective-permute-start | bytes 1572872 | tf_op jit(solution)/shard_map/ppermute | solution.py:24
  106.6 0.8 copy-start.9

commit v2 on v1

--- a/solution.py
+++ b/solution.py
@@ -13,7 +13,8 @@
 LANES = 128
 HALF = 64
 INNER = 64
-STEP = 8
+STEP = 16
+WIDE = 16
 F32 = jnp.float32
 BF16 = jnp.bfloat16
 
@@ -167,61 +168,71 @@
     return forward_a, forward_b, back_b, back_a, coarse, fine
 
 
-def pack_kernel(parts, k_ref, v_ref, h_ref, q_ref, kvh_ref, q_out_ref):
-    length = k_ref.shape[0]
-    rows = length // 2
+def pack(parts, source, low, place):
+    rows = source.shape[0] // 2
+    for e in range(parts // 2):
+        tile = source[:, LANES * e : LANES * (e + 1)].astype(F32)
+        early, late = tile[:rows], tile[rows:]
+        place(2 * e, jnp.where(low, early, swap_halves(late)).astype(BF16))
+        place(2 * e + 1, jnp.where(low, swap_halves(early), late).astype(BF16))
+
+
+def pack_kernel(parts, index_ref, k_ref, v_ref, h_ref, *refs):
+    outs, held = refs[:-1], refs[-1]
+    rows = k_ref.shape[0] // 2
     low = lower_half((rows, LANES))
-
-    def pack(source, place):
-        for e in range(parts // 2):
-            tile = source[:, LANES * e : LANES * (e + 1)].astype(F32)
-            early, late = tile[:rows], tile[rows:]
-            place(2 * e, jnp.where(low, early, swap_halves(late)).astype(BF16))
-            place(2 * e + 1, jnp.where(low, swap_halves(early), late).astype(BF16))
-
     for n, source in enumerate((k_ref, v_ref, h_ref)):
 
         def place(d, value, n=n):
-            kvh_ref[d, n * rows : (n + 1) * rows, :] = value
-
-        pack(source, place)
-
-    def place_q(d, value):
-        q_out_ref[d] = value
-
-    pack(q_ref, place_q)
-
-
-def unpack_kernel(parts, g_ref, out_ref):
-    rows = g_ref.shape[1]
+            held[d, n * rows : (n + 1) * rows, :] = value
+
+        pack(parts, source, low, place)
+    for n, out in enumerate(outs):
+        out[...] = held[lax.rem(index_ref[0] + n, parts)]
+
+
+def pack_gate_kernel(parts, q_ref, out_ref):
+    low = lower_half((q_ref.shape[0] // 2, LANES))
+
+    def place(d, value):
+        out_ref[d] = value
+
+    pack(parts, q_ref, low, place)
+
+
+def unpack_kernel(parts, index_ref, *refs):
+    blocks, out_ref, held = refs[:parts], refs[parts], refs[parts + 1]
+    rows = held.shape[1]
     low = lower_half((rows, LANES))
+    for n, block in enumerate(blocks):
+        held[lax.rem(index_ref[0] + n, parts)] = block[...]
     for e in range(parts // 2):
-        even, odd = g_ref[2 * e].astype(F32), g_ref[2 * e + 1].astype(F32)
+        even, odd = held[2 * e].astype(F32), held[2 * e + 1].astype(F32)
         out_ref[:rows, LANES * e : LANES * (e + 1)] = jnp.where(low, even, swap_halves(odd)).astype(BF16)
         out_ref[rows:, LANES * e : LANES * (e + 1)] = jnp.where(low, swap_halves(even), odd).astype(BF16)
 
 
-def convolve_kernel(
-    parts, outer, kvh_ref, fa_ref, fb_ref, bb_ref, ba_ref, coarse_ref, fine_ref, y_ref, x_s, z_s, w_s
-):
-    rows = kvh_ref.shape[1] // 3
+def convolve_kernel(parts, outer, index_ref, *refs):
+    blocks = refs[:parts]
+    skip_ref, fa_ref, fb_ref, bb_ref, ba_ref, coarse_ref, fine_ref, out_ref, x_s, z_s, w_s, y_s = refs[parts:]
+    rows = out_ref.shape[1]
     per = rows // INNER
     low = lower_half((INNER, LANES))
     lowc = lower_half((outer, LANES))
 
-    def load(part, carry):
+    def origin(n):
+        return lax.rem(index_ref[0] + parts - n, parts)
+
+    for n, block in enumerate(blocks):
         for m in range(per):
             at = m * INNER
-            k = kvh_ref[part, at : at + INNER, :].astype(F32)
-            v = kvh_ref[part, rows + at : rows + at + INNER, :].astype(F32)
-            h = kvh_ref[part, 2 * rows + at : 2 * rows + at + INNER, :].astype(F32)
+            k = block[at : at + INNER, :].astype(F32)
+            v = block[rows + at : rows + at + INNER, :].astype(F32)
+            h = block[2 * rows + at : 2 * rows + at + INNER, :].astype(F32)
             p = k * v
-            a = part * (2 * per) + m
+            a = origin(n) * (2 * per) + m
             x_s[pl.ds(a, INNER, stride=outer), :] = jnp.where(low, p, swap_halves(h))
             x_s[pl.ds(a + per, INNER, stride=outer), :] = jnp.where(low, swap_halves(p), h)
-        return carry
-
-    lax.fori_loop(0, parts, load, 0)
 
     def turn(group, n):
         cos_1, sin_1 = coarse_ref[group, 0], coarse_ref[group, 1]
@@ -231,17 +242,17 @@
         return cos_1 * cos_2 - sin_1 * sin_2, sin_1 * cos_2 + cos_1 * sin_2
 
     def forward_outer(group, carry):
-        for n in range(0, STEP, 2):
+        for n in range(0, STEP, WIDE):
             b = group * STEP + n
             data = jnp.concatenate(
                 [
                     stacked(x_s[pl.ds(pl.multiple_of((b + j) * outer, outer), outer), :])
-                    for j in range(2)
+                    for j in range(WIDE)
                 ],
                 axis=1,
             )
             both = jnp.dot(fa_ref[...], data, preferred_element_type=F32)
-            for j in range(2):
+            for j in range(WIDE):
                 re = both[:outer, LANES * j : LANES * (j + 1)]
                 im = both[outer:, LANES * j : LANES * (j + 1)]
                 cos, sin = turn(group, n + j)
@@ -252,18 +263,18 @@
     lax.fori_loop(0, INNER // STEP, forward_outer, 0)
 
     def middle(group, carry):
-        for n in range(0, STEP, 2):
+        for n in range(0, STEP, WIDE):
             c = group * STEP + n
             data = jnp.concatenate(
                 [
                     stacked(z_s[pl.ds(pl.multiple_of((c + j) * 2 * INNER, 2 * INNER), 2 * INNER), :])
-                    for j in range(2)
+                    for j in range(WIDE)
                 ],
                 axis=1,
             )
             both = jnp.dot(fb_ref[...], data, preferred_element_type=F32)
             mixed = []
-            for j in range(2):
+            for j in range(WIDE):
                 re = both[:INNER, LANES * j : LANES * (j + 1)]
                 im = both[INNER:, LANES * j : LANES * (j + 1)]
                 re_2, im_2 = swap_halves(re), swap_halves(im)
@@ -271,7 +282,7 @@
                     stacked(jnp.where(low, re * re_2 - im * im_2, re * im_2 + im * re_2))
                 )
             both = jnp.dot(bb_ref[...], jnp.concatenate(mixed, axis=1), preferred_element_type=F32)
-            for j in range(2):
+            for j in range(WIDE):
                 straight = both[:INNER, LANES * j : LANES * (j + 1)]
                 crossed = swap_halves(both[INNER:, LANES * j : LANES * (j + 1)])
                 w_s[pl.ds(c + j, INNER, stride=outer), :] = jnp.where(
@@ -282,39 +293,47 @@
     lax.fori_loop(0, outer // STEP, middle, 0)
 
     def back_outer(group, carry):
-        for n in range(0, STEP, 2):
+        for n in range(0, STEP, WIDE):
             b = group * STEP + n
             data = []
-            for j in range(2):
+            for j in range(WIDE):
                 value = w_s[pl.ds(pl.multiple_of((b + j) * outer, outer), outer), :]
                 cos, sin = turn(group, n + j)
                 other = swap_halves(value) * sin
                 straight = value * cos
                 data.append(stacked(jnp.where(lowc, straight - other, straight + other)))
             both = jnp.dot(ba_ref[...], jnp.concatenate(data, axis=1), preferred_element_type=F32)
-            for j in range(2):
+            for j in range(WIDE):
                 re = both[:outer, LANES * j : LANES * (j + 1)]
                 im = both[outer:, LANES * j : LANES * (j + 1)]
-                y_ref[pl.ds(b + j, outer, stride=INNER), :] = re + swap_halves(im)
+                y_s[pl.ds(b + j, outer, stride=INNER), :] = re + swap_halves(im)
         return carry
 
     lax.fori_loop(0, INNER // STEP, back_outer, 0)
 
-
-def gate_kernel(parts, y_ref, kvh_ref, q_ref, skip_ref, g_ref):
-    rows = q_ref.shape[1]
-    low = lower_half((rows, LANES))
-
-    def one(part, carry):
-        at = pl.multiple_of(part * 2 * rows, 2 * rows)
-        early = y_ref[pl.ds(at, rows), :]
-        late = y_ref[pl.ds(at + rows, rows), :]
-        y = jnp.where(low, early, swap_halves(late))
-        p = kvh_ref[part, :rows, :].astype(F32) * kvh_ref[part, rows : 2 * rows, :].astype(F32)
-        g_ref[part] = (q_ref[part].astype(F32) * (y + skip_ref[...] * p)).astype(BF16)
-        return carry
-
-    lax.fori_loop(0, parts, one, 0)
+    lowr = lower_half((rows, LANES))
+    for n, block in enumerate(blocks):
+        at = pl.multiple_of(origin(n) * 2 * rows, 2 * rows)
+        early = y_s[pl.ds(at, rows), :]
+        late = y_s[pl.ds(at + rows, rows), :]
+        p = block[:rows, :].astype(F32) * block[rows : 2 * rows, :].astype(F32)
+        out_ref[n] = jnp.where(lowr, early, swap_halves(late)) + skip_ref[...] * p
+
+
+def gate_kernel(parts, index_ref, y_ref, q_ref, *outs):
+    for n, out in enumerate(outs):
+        q = q_ref[lax.rem(index_ref[0] + parts - n, parts)]
+        out[...] = (q.astype(F32) * y_ref[n]).astype(BF16)
+
+
+def joint_shift(value, segment_step, ctx_step):
+    segments, parts = lax.axis_size("segment"), lax.axis_size("ctx")
+    pairs = [
+        (s * parts + c, (s + segment_step) % segments * parts + (c + ctx_step) % parts)
+        for s in range(segments)
+        for c in range(parts)
+    ]
+    return lax.ppermute(value, ("segment", "ctx"), pairs)
 
 
 def fast_on_device(query_stream, key_stream, value_stream, filter_taps, skip_weight):
@@ -323,42 +342,57 @@
     length, channels = query_stream.shape[1:]
     rows = length // 2
     outer = parts * length // INNER
-    kvh, q = pl.pallas_call(
+    index = jnp.full((1,), device, jnp.int32)
+    scalar = pl.BlockSpec(memory_space=pltpu.SMEM)
+    whole = pl.BlockSpec(memory_space=pltpu.VMEM)
+    small = pltpu.CompilerParams(vmem_limit_bytes=24 * 2**20)
+
+    def block(*shape, dtype=BF16):
+        return jax.ShapeDtypeStruct(shape, dtype)
+
+    sent = pl.pallas_call(
         functools.partial(pack_kernel, parts),
-        out_shape=(
-            jax.ShapeDtypeStruct((parts, 3 * rows, LANES), BF16),
-            jax.ShapeDtypeStruct((parts, rows, LANES), BF16),
-        ),
-    )(key_stream[0], value_stream[0], filter_taps[0], query_stream[0])
-
-    def spread(value):
-        return lax.all_to_all(value, "ctx", split_axis=0, concat_axis=0, tiled=True)
-
-    kvh = spread(kvh)
-    q = spread(q)
+        out_shape=(block(3 * rows, LANES),) * parts,
+        in_specs=[scalar, whole, whole, whole],
+        scratch_shapes=[pltpu.VMEM((parts, 3 * rows, LANES), BF16)],
+        compiler_params=small,
+    )(index, key_stream[0], value_stream[0], filter_taps[0])
+    slabs = [sent[0]] + [joint_shift(sent[n], 0, n) for n in range(1, parts)]
+    q = pl.pallas_call(
+        functools.partial(pack_gate_kernel, parts),
+        out_shape=block(parts, rows, LANES),
+        compiler_params=small,
+    )(query_stream[0])
+    q, *_ = lax.optimization_barrier((q, *slabs))
+    q = lax.all_to_all(q, "ctx", split_axis=0, concat_axis=0, tiled=True)
+    skip = lax.dynamic_slice(skip_weight, (0, device * HALF), (1, HALF))
     consts = [jnp.asarray(t) for t in tables(outer)]
     y = pl.pallas_call(
         functools.partial(convolve_kernel, parts, outer),
-        out_shape=jax.ShapeDtypeStruct((parts * length, LANES), F32),
+        out_shape=block(parts, rows, LANES, dtype=F32),
+        in_specs=[scalar] + [whole] * (parts + 1 + len(consts)),
         scratch_shapes=[
             pltpu.VMEM((outer * INNER, LANES), F32),
             pltpu.VMEM((2 * outer * INNER, LANES), F32),
             pltpu.VMEM((outer * INNER, LANES), F32),
+            pltpu.VMEM((outer * INNER, LANES), F32),
         ],
         compiler_params=pltpu.CompilerParams(vmem_limit_bytes=40 * 2**20),
-    )(kvh, *consts)
-    skip = lax.dynamic_slice(skip_weight, (0, device * HALF), (1, HALF))
-    g = pl.pallas_call(
+    )(index, *slabs, jnp.concatenate([skip, skip], axis=1), *consts)
+    gated = pl.pallas_call(
         functools.partial(gate_kernel, parts),
-        out_shape=jax.ShapeDtypeStruct((parts, rows, LANES), BF16),
-        compiler_params=pltpu.CompilerParams(vmem_limit_bytes=40 * 2**20),
-    )(y, kvh, q, jnp.concatenate([skip, skip], axis=1))
-    g = spread(g)
-    g = from_behind(g, "segment", 1)
+        out_shape=(block(rows, LANES),) * parts,
+        in_specs=[scalar, whole, whole],
+        compiler_params=small,
+    )(index, y, q)
+    gated = [joint_shift(gated[n], 1, -n) for n in range(parts)]
     out = pl.pallas_call(
         functools.partial(unpack_kernel, parts),
-        out_shape=jax.ShapeDtypeStruct((length, channels), BF16),
-    )(g)
+        out_shape=block(length, channels),
+        in_specs=[scalar] + [whole] * parts,
+        scratch_shapes=[pltpu.VMEM((parts, rows, LANES), BF16)],
+        compiler_params=small,
+    )(index, *gated)
     return out[None]
 
 

time: 110 us -> 95.1 us (0.86)
  blocking collectives: 63.8 us -> 0 us
  starting transfers between devices: 3.59 us -> 43.7 us
  Pallas kernels: 29.5 us -> 18.1 us
  waiting for transfers between devices: 8.61 us -> 19.3 us
  local copies, waits for them, and re-layouts: 3.82 us -> 13.2 us
    all_to_all x2 -> x0, blocking collectives: 63.8 us -> none  [spread(): return lax.all_to_all(value, 'ctx', split_axis=0, concat_axis=0, tiled=True)]
    ppermute x1 -> x15, starting transfers between devices: 0.01 us -> 28.5 us  [joint_shift(): return lax.ppermute(value, ('segment', 'ctx'), pairs)]
    all_to_all x1, starting transfers between devices: 3.59 us -> 15.2 us  [fast_on_device(): q = lax.all_to_all(q, 'ctx', split_axis=0, concat_axis=0, tiled=True)]
    ppermute x1 -> x15, waiting for transfers between devices: 8.6 us -> 19.3 us  [joint_shift(): return lax.ppermute(value, ('segment', 'ctx'), pairs)]
    unnamed x20 -> x42, local copies, waits for them, and re-layouts: 3.74 us -> 13.1 us
    pallas_call x1, Pallas kernels: 23.2 us -> 15.3 us  [fast_on_device(): pl.pallas_call(functools.partial(convolve_kernel, parts, outer), out_shap...]
    pallas_call x3 -> x4, Pallas kernels: 6.33 us -> 2.88 us  [the longest x1 1.05 us: fast_on_device(): pl.pallas_call(functools.partial(unpack_kernel, parts), out_shape=block(l...]
  transfers between devices with their start and end apart: 2 -> 16, of which waited for: 1 -> 4; matrix products, arithmetic and copies ran while one was open for 0% -> 0% of each run, Pallas kernels for 21% -> 17%
where the time goes in v2:
time: 95.1 us; the launch traced here: 94.5 us
  starting transfers between devices  43.7 us (46%)
  waiting for transfers between devices  19.3 us (20%)
  Pallas kernels  18.1 us (19%)
  local copies, waits for them, and re-layouts  13.2 us (14%)
    ppermute x15, starting transfers between devices, joint_shift(): return lax.ppermute(value, ('segment', 'ctx'), pairs)  28.5 us
    ppermute x15, waiting for transfers between devices, joint_shift(): return lax.ppermute(value, ('segment', 'ctx'), pairs)  19.3 us
    pallas_call x1, Pallas kernels, fast_on_device(): pl.pallas_call(functools.partial(convolve_kernel, parts, outer), out_shap...  15.3 us
    all_to_all x1, starting transfers between devices, fast_on_device(): q = lax.all_to_all(q, 'ctx', split_axis=0, concat_axis=0, tiled=True)  15.2 us
    unnamed x42, local copies, waits for them, and re-layouts  13.1 us
  transfers between devices with their start and end apart: 16, of which 4 were waited for; matrix products, arithmetic and copies ran while one was open for 0% of the time, Pallas kernels for 17%

profile of v2, /device:TPU:0, one launch (start us, length us, event | category | flops | bytes accessed | tf_op | source)
XLA Modules:
  0.0 94.5 jit_solution(14800349208775297084)
XLA Ops:
  0.0 1.1 %copy-done.2 = bf16[1,512,512]{2,1,0:T(8,128)(2,1)S(1)} copy-done((bf16[1,512,512]{2,1,0:T(8,128)(2,1)S(1)}, bf16[1,512,512]{2,1,0:T(8,128)(2,1)}, u32[]{:S(2)}) %copy-start.2) | copy-done | bytes 524312
  1.1 1.0 %copy-done.3 = bf16[1,512,512]{2,1,0:T(8,128)(2,1)S(1)} copy-done((bf16[1,512,512]{2,1,0:T(8,128)(2,1)S(1)}, bf16[1,512,512]{2,1,0:T(8,128)(2,1)}, u32[]{:S(2)}) %copy-start.3) | copy-done | bytes 524312
  2.1 1.0 %copy-done.4 = bf16[1,512,512]{2,1,0:T(8,128)(2,1)S(1)} copy-done((bf16[1,512,512]{2,1,0:T(8,128)(2,1)S(1)}, bf16[1,512,512]{2,1,0:T(8,128)(2,1)}, u32[]{:S(2)}) %copy-start.4) | copy-done | bytes 524312
  3.1 0.7 shard_map.109
  3.9 3.0 %collective-permute-start = (bf16[768,128]{1,0:T(8,128)(2,1)S(1)}, bf16[768,128]{1,0:T(8,128)(2,1)S(1)}, u32[]{:S(2)}, u32[]{:S(2)}) collective-permute-start(bf16[768,128]{1,0:T(8,128)(2,1)S(1)} %get-tuple-element.23), channel_id=1, source_target_pairs={{0,1},{1,2},{2,3},{3,4},{4,5},{5,6},{6,7},{7,0},{8,9},{9,10},{10,1... | collective-permute-start | bytes 589832 | tf_op jit(solution)/shard_map/ppermute | solution.py:336
  6.9 1.6 %collective-permute-start.1 = (bf16[768,128]{1,0:T(8,128)(2,1)S(1)}, bf16[768,128]{1,0:T(8,128)(2,1)S(1)}, u32[]{:S(2)}, u32[]{:S(2)}) collective-permute-start(bf16[768,128]{1,0:T(8,128)(2,1)S(1)} %get-tuple-element.24), channel_id=1, source_target_pairs={{0,2},{1,3},{2,4},{3,5},{4,6},{5,7},{6,0},{7,1},{8,10},{9,11},{10,... | collective-permute-start | bytes 589832 | tf_op jit(solution)/shard_map/ppermute | solution.py:336
  8.5 2.5 %collective-permute-start.2 = (bf16[768,128]{1,0:T(8,128)(2,1)S(1)}, bf16[768,128]{1,0:T(8,128)(2,1)S(1)}, u32[]{:S(2)}, u32[]{:S(2)}) collective-permute-start(bf16[768,128]{1,0:T(8,128)(2,1)S(1)} %get-tuple-element.25), channel_id=1, source_target_pairs={{0,3},{1,4},{2,5},{3,6},{4,7},{5,0},{6,1},{7,2},{8,11},{9,12},{10,... | collective-permute-start | bytes 589832 | tf_op jit(solution)/shard_map/ppermute | solution.py:336
  11.0 1.2 %collective-permute-start.3 = (bf16[768,128]{1,0:T(8,128)(2,1)S(1)}, bf16[768,128]{1,0:T(8,128)(2,1)S(1)}, u32[]{:S(2)}, u32[]{:S(2)}) collective-permute-start(bf16[768,128]{1,0:T(8,128)(2,1)S(1)} %get-tuple-element.26), channel_id=1, source_target_pairs={{0,4},{1,5},{2,6},{3,7},{4,0},{5,1},{6,2},{7,3},{8,12},{9,13},{10,... | collective-permute-start | bytes 589832 | tf_op jit(solution)/shard_map/ppermute | solution.py:336
  12.2 2.6 %collective-permute-start.4 = (bf16[768,128]{1,0:T(8,128)(2,1)S(1)}, bf16[768,128]{1,0:T(8,128)(2,1)S(1)}, u32[]{:S(2)}, u32[]{:S(2)}) collective-permute-start(bf16[768,128]{1,0:T(8,128)(2,1)S(1)} %get-tuple-element.27), channel_id=1, source_target_pairs={{0,5},{1,6},{2,7},{3,0},{4,1},{5,2},{6,3},{7,4},{8,13},{9,14},{10,... | collective-permute-start | bytes 589832 | tf_op jit(solution)/shard_map/ppermute | solution.py:336
  14.9 1.0 %collective-permute-done.refs_1_ = bf16[768,128]{1,0:T(8,128)(2,1)S(1)} collective-permute-done((bf16[768,128]{1,0:T(8,128)(2,1)S(1)}, bf16[768,128]{1,0:T(8,128)(2,1)S(1)}, u32[]{:S(2)}, u32[]{:S(2)}) %collective-permute-start) | collective-permute-done | bytes 196640 | tf_op jit(solution)/shard_map/ppermute | solution.py:336
  15.8 1.8 %collective-permute-start.5 = (bf16[768,128]{1,0:T(8,128)(2,1)S(1)}, bf16[768,128]{1,0:T(8,128)(2,1)S(1)}, u32[]{:S(2)}, u32[]{:S(2)}) collective-permute-start(bf16[768,128]{1,0:T(8,128)(2,1)S(1)} %get-tuple-element.28), channel_id=1, source_target_pairs={{0,6},{1,7},{2,0},{3,1},{4,2},{5,3},{6,4},{7,5},{8,14},{9,15},{10,... | collective-permute-start | bytes 589832 | tf_op jit(solution)/shard_map/ppermute | solution.py:336
  17.7 3.4 %collective-permute-start.6 = (bf16[768,128]{1,0:T(8,128)(2,1)S(1)}, bf16[768,128]{1,0:T(8,128)(2,1)S(1)}, u32[]{:S(2)}, u32[]{:S(2)}) collective-permute-start(bf16[768,128]{1,0:T(8,128)(2,1)S(1)} %get-tuple-element.29), channel_id=1, source_target_pairs={{0,7},{1,0},{2,1},{3,2},{4,3},{5,4},{6,5},{7,6},{8,15},{9,8},{10,9... | collective-permute-start | bytes 589832 | tf_op jit(solution)/shard_map/ppermute | solution.py:336
  21.1 1.0 %shard_map.111 = bf16[8,256,128]{2,1,0:T(8,128)(2,1)} custom-call(bf16[512,512]{1,0:T(8,128)(2,1)S(1)} %bitcast.9), custom_call_target="tpu_custom_call" | custom-call | tf_op jit(solution)/shard_map/pallas_call | solution.py:361
  22.1 9.7 %collective-permute-done.2.refs_3_ = bf16[768,128]{1,0:T(8,128)(2,1)S(1)} collective-permute-done((bf16[768,128]{1,0:T(8,128)(2,1)S(1)}, bf16[768,128]{1,0:T(8,128)(2,1)S(1)}, u32[]{:S(2)}, u32[]{:S(2)}) %collective-permute-start.2) | collective-permute-done | bytes 196640 | tf_op jit(solution)/shard_map/ppermute | solution.py:336
  34.6 15.2 %all-to-all-start = ((bf16[8,256,128]{2,1,0:T(8,128)(2,1)}), bf16[8,256,128]{2,1,0:T(8,128)(2,1)S(1)}, u32[]{:S(2)}, u32[]{:S(2)}) async-start(bf16[8,256,128]{2,1,0:T(8,128)(2,1)} %shard_map.111), calls=%async_computation | async-start | bytes 1048576 | tf_op jit(solution)/shard_map/all_to_all | solution.py:367
  50.0 0.9 copy-done.8
  51.0 0.9 copy-done.10
  51.9 0.9 copy-done.12
  52.8 0.9 copy-done.14
  53.7 0.9 copy-done.16
  54.7 0.9 copy-done.17
  55.6 0.8 copy-done.19
  56.4 0.8 copy-done.20
  57.2 15.3 %shard_map.110.y_ref = f32[8,256,128]{2,1,0:T(8,128)S(1)} custom-call(s32[1]{0:T(128)} %bitcast.index_ref, bf16[768,128]{1,0:T(8,128)(2,1)S(1)} %get-tuple-element.22.refs_0_, bf16[768,128]{1,0:T(8,128)(2,1)S(1)} %collective-permute-done.refs_1_, bf16[768,128]{1,0:T(8,128)(2,1)S(1)} %collective-permute-done.1.refs_2_, bf16[768,128]{1,0:T(8,128)(2,1)S(1)} %copy-done.8, ...), custom_call_target="tpu_custom_call" | custom-call | tf_op jit(solution)/shard_map/pallas_call | solution.py:370
  72.7 5.9 %collective-permute-start.8 = (bf16[256,128]{1,0:T(8,128)(2,1)S(1)}, bf16[256,128]{1,0:T(8,128)(2,1)S(1)}, u32[]{:S(2)}, u32[]{:S(2)}) collective-permute-start(bf16[256,128]{1,0:T(8,128)(2,1)S(1)} %get-tuple-element.32), channel_id=1, source_target_pairs={{0,15},{1,8},{2,9},{3,10},{4,11},{5,12},{6,13},{7,14},{8,23},{9,16... | collective-permute-start | bytes 196616 | tf_op jit(solution)/shard_map/ppermute | solution.py:336
  78.7 2.6 %collective-permute-start.11 = (bf16[256,128]{1,0:T(8,128)(2,1)S(1)}, bf16[256,128]{1,0:T(8,128)(2,1)S(1)}, u32[]{:S(2)}, u32[]{:S(2)}) collective-permute-start(bf16[256,128]{1,0:T(8,128)(2,1)S(1)} %get-tuple-element.35), channel_id=1, source_target_pairs={{0,12},{1,13},{2,14},{3,15},{4,8},{5,9},{6,10},{7,11},{8,20},{9,21... | collective-permute-start | bytes 196616 | tf_op jit(solution)/shard_map/ppermute | solution.py:336
  81.3 0.8 collective-permute-start.12
  82.1 1.9 %collective-permute-start.13 = (bf16[256,128]{1,0:T(8,128)(2,1)S(1)}, bf16[256,128]{1,0:T(8,128)(2,1)S(1)}, u32[]{:S(2)}, u32[]{:S(2)}) collective-permute-start(bf16[256,128]{1,0:T(8,128)(2,1)S(1)} %get-tuple-element.37), channel_id=1, source_target_pairs={{0,10},{1,11},{2,12},{3,13},{4,14},{5,15},{6,8},{7,9},{8,18},{9,19... | collective-permute-start | bytes 196616 | tf_op jit(solution)/shard_map/ppermute | solution.py:336
  84.0 0.9 collective-permute-start.14
  84.9 6.2 %collective-permute-done.11.refs_4_ = bf16[256,128]{1,0:T(8,128)(2,1)S(1)} collective-permute-done((bf16[256,128]{1,0:T(8,128)(2,1)S(1)}, bf16[256,128]{1,0:T(8,128)(2,1)S(1)}, u32[]{:S(2)}, u32[]{:S(2)}) %collective-permute-start.11) | collective-permute-done | bytes 65568 | tf_op jit(solution)/shard_map/ppermute | solution.py:336
  91.1 2.4 %collective-permute-done.12.refs_5_ = bf16[256,128]{1,0:T(8,128)(2,1)S(1)} collective-permute-done((bf16[256,128]{1,0:T(8,128)(2,1)S(1)}, bf16[256,128]{1,0:T(8,128)(2,1)S(1)}, u32[]{:S(2)}, u32[]{:S(2)}) %collective-permute-start.12) | collective-permute-done | bytes 65568 | tf_op jit(solution)/shard_map/ppermute | solution.py:336
  93.5 1.0 %shard_map.113 = bf16[512,512]{1,0:T(8,128)(2,1)} custom-call(s32[1]{0:T(128)} %bitcast.index_ref, bf16[256,128]{1,0:T(8,128)(2,1)S(1)} %collective-permute-done.7.refs_0_, bf16[256,128]{1,0:T(8,128)(2,1)S(1)} %collective-permute-done.8.refs_1_, bf16[256,128]{1,0:T(8,128)(2,1)S(1)} %collective-permute-done.9.refs_2_, ...), custom_call_target="tpu_custom_call" | custom-call | tf_op jit(solution)/shard_map/pallas_call | solution.py:389
  (49 shorter events, 3.2 us)
Async XLA Ops:
  0.0 49.9 %copy-start = (f32[1,512]{1,0:T(1,128)S(1)}, f32[1,512]{1,0:T(1,128)}, u32[]{:S(2)}) copy-start(f32[1,512]{1,0:T(1,128)} %param.15) | copy-start | bytes 6148
  0.0 1.1 %copy-start.2 = (bf16[1,512,512]{2,1,0:T(8,128)(2,1)S(1)}, bf16[1,512,512]{2,1,0:T(8,128)(2,1)}, u32[]{:S(2)}) copy-start(bf16[1,512,512]{2,1,0:T(8,128)(2,1)} %param.12) | copy-start | bytes 1572868
  1.1 1.0 %copy-start.3 = (bf16[1,512,512]{2,1,0:T(8,128)(2,1)S(1)}, bf16[1,512,512]{2,1,0:T(8,128)(2,1)}, u32[]{:S(2)}) copy-start(bf16[1,512,512]{2,1,0:T(8,128)(2,1)} %param.13) | copy-start | bytes 1572868
  2.1 1.0 %copy-start.4 = (bf16[1,512,512]{2,1,0:T(8,128)(2,1)S(1)}, bf16[1,512,512]{2,1,0:T(8,128)(2,1)}, u32[]{:S(2)}) copy-start(bf16[1,512,512]{2,1,0:T(8,128)(2,1)} %param.14) | copy-start | bytes 1572868
  3.1 18.0 %copy-start.5 = (bf16[1,512,512]{2,1,0:T(8,128)(2,1)S(1)}, bf16[1,512,512]{2,1,0:T(8,128)(2,1)}, u32[]{:S(2)}) copy-start(bf16[1,512,512]{2,1,0:T(8,128)(2,1)} %param.11) | copy-start | bytes 1572868
  3.9 12.0 %collective-permute-start = (bf16[768,128]{1,0:T(8,128)(2,1)S(1)}, bf16[768,128]{1,0:T(8,128)(2,1)S(1)}, u32[]{:S(2)}, u32[]{:S(2)}) collective-permute-start(bf16[768,128]{1,0:T(8,128)(2,1)S(1)} %get-tuple-element.23), channel_id=1, source_target_pairs={{0,1},{1,2},{2,3},{3,4},{4,5},{5,6},{6,7},{7,0},{8,9},{9,10},{10,1... | collective-permute-start | bytes 589832 | tf_op jit(solution)/shard_map/ppermute | solution.py:336
  6.9 10.8 %collective-permute-start.1 = (bf16[768,128]{1,0:T(8,128)(2,1)S(1)}, bf16[768,128]{1,0:T(8,128)(2,1)S(1)}, u32[]{:S(2)}, u32[]{:S(2)}) collective-permute-start(bf16[768,128]{1,0:T(8,128)(2,1)S(1)} %get-tuple-element.24), channel_id=1, source_target_pairs={{0,2},{1,3},{2,4},{3,5},{4,6},{5,7},{6,0},{7,1},{8,10},{9,11},{10,... | collective-permute-start | bytes 589832 | tf_op jit(solution)/shard_map/ppermute | solution.py:336
  8.5 23.4 %collective-permute-start.2 = (bf16[768,128]{1,0:T(8,128)(2,1)S(1)}, bf16[768,128]{1,0:T(8,128)(2,1)S(1)}, u32[]{:S(2)}, u32[]{:S(2)}) collective-permute-start(bf16[768,128]{1,0:T(8,128)(2,1)S(1)} %get-tuple-element.25), channel_id=1, source_target_pairs={{0,3},{1,4},{2,5},{3,6},{4,7},{5,0},{6,1},{7,2},{8,11},{9,12},{10,... | collective-permute-start | bytes 589832 | tf_op jit(solution)/shard_map/ppermute | solution.py:336
  11.0 21.5 %collective-permute-start.3 = (bf16[768,128]{1,0:T(8,128)(2,1)S(1)}, bf16[768,128]{1,0:T(8,128)(2,1)S(1)}, u32[]{:S(2)}, u32[]{:S(2)}) collective-permute-start(bf16[768,128]{1,0:T(8,128)(2,1)S(1)} %get-tuple-element.26), channel_id=1, source_target_pairs={{0,4},{1,5},{2,6},{3,7},{4,0},{5,1},{6,2},{7,3},{8,12},{9,13},{10,... | collective-permute-start | bytes 589832 | tf_op jit(solution)/shard_map/ppermute | solution.py:336
  12.2 20.9 %collective-permute-start.4 = (bf16[768,128]{1,0:T(8,128)(2,1)S(1)}, bf16[768,128]{1,0:T(8,128)(2,1)S(1)}, u32[]{:S(2)}, u32[]{:S(2)}) collective-permute-start(bf16[768,128]{1,0:T(8,128)(2,1)S(1)} %get-tuple-element.27), channel_id=1, source_target_pairs={{0,5},{1,6},{2,7},{3,0},{4,1},{5,2},{6,3},{7,4},{8,13},{9,14},{10,... | collective-permute-start | bytes 589832 | tf_op jit(solution)/shard_map/ppermute | solution.py:336
  15.8 18.0 %collective-permute-start.5 = (bf16[768,128]{1,0:T(8,128)(2,1)S(1)}, bf16[768,128]{1,0:T(8,128)(2,1)S(1)}, u32[]{:S(2)}, u32[]{:S(2)}) collective-permute-start(bf16[768,128]{1,0:T(8,128)(2,1)S(1)} %get-tuple-element.28), channel_id=1, source_target_pairs={{0,6},{1,7},{2,0},{3,1},{4,2},{5,3},{6,4},{7,5},{8,14},{9,15},{10,... | collective-permute-start | bytes 589832 | tf_op jit(solution)/shard_map/ppermute | solution.py:336
  17.7 16.2 %collective-permute-start.6 = (bf16[768,128]{1,0:T(8,128)(2,1)S(1)}, bf16[768,128]{1,0:T(8,128)(2,1)S(1)}, u32[]{:S(2)}, u32[]{:S(2)}) collective-permute-start(bf16[768,128]{1,0:T(8,128)(2,1)S(1)} %get-tuple-element.29), channel_id=1, source_target_pairs={{0,7},{1,0},{2,1},{3,2},{4,3},{5,4},{6,5},{7,6},{8,15},{9,8},{10,9... | collective-permute-start | bytes 589832 | tf_op jit(solution)/shard_map/ppermute | solution.py:336
  21.1 28.9 %copy-start.1 = (f32[16,2,64,128]{3,2,1,0:T(8,128)S(1)}, f32[16,2,64,128]{3,2,1,0:T(8,128)}, u32[]{:S(2)}) copy-start(f32[16,2,64,128]{3,2,1,0:T(8,128)} %constant.27.clone.refs_14_) | copy-start | bytes 3145732
  33.9 16.1 %copy-start.6 = (f32[4,2,64,128]{3,2,1,0:T(8,128)S(1)}, f32[4,2,64,128]{3,2,1,0:T(8,128)}, u32[]{:S(2)}) copy-start(f32[4,2,64,128]{3,2,1,0:T(8,128)} %constant.26.clone.refs_13_) | copy-start | bytes 786436
  33.9 16.1 %copy-start.18 = (bf16[128,192]{1,0:T(8,128)(2,1)S(1)}, bf16[128,192]{1,0:T(8,128)(2,1)}, u32[]{:S(2)}) copy-start(bf16[128,192]{1,0:T(8,128)(2,1)} %constant.22.clone.refs_9_) | copy-start | bytes 147460
  34.6 37.9 %all-to-all-start = ((bf16[8,256,128]{2,1,0:T(8,128)(2,1)}), bf16[8,256,128]{2,1,0:T(8,128)(2,1)S(1)}, u32[]{:S(2)}, u32[]{:S(2)}) async-start(bf16[8,256,128]{2,1,0:T(8,128)(2,1)} %shard_map.111), calls=%async_computation | async-start | bytes 1048576 | tf_op jit(solution)/shard_map/all_to_all | solution.py:367
  50.0 0.9 copy-start.8
  51.0 0.9 copy-start.10
  51.9 0.9 copy-start.12
  52.8 0.9 copy-start.14
  53.7 0.9 copy-start.16
  54.7 0.9 copy-start.17
  55.6 0.8 copy-start.19
  56.4 0.8 copy-start.20
  72.6 8.7 %collective-permute-start.7 = (bf16[256,128]{1,0:T(8,128)(2,1)S(1)}, bf16[256,128]{1,0:T(8,128)(2,1)S(1)}, u32[]{:S(2)}, u32[]{:S(2)}) collective-permute-start(bf16[256,128]{1,0:T(8,128)(2,1)S(1)} %get-tuple-element.31), channel_id=1, source_target_pairs={{0,8},{1,9},{2,10},{3,11},{4,12},{5,13},{6,14},{7,15},{8,16},{9,17... | collective-permute-start | bytes 196616 | tf_op jit(solution)/shard_map/ppermute | solution.py:336
  72.7 9.4 %collective-permute-start.8 = (bf16[256,128]{1,0:T(8,128)(2,1)S(1)}, bf16[256,128]{1,0:T(8,128)(2,1)S(1)}, u32[]{:S(2)}, u32[]{:S(2)}) collective-permute-start(bf16[256,128]{1,0:T(8,128)(2,1)S(1)} %get-tuple-element.32), channel_id=1, source_target_pairs={{0,15},{1,8},{2,9},{3,10},{4,11},{5,12},{6,13},{7,14},{8,23},{9,16... | collective-permute-start | bytes 196616 | tf_op jit(solution)/shard_map/ppermute | solution.py:336
  78.6 5.4 %collective-permute-start.9 = (bf16[256,128]{1,0:T(8,128)(2,1)S(1)}, bf16[256,128]{1,0:T(8,128)(2,1)S(1)}, u32[]{:S(2)}, u32[]{:S(2)}) collective-permute-start(bf16[256,128]{1,0:T(8,128)(2,1)S(1)} %get-tuple-element.33), channel_id=1, source_target_pairs={{0,14},{1,15},{2,8},{3,9},{4,10},{5,11},{6,12},{7,13},{8,22},{9,23... | collective-permute-start | bytes 196616 | tf_op jit(solution)/shard_map/ppermute | solution.py:336
  78.7 6.2 %collective-permute-start.10 = (bf16[256,128]{1,0:T(8,128)(2,1)S(1)}, bf16[256,128]{1,0:T(8,128)(2,1)S(1)}, u32[]{:S(2)}, u32[]{:S(2)}) collective-permute-start(bf16[256,128]{1,0:T(8,128)(2,1)S(1)} %get-tuple-element.34), channel_id=1, source_target_pairs={{0,13},{1,14},{2,15},{3,8},{4,9},{5,10},{6,11},{7,12},{8,21},{9,22... | collective-permute-start | bytes 196616 | tf_op jit(solution)/shard_map/ppermute | solution.py:336
  78.7 12.4 %collective-permute-start.11 = (bf16[256,128]{1,0:T(8,128)(2,1)S(1)}, bf16[256,128]{1,0:T(8,128)(2,1)S(1)}, u32[]{:S(2)}, u32[]{:S(2)}) collective-permute-start(bf16[256,128]{1,0:T(8,128)(2,1)S(1)} %get-tuple-element.35), channel_id=1, source_target_pairs={{0,12},{1,13},{2,14},{3,15},{4,8},{5,9},{6,10},{7,11},{8,20},{9,21... | collective-permute-start | bytes 196616 | tf_op jit(solution)/shard_map/ppermute | solution.py:336
  81.3 12.2 %collective-permute-start.12 = (bf16[256,128]{1,0:T(8,128)(2,1)S(1)}, bf16[256,128]{1,0:T(8,128)(2,1)S(1)}, u32[]{:S(2)}, u32[]{:S(2)}) collective-permute-start(bf16[256,128]{1,0:T(8,128)(2,1)S(1)} %get-tuple-element.36), channel_id=1, source_target_pairs={{0,11},{1,12},{2,13},{3,14},{4,15},{5,8},{6,9},{7,10},{8,19},{9,20... | collective-permute-start | bytes 196616 | tf_op jit(solution)/shard_map/ppermute | solution.py:336
  82.1 11.4 %collective-permute-start.13 = (bf16[256,128]{1,0:T(8,128)(2,1)S(1)}, bf16[256,128]{1,0:T(8,128)(2,1)S(1)}, u32[]{:S(2)}, u32[]{:S(2)}) collective-permute-start(bf16[256,128]{1,0:T(8,128)(2,1)S(1)} %get-tuple-element.37), channel_id=1, source_target_pairs={{0,10},{1,11},{2,12},{3,13},{4,14},{5,15},{6,8},{7,9},{8,18},{9,19... | collective-permute-start | bytes 196616 | tf_op jit(solution)/shard_map/ppermute | solution.py:336
  84.0 9.5 %collective-permute-start.14 = (bf16[256,128]{1,0:T(8,128)(2,1)S(1)}, bf16[256,128]{1,0:T(8,128)(2,1)S(1)}, u32[]{:S(2)}, u32[]{:S(2)}) collective-permute-start(bf16[256,128]{1,0:T(8,128)(2,1)S(1)} %get-tuple-element.38), channel_id=1, source_target_pairs={{0,9},{1,10},{2,11},{3,12},{4,13},{5,14},{6,15},{7,8},{8,17},{9,18... | collective-permute-start | bytes 196616 | tf_op jit(solution)/shard_map/ppermute | solution.py:336
  (5 other events, 3.5 us)

commit v3 on v0

--- a/solution.py
+++ b/solution.py
@@ -1,11 +1,23 @@
+import functools
 import math
 
 import jax
 import jax.numpy as jnp
+import numpy as np
 from jax import lax
+from jax.experimental import pallas as pl
+from jax.experimental.pallas import tpu as pltpu
 from jax.sharding import PartitionSpec as P
 
 HIGHEST = lax.Precision.HIGHEST
+LANES = 128
+HALF = 64
+INNER = 64
+SPAN = INNER // 2
+QUARTER = LANES // 4
+WIDE = 16
+F32 = jnp.float32
+BF16 = jnp.bfloat16
 
 
 def from_behind(value, axis, steps):
@@ -38,7 +50,7 @@
     return (real_part * cosine + imag_part * sine, imag_part * cosine - real_part * sine)
 
 
-def on_device(query_stream, key_stream, value_stream, filter_taps, skip_weight):
+def general_on_device(query_stream, key_stream, value_stream, filter_taps, skip_weight):
     parts = lax.axis_size("ctx")
     device = lax.axis_index("ctx")
     length = query_stream.shape[1]
@@ -108,6 +120,251 @@
     return from_behind(gated, "segment", 1)
 
 
+def split_two(value):
+    high = value.astype(BF16)
+    return high, (value - high.astype(F32)).astype(BF16)
+
+
+def stacked(value):
+    high, low = split_two(value)
+    return jnp.concatenate([high, low, high], axis=0)
+
+
+def split_table(table):
+    table = table.astype(np.float32)
+    high = table.astype(jnp.bfloat16)
+    low = (table - high.astype(np.float32)).astype(jnp.bfloat16)
+    return np.concatenate([high, high, low], axis=1)
+
+
+def group(shape):
+    return lax.broadcasted_iota(jnp.int32, shape, len(shape) - 1) // QUARTER
+
+
+def turned(value, groups):
+    groups %= LANES // QUARTER
+    return pltpu.roll(value, groups * QUARTER, value.ndim - 1) if groups else value
+
+
+def chosen(where, values):
+    result = values[0]
+    for i in range(1, len(values)):
+        result = jnp.where(where == i, values[i], result)
+    return result
+
+
+def tables(outer):
+    total = outer * INNER
+    a = np.arange(outer)
+    b = np.arange(INNER)
+    c = np.arange(outer) + 0.25
+    first = 2.0 * np.pi * np.outer(c, a) / outer
+    second = 2.0 * np.pi * np.outer(b, b) / INNER
+    forward_a = split_table(np.concatenate([np.cos(first), -np.sin(first)], axis=0))
+    back_a = split_table(np.concatenate([np.cos(first).T, -np.sin(first).T], axis=0) / total)
+    forward_b, back_b = [], []
+    for half in (second[:, :SPAN], second[:, SPAN:]):
+        cos, sin = np.cos(half), np.sin(half)
+        forward_b.append(split_table(np.block([[cos, sin], [-sin, cos]])))
+        back_b.append(split_table(np.concatenate([cos, sin], axis=0)))
+    theta = 2.0 * np.pi * np.outer(b, c) / total
+    wide = np.stack([np.cos(theta), np.sin(theta)], axis=1).astype(np.float32)
+    wide = np.broadcast_to(wide[..., None], wide.shape + (LANES // 2,))
+    turns = np.concatenate([wide[:SPAN], wide[SPAN:]], axis=-1)
+    return forward_a, np.concatenate(forward_b), np.concatenate(back_b), back_a, turns
+
+
+def pack_kernel(parts, chunk, index_ref, k_ref, v_ref, h_ref, q_ref, *refs):
+    outs, held = refs[:-1], refs[-1]
+    length = k_ref.shape[0]
+    rows = length // 2
+    where = group((rows, LANES))
+
+    def halves(ref, e):
+        tile = ref[:, LANES * e : LANES * (e + 1)].astype(F32).reshape(length // INNER, INNER, LANES)
+        return tile[:, :SPAN].reshape(rows, LANES), tile[:, SPAN:].reshape(rows, LANES)
+
+    for e in range(parts // 2):
+        for at, (even_ref, odd_ref) in enumerate(((k_ref, h_ref), (v_ref, q_ref))):
+            even_lo, even_hi = halves(even_ref, e)
+            odd_lo, odd_hi = halves(odd_ref, e)
+            for side in range(2):
+                g = 2 * side + chunk
+                moved = [turned(x, j - g) for j, x in enumerate((even_lo, odd_lo, even_hi, odd_hi))]
+                held[2 * e + side, at * rows : (at + 1) * rows, :] = chosen(where, moved).astype(BF16)
+    for n, out in enumerate(outs):
+        out[...] = held[lax.rem(index_ref[0] + n, parts)]
+
+
+def unpack_kernel(parts, index_ref, *refs):
+    blocks, out_ref, held = refs[: 2 * parts], refs[2 * parts], refs[2 * parts + 1]
+    for chunk in range(2):
+        for n in range(parts):
+            held[chunk, lax.rem(index_ref[0] + n, parts)] = blocks[chunk * parts + n][...].astype(F32)
+    rows = held.shape[2]
+    spans = rows // SPAN
+    where = group((rows, LANES))
+    for e in range(parts // 2):
+        pieces = [held[g % 2, 2 * e + g // 2] for g in range(4)]
+        for j in range(4):
+            value = chosen(where, [turned(piece, g - j) for g, piece in enumerate(pieces)])
+            out_ref[
+                spans * (j % 2) : spans * (j % 2 + 1),
+                SPAN * (j // 2) : SPAN * (j // 2 + 1),
+                LANES * e : LANES * (e + 1),
+            ] = value.astype(BF16).reshape(spans, SPAN, LANES)
+
+
+def convolve_kernel(parts, outer, index_ref, *refs):
+    blocks, refs = refs[:parts], refs[parts:]
+    skip_ref, fa_ref, fb_ref, bb_ref, ba_ref, turn_ref = refs[:6]
+    outs, (x_s, z_s, w_s, y_s) = refs[6 : 6 + parts], refs[6 + parts :]
+    rows = blocks[0].shape[0] // 2
+    per = rows // SPAN
+
+    def even(count):
+        return group((count, LANES)) % 2 == 0
+
+    def low(count):
+        return group((count, LANES)) < 2
+
+    def origin(n):
+        return lax.rem(index_ref[0] + parts - n, parts)
+
+    def folded(both):
+        half = both.shape[0] // 2
+        value = jnp.where(low(half), both[:half], both[half:])
+        return value + turned(value, 2)
+
+    def lanes(value, j):
+        return value[:, LANES * j : LANES * (j + 1)]
+
+    for n, block in enumerate(blocks):
+        value = block[:rows, :].astype(F32) * jnp.where(even(rows), block[rows:, :].astype(F32), 1.0)
+        for m in range(per):
+            x_s[pl.ds(origin(n) * per + m, SPAN, stride=outer), :] = value[m * SPAN : (m + 1) * SPAN]
+
+    def forward_outer(step, carry):
+        at = step * WIDE
+        data = [
+            stacked(x_s[pl.ds(pl.multiple_of((at + j) * outer, outer), outer), :]) for j in range(WIDE)
+        ]
+        both = jnp.dot(fa_ref[...], jnp.concatenate(data, axis=1), preferred_element_type=F32)
+        for j in range(WIDE):
+            re, im = lanes(both[:outer], j), lanes(both[outer:], j)
+            cos, sin = turn_ref[at + j, 0], turn_ref[at + j, 1]
+            z_s[pl.ds(at + j, outer, stride=2 * SPAN), :] = re * cos + im * sin
+            z_s[pl.ds(at + j + SPAN, outer, stride=2 * SPAN), :] = im * cos - re * sin
+        return carry
+
+    lax.fori_loop(0, SPAN // WIDE, forward_outer, 0)
+
+    def middle(step, carry):
+        at = step * WIDE
+        data = [
+            stacked(z_s[pl.ds(pl.multiple_of((at + j) * 2 * SPAN, 2 * SPAN), 2 * SPAN), :])
+            for j in range(WIDE)
+        ]
+        both = jnp.dot(fb_ref[...], jnp.concatenate(data, axis=1), preferred_element_type=F32)
+        data = []
+        for j in range(WIDE):
+            value = folded(lanes(both, j))
+            re, im = value[:INNER], value[INNER:]
+            re_2, im_2 = turned(re, 1), turned(im, 1)
+            value = jnp.where(even(INNER), re * re_2 - im * im_2, re * im_2 + im * re_2)
+            data.append(stacked(jnp.where(low(SPAN), value[:SPAN], value[SPAN:])))
+        both = jnp.dot(bb_ref[...], jnp.concatenate(data, axis=1), preferred_element_type=F32)
+        for j in range(WIDE):
+            value = folded(lanes(both, j))
+            straight, crossed = value[:INNER], turned(value[INNER:], 1)
+            value = jnp.where(even(INNER), straight - crossed, straight + crossed)
+            w_s[pl.ds(at + j, SPAN, stride=outer), :] = jnp.where(low(SPAN), value[:SPAN], value[SPAN:])
+        return carry
+
+    lax.fori_loop(0, outer // WIDE, middle, 0)
+
+    def back_outer(step, carry):
+        at = step * WIDE
+        data = []
+        for j in range(WIDE):
+            value = w_s[pl.ds(pl.multiple_of((at + j) * outer, outer), outer), :]
+            other = jnp.where(even(outer), -turned(value, -1), turned(value, 1))
+            data.append(stacked(value * turn_ref[at + j, 0] + other * turn_ref[at + j, 1]))
+        both = jnp.dot(ba_ref[...], jnp.concatenate(data, axis=1), preferred_element_type=F32)
+        for j in range(WIDE):
+            y_s[pl.ds(at + j, outer, stride=SPAN), :] = lanes(both[:outer], j) + turned(
+                lanes(both[outer:], j), -1
+            )
+        return carry
+
+    lax.fori_loop(0, SPAN // WIDE, back_outer, 0)
+
+    for n, (block, out) in enumerate(zip(blocks, outs)):
+        y = y_s[pl.ds(pl.multiple_of(origin(n) * rows, rows), rows), :]
+        second = block[rows:, :].astype(F32)
+        product = block[:rows, :].astype(F32) * second
+        gated = turned(second, -1) * (y + skip_ref[...] * product)
+        half = rows // 2
+        out[...] = jnp.where(even(half), gated[:half], turned(gated[half:], 1)).astype(BF16)
+
+
+def joint_shift(value, segment_step, ctx_step):
+    segments, parts = lax.axis_size("segment"), lax.axis_size("ctx")
+    pairs = [
+        (s * parts + c, (s + segment_step) % segments * parts + (c + ctx_step) % parts)
+        for s in range(segments)
+        for c in range(parts)
+    ]
+    return lax.ppermute(value, ("segment", "ctx"), pairs)
+
+
+def fast_on_device(query_stream, key_stream, value_stream, filter_taps, skip_weight):
+    parts = lax.axis_size("ctx")
+    device = lax.axis_index("ctx")
+    length, channels = query_stream.shape[1:]
+    rows = length // 2
+    outer = parts * length // INNER
+    index = jnp.full((1,), device, jnp.int32)
+    scalar = pl.BlockSpec(memory_space=pltpu.SMEM)
+    whole = pl.BlockSpec(memory_space=pltpu.VMEM)
+    consts = [jnp.asarray(t) for t in tables(outer)]
+    back = []
+    packed = []
+    for chunk in range(2):
+        sent = pl.pallas_call(
+            functools.partial(pack_kernel, parts, chunk),
+            out_shape=(jax.ShapeDtypeStruct((length, LANES), BF16),) * parts,
+            in_specs=[scalar] + [whole] * 4,
+            scratch_shapes=[pltpu.VMEM((parts, length, LANES), BF16)],
+            compiler_params=pltpu.CompilerParams(vmem_limit_bytes=20 * 2**20),
+        )(index, key_stream[0], value_stream[0], filter_taps[0], query_stream[0])
+        packed.append([sent[0]] + [joint_shift(sent[n], 0, n) for n in range(1, parts)])
+    for chunk in range(2):
+        skip = lax.dynamic_slice(skip_weight, (0, device * HALF + chunk * QUARTER), (1, QUARTER))
+        gated = pl.pallas_call(
+            functools.partial(convolve_kernel, parts, outer),
+            out_shape=(jax.ShapeDtypeStruct((rows // 2, LANES), BF16),) * parts,
+            in_specs=[scalar] + [whole] * (parts + 1 + len(consts)),
+            scratch_shapes=[
+                pltpu.VMEM((outer * SPAN, LANES), F32),
+                pltpu.VMEM((2 * outer * SPAN, LANES), F32),
+                pltpu.VMEM((outer * SPAN, LANES), F32),
+                pltpu.VMEM((outer * SPAN, LANES), F32),
+            ],
+            compiler_params=pltpu.CompilerParams(vmem_limit_bytes=24 * 2**20),
+            cost_estimate=pl.CostEstimate(flops=6 * 10**9, bytes_accessed=4 * 10**6, transcendentals=0),
+        )(index, *packed[chunk], jnp.concatenate([skip] * 4, axis=1), *consts)
+        back += [joint_shift(gated[n], 1, -n) for n in range(parts)]
+    out = pl.pallas_call(
+        functools.partial(unpack_kernel, parts),
+        out_shape=jax.ShapeDtypeStruct((length // INNER, INNER, channels), BF16),
+        in_specs=[scalar] + [whole] * (2 * parts),
+        scratch_shapes=[pltpu.VMEM((2, parts, rows // 2, LANES), F32)],
+        compiler_params=pltpu.CompilerParams(vmem_limit_bytes=20 * 2**20),
+    )(index, *back)
+    return out.reshape(1, length, channels)
+
+
 def solution(mesh):
     placed = (
         P("segment", "ctx", None),
@@ -116,6 +373,14 @@
         P("segment", "ctx", None),
         P("segment", None),
     )
+
+    def on_device(*arrays):
+        parts = lax.axis_size("ctx")
+        length, channels = arrays[0].shape[1:]
+        small = parts * length <= 4096 and length % (2 * INNER) == 0 and parts % 2 == 0
+        run = fast_on_device if small and channels == parts * HALF else general_on_device
+        return run(*arrays)
+
     return jax.shard_map(
         on_device, mesh=mesh, in_specs=placed, out_specs=P("segment", "ctx", None), check_vma=False
     )

time: 536 us -> 114 us (0.21)
  waiting for transfers between devices: 268 us -> 13.2 us
  matrix products: 146 us -> 0 us
  local copies, waits for them, and re-layouts: 47.6 us -> 5.85 us
  Pallas kernels: 0 us -> 33.4 us
  blocking collectives: 29.3 us -> 0 us
  starting transfers between devices: 39.5 us -> 60.8 us
    all_to_all x8 -> x0, waiting for transfers between devices: 259 us -> none  [the longest x1 45.1 us: on_device(): lax.all_to_all(prod_imag, 'ctx', split_axis=0, concat_axis=1, tiled=True)]
    dot_general x18 -> x0, matrix products: 146 us -> none  [the longest x12 126 us: along(): return jnp.einsum('kb,rbc->rkc', table, data, precision=HIGHEST)]
    ppermute x1 -> x30, starting transfers between devices: 0.06 us -> 60.8 us  [joint_shift(): return lax.ppermute(value, ('segment', 'ctx'), pairs)]
    all_to_all x8 -> x0, starting transfers between devices: 39.4 us -> none  [the longest x1 7.28 us: on_device(): lax.all_to_all(product.reshape(1, length, channels), 'ctx', split_axis=1,...]
    pallas_call x0 -> x5, Pallas kernels: none -> 33.4 us  [the longest x2 30 us: fast_on_device(): pl.pallas_call(functools.partial(convolve_kernel, parts, outer), out_shap...]
    all_to_all x1 -> x0, blocking collectives: 29.3 us -> none  [on_device(): lax.all_to_all(by_block, 'ctx', split_axis=0, concat_axis=1, tiled=True)[0]]
    all_to_all x10 -> x0, local copies, waits for them, and re-layouts: 22 us -> none  [the longest x3 8.62 us: on_device(): lax.all_to_all(spec_real, 'ctx', split_axis=1, concat_axis=0, tiled=True)]
    add x3 -> x0, local copies, waits for them, and re-layouts: 10.9 us -> none  [rotate(): real_part * cosine + imag_part * sine]
  transfers between devices with their start and end apart: 9 -> 30, of which waited for: 8 -> 6; matrix products, arithmetic and copies ran while one was open for 17% -> 0% of each run, Pallas kernels for 0% -> 27%
where the time goes in v3:
time: 114 us
  starting transfers between devices  60.8 us (53%)
  Pallas kernels  33.4 us (29%)
  waiting for transfers between devices  13.2 us (12%)
  local copies, waits for them, and re-layouts  5.85 us (5%)
    ppermute x30, starting transfers between devices, joint_shift(): return lax.ppermute(value, ('segment', 'ctx'), pairs)  60.8 us
    pallas_call x2, Pallas kernels, fast_on_device(): pl.pallas_call(functools.partial(convolve_kernel, parts, outer), out_shap...  30 us
    ppermute x30, waiting for transfers between devices, joint_shift(): return lax.ppermute(value, ('segment', 'ctx'), pairs)  13.2 us
    unnamed x22, local copies, waits for them, and re-layouts  5.78 us
  transfers between devices with their start and end apart: 30, of which 6 were waited for; matrix products, arithmetic and copies ran while one was open for 0% of the time, Pallas kernels for 27%

profile of v3, /device:TPU:0, one launch (start us, length us, event | category | flops | bytes accessed | tf_op | source)
XLA Modules:
  0.0 113.5 jit_solution(6238928316102334671)
XLA Ops:
  1.0 1.0 copy-done.1
  2.1 1.0 copy-done.2
  3.1 1.0 copy-done.3
  5.2 3.0 %collective-permute-start.15 = (bf16[512,128]{1,0:T(8,128)(2,1)S(1)}, bf16[512,128]{1,0:T(8,128)(2,1)S(1)}, u32[]{:S(2)}, u32[]{:S(2)}) collective-permute-start(bf16[512,128]{1,0:T(8,128)(2,1)S(1)} %get-tuple-element.54), channel_id=1, source_target_pairs={{0,1},{1,2},{2,3},{3,4},{4,5},{5,6},{6,7},{7,0},{8,9},{9,10},{10,1... | collective-permute-start | bytes 393224 | tf_op jit(solution)/shard_map/ppermute | solution.py:318
  8.3 1.6 %collective-permute-start.16 = (bf16[512,128]{1,0:T(8,128)(2,1)S(1)}, bf16[512,128]{1,0:T(8,128)(2,1)S(1)}, u32[]{:S(2)}, u32[]{:S(2)}) collective-permute-start(bf16[512,128]{1,0:T(8,128)(2,1)S(1)} %get-tuple-element.55), channel_id=1, source_target_pairs={{0,2},{1,3},{2,4},{3,5},{4,6},{5,7},{6,0},{7,1},{8,10},{9,11},{10,... | collective-permute-start | bytes 393224 | tf_op jit(solution)/shard_map/ppermute | solution.py:318
  9.8 2.5 %collective-permute-start.17 = (bf16[512,128]{1,0:T(8,128)(2,1)S(1)}, bf16[512,128]{1,0:T(8,128)(2,1)S(1)}, u32[]{:S(2)}, u32[]{:S(2)}) collective-permute-start(bf16[512,128]{1,0:T(8,128)(2,1)S(1)} %get-tuple-element.56), channel_id=1, source_target_pairs={{0,3},{1,4},{2,5},{3,6},{4,7},{5,0},{6,1},{7,2},{8,11},{9,12},{10,... | collective-permute-start | bytes 393224 | tf_op jit(solution)/shard_map/ppermute | solution.py:318
  12.4 1.2 %collective-permute-start.18 = (bf16[512,128]{1,0:T(8,128)(2,1)S(1)}, bf16[512,128]{1,0:T(8,128)(2,1)S(1)}, u32[]{:S(2)}, u32[]{:S(2)}) collective-permute-start(bf16[512,128]{1,0:T(8,128)(2,1)S(1)} %get-tuple-element.57), channel_id=1, source_target_pairs={{0,4},{1,5},{2,6},{3,7},{4,0},{5,1},{6,2},{7,3},{8,12},{9,13},{10,... | collective-permute-start | bytes 393224 | tf_op jit(solution)/shard_map/ppermute | solution.py:318
  13.6 2.6 %collective-permute-start.19 = (bf16[512,128]{1,0:T(8,128)(2,1)S(1)}, bf16[512,128]{1,0:T(8,128)(2,1)S(1)}, u32[]{:S(2)}, u32[]{:S(2)}) collective-permute-start(bf16[512,128]{1,0:T(8,128)(2,1)S(1)} %get-tuple-element.58), channel_id=1, source_target_pairs={{0,5},{1,6},{2,7},{3,0},{4,1},{5,2},{6,3},{7,4},{8,13},{9,14},{10,... | collective-permute-start | bytes 393224 | tf_op jit(solution)/shard_map/ppermute | solution.py:318
  17.3 1.4 %collective-permute-start.20 = (bf16[512,128]{1,0:T(8,128)(2,1)S(1)}, bf16[512,128]{1,0:T(8,128)(2,1)S(1)}, u32[]{:S(2)}, u32[]{:S(2)}) collective-permute-start(bf16[512,128]{1,0:T(8,128)(2,1)S(1)} %get-tuple-element.59), channel_id=1, source_target_pairs={{0,6},{1,7},{2,0},{3,1},{4,2},{5,3},{6,4},{7,5},{8,14},{9,15},{10,... | collective-permute-start | bytes 393224 | tf_op jit(solution)/shard_map/ppermute | solution.py:318
  18.7 1.4 %collective-permute-start.21 = (bf16[512,128]{1,0:T(8,128)(2,1)S(1)}, bf16[512,128]{1,0:T(8,128)(2,1)S(1)}, u32[]{:S(2)}, u32[]{:S(2)}) collective-permute-start(bf16[512,128]{1,0:T(8,128)(2,1)S(1)} %get-tuple-element.60), channel_id=1, source_target_pairs={{0,7},{1,0},{2,1},{3,2},{4,3},{5,4},{6,5},{7,6},{8,15},{9,8},{10,9... | collective-permute-start | bytes 393224 | tf_op jit(solution)/shard_map/ppermute | solution.py:318
  20.1 6.1 %collective-permute-done.17.refs_3_ = bf16[512,128]{1,0:T(8,128)(2,1)S(1)} collective-permute-done((bf16[512,128]{1,0:T(8,128)(2,1)S(1)}, bf16[512,128]{1,0:T(8,128)(2,1)S(1)}, u32[]{:S(2)}, u32[]{:S(2)}) %collective-permute-start.17) | collective-permute-done | bytes 131104 | tf_op jit(solution)/shard_map/ppermute | solution.py:318
  26.5 5.7 %collective-permute-start.1 = (bf16[512,128]{1,0:T(8,128)(2,1)S(1)}, bf16[512,128]{1,0:T(8,128)(2,1)S(1)}, u32[]{:S(2)}, u32[]{:S(2)}) collective-permute-start(bf16[512,128]{1,0:T(8,128)(2,1)S(1)} %get-tuple-element.39), channel_id=1, source_target_pairs={{0,2},{1,3},{2,4},{3,5},{4,6},{5,7},{6,0},{7,1},{8,10},{9,11},{10,... | collective-permute-start | bytes 393224 | tf_op jit(solution)/shard_map/ppermute | solution.py:318
  32.4 4.2 %collective-permute-start.2 = (bf16[512,128]{1,0:T(8,128)(2,1)S(1)}, bf16[512,128]{1,0:T(8,128)(2,1)S(1)}, u32[]{:S(2)}, u32[]{:S(2)}) collective-permute-start(bf16[512,128]{1,0:T(8,128)(2,1)S(1)} %get-tuple-element.40), channel_id=1, source_target_pairs={{0,3},{1,4},{2,5},{3,6},{4,7},{5,0},{6,1},{7,2},{8,11},{9,12},{10,... | collective-permute-start | bytes 393224 | tf_op jit(solution)/shard_map/ppermute | solution.py:318
  36.6 2.8 %collective-permute-start.3 = (bf16[512,128]{1,0:T(8,128)(2,1)S(1)}, bf16[512,128]{1,0:T(8,128)(2,1)S(1)}, u32[]{:S(2)}, u32[]{:S(2)}) collective-permute-start(bf16[512,128]{1,0:T(8,128)(2,1)S(1)} %get-tuple-element.41), channel_id=1, source_target_pairs={{0,4},{1,5},{2,6},{3,7},{4,0},{5,1},{6,2},{7,3},{8,12},{9,13},{10,... | collective-permute-start | bytes 393224 | tf_op jit(solution)/shard_map/ppermute | solution.py:318
  39.3 3.5 %collective-permute-start.4 = (bf16[512,128]{1,0:T(8,128)(2,1)S(1)}, bf16[512,128]{1,0:T(8,128)(2,1)S(1)}, u32[]{:S(2)}, u32[]{:S(2)}) collective-permute-start(bf16[512,128]{1,0:T(8,128)(2,1)S(1)} %get-tuple-element.42), channel_id=1, source_target_pairs={{0,5},{1,6},{2,7},{3,0},{4,1},{5,2},{6,3},{7,4},{8,13},{9,14},{10,... | collective-permute-start | bytes 393224 | tf_op jit(solution)/shard_map/ppermute | solution.py:318
  42.8 3.4 %collective-permute-start.5 = (bf16[512,128]{1,0:T(8,128)(2,1)S(1)}, bf16[512,128]{1,0:T(8,128)(2,1)S(1)}, u32[]{:S(2)}, u32[]{:S(2)}) collective-permute-start(bf16[512,128]{1,0:T(8,128)(2,1)S(1)} %get-tuple-element.43), channel_id=1, source_target_pairs={{0,6},{1,7},{2,0},{3,1},{4,2},{5,3},{6,4},{7,5},{8,14},{9,15},{10,... | collective-permute-start | bytes 393224 | tf_op jit(solution)/shard_map/ppermute | solution.py:318
  46.4 1.6 %copy-done.4 = f32[32,2,64,128]{3,2,1,0:T(8,128)S(1)} copy-done((f32[32,2,64,128]{3,2,1,0:T(8,128)S(1)}, f32[32,2,64,128]{3,2,1,0:T(8,128)}, u32[]{:S(2)}) %copy-start.4) | copy-done | bytes 2097176
  48.0 15.0 %shard_map.103 = (bf16[128,128]{1,0:T(8,128)(2,1)S(1)}, bf16[128,128]{1,0:T(8,128)(2,1)S(1)}, bf16[128,128]{1,0:T(8,128)(2,1)S(1)}, bf16[128,128]{1,0:T(8,128)(2...) custom-call(s32[1]{0:T(128)} %bitcast.index_ref, ...), custom_call_target="tpu_custom_call" | custom-call | flops 6000000000 | bytes 4000000 | tf_op jit(solution)/shard_map/pallas_call | solution.py:344
  63.2 3.5 %collective-permute-start.23 = (bf16[128,128]{1,0:T(8,128)(2,1)S(1)}, bf16[128,128]{1,0:T(8,128)(2,1)S(1)}, u32[]{:S(2)}, u32[]{:S(2)}) collective-permute-start(bf16[128,128]{1,0:T(8,128)(2,1)S(1)} %get-tuple-element.62), channel_id=1, source_target_pairs={{0,15},{1,8},{2,9},{3,10},{4,11},{5,12},{6,13},{7,14},{8,23},{9,16... | collective-permute-start | bytes 98312 | tf_op jit(solution)/shard_map/ppermute | solution.py:318
  66.6 6.0 %collective-permute-start.24 = (bf16[128,128]{1,0:T(8,128)(2,1)S(1)}, bf16[128,128]{1,0:T(8,128)(2,1)S(1)}, u32[]{:S(2)}, u32[]{:S(2)}) collective-permute-start(bf16[128,128]{1,0:T(8,128)(2,1)S(1)} %get-tuple-element.63), channel_id=1, source_target_pairs={{0,14},{1,15},{2,8},{3,9},{4,10},{5,11},{6,12},{7,13},{8,22},{9,23... | collective-permute-start | bytes 98312 | tf_op jit(solution)/shard_map/ppermute | solution.py:318
  72.6 3.5 %collective-permute-start.26 = (bf16[128,128]{1,0:T(8,128)(2,1)S(1)}, bf16[128,128]{1,0:T(8,128)(2,1)S(1)}, u32[]{:S(2)}, u32[]{:S(2)}) collective-permute-start(bf16[128,128]{1,0:T(8,128)(2,1)S(1)} %get-tuple-element.65), channel_id=1, source_target_pairs={{0,12},{1,13},{2,14},{3,15},{4,8},{5,9},{6,10},{7,11},{8,20},{9,21... | collective-permute-start | bytes 98312 | tf_op jit(solution)/shard_map/ppermute | solution.py:318
  76.1 15.0 %shard_map.101 = (bf16[128,128]{1,0:T(8,128)(2,1)S(1)}, bf16[128,128]{1,0:T(8,128)(2,1)S(1)}, bf16[128,128]{1,0:T(8,128)(2,1)S(1)}, bf16[128,128]{1,0:T(8,128)(2...) custom-call(s32[1]{0:T(128)} %bitcast.index_ref, ...), custom_call_target="tpu_custom_call" | custom-call | flops 6000000000 | bytes 4000000 | tf_op jit(solution)/shard_map/pallas_call | solution.py:344
  91.1 1.9 %collective-permute-start.28 = (bf16[128,128]{1,0:T(8,128)(2,1)S(1)}, bf16[128,128]{1,0:T(8,128)(2,1)S(1)}, u32[]{:S(2)}, u32[]{:S(2)}) collective-permute-start(bf16[128,128]{1,0:T(8,128)(2,1)S(1)} %get-tuple-element.67), channel_id=1, source_target_pairs={{0,10},{1,11},{2,12},{3,13},{4,14},{5,15},{6,8},{7,9},{8,18},{9,19... | collective-permute-start | bytes 98312 | tf_op jit(solution)/shard_map/ppermute | solution.py:318
  93.0 1.1 %collective-permute-start.29 = (bf16[128,128]{1,0:T(8,128)(2,1)S(1)}, bf16[128,128]{1,0:T(8,128)(2,1)S(1)}, u32[]{:S(2)}, u32[]{:S(2)}) collective-permute-start(bf16[128,128]{1,0:T(8,128)(2,1)S(1)} %get-tuple-element.68), channel_id=1, source_target_pairs={{0,9},{1,10},{2,11},{3,12},{4,13},{5,14},{6,15},{7,8},{8,17},{9,18... | collective-permute-start | bytes 98312 | tf_op jit(solution)/shard_map/ppermute | solution.py:318
  94.5 3.1 %collective-permute-start.8 = (bf16[128,128]{1,0:T(8,128)(2,1)S(1)}, bf16[128,128]{1,0:T(8,128)(2,1)S(1)}, u32[]{:S(2)}, u32[]{:S(2)}) collective-permute-start(bf16[128,128]{1,0:T(8,128)(2,1)S(1)} %get-tuple-element.46), channel_id=1, source_target_pairs={{0,15},{1,8},{2,9},{3,10},{4,11},{5,12},{6,13},{7,14},{8,23},{9,16... | collective-permute-start | bytes 98312 | tf_op jit(solution)/shard_map/ppermute | solution.py:318
  97.6 2.2 %collective-permute-start.9 = (bf16[128,128]{1,0:T(8,128)(2,1)S(1)}, bf16[128,128]{1,0:T(8,128)(2,1)S(1)}, u32[]{:S(2)}, u32[]{:S(2)}) collective-permute-start(bf16[128,128]{1,0:T(8,128)(2,1)S(1)} %get-tuple-element.47), channel_id=1, source_target_pairs={{0,14},{1,15},{2,8},{3,9},{4,10},{5,11},{6,12},{7,13},{8,22},{9,23... | collective-permute-start | bytes 98312 | tf_op jit(solution)/shard_map/ppermute | solution.py:318
  100.9 1.9 %collective-permute-start.11 = (bf16[128,128]{1,0:T(8,128)(2,1)S(1)}, bf16[128,128]{1,0:T(8,128)(2,1)S(1)}, u32[]{:S(2)}, u32[]{:S(2)}) collective-permute-start(bf16[128,128]{1,0:T(8,128)(2,1)S(1)} %get-tuple-element.49), channel_id=1, source_target_pairs={{0,12},{1,13},{2,14},{3,15},{4,8},{5,9},{6,10},{7,11},{8,20},{9,21... | collective-permute-start | bytes 98312 | tf_op jit(solution)/shard_map/ppermute | solution.py:318
  103.0 2.2 %collective-permute-start.13 = (bf16[128,128]{1,0:T(8,128)(2,1)S(1)}, bf16[128,128]{1,0:T(8,128)(2,1)S(1)}, u32[]{:S(2)}, u32[]{:S(2)}) collective-permute-start(bf16[128,128]{1,0:T(8,128)(2,1)S(1)} %get-tuple-element.51), channel_id=1, source_target_pairs={{0,10},{1,11},{2,12},{3,13},{4,14},{5,15},{6,8},{7,9},{8,18},{9,19... | collective-permute-start | bytes 98312 | tf_op jit(solution)/shard_map/ppermute | solution.py:318
  105.5 1.2 %collective-permute-done.11.refs_4_ = bf16[128,128]{1,0:T(8,128)(2,1)S(1)} collective-permute-done((bf16[128,128]{1,0:T(8,128)(2,1)S(1)}, bf16[128,128]{1,0:T(8,128)(2,1)S(1)}, u32[]{:S(2)}, u32[]{:S(2)}) %collective-permute-start.11) | collective-permute-done | bytes 32800 | tf_op jit(solution)/shard_map/ppermute | solution.py:318
  106.6 2.2 %collective-permute-done.12.refs_5_ = bf16[128,128]{1,0:T(8,128)(2,1)S(1)} collective-permute-done((bf16[128,128]{1,0:T(8,128)(2,1)S(1)}, bf16[128,128]{1,0:T(8,128)(2,1)S(1)}, u32[]{:S(2)}, u32[]{:S(2)}) %collective-permute-start.12) | collective-permute-done | bytes 32800 | tf_op jit(solution)/shard_map/ppermute | solution.py:318
  109.4 2.8 %collective-permute-done.14.refs_7_ = bf16[128,128]{1,0:T(8,128)(2,1)S(1)} collective-permute-done((bf16[128,128]{1,0:T(8,128)(2,1)S(1)}, bf16[128,128]{1,0:T(8,128)(2,1)S(1)}, u32[]{:S(2)}, u32[]{:S(2)}) %collective-permute-start.14) | collective-permute-done | bytes 32800 | tf_op jit(solution)/shard_map/ppermute | solution.py:318
  112.2 1.3 %shard_map.104 = bf16[8,64,512]{2,1,0:T(8,128)(2,1)} custom-call(s32[1]{0:T(128)} %bitcast.index_ref, bf16[128,128]{1,0:T(8,128)(2,1)S(1)} %collective-permute-done.7.refs_0_, bf16[128,128]{1,0:T(8,128)(2,1)S(1)} %collective-permute-done.8.refs_1_, bf16[128,128]{1,0:T(8,128)(2,1)S(1)} %collective-permute-done.9.refs_2_, ...), custom_call_target="tpu_custom_call" | custom-call | tf_op jit(solution)/shard_map/pallas_call | solution.py:358
  (58 shorter events, 6.3 us)
Async XLA Ops:
  4.2 42.2 %copy-start.7 = (bf16[128,192]{1,0:T(8,128)(2,1)S(1)}, bf16[128,192]{1,0:T(8,128)(2,1)}, u32[]{:S(2)}) copy-start(bf16[128,192]{1,0:T(8,128)(2,1)} %constant.27.clone.refs_12_) | copy-start | bytes 147460
  4.2 42.2 %copy-start.8 = (bf16[256,96]{1,0:T(8,128)(2,1)S(1)}, bf16[256,96]{1,0:T(8,128)(2,1)}, u32[]{:S(2)}) copy-start(bf16[256,96]{1,0:T(8,128)(2,1)} %constant.26.clone.refs_11_) | copy-start | bytes 147460
  5.2 12.0 %collective-permute-start.15 = (bf16[512,128]{1,0:T(8,128)(2,1)S(1)}, bf16[512,128]{1,0:T(8,128)(2,1)S(1)}, u32[]{:S(2)}, u32[]{:S(2)}) collective-permute-start(bf16[512,128]{1,0:T(8,128)(2,1)S(1)} %get-tuple-element.54), channel_id=1, source_target_pairs={{0,1},{1,2},{2,3},{3,4},{4,5},{5,6},{6,7},{7,0},{8,9},{9,10},{10,1... | collective-permute-start | bytes 393224 | tf_op jit(solution)/shard_map/ppermute | solution.py:318
  8.3 10.4 %collective-permute-start.16 = (bf16[512,128]{1,0:T(8,128)(2,1)S(1)}, bf16[512,128]{1,0:T(8,128)(2,1)S(1)}, u32[]{:S(2)}, u32[]{:S(2)}) collective-permute-start(bf16[512,128]{1,0:T(8,128)(2,1)S(1)} %get-tuple-element.55), channel_id=1, source_target_pairs={{0,2},{1,3},{2,4},{3,5},{4,6},{5,7},{6,0},{7,1},{8,10},{9,11},{10,... | collective-permute-start | bytes 393224 | tf_op jit(solution)/shard_map/ppermute | solution.py:318
  9.8 16.3 %collective-permute-start.17 = (bf16[512,128]{1,0:T(8,128)(2,1)S(1)}, bf16[512,128]{1,0:T(8,128)(2,1)S(1)}, u32[]{:S(2)}, u32[]{:S(2)}) collective-permute-start(bf16[512,128]{1,0:T(8,128)(2,1)S(1)} %get-tuple-element.56), channel_id=1, source_target_pairs={{0,3},{1,4},{2,5},{3,6},{4,7},{5,0},{6,1},{7,2},{8,11},{9,12},{10,... | collective-permute-start | bytes 393224 | tf_op jit(solution)/shard_map/ppermute | solution.py:318
  12.4 14.1 %collective-permute-start.18 = (bf16[512,128]{1,0:T(8,128)(2,1)S(1)}, bf16[512,128]{1,0:T(8,128)(2,1)S(1)}, u32[]{:S(2)}, u32[]{:S(2)}) collective-permute-start(bf16[512,128]{1,0:T(8,128)(2,1)S(1)} %get-tuple-element.57), channel_id=1, source_target_pairs={{0,4},{1,5},{2,6},{3,7},{4,0},{5,1},{6,2},{7,3},{8,12},{9,13},{10,... | collective-permute-start | bytes 393224 | tf_op jit(solution)/shard_map/ppermute | solution.py:318
  13.6 18.8 %collective-permute-start.19 = (bf16[512,128]{1,0:T(8,128)(2,1)S(1)}, bf16[512,128]{1,0:T(8,128)(2,1)S(1)}, u32[]{:S(2)}, u32[]{:S(2)}) collective-permute-start(bf16[512,128]{1,0:T(8,128)(2,1)S(1)} %get-tuple-element.58), channel_id=1, source_target_pairs={{0,5},{1,6},{2,7},{3,0},{4,1},{5,2},{6,3},{7,4},{8,13},{9,14},{10,... | collective-permute-start | bytes 393224 | tf_op jit(solution)/shard_map/ppermute | solution.py:318
  17.3 19.3 %collective-permute-start.20 = (bf16[512,128]{1,0:T(8,128)(2,1)S(1)}, bf16[512,128]{1,0:T(8,128)(2,1)S(1)}, u32[]{:S(2)}, u32[]{:S(2)}) collective-permute-start(bf16[512,128]{1,0:T(8,128)(2,1)S(1)} %get-tuple-element.59), channel_id=1, source_target_pairs={{0,6},{1,7},{2,0},{3,1},{4,2},{5,3},{6,4},{7,5},{8,14},{9,15},{10,... | collective-permute-start | bytes 393224 | tf_op jit(solution)/shard_map/ppermute | solution.py:318
  18.7 20.7 %collective-permute-start.21 = (bf16[512,128]{1,0:T(8,128)(2,1)S(1)}, bf16[512,128]{1,0:T(8,128)(2,1)S(1)}, u32[]{:S(2)}, u32[]{:S(2)}) collective-permute-start(bf16[512,128]{1,0:T(8,128)(2,1)S(1)} %get-tuple-element.60), channel_id=1, source_target_pairs={{0,7},{1,0},{2,1},{3,2},{4,3},{5,4},{6,5},{7,6},{8,15},{9,8},{10,9... | collective-permute-start | bytes 393224 | tf_op jit(solution)/shard_map/ppermute | solution.py:318
  26.2 16.7 %collective-permute-start = (bf16[512,128]{1,0:T(8,128)(2,1)S(1)}, bf16[512,128]{1,0:T(8,128)(2,1)S(1)}, u32[]{:S(2)}, u32[]{:S(2)}) collective-permute-start(bf16[512,128]{1,0:T(8,128)(2,1)S(1)} %get-tuple-element.38), channel_id=1, source_target_pairs={{0,1},{1,2},{2,3},{3,4},{4,5},{5,6},{6,7},{7,0},{8,9},{9,10},{10,1... | collective-permute-start | bytes 393224 | tf_op jit(solution)/shard_map/ppermute | solution.py:318
  26.5 19.8 %collective-permute-start.1 = (bf16[512,128]{1,0:T(8,128)(2,1)S(1)}, bf16[512,128]{1,0:T(8,128)(2,1)S(1)}, u32[]{:S(2)}, u32[]{:S(2)}) collective-permute-start(bf16[512,128]{1,0:T(8,128)(2,1)S(1)} %get-tuple-element.39), channel_id=1, source_target_pairs={{0,2},{1,3},{2,4},{3,5},{4,6},{5,7},{6,0},{7,1},{8,10},{9,11},{10,... | collective-permute-start | bytes 393224 | tf_op jit(solution)/shard_map/ppermute | solution.py:318
  32.4 30.6 %collective-permute-start.2 = (bf16[512,128]{1,0:T(8,128)(2,1)S(1)}, bf16[512,128]{1,0:T(8,128)(2,1)S(1)}, u32[]{:S(2)}, u32[]{:S(2)}) collective-permute-start(bf16[512,128]{1,0:T(8,128)(2,1)S(1)} %get-tuple-element.40), channel_id=1, source_target_pairs={{0,3},{1,4},{2,5},{3,6},{4,7},{5,0},{6,1},{7,2},{8,11},{9,12},{10,... | collective-permute-start | bytes 393224 | tf_op jit(solution)/shard_map/ppermute | solution.py:318
  36.6 26.6 %collective-permute-start.3 = (bf16[512,128]{1,0:T(8,128)(2,1)S(1)}, bf16[512,128]{1,0:T(8,128)(2,1)S(1)}, u32[]{:S(2)}, u32[]{:S(2)}) collective-permute-start(bf16[512,128]{1,0:T(8,128)(2,1)S(1)} %get-tuple-element.41), channel_id=1, source_target_pairs={{0,4},{1,5},{2,6},{3,7},{4,0},{5,1},{6,2},{7,3},{8,12},{9,13},{10,... | collective-permute-start | bytes 393224 | tf_op jit(solution)/shard_map/ppermute | solution.py:318
  39.3 27.3 %collective-permute-start.4 = (bf16[512,128]{1,0:T(8,128)(2,1)S(1)}, bf16[512,128]{1,0:T(8,128)(2,1)S(1)}, u32[]{:S(2)}, u32[]{:S(2)}) collective-permute-start(bf16[512,128]{1,0:T(8,128)(2,1)S(1)} %get-tuple-element.42), channel_id=1, source_target_pairs={{0,5},{1,6},{2,7},{3,0},{4,1},{5,2},{6,3},{7,4},{8,13},{9,14},{10,... | collective-permute-start | bytes 393224 | tf_op jit(solution)/shard_map/ppermute | solution.py:318
  42.8 29.8 %collective-permute-start.5 = (bf16[512,128]{1,0:T(8,128)(2,1)S(1)}, bf16[512,128]{1,0:T(8,128)(2,1)S(1)}, u32[]{:S(2)}, u32[]{:S(2)}) collective-permute-start(bf16[512,128]{1,0:T(8,128)(2,1)S(1)} %get-tuple-element.43), channel_id=1, source_target_pairs={{0,6},{1,7},{2,0},{3,1},{4,2},{5,3},{6,4},{7,5},{8,14},{9,15},{10,... | collective-permute-start | bytes 393224 | tf_op jit(solution)/shard_map/ppermute | solution.py:318
  46.3 26.4 %collective-permute-start.6 = (bf16[512,128]{1,0:T(8,128)(2,1)S(1)}, bf16[512,128]{1,0:T(8,128)(2,1)S(1)}, u32[]{:S(2)}, u32[]{:S(2)}) collective-permute-start(bf16[512,128]{1,0:T(8,128)(2,1)S(1)} %get-tuple-element.44), channel_id=1, source_target_pairs={{0,7},{1,0},{2,1},{3,2},{4,3},{5,4},{6,5},{7,6},{8,15},{9,8},{10,9... | collective-permute-start | bytes 393224 | tf_op jit(solution)/shard_map/ppermute | solution.py:318
  63.0 13.1 %collective-permute-start.22 = (bf16[128,128]{1,0:T(8,128)(2,1)S(1)}, bf16[128,128]{1,0:T(8,128)(2,1)S(1)}, u32[]{:S(2)}, u32[]{:S(2)}) collective-permute-start(bf16[128,128]{1,0:T(8,128)(2,1)S(1)} %get-tuple-element.61), channel_id=1, source_target_pairs={{0,8},{1,9},{2,10},{3,11},{4,12},{5,13},{6,14},{7,15},{8,16},{9,17... | collective-permute-start | bytes 98312 | tf_op jit(solution)/shard_map/ppermute | solution.py:318
  63.2 28.0 %collective-permute-start.23 = (bf16[128,128]{1,0:T(8,128)(2,1)S(1)}, bf16[128,128]{1,0:T(8,128)(2,1)S(1)}, u32[]{:S(2)}, u32[]{:S(2)}) collective-permute-start(bf16[128,128]{1,0:T(8,128)(2,1)S(1)} %get-tuple-element.62), channel_id=1, source_target_pairs={{0,15},{1,8},{2,9},{3,10},{4,11},{5,12},{6,13},{7,14},{8,23},{9,16... | collective-permute-start | bytes 98312 | tf_op jit(solution)/shard_map/ppermute | solution.py:318
  66.6 26.3 %collective-permute-start.24 = (bf16[128,128]{1,0:T(8,128)(2,1)S(1)}, bf16[128,128]{1,0:T(8,128)(2,1)S(1)}, u32[]{:S(2)}, u32[]{:S(2)}) collective-permute-start(bf16[128,128]{1,0:T(8,128)(2,1)S(1)} %get-tuple-element.63), channel_id=1, source_target_pairs={{0,14},{1,15},{2,8},{3,9},{4,10},{5,11},{6,12},{7,13},{8,22},{9,23... | collective-permute-start | bytes 98312 | tf_op jit(solution)/shard_map/ppermute | solution.py:318
  72.6 21.5 %collective-permute-start.25 = (bf16[128,128]{1,0:T(8,128)(2,1)S(1)}, bf16[128,128]{1,0:T(8,128)(2,1)S(1)}, u32[]{:S(2)}, u32[]{:S(2)}) collective-permute-start(bf16[128,128]{1,0:T(8,128)(2,1)S(1)} %get-tuple-element.64), channel_id=1, source_target_pairs={{0,13},{1,14},{2,15},{3,8},{4,9},{5,10},{6,11},{7,12},{8,21},{9,22... | collective-permute-start | bytes 98312 | tf_op jit(solution)/shard_map/ppermute | solution.py:318
  72.6 21.9 %collective-permute-start.26 = (bf16[128,128]{1,0:T(8,128)(2,1)S(1)}, bf16[128,128]{1,0:T(8,128)(2,1)S(1)}, u32[]{:S(2)}, u32[]{:S(2)}) collective-permute-start(bf16[128,128]{1,0:T(8,128)(2,1)S(1)} %get-tuple-element.65), channel_id=1, source_target_pairs={{0,12},{1,13},{2,14},{3,15},{4,8},{5,9},{6,10},{7,11},{8,20},{9,21... | collective-permute-start | bytes 98312 | tf_op jit(solution)/shard_map/ppermute | solution.py:318
  76.1 21.6 %collective-permute-start.27 = (bf16[128,128]{1,0:T(8,128)(2,1)S(1)}, bf16[128,128]{1,0:T(8,128)(2,1)S(1)}, u32[]{:S(2)}, u32[]{:S(2)}) collective-permute-start(bf16[128,128]{1,0:T(8,128)(2,1)S(1)} %get-tuple-element.66), channel_id=1, source_target_pairs={{0,11},{1,12},{2,13},{3,14},{4,15},{5,8},{6,9},{7,10},{8,19},{9,20... | collective-permute-start | bytes 98312 | tf_op jit(solution)/shard_map/ppermute | solution.py:318
  91.1 8.8 %collective-permute-start.28 = (bf16[128,128]{1,0:T(8,128)(2,1)S(1)}, bf16[128,128]{1,0:T(8,128)(2,1)S(1)}, u32[]{:S(2)}, u32[]{:S(2)}) collective-permute-start(bf16[128,128]{1,0:T(8,128)(2,1)S(1)} %get-tuple-element.67), channel_id=1, source_target_pairs={{0,10},{1,11},{2,12},{3,13},{4,14},{5,15},{6,8},{7,9},{8,18},{9,19... | collective-permute-start | bytes 98312 | tf_op jit(solution)/shard_map/ppermute | solution.py:318
  93.0 7.9 %collective-permute-start.29 = (bf16[128,128]{1,0:T(8,128)(2,1)S(1)}, bf16[128,128]{1,0:T(8,128)(2,1)S(1)}, u32[]{:S(2)}, u32[]{:S(2)}) collective-permute-start(bf16[128,128]{1,0:T(8,128)(2,1)S(1)} %get-tuple-element.68), channel_id=1, source_target_pairs={{0,9},{1,10},{2,11},{3,12},{4,13},{5,14},{6,15},{7,8},{8,17},{9,18... | collective-permute-start | bytes 98312 | tf_op jit(solution)/shard_map/ppermute | solution.py:318
  94.1 8.6 %collective-permute-start.7 = (bf16[128,128]{1,0:T(8,128)(2,1)S(1)}, bf16[128,128]{1,0:T(8,128)(2,1)S(1)}, u32[]{:S(2)}, u32[]{:S(2)}) collective-permute-start(bf16[128,128]{1,0:T(8,128)(2,1)S(1)} %get-tuple-element.45), channel_id=1, source_target_pairs={{0,8},{1,9},{2,10},{3,11},{4,12},{5,13},{6,14},{7,15},{8,16},{9,17... | collective-permute-start | bytes 98312 | tf_op jit(solution)/shard_map/ppermute | solution.py:318
  94.5 8.5 %collective-permute-start.8 = (bf16[128,128]{1,0:T(8,128)(2,1)S(1)}, bf16[128,128]{1,0:T(8,128)(2,1)S(1)}, u32[]{:S(2)}, u32[]{:S(2)}) collective-permute-start(bf16[128,128]{1,0:T(8,128)(2,1)S(1)} %get-tuple-element.46), channel_id=1, source_target_pairs={{0,15},{1,8},{2,9},{3,10},{4,11},{5,12},{6,13},{7,14},{8,23},{9,16... | collective-permute-start | bytes 98312 | tf_op jit(solution)/shard_map/ppermute | solution.py:318
  97.6 7.6 %collective-permute-start.9 = (bf16[128,128]{1,0:T(8,128)(2,1)S(1)}, bf16[128,128]{1,0:T(8,128)(2,1)S(1)}, u32[]{:S(2)}, u32[]{:S(2)}) collective-permute-start(bf16[128,128]{1,0:T(8,128)(2,1)S(1)} %get-tuple-element.47), channel_id=1, source_target_pairs={{0,14},{1,15},{2,8},{3,9},{4,10},{5,11},{6,12},{7,13},{8,22},{9,23... | collective-permute-start | bytes 98312 | tf_op jit(solution)/shard_map/ppermute | solution.py:318
  99.9 5.6 %collective-permute-start.10 = (bf16[128,128]{1,0:T(8,128)(2,1)S(1)}, bf16[128,128]{1,0:T(8,128)(2,1)S(1)}, u32[]{:S(2)}, u32[]{:S(2)}) collective-permute-start(bf16[128,128]{1,0:T(8,128)(2,1)S(1)} %get-tuple-element.48), channel_id=1, source_target_pairs={{0,13},{1,14},{2,15},{3,8},{4,9},{5,10},{6,11},{7,12},{8,21},{9,22... | collective-permute-start | bytes 98312 | tf_op jit(solution)/shard_map/ppermute | solution.py:318
  100.9 5.8 %collective-permute-start.11 = (bf16[128,128]{1,0:T(8,128)(2,1)S(1)}, bf16[128,128]{1,0:T(8,128)(2,1)S(1)}, u32[]{:S(2)}, u32[]{:S(2)}) collective-permute-start(bf16[128,128]{1,0:T(8,128)(2,1)S(1)} %get-tuple-element.49), channel_id=1, source_target_pairs={{0,12},{1,13},{2,14},{3,15},{4,8},{5,9},{6,10},{7,11},{8,20},{9,21... | collective-permute-start | bytes 98312 | tf_op jit(solution)/shard_map/ppermute | solution.py:318
  102.7 6.1 %collective-permute-start.12 = (bf16[128,128]{1,0:T(8,128)(2,1)S(1)}, bf16[128,128]{1,0:T(8,128)(2,1)S(1)}, u32[]{:S(2)}, u32[]{:S(2)}) collective-permute-start(bf16[128,128]{1,0:T(8,128)(2,1)S(1)} %get-tuple-element.50), channel_id=1, source_target_pairs={{0,11},{1,12},{2,13},{3,14},{4,15},{5,8},{6,9},{7,10},{8,19},{9,20... | collective-permute-start | bytes 98312 | tf_op jit(solution)/shard_map/ppermute | solution.py:318
  103.0 6.4 %collective-permute-start.13 = (bf16[128,128]{1,0:T(8,128)(2,1)S(1)}, bf16[128,128]{1,0:T(8,128)(2,1)S(1)}, u32[]{:S(2)}, u32[]{:S(2)}) collective-permute-start(bf16[128,128]{1,0:T(8,128)(2,1)S(1)} %get-tuple-element.51), channel_id=1, source_target_pairs={{0,10},{1,11},{2,12},{3,13},{4,14},{5,15},{6,8},{7,9},{8,18},{9,19... | collective-permute-start | bytes 98312 | tf_op jit(solution)/shard_map/ppermute | solution.py:318
  105.2 6.9 %collective-permute-start.14 = (bf16[128,128]{1,0:T(8,128)(2,1)S(1)}, bf16[128,128]{1,0:T(8,128)(2,1)S(1)}, u32[]{:S(2)}, u32[]{:S(2)}) collective-permute-start(bf16[128,128]{1,0:T(8,128)(2,1)S(1)} %get-tuple-element.52), channel_id=1, source_target_pairs={{0,9},{1,10},{2,11},{3,12},{4,13},{5,14},{6,15},{7,8},{8,17},{9,18... | collective-permute-start | bytes 98312 | tf_op jit(solution)/shard_map/ppermute | solution.py:318
  (9 other events, 146.3 us)

commit v4 on v2

--- a/solution.py
+++ b/solution.py
@@ -14,6 +14,10 @@
 HALF = 64
 INNER = 64
 STEP = 16
+EXTRA = 16
+DOUBLINGS = 4
+SCALE = 215.0
+SMALLEST = 1e-30
 WIDE = 16
 F32 = jnp.float32
 BF16 = jnp.bfloat16
@@ -163,41 +167,45 @@
         wide = np.stack([np.cos(theta), np.sin(theta)], axis=1).astype(np.float32)
         return np.ascontiguousarray(np.broadcast_to(wide[..., None], wide.shape + (LANES,)))
 
-    coarse = turns(np.arange(0, INNER, STEP))
-    fine = turns(np.arange(STEP))
-    return forward_a, forward_b, back_b, back_a, coarse, fine
-
-
-def pack(parts, source, low, place):
-    rows = source.shape[0] // 2
-    for e in range(parts // 2):
-        tile = source[:, LANES * e : LANES * (e + 1)].astype(F32)
-        early, late = tile[:rows], tile[rows:]
-        place(2 * e, jnp.where(low, early, swap_halves(late)).astype(BF16))
-        place(2 * e + 1, jnp.where(low, swap_halves(early), late).astype(BF16))
-
-
-def pack_kernel(parts, index_ref, k_ref, v_ref, h_ref, *refs):
-    outs, held = refs[:-1], refs[-1]
+    return np.concatenate([forward_a, back_a, forward_b, back_b], axis=1), turns(b)
+
+
+def fetched(sources, targets, sems):
+    copies = [pltpu.make_async_copy(a, b, sems.at[i]) for i, (a, b) in enumerate(zip(sources, targets))]
+    for copy in copies:
+        copy.start()
+    return copies
+
+
+def pack_kernel(parts, index_ref, *refs):
+    sources, outs, held, arrived, sems = refs[:4], refs[4 : 4 + parts], refs[-6], refs[-5:-1], refs[-1]
+    k_ref, v_ref, h_ref, q_ref = arrived
     rows = k_ref.shape[0] // 2
     low = lower_half((rows, LANES))
-    for n, source in enumerate((k_ref, v_ref, h_ref)):
-
-        def place(d, value, n=n):
-            held[d, n * rows : (n + 1) * rows, :] = value
-
-        pack(parts, source, low, place)
+    for copy in fetched(sources, arrived, sems):
+        copy.wait()
+
+    def place(e, at, tile, low):
+        half = tile.shape[0] // 2
+        early, late = tile[:half], tile[half:]
+        held[2 * e, at : at + half, :] = jnp.where(low, early, swap_halves(late)).astype(BF16)
+        held[2 * e + 1, at : at + half, :] = jnp.where(low, swap_halves(early), late).astype(BF16)
+
+    for e in range(parts // 2):
+        lanes = slice(LANES * e, LANES * (e + 1))
+        product = k_ref[:, lanes].astype(F32) * v_ref[:, lanes].astype(F32)
+        largest = jnp.max(jnp.abs(product), axis=0, keepdims=True)
+        largest = jnp.maximum(largest * 1.01, SMALLEST).astype(BF16).astype(F32)
+        code = product * (SCALE / largest)
+        power = code * code
+        for _ in range(DOUBLINGS - 1):
+            power = power * power
+        place(e, 0, jnp.where(code < 0.0, -power, power), low)
+        place(e, rows, h_ref[:, lanes].astype(F32), low)
+        place(e, 2 * rows, q_ref[:, lanes].astype(F32), low)
+        place(e, 3 * rows, jnp.broadcast_to(largest, (2 * EXTRA, LANES)), low[:EXTRA])
     for n, out in enumerate(outs):
         out[...] = held[lax.rem(index_ref[0] + n, parts)]
-
-
-def pack_gate_kernel(parts, q_ref, out_ref):
-    low = lower_half((q_ref.shape[0] // 2, LANES))
-
-    def place(d, value):
-        out_ref[d] = value
-
-    pack(parts, q_ref, low, place)
 
 
 def unpack_kernel(parts, index_ref, *refs):
@@ -214,8 +222,12 @@
 
 def convolve_kernel(parts, outer, index_ref, *refs):
     blocks = refs[:parts]
-    skip_ref, fa_ref, fb_ref, bb_ref, ba_ref, coarse_ref, fine_ref, out_ref, x_s, z_s, w_s, y_s = refs[parts:]
-    rows = out_ref.shape[1]
+    skip_ref, sources = refs[parts], refs[parts + 1 : parts + 3]
+    outs, (x_s, z_s, w_s, y_s, p_s) = refs[parts + 3 : 2 * parts + 3], refs[2 * parts + 3 : 2 * parts + 8]
+    matrix_ref, turn_ref = arrived = refs[2 * parts + 8 : 2 * parts + 10]
+    copies = fetched(sources, arrived, refs[-1])
+    edges = (0, 3 * outer, 6 * outer, 6 * outer + 6 * INNER, 6 * outer + 9 * INNER)
+    rows = outs[0].shape[0]
     per = rows // INNER
     low = lower_half((INNER, LANES))
     lowc = lower_half((outer, LANES))
@@ -224,22 +236,26 @@
         return lax.rem(index_ref[0] + parts - n, parts)
 
     for n, block in enumerate(blocks):
+        scale = block[3 * rows : 3 * rows + EXTRA, :].astype(F32)[:1] * (1.0 / SCALE)
         for m in range(per):
             at = m * INNER
-            k = block[at : at + INNER, :].astype(F32)
-            v = block[rows + at : rows + at + INNER, :].astype(F32)
-            h = block[2 * rows + at : 2 * rows + at + INNER, :].astype(F32)
-            p = k * v
+            code = block[at : at + INNER, :].astype(F32)
+            size = jnp.exp(jnp.log(jnp.abs(code)) * (0.5**DOUBLINGS)) * scale
+            p = jnp.where(code == 0.0, 0.0, jnp.where(code < 0.0, -size, size))
+            p_s[n, at : at + INNER, :] = p
+            h = block[rows + at : rows + at + INNER, :].astype(F32)
             a = origin(n) * (2 * per) + m
             x_s[pl.ds(a, INNER, stride=outer), :] = jnp.where(low, p, swap_halves(h))
             x_s[pl.ds(a + per, INNER, stride=outer), :] = jnp.where(low, swap_halves(p), h)
 
+    for copy in copies:
+        copy.wait()
+
+    def matrix(i):
+        return matrix_ref[:, edges[i] : edges[i + 1]]
+
     def turn(group, n):
-        cos_1, sin_1 = coarse_ref[group, 0], coarse_ref[group, 1]
-        if n == 0:
-            return cos_1, sin_1
-        cos_2, sin_2 = fine_ref[n, 0], fine_ref[n, 1]
-        return cos_1 * cos_2 - sin_1 * sin_2, sin_1 * cos_2 + cos_1 * sin_2
+        return turn_ref[group * STEP + n, 0], turn_ref[group * STEP + n, 1]
 
     def forward_outer(group, carry):
         for n in range(0, STEP, WIDE):
@@ -251,7 +267,7 @@
                 ],
                 axis=1,
             )
-            both = jnp.dot(fa_ref[...], data, preferred_element_type=F32)
+            both = jnp.dot(matrix(0), data, preferred_element_type=F32)
             for j in range(WIDE):
                 re = both[:outer, LANES * j : LANES * (j + 1)]
                 im = both[outer:, LANES * j : LANES * (j + 1)]
@@ -272,7 +288,7 @@
                 ],
                 axis=1,
             )
-            both = jnp.dot(fb_ref[...], data, preferred_element_type=F32)
+            both = jnp.dot(matrix(2), data, preferred_element_type=F32)
             mixed = []
             for j in range(WIDE):
                 re = both[:INNER, LANES * j : LANES * (j + 1)]
@@ -281,7 +297,7 @@
                 mixed.append(
                     stacked(jnp.where(low, re * re_2 - im * im_2, re * im_2 + im * re_2))
                 )
-            both = jnp.dot(bb_ref[...], jnp.concatenate(mixed, axis=1), preferred_element_type=F32)
+            both = jnp.dot(matrix(3), jnp.concatenate(mixed, axis=1), preferred_element_type=F32)
             for j in range(WIDE):
                 straight = both[:INNER, LANES * j : LANES * (j + 1)]
                 crossed = swap_halves(both[INNER:, LANES * j : LANES * (j + 1)])
@@ -302,7 +318,7 @@
                 other = swap_halves(value) * sin
                 straight = value * cos
                 data.append(stacked(jnp.where(lowc, straight - other, straight + other)))
-            both = jnp.dot(ba_ref[...], jnp.concatenate(data, axis=1), preferred_element_type=F32)
+            both = jnp.dot(matrix(1), jnp.concatenate(data, axis=1), preferred_element_type=F32)
             for j in range(WIDE):
                 re = both[:outer, LANES * j : LANES * (j + 1)]
                 im = both[outer:, LANES * j : LANES * (j + 1)]
@@ -312,18 +328,12 @@
     lax.fori_loop(0, INNER // STEP, back_outer, 0)
 
     lowr = lower_half((rows, LANES))
-    for n, block in enumerate(blocks):
+    for n, (block, out) in enumerate(zip(blocks, outs)):
         at = pl.multiple_of(origin(n) * 2 * rows, 2 * rows)
         early = y_s[pl.ds(at, rows), :]
         late = y_s[pl.ds(at + rows, rows), :]
-        p = block[:rows, :].astype(F32) * block[rows : 2 * rows, :].astype(F32)
-        out_ref[n] = jnp.where(lowr, early, swap_halves(late)) + skip_ref[...] * p
-
-
-def gate_kernel(parts, index_ref, y_ref, q_ref, *outs):
-    for n, out in enumerate(outs):
-        q = q_ref[lax.rem(index_ref[0] + parts - n, parts)]
-        out[...] = (q.astype(F32) * y_ref[n]).astype(BF16)
+        y = jnp.where(lowr, early, swap_halves(late)) + skip_ref[...] * p_s[n]
+        out[...] = (block[2 * rows : 3 * rows, :].astype(F32) * y).astype(BF16)
 
 
 def joint_shift(value, segment_step, ctx_step):
@@ -345,46 +355,41 @@
     index = jnp.full((1,), device, jnp.int32)
     scalar = pl.BlockSpec(memory_space=pltpu.SMEM)
     whole = pl.BlockSpec(memory_space=pltpu.VMEM)
+    far = pl.BlockSpec(memory_space=pltpu.HBM)
     small = pltpu.CompilerParams(vmem_limit_bytes=24 * 2**20)
+    large = pltpu.CompilerParams(vmem_limit_bytes=60 * 2**20)
 
     def block(*shape, dtype=BF16):
         return jax.ShapeDtypeStruct(shape, dtype)
 
+    size = 3 * rows + EXTRA
     sent = pl.pallas_call(
         functools.partial(pack_kernel, parts),
-        out_shape=(block(3 * rows, LANES),) * parts,
-        in_specs=[scalar, whole, whole, whole],
-        scratch_shapes=[pltpu.VMEM((parts, 3 * rows, LANES), BF16)],
-        compiler_params=small,
-    )(index, key_stream[0], value_stream[0], filter_taps[0])
+        out_shape=(block(size, LANES),) * parts,
+        in_specs=[scalar] + [far] * 4,
+        scratch_shapes=[pltpu.VMEM((parts, size, LANES), BF16)]
+        + [pltpu.VMEM((length, channels), BF16)] * 4
+        + [pltpu.SemaphoreType.DMA((4,))],
+        compiler_params=large,
+    )(index, key_stream[0], value_stream[0], filter_taps[0], query_stream[0])
     slabs = [sent[0]] + [joint_shift(sent[n], 0, n) for n in range(1, parts)]
-    q = pl.pallas_call(
-        functools.partial(pack_gate_kernel, parts),
-        out_shape=block(parts, rows, LANES),
-        compiler_params=small,
-    )(query_stream[0])
-    q, *_ = lax.optimization_barrier((q, *slabs))
-    q = lax.all_to_all(q, "ctx", split_axis=0, concat_axis=0, tiled=True)
     skip = lax.dynamic_slice(skip_weight, (0, device * HALF), (1, HALF))
     consts = [jnp.asarray(t) for t in tables(outer)]
-    y = pl.pallas_call(
+    gated = pl.pallas_call(
         functools.partial(convolve_kernel, parts, outer),
-        out_shape=block(parts, rows, LANES, dtype=F32),
-        in_specs=[scalar] + [whole] * (parts + 1 + len(consts)),
+        out_shape=(block(rows, LANES),) * parts,
+        in_specs=[scalar] + [whole] * (parts + 1) + [far] * len(consts),
         scratch_shapes=[
             pltpu.VMEM((outer * INNER, LANES), F32),
             pltpu.VMEM((2 * outer * INNER, LANES), F32),
             pltpu.VMEM((outer * INNER, LANES), F32),
             pltpu.VMEM((outer * INNER, LANES), F32),
-        ],
-        compiler_params=pltpu.CompilerParams(vmem_limit_bytes=40 * 2**20),
+            pltpu.VMEM((parts, rows, LANES), F32),
+        ]
+        + [pltpu.VMEM(t.shape, t.dtype) for t in consts]
+        + [pltpu.SemaphoreType.DMA((len(consts),))],
+        compiler_params=large,
     )(index, *slabs, jnp.concatenate([skip, skip], axis=1), *consts)
-    gated = pl.pallas_call(
-        functools.partial(gate_kernel, parts),
-        out_shape=(block(rows, LANES),) * parts,
-        in_specs=[scalar, whole, whole],
-        compiler_params=small,
-    )(index, y, q)
     gated = [joint_shift(gated[n], 1, -n) for n in range(parts)]
     out = pl.pallas_call(
         functools.partial(unpack_kernel, parts),
@@ -408,8 +413,8 @@
     def on_device(*arrays):
         parts = lax.axis_size("ctx")
         length, channels = arrays[0].shape[1:]
-        small = parts * length <= 4096 and length % (2 * INNER) == 0 and parts % 2 == 0
-        run = fast_on_device if small and channels == parts * HALF else general_on_device
+        square = parts * length == INNER * INNER
+        run = fast_on_device if square and channels == parts * HALF else general_on_device
         return run(*arrays)
 
     return jax.shard_map(

time: 95.1 us -> 84.4 us (0.89)
  local copies, waits for them, and re-layouts: 13.2 us -> 0.74 us
  starting transfers between devices: 43.7 us -> 37.6 us
  Pallas kernels: 18.1 us -> 22.5 us
  waiting for transfers between devices: 19.3 us -> 22.7 us
    all_to_all x1 -> x0, starting transfers between devices: 15.2 us -> none  [fast_on_device(): q = lax.all_to_all(q, 'ctx', split_axis=0, concat_axis=0, tiled=True)]
    unnamed x42 -> x16, local copies, waits for them, and re-layouts: 13.1 us -> 0.67 us
    ppermute x15, starting transfers between devices: 28.5 us -> 37.6 us  [joint_shift(): return lax.ppermute(value, ('segment', 'ctx'), pairs)]
    ppermute x15, waiting for transfers between devices: 19.3 us -> 22.7 us  [joint_shift(): return lax.ppermute(value, ('segment', 'ctx'), pairs)]
    pallas_call x1, Pallas kernels: 15.3 us -> 17.8 us  [fast_on_device(): pl.pallas_call(functools.partial(convolve_kernel, parts, outer), out_shap...]
    pallas_call x3 -> x1, Pallas kernels: 1.84 us -> 3.6 us  [fast_on_device(): pl.pallas_call(functools.partial(pack_kernel, parts), out_shape=(block(si...]
  transfers between devices with their start and end apart: 16 -> 15, of which waited for: 4 -> 7; matrix products, arithmetic and copies ran while one was open for 0% -> 1% of each run, Pallas kernels for 17% -> 0%
where the time goes in v4:
time: 84.4 us; the launch traced here: 84.2 us
  starting transfers between devices  37.6 us (45%)
  waiting for transfers between devices  22.7 us (27%)
  Pallas kernels  22.5 us (27%)
    ppermute x15, starting transfers between devices, joint_shift(): return lax.ppermute(value, ('segment', 'ctx'), pairs)  37.6 us
    ppermute x15, waiting for transfers between devices, joint_shift(): return lax.ppermute(value, ('segment', 'ctx'), pairs)  22.7 us
    pallas_call x1, Pallas kernels, fast_on_device(): pl.pallas_call(functools.partial(convolve_kernel, parts, outer), out_shap...  17.8 us
    pallas_call x1, Pallas kernels, fast_on_device(): pl.pallas_call(functools.partial(pack_kernel, parts), out_shape=(block(si...  3.6 us
  transfers between devices with their start and end apart: 15, of which 7 were waited for; matrix products, arithmetic and copies ran while one was open for 1% of the time, Pallas kernels for 0%

profile of v4, /device:TPU:0, one launch (start us, length us, event | category | flops | bytes accessed | tf_op | source)
XLA Modules:
  0.0 84.2 jit_solution(7868810550188590387)
XLA Ops:
  0.0 3.6 %shard_map.73 = (bf16[784,128]{1,0:T(8,128)(2,1)}, bf16[784,128]{1,0:T(8,128)(2,1)}, bf16[784,128]{1,0:T(8,128)(2,1)}, bf16[784,128]{1,0:T(8,128)(2,1)}, bf16[78...) custom-call(s32[1]{0:T(128)} %bitcast.index_ref, ...), custom_call_target="tpu_custom_call" | custom-call | tf_op jit(solution)/shard_map/pallas_call | solution.py:366
  3.6 3.0 %collective-permute-start = (bf16[784,128]{1,0:T(8,128)(2,1)}, bf16[784,128]{1,0:T(8,128)(2,1)S(1)}, u32[]{:S(2)}, u32[]{:S(2)}) collective-permute-start(bf16[784,128]{1,0:T(8,128)(2,1)} %get-tuple-element.22), channel_id=1, source_target_pairs={{0,1},{1,2},{2,3},{3,4},{4,5},{5,6},{6,7},{7,0},{8,9},{9,10},{10,1... | collective-permute-start | bytes 602120 | tf_op jit(solution)/shard_map/ppermute | solution.py:346
  6.6 1.6 %collective-permute-start.1 = (bf16[784,128]{1,0:T(8,128)(2,1)}, bf16[784,128]{1,0:T(8,128)(2,1)S(1)}, u32[]{:S(2)}, u32[]{:S(2)}) collective-permute-start(bf16[784,128]{1,0:T(8,128)(2,1)} %get-tuple-element.23), channel_id=1, source_target_pairs={{0,2},{1,3},{2,4},{3,5},{4,6},{5,7},{6,0},{7,1},{8,10},{9,11},{10,... | collective-permute-start | bytes 602120 | tf_op jit(solution)/shard_map/ppermute | solution.py:346
  8.2 2.5 %collective-permute-start.2 = (bf16[784,128]{1,0:T(8,128)(2,1)}, bf16[784,128]{1,0:T(8,128)(2,1)S(1)}, u32[]{:S(2)}, u32[]{:S(2)}) collective-permute-start(bf16[784,128]{1,0:T(8,128)(2,1)} %get-tuple-element.24), channel_id=1, source_target_pairs={{0,3},{1,4},{2,5},{3,6},{4,7},{5,0},{6,1},{7,2},{8,11},{9,12},{10,... | collective-permute-start | bytes 602120 | tf_op jit(solution)/shard_map/ppermute | solution.py:346
  10.7 1.2 %collective-permute-start.3 = (bf16[784,128]{1,0:T(8,128)(2,1)}, bf16[784,128]{1,0:T(8,128)(2,1)S(1)}, u32[]{:S(2)}, u32[]{:S(2)}) collective-permute-start(bf16[784,128]{1,0:T(8,128)(2,1)} %get-tuple-element.25), channel_id=1, source_target_pairs={{0,4},{1,5},{2,6},{3,7},{4,0},{5,1},{6,2},{7,3},{8,12},{9,13},{10,... | collective-permute-start | bytes 602120 | tf_op jit(solution)/shard_map/ppermute | solution.py:346
  12.0 2.6 %collective-permute-start.4 = (bf16[784,128]{1,0:T(8,128)(2,1)}, bf16[784,128]{1,0:T(8,128)(2,1)S(1)}, u32[]{:S(2)}, u32[]{:S(2)}) collective-permute-start(bf16[784,128]{1,0:T(8,128)(2,1)} %get-tuple-element.26), channel_id=1, source_target_pairs={{0,5},{1,6},{2,7},{3,0},{4,1},{5,2},{6,3},{7,4},{8,13},{9,14},{10,... | collective-permute-start | bytes 602120 | tf_op jit(solution)/shard_map/ppermute | solution.py:346
  14.6 1.3 %collective-permute-done.refs_1_ = bf16[784,128]{1,0:T(8,128)(2,1)S(1)} collective-permute-done((bf16[784,128]{1,0:T(8,128)(2,1)}, bf16[784,128]{1,0:T(8,128)(2,1)S(1)}, u32[]{:S(2)}, u32[]{:S(2)}) %collective-permute-start) | collective-permute-done | bytes 200736 | tf_op jit(solution)/shard_map/ppermute | solution.py:346
  15.9 1.8 %collective-permute-start.5 = (bf16[784,128]{1,0:T(8,128)(2,1)}, bf16[784,128]{1,0:T(8,128)(2,1)S(1)}, u32[]{:S(2)}, u32[]{:S(2)}) collective-permute-start(bf16[784,128]{1,0:T(8,128)(2,1)} %get-tuple-element.27), channel_id=1, source_target_pairs={{0,6},{1,7},{2,0},{3,1},{4,2},{5,3},{6,4},{7,5},{8,14},{9,15},{10,... | collective-permute-start | bytes 602120 | tf_op jit(solution)/shard_map/ppermute | solution.py:346
  17.7 0.0 collective-permute-done.1.refs_2_
  17.7 3.5 %collective-permute-start.6 = (bf16[784,128]{1,0:T(8,128)(2,1)}, bf16[784,128]{1,0:T(8,128)(2,1)S(1)}, u32[]{:S(2)}, u32[]{:S(2)}) collective-permute-start(bf16[784,128]{1,0:T(8,128)(2,1)} %get-tuple-element.28), channel_id=1, source_target_pairs={{0,7},{1,0},{2,1},{3,2},{4,3},{5,4},{6,5},{7,6},{8,15},{9,8},{10,9... | collective-permute-start | bytes 602120 | tf_op jit(solution)/shard_map/ppermute | solution.py:346
  21.2 0.1 constant_dynamic-slice_fusion
  21.3 0.6 pad_maximum_fusion.refs_8_
  21.9 10.3 %collective-permute-done.2.refs_3_ = bf16[784,128]{1,0:T(8,128)(2,1)S(1)} collective-permute-done((bf16[784,128]{1,0:T(8,128)(2,1)}, bf16[784,128]{1,0:T(8,128)(2,1)S(1)}, u32[]{:S(2)}, u32[]{:S(2)}) %collective-permute-start.2) | collective-permute-done | bytes 200736 | tf_op jit(solution)/shard_map/ppermute | solution.py:346
  32.2 0.2 collective-permute-done.3.refs_4_
  32.5 0.0 collective-permute-done.4.refs_5_
  32.5 0.0 collective-permute-done.5.refs_6_
  32.5 1.6 %collective-permute-done.6.refs_7_ = bf16[784,128]{1,0:T(8,128)(2,1)S(1)} collective-permute-done((bf16[784,128]{1,0:T(8,128)(2,1)}, bf16[784,128]{1,0:T(8,128)(2,1)S(1)}, u32[]{:S(2)}, u32[]{:S(2)}) %collective-permute-start.6) | collective-permute-done | bytes 200736 | tf_op jit(solution)/shard_map/ppermute | solution.py:346
  34.1 0.6 copy-done.7
  34.7 17.8 %shard_map.74 = (bf16[256,128]{1,0:T(8,128)(2,1)}, bf16[256,128]{1,0:T(8,128)(2,1)}, bf16[256,128]{1,0:T(8,128)(2,1)}, bf16[256,128]{1,0:T(8,128)(2,1)}, bf16[25...) custom-call(s32[1]{0:T(128)} %bitcast.index_ref, ...), custom_call_target="tpu_custom_call" | custom-call | tf_op jit(solution)/shard_map/pallas_call | solution.py:378
  52.6 0.1 collective-permute-start.7
  52.6 15.1 %collective-permute-start.8 = (bf16[256,128]{1,0:T(8,128)(2,1)}, bf16[256,128]{1,0:T(8,128)(2,1)S(1)}, u32[]{:S(2)}, u32[]{:S(2)}) collective-permute-start(bf16[256,128]{1,0:T(8,128)(2,1)} %get-tuple-element.30), channel_id=1, source_target_pairs={{0,15},{1,8},{2,9},{3,10},{4,11},{5,12},{6,13},{7,14},{8,23},{9,16... | collective-permute-start | bytes 196616 | tf_op jit(solution)/shard_map/ppermute | solution.py:346
  67.8 0.0 collective-permute-start.10
  67.8 2.6 %collective-permute-start.11 = (bf16[256,128]{1,0:T(8,128)(2,1)}, bf16[256,128]{1,0:T(8,128)(2,1)S(1)}, u32[]{:S(2)}, u32[]{:S(2)}) collective-permute-start(bf16[256,128]{1,0:T(8,128)(2,1)} %get-tuple-element.33), channel_id=1, source_target_pairs={{0,12},{1,13},{2,14},{3,15},{4,8},{5,9},{6,10},{7,11},{8,20},{9,21... | collective-permute-start | bytes 196616 | tf_op jit(solution)/shard_map/ppermute | solution.py:346
  70.4 0.0 collective-permute-start.12
  70.4 0.1 collective-permute-done.8.refs_1_
  70.5 3.2 %collective-permute-start.13 = (bf16[256,128]{1,0:T(8,128)(2,1)}, bf16[256,128]{1,0:T(8,128)(2,1)S(1)}, u32[]{:S(2)}, u32[]{:S(2)}) collective-permute-start(bf16[256,128]{1,0:T(8,128)(2,1)} %get-tuple-element.35), channel_id=1, source_target_pairs={{0,10},{1,11},{2,12},{3,13},{4,14},{5,15},{6,8},{7,9},{8,18},{9,19... | collective-permute-start | bytes 196616 | tf_op jit(solution)/shard_map/ppermute | solution.py:346
  73.7 0.3 collective-permute-start.14
  74.0 3.3 %collective-permute-done.11.refs_4_ = bf16[256,128]{1,0:T(8,128)(2,1)S(1)} collective-permute-done((bf16[256,128]{1,0:T(8,128)(2,1)}, bf16[256,128]{1,0:T(8,128)(2,1)S(1)}, u32[]{:S(2)}, u32[]{:S(2)}) %collective-permute-start.11) | collective-permute-done | bytes 65568 | tf_op jit(solution)/shard_map/ppermute | solution.py:346
  77.4 5.8 %collective-permute-done.12.refs_5_ = bf16[256,128]{1,0:T(8,128)(2,1)S(1)} collective-permute-done((bf16[256,128]{1,0:T(8,128)(2,1)}, bf16[256,128]{1,0:T(8,128)(2,1)S(1)}, u32[]{:S(2)}, u32[]{:S(2)}) %collective-permute-start.12) | collective-permute-done | bytes 65568 | tf_op jit(solution)/shard_map/ppermute | solution.py:346
  83.2 0.0 collective-permute-done.13.refs_6_
  83.2 0.0 collective-permute-done.14.refs_7_
  83.2 1.0 %shard_map.75 = bf16[512,512]{1,0:T(8,128)(2,1)} custom-call(s32[1]{0:T(128)} %bitcast.index_ref, bf16[256,128]{1,0:T(8,128)(2,1)S(1)} %collective-permute-done.7.refs_0_, bf16[256,128]{1,0:T(8,128)(2,1)S(1)} %collective-permute-done.8.refs_1_, bf16[256,128]{1,0:T(8,128)(2,1)S(1)} %collective-permute-done.9.refs_2_, ...), custom_call_target="tpu_custom_call" | custom-call | tf_op jit(solution)/shard_map/pallas_call | solution.py:394
  (19 shorter events, 0.0 us)
Async XLA Ops:
  0.0 21.2 %copy-start = (f32[1,512]{1,0:T(1,128)S(1)}, f32[1,512]{1,0:T(1,128)}, u32[]{:S(2)}) copy-start(f32[1,512]{1,0:T(1,128)} %param.11) | copy-start | bytes 6148
  3.6 12.3 %collective-permute-start = (bf16[784,128]{1,0:T(8,128)(2,1)}, bf16[784,128]{1,0:T(8,128)(2,1)S(1)}, u32[]{:S(2)}, u32[]{:S(2)}) collective-permute-start(bf16[784,128]{1,0:T(8,128)(2,1)} %get-tuple-element.22), channel_id=1, source_target_pairs={{0,1},{1,2},{2,3},{3,4},{4,5},{5,6},{6,7},{7,0},{8,9},{9,10},{10,1... | collective-permute-start | bytes 602120 | tf_op jit(solution)/shard_map/ppermute | solution.py:346
  6.6 11.1 %collective-permute-start.1 = (bf16[784,128]{1,0:T(8,128)(2,1)}, bf16[784,128]{1,0:T(8,128)(2,1)S(1)}, u32[]{:S(2)}, u32[]{:S(2)}) collective-permute-start(bf16[784,128]{1,0:T(8,128)(2,1)} %get-tuple-element.23), channel_id=1, source_target_pairs={{0,2},{1,3},{2,4},{3,5},{4,6},{5,7},{6,0},{7,1},{8,10},{9,11},{10,... | collective-permute-start | bytes 602120 | tf_op jit(solution)/shard_map/ppermute | solution.py:346
  8.2 24.0 %collective-permute-start.2 = (bf16[784,128]{1,0:T(8,128)(2,1)}, bf16[784,128]{1,0:T(8,128)(2,1)S(1)}, u32[]{:S(2)}, u32[]{:S(2)}) collective-permute-start(bf16[784,128]{1,0:T(8,128)(2,1)} %get-tuple-element.24), channel_id=1, source_target_pairs={{0,3},{1,4},{2,5},{3,6},{4,7},{5,0},{6,1},{7,2},{8,11},{9,12},{10,... | collective-permute-start | bytes 602120 | tf_op jit(solution)/shard_map/ppermute | solution.py:346
  10.7 21.7 %collective-permute-start.3 = (bf16[784,128]{1,0:T(8,128)(2,1)}, bf16[784,128]{1,0:T(8,128)(2,1)S(1)}, u32[]{:S(2)}, u32[]{:S(2)}) collective-permute-start(bf16[784,128]{1,0:T(8,128)(2,1)} %get-tuple-element.25), channel_id=1, source_target_pairs={{0,4},{1,5},{2,6},{3,7},{4,0},{5,1},{6,2},{7,3},{8,12},{9,13},{10,... | collective-permute-start | bytes 602120 | tf_op jit(solution)/shard_map/ppermute | solution.py:346
  12.0 20.5 %collective-permute-start.4 = (bf16[784,128]{1,0:T(8,128)(2,1)}, bf16[784,128]{1,0:T(8,128)(2,1)S(1)}, u32[]{:S(2)}, u32[]{:S(2)}) collective-permute-start(bf16[784,128]{1,0:T(8,128)(2,1)} %get-tuple-element.26), channel_id=1, source_target_pairs={{0,5},{1,6},{2,7},{3,0},{4,1},{5,2},{6,3},{7,4},{8,13},{9,14},{10,... | collective-permute-start | bytes 602120 | tf_op jit(solution)/shard_map/ppermute | solution.py:346
  15.9 18.2 %copy-start.1 = (bf16[784,128]{1,0:T(8,128)(2,1)}, bf16[784,128]{1,0:T(8,128)(2,1)S(1)}, u32[]{:S(2)}) copy-start(bf16[784,128]{1,0:T(8,128)(2,1)S(1)} %collective-permute-done.refs_1_) | copy-start | bytes 602116
  15.9 16.6 %collective-permute-start.5 = (bf16[784,128]{1,0:T(8,128)(2,1)}, bf16[784,128]{1,0:T(8,128)(2,1)S(1)}, u32[]{:S(2)}, u32[]{:S(2)}) collective-permute-start(bf16[784,128]{1,0:T(8,128)(2,1)} %get-tuple-element.27), channel_id=1, source_target_pairs={{0,6},{1,7},{2,0},{3,1},{4,2},{5,3},{6,4},{7,5},{8,14},{9,15},{10,... | collective-permute-start | bytes 602120 | tf_op jit(solution)/shard_map/ppermute | solution.py:346
  17.7 16.3 %copy-start.2 = (bf16[784,128]{1,0:T(8,128)(2,1)}, bf16[784,128]{1,0:T(8,128)(2,1)S(1)}, u32[]{:S(2)}) copy-start(bf16[784,128]{1,0:T(8,128)(2,1)S(1)} %collective-permute-done.1.refs_2_) | copy-start | bytes 602116
  17.7 16.3 %collective-permute-start.6 = (bf16[784,128]{1,0:T(8,128)(2,1)}, bf16[784,128]{1,0:T(8,128)(2,1)S(1)}, u32[]{:S(2)}, u32[]{:S(2)}) collective-permute-start(bf16[784,128]{1,0:T(8,128)(2,1)} %get-tuple-element.28), channel_id=1, source_target_pairs={{0,7},{1,0},{2,1},{3,2},{4,3},{5,4},{6,5},{7,6},{8,15},{9,8},{10,9... | collective-permute-start | bytes 602120 | tf_op jit(solution)/shard_map/ppermute | solution.py:346
  32.2 1.8 %copy-start.3 = (bf16[784,128]{1,0:T(8,128)(2,1)}, bf16[784,128]{1,0:T(8,128)(2,1)S(1)}, u32[]{:S(2)}) copy-start(bf16[784,128]{1,0:T(8,128)(2,1)S(1)} %collective-permute-done.2.refs_3_) | copy-start | bytes 602116
  32.5 1.6 %copy-start.4 = (bf16[784,128]{1,0:T(8,128)(2,1)}, bf16[784,128]{1,0:T(8,128)(2,1)S(1)}, u32[]{:S(2)}) copy-start(bf16[784,128]{1,0:T(8,128)(2,1)S(1)} %collective-permute-done.3.refs_4_) | copy-start | bytes 602116
  32.5 1.6 %copy-start.5 = (bf16[784,128]{1,0:T(8,128)(2,1)}, bf16[784,128]{1,0:T(8,128)(2,1)S(1)}, u32[]{:S(2)}) copy-start(bf16[784,128]{1,0:T(8,128)(2,1)S(1)} %collective-permute-done.4.refs_5_) | copy-start | bytes 602116
  32.5 1.6 %copy-start.6 = (bf16[784,128]{1,0:T(8,128)(2,1)}, bf16[784,128]{1,0:T(8,128)(2,1)S(1)}, u32[]{:S(2)}) copy-start(bf16[784,128]{1,0:T(8,128)(2,1)S(1)} %collective-permute-done.5.refs_6_) | copy-start | bytes 602116
  34.0 0.7 copy-start.7
  52.6 17.8 %collective-permute-start.7 = (bf16[256,128]{1,0:T(8,128)(2,1)}, bf16[256,128]{1,0:T(8,128)(2,1)S(1)}, u32[]{:S(2)}, u32[]{:S(2)}) collective-permute-start(bf16[256,128]{1,0:T(8,128)(2,1)} %get-tuple-element.29), channel_id=1, source_target_pairs={{0,8},{1,9},{2,10},{3,11},{4,12},{5,13},{6,14},{7,15},{8,16},{9,17... | collective-permute-start | bytes 196616 | tf_op jit(solution)/shard_map/ppermute | solution.py:346
  52.6 17.9 %collective-permute-start.8 = (bf16[256,128]{1,0:T(8,128)(2,1)}, bf16[256,128]{1,0:T(8,128)(2,1)S(1)}, u32[]{:S(2)}, u32[]{:S(2)}) collective-permute-start(bf16[256,128]{1,0:T(8,128)(2,1)} %get-tuple-element.30), channel_id=1, source_target_pairs={{0,15},{1,8},{2,9},{3,10},{4,11},{5,12},{6,13},{7,14},{8,23},{9,16... | collective-permute-start | bytes 196616 | tf_op jit(solution)/shard_map/ppermute | solution.py:346
  67.8 5.9 %collective-permute-start.9 = (bf16[256,128]{1,0:T(8,128)(2,1)}, bf16[256,128]{1,0:T(8,128)(2,1)S(1)}, u32[]{:S(2)}, u32[]{:S(2)}) collective-permute-start(bf16[256,128]{1,0:T(8,128)(2,1)} %get-tuple-element.31), channel_id=1, source_target_pairs={{0,14},{1,15},{2,8},{3,9},{4,10},{5,11},{6,12},{7,13},{8,22},{9,23... | collective-permute-start | bytes 196616 | tf_op jit(solution)/shard_map/ppermute | solution.py:346
  67.8 6.3 %collective-permute-start.10 = (bf16[256,128]{1,0:T(8,128)(2,1)}, bf16[256,128]{1,0:T(8,128)(2,1)S(1)}, u32[]{:S(2)}, u32[]{:S(2)}) collective-permute-start(bf16[256,128]{1,0:T(8,128)(2,1)} %get-tuple-element.32), channel_id=1, source_target_pairs={{0,13},{1,14},{2,15},{3,8},{4,9},{5,10},{6,11},{7,12},{8,21},{9,22... | collective-permute-start | bytes 196616 | tf_op jit(solution)/shard_map/ppermute | solution.py:346
  67.8 9.6 %collective-permute-start.11 = (bf16[256,128]{1,0:T(8,128)(2,1)}, bf16[256,128]{1,0:T(8,128)(2,1)S(1)}, u32[]{:S(2)}, u32[]{:S(2)}) collective-permute-start(bf16[256,128]{1,0:T(8,128)(2,1)} %get-tuple-element.33), channel_id=1, source_target_pairs={{0,12},{1,13},{2,14},{3,15},{4,8},{5,9},{6,10},{7,11},{8,20},{9,21... | collective-permute-start | bytes 196616 | tf_op jit(solution)/shard_map/ppermute | solution.py:346
  70.4 12.8 %collective-permute-start.12 = (bf16[256,128]{1,0:T(8,128)(2,1)}, bf16[256,128]{1,0:T(8,128)(2,1)S(1)}, u32[]{:S(2)}, u32[]{:S(2)}) collective-permute-start(bf16[256,128]{1,0:T(8,128)(2,1)} %get-tuple-element.34), channel_id=1, source_target_pairs={{0,11},{1,12},{2,13},{3,14},{4,15},{5,8},{6,9},{7,10},{8,19},{9,20... | collective-permute-start | bytes 196616 | tf_op jit(solution)/shard_map/ppermute | solution.py:346
  70.5 12.7 %collective-permute-start.13 = (bf16[256,128]{1,0:T(8,128)(2,1)}, bf16[256,128]{1,0:T(8,128)(2,1)S(1)}, u32[]{:S(2)}, u32[]{:S(2)}) collective-permute-start(bf16[256,128]{1,0:T(8,128)(2,1)} %get-tuple-element.35), channel_id=1, source_target_pairs={{0,10},{1,11},{2,12},{3,13},{4,14},{5,15},{6,8},{7,9},{8,18},{9,19... | collective-permute-start | bytes 196616 | tf_op jit(solution)/shard_map/ppermute | solution.py:346
  73.7 9.5 %collective-permute-start.14 = (bf16[256,128]{1,0:T(8,128)(2,1)}, bf16[256,128]{1,0:T(8,128)(2,1)S(1)}, u32[]{:S(2)}, u32[]{:S(2)}) collective-permute-start(bf16[256,128]{1,0:T(8,128)(2,1)} %get-tuple-element.36), channel_id=1, source_target_pairs={{0,9},{1,10},{2,11},{3,12},{4,13},{5,14},{6,15},{7,8},{8,17},{9,18... | collective-permute-start | bytes 196616 | tf_op jit(solution)/shard_map/ppermute | solution.py:346

commit v5 on v4

--- a/solution.py
+++ b/solution.py
@@ -178,8 +178,8 @@
 
 
 def pack_kernel(parts, index_ref, *refs):
-    sources, outs, held, arrived, sems = refs[:4], refs[4 : 4 + parts], refs[-6], refs[-5:-1], refs[-1]
-    k_ref, v_ref, h_ref, q_ref = arrived
+    sources, outs, held, arrived, sems = refs[:3], refs[3 : 3 + parts], refs[-5], refs[-4:-1], refs[-1]
+    k_ref, v_ref, h_ref = arrived
     rows = k_ref.shape[0] // 2
     low = lower_half((rows, LANES))
     for copy in fetched(sources, arrived, sems):
@@ -202,10 +202,19 @@
             power = power * power
         place(e, 0, jnp.where(code < 0.0, -power, power), low)
         place(e, rows, h_ref[:, lanes].astype(F32), low)
-        place(e, 2 * rows, q_ref[:, lanes].astype(F32), low)
-        place(e, 3 * rows, jnp.broadcast_to(largest, (2 * EXTRA, LANES)), low[:EXTRA])
+        place(e, 2 * rows, jnp.broadcast_to(largest, (2 * EXTRA, LANES)), low[:EXTRA])
     for n, out in enumerate(outs):
         out[...] = held[lax.rem(index_ref[0] + n, parts)]
+
+
+def pack_gate_kernel(parts, q_ref, out_ref):
+    rows = q_ref.shape[0] // 2
+    low = lower_half((rows, LANES))
+    for e in range(parts // 2):
+        tile = q_ref[:, LANES * e : LANES * (e + 1)].astype(F32)
+        early, late = tile[:rows], tile[rows:]
+        out_ref[2 * e] = jnp.where(low, early, swap_halves(late)).astype(BF16)
+        out_ref[2 * e + 1] = jnp.where(low, swap_halves(early), late).astype(BF16)
 
 
 def unpack_kernel(parts, index_ref, *refs):
@@ -223,11 +232,11 @@
 def convolve_kernel(parts, outer, index_ref, *refs):
     blocks = refs[:parts]
     skip_ref, sources = refs[parts], refs[parts + 1 : parts + 3]
-    outs, (x_s, z_s, w_s, y_s, p_s) = refs[parts + 3 : 2 * parts + 3], refs[2 * parts + 3 : 2 * parts + 8]
-    matrix_ref, turn_ref = arrived = refs[2 * parts + 8 : 2 * parts + 10]
+    out_ref, x_s, z_s, w_s, y_s, p_s = refs[parts + 3 : parts + 9]
+    matrix_ref, turn_ref = arrived = refs[parts + 9 : parts + 11]
     copies = fetched(sources, arrived, refs[-1])
     edges = (0, 3 * outer, 6 * outer, 6 * outer + 6 * INNER, 6 * outer + 9 * INNER)
-    rows = outs[0].shape[0]
+    rows = out_ref.shape[1]
     per = rows // INNER
     low = lower_half((INNER, LANES))
     lowc = lower_half((outer, LANES))
@@ -236,7 +245,7 @@
         return lax.rem(index_ref[0] + parts - n, parts)
 
     for n, block in enumerate(blocks):
-        scale = block[3 * rows : 3 * rows + EXTRA, :].astype(F32)[:1] * (1.0 / SCALE)
+        scale = block[2 * rows : 2 * rows + EXTRA, :].astype(F32)[:1] * (1.0 / SCALE)
         for m in range(per):
             at = m * INNER
             code = block[at : at + INNER, :].astype(F32)
@@ -328,12 +337,17 @@
     lax.fori_loop(0, INNER // STEP, back_outer, 0)
 
     lowr = lower_half((rows, LANES))
-    for n, (block, out) in enumerate(zip(blocks, outs)):
+    for n in range(parts):
         at = pl.multiple_of(origin(n) * 2 * rows, 2 * rows)
         early = y_s[pl.ds(at, rows), :]
         late = y_s[pl.ds(at + rows, rows), :]
-        y = jnp.where(lowr, early, swap_halves(late)) + skip_ref[...] * p_s[n]
-        out[...] = (block[2 * rows : 3 * rows, :].astype(F32) * y).astype(BF16)
+        out_ref[n] = jnp.where(lowr, early, swap_halves(late)) + skip_ref[...] * p_s[n]
+
+
+def gate_kernel(parts, index_ref, y_ref, q_ref, *outs):
+    for n, out in enumerate(outs):
+        q = q_ref[lax.rem(index_ref[0] + parts - n, parts)]
+        out[...] = (q.astype(F32) * y_ref[n]).astype(BF16)
 
 
 def joint_shift(value, segment_step, ctx_step):
@@ -362,22 +376,29 @@
     def block(*shape, dtype=BF16):
         return jax.ShapeDtypeStruct(shape, dtype)
 
-    size = 3 * rows + EXTRA
+    size = 2 * rows + EXTRA
     sent = pl.pallas_call(
         functools.partial(pack_kernel, parts),
         out_shape=(block(size, LANES),) * parts,
-        in_specs=[scalar] + [far] * 4,
+        in_specs=[scalar] + [far] * 3,
         scratch_shapes=[pltpu.VMEM((parts, size, LANES), BF16)]
-        + [pltpu.VMEM((length, channels), BF16)] * 4
-        + [pltpu.SemaphoreType.DMA((4,))],
+        + [pltpu.VMEM((length, channels), BF16)] * 3
+        + [pltpu.SemaphoreType.DMA((3,))],
         compiler_params=large,
-    )(index, key_stream[0], value_stream[0], filter_taps[0], query_stream[0])
+    )(index, key_stream[0], value_stream[0], filter_taps[0])
     slabs = [sent[0]] + [joint_shift(sent[n], 0, n) for n in range(1, parts)]
+    q = pl.pallas_call(
+        functools.partial(pack_gate_kernel, parts),
+        out_shape=block(parts, rows, LANES),
+        compiler_params=large,
+    )(query_stream[0])
+    q, *_ = lax.optimization_barrier((q, *slabs))
+    q = lax.all_to_all(q, "ctx", split_axis=0, concat_axis=0, tiled=True)
     skip = lax.dynamic_slice(skip_weight, (0, device * HALF), (1, HALF))
     consts = [jnp.asarray(t) for t in tables(outer)]
-    gated = pl.pallas_call(
+    y = pl.pallas_call(
         functools.partial(convolve_kernel, parts, outer),
-        out_shape=(block(rows, LANES),) * parts,
+        out_shape=block(parts, rows, LANES, dtype=F32),
         in_specs=[scalar] + [whole] * (parts + 1) + [far] * len(consts),
         scratch_shapes=[
             pltpu.VMEM((outer * INNER, LANES), F32),
@@ -390,6 +411,12 @@
         + [pltpu.SemaphoreType.DMA((len(consts),))],
         compiler_params=large,
     )(index, *slabs, jnp.concatenate([skip, skip], axis=1), *consts)
+    gated = pl.pallas_call(
+        functools.partial(gate_kernel, parts),
+        out_shape=(block(rows, LANES),) * parts,
+        in_specs=[scalar, whole, whole],
+        compiler_params=small,
+    )(index, y, q)
     gated = [joint_shift(gated[n], 1, -n) for n in range(parts)]
     out = pl.pallas_call(
         functools.partial(unpack_kernel, parts),

time: 84.4 us -> 79.3 us (0.940)
  waiting for transfers between devices: 22.7 us -> 13.7 us
  starting transfers between devices: 37.6 us -> 39.3 us
  Pallas kernels: 22.5 us -> 23.9 us
    all_to_all x0 -> x1, starting transfers between devices: none -> 12.2 us  [fast_on_device(): q = lax.all_to_all(q, 'ctx', split_axis=0, concat_axis=0, tiled=True)]
    ppermute x15, starting transfers between devices: 37.6 us -> 27 us  [joint_shift(): return lax.ppermute(value, ('segment', 'ctx'), pairs)]
    ppermute x15, waiting for transfers between devices: 22.7 us -> 13.7 us  [joint_shift(): return lax.ppermute(value, ('segment', 'ctx'), pairs)]
    pallas_call x0 -> x2, Pallas kernels: none -> 2.15 us  [the longest x1 2.06 us: fast_on_device(): pl.pallas_call(functools.partial(pack_gate_kernel, parts), out_shape=bloc...]
  transfers between devices with their start and end apart: 15 -> 16, of which waited for: 7 -> 5; matrix products, arithmetic and copies ran while one was open for 1% -> 1% of each run, Pallas kernels for 0% -> 25%
where the time goes in v5:
time: 79.3 us; the launch traced here: 79 us
  starting transfers between devices  39.3 us (50%)
  Pallas kernels  23.9 us (30%)
  waiting for transfers between devices  13.7 us (17%)
  local copies, waits for them, and re-layouts  1.32 us (2%)
    ppermute x15, starting transfers between devices, joint_shift(): return lax.ppermute(value, ('segment', 'ctx'), pairs)  27 us
    pallas_call x1, Pallas kernels, fast_on_device(): pl.pallas_call(functools.partial(convolve_kernel, parts, outer), out_shap...  17.6 us
    ppermute x15, waiting for transfers between devices, joint_shift(): return lax.ppermute(value, ('segment', 'ctx'), pairs)  13.7 us
    all_to_all x1, starting transfers between devices, fast_on_device(): q = lax.all_to_all(q, 'ctx', split_axis=0, concat_axis=0, tiled=True)  12.2 us
    pallas_call x1, Pallas kernels, fast_on_device(): pl.pallas_call(functools.partial(pack_kernel, parts), out_shape=(block(si...  3.1 us
    pallas_call x1, Pallas kernels, fast_on_device(): pl.pallas_call(functools.partial(pack_gate_kernel, parts), out_shape=bloc...  2.06 us
  transfers between devices with their start and end apart: 16, of which 5 were waited for; matrix products, arithmetic and copies ran while one was open for 1% of the time, Pallas kernels for 25%

profile of v5, /device:TPU:0, one launch (start us, length us, event | category | flops | bytes accessed | tf_op | source)
XLA Modules:
  0.0 79.0 jit_solution(13601500918819620533)
XLA Ops:
  0.0 3.1 %shard_map.73 = (bf16[528,128]{1,0:T(8,128)(2,1)}, bf16[528,128]{1,0:T(8,128)(2,1)}, bf16[528,128]{1,0:T(8,128)(2,1)}, bf16[528,128]{1,0:T(8,128)(2,1)}, bf16[52...) custom-call(s32[1]{0:T(128)} %bitcast.index_ref, ...), custom_call_target="tpu_custom_call" | custom-call | tf_op jit(solution)/shard_map/pallas_call | solution.py:380
  3.1 3.0 %collective-permute-start = (bf16[528,128]{1,0:T(8,128)(2,1)}, bf16[528,128]{1,0:T(8,128)(2,1)S(1)}, u32[]{:S(2)}, u32[]{:S(2)}) collective-permute-start(bf16[528,128]{1,0:T(8,128)(2,1)} %get-tuple-element.23), channel_id=1, source_target_pairs={{0,1},{1,2},{2,3},{3,4},{4,5},{5,6},{6,7},{7,0},{8,9},{9,10},{10,1... | collective-permute-start | bytes 405512 | tf_op jit(solution)/shard_map/ppermute | solution.py:360
  6.1 1.6 %collective-permute-start.1 = (bf16[528,128]{1,0:T(8,128)(2,1)}, bf16[528,128]{1,0:T(8,128)(2,1)S(1)}, u32[]{:S(2)}, u32[]{:S(2)}) collective-permute-start(bf16[528,128]{1,0:T(8,128)(2,1)} %get-tuple-element.24), channel_id=1, source_target_pairs={{0,2},{1,3},{2,4},{3,5},{4,6},{5,7},{6,0},{7,1},{8,10},{9,11},{10,... | collective-permute-start | bytes 405512 | tf_op jit(solution)/shard_map/ppermute | solution.py:360
  7.7 2.5 %collective-permute-start.2 = (bf16[528,128]{1,0:T(8,128)(2,1)}, bf16[528,128]{1,0:T(8,128)(2,1)S(1)}, u32[]{:S(2)}, u32[]{:S(2)}) collective-permute-start(bf16[528,128]{1,0:T(8,128)(2,1)} %get-tuple-element.25), channel_id=1, source_target_pairs={{0,3},{1,4},{2,5},{3,6},{4,7},{5,0},{6,1},{7,2},{8,11},{9,12},{10,... | collective-permute-start | bytes 405512 | tf_op jit(solution)/shard_map/ppermute | solution.py:360
  10.2 1.2 %collective-permute-start.3 = (bf16[528,128]{1,0:T(8,128)(2,1)}, bf16[528,128]{1,0:T(8,128)(2,1)S(1)}, u32[]{:S(2)}, u32[]{:S(2)}) collective-permute-start(bf16[528,128]{1,0:T(8,128)(2,1)} %get-tuple-element.26), channel_id=1, source_target_pairs={{0,4},{1,5},{2,6},{3,7},{4,0},{5,1},{6,2},{7,3},{8,12},{9,13},{10,... | collective-permute-start | bytes 405512 | tf_op jit(solution)/shard_map/ppermute | solution.py:360
  11.5 2.6 %collective-permute-start.4 = (bf16[528,128]{1,0:T(8,128)(2,1)}, bf16[528,128]{1,0:T(8,128)(2,1)S(1)}, u32[]{:S(2)}, u32[]{:S(2)}) collective-permute-start(bf16[528,128]{1,0:T(8,128)(2,1)} %get-tuple-element.27), channel_id=1, source_target_pairs={{0,5},{1,6},{2,7},{3,0},{4,1},{5,2},{6,3},{7,4},{8,13},{9,14},{10,... | collective-permute-start | bytes 405512 | tf_op jit(solution)/shard_map/ppermute | solution.py:360
  14.1 0.0 collective-permute-done.refs_1_
  14.1 1.7 %collective-permute-start.5 = (bf16[528,128]{1,0:T(8,128)(2,1)}, bf16[528,128]{1,0:T(8,128)(2,1)S(1)}, u32[]{:S(2)}, u32[]{:S(2)}) collective-permute-start(bf16[528,128]{1,0:T(8,128)(2,1)} %get-tuple-element.28), channel_id=1, source_target_pairs={{0,6},{1,7},{2,0},{3,1},{4,2},{5,3},{6,4},{7,5},{8,14},{9,15},{10,... | collective-permute-start | bytes 405512 | tf_op jit(solution)/shard_map/ppermute | solution.py:360
  15.8 0.0 collective-permute-done.1.refs_2_
  15.8 2.1 %collective-permute-start.6 = (bf16[528,128]{1,0:T(8,128)(2,1)}, bf16[528,128]{1,0:T(8,128)(2,1)S(1)}, u32[]{:S(2)}, u32[]{:S(2)}) collective-permute-start(bf16[528,128]{1,0:T(8,128)(2,1)} %get-tuple-element.29), channel_id=1, source_target_pairs={{0,7},{1,0},{2,1},{3,2},{4,3},{5,4},{6,5},{7,6},{8,15},{9,8},{10,9... | collective-permute-start | bytes 405512 | tf_op jit(solution)/shard_map/ppermute | solution.py:360
  17.9 2.1 %shard_map.75 = bf16[8,256,128]{2,1,0:T(8,128)(2,1)} custom-call(bf16[512,512]{1,0:T(8,128)(2,1)} %bitcast.9), custom_call_target="tpu_custom_call" | custom-call | tf_op jit(solution)/shard_map/pallas_call | solution.py:390
  20.0 4.7 %collective-permute-done.2.refs_3_ = bf16[528,128]{1,0:T(8,128)(2,1)S(1)} collective-permute-done((bf16[528,128]{1,0:T(8,128)(2,1)}, bf16[528,128]{1,0:T(8,128)(2,1)S(1)}, u32[]{:S(2)}, u32[]{:S(2)}) %collective-permute-start.2) | collective-permute-done | bytes 135200 | tf_op jit(solution)/shard_map/ppermute | solution.py:360
  24.7 0.4 collective-permute-done.3.refs_4_
  25.0 0.0 collective-permute-done.5.refs_6_
  25.1 0.1 collective-permute-done.6.refs_7_
  25.1 12.2 %all-to-all-start = ((bf16[8,256,128]{2,1,0:T(8,128)(2,1)}), bf16[8,256,128]{2,1,0:T(8,128)(2,1)S(1)}, u32[]{:S(2)}, u32[]{:S(2)}) async-start(bf16[8,256,128]{2,1,0:T(8,128)(2,1)} %shard_map.75), calls=%async_computation | async-start | bytes 1048576 | tf_op jit(solution)/shard_map/all_to_all | solution.py:396
  37.4 0.1 constant_dynamic-slice_fusion
  37.4 0.7 pad_maximum_fusion.refs_8_
  38.2 17.6 %shard_map.74.y_ref = f32[8,256,128]{2,1,0:T(8,128)} custom-call(s32[1]{0:T(128)} %bitcast.index_ref, bf16[528,128]{1,0:T(8,128)(2,1)} %get-tuple-element.22.refs_0_, bf16[528,128]{1,0:T(8,128)(2,1)} %copy-done.2, bf16[528,128]{1,0:T(8,128)(2,1)} %copy-done.3, bf16[528,128]{1,0:T(8,128)(2,1)} %copy-done.4, bf16[528,128]{1,0:T(8,128)(2,1)} %copy-done.5, ...), custom_call_target="tpu_custom_call" | custom-call | tf_op jit(solution)/shard_map/pallas_call | solution.py:399
  55.7 1.2 %copy-done.1 = f32[8,256,128]{2,1,0:T(8,128)S(1)} copy-done((f32[8,256,128]{2,1,0:T(8,128)S(1)}, f32[8,256,128]{2,1,0:T(8,128)}, u32[]{:S(2)}) %copy-start.1) | copy-done | bytes 1048600
  57.0 0.1 shard_map.76
  57.0 0.1 collective-permute-start.7
  57.1 5.9 %collective-permute-start.8 = (bf16[256,128]{1,0:T(8,128)(2,1)S(1)}, bf16[256,128]{1,0:T(8,128)(2,1)S(1)}, u32[]{:S(2)}, u32[]{:S(2)}) collective-permute-start(bf16[256,128]{1,0:T(8,128)(2,1)S(1)} %get-tuple-element.32), channel_id=1, source_target_pairs={{0,15},{1,8},{2,9},{3,10},{4,11},{5,12},{6,13},{7,14},{8,23},{9,16... | collective-permute-start | bytes 196616 | tf_op jit(solution)/shard_map/ppermute | solution.py:360
  63.0 0.1 collective-permute-start.9
  63.1 0.0 collective-permute-start.10
  63.1 2.6 %collective-permute-start.11 = (bf16[256,128]{1,0:T(8,128)(2,1)S(1)}, bf16[256,128]{1,0:T(8,128)(2,1)S(1)}, u32[]{:S(2)}, u32[]{:S(2)}) collective-permute-start(bf16[256,128]{1,0:T(8,128)(2,1)S(1)} %get-tuple-element.35), channel_id=1, source_target_pairs={{0,12},{1,13},{2,14},{3,15},{4,8},{5,9},{6,10},{7,11},{8,20},{9,21... | collective-permute-start | bytes 196616 | tf_op jit(solution)/shard_map/ppermute | solution.py:360
  65.7 0.8 %collective-permute-start.12 = (bf16[256,128]{1,0:T(8,128)(2,1)S(1)}, bf16[256,128]{1,0:T(8,128)(2,1)S(1)}, u32[]{:S(2)}, u32[]{:S(2)}) collective-permute-start(bf16[256,128]{1,0:T(8,128)(2,1)S(1)} %get-tuple-element.36), channel_id=1, source_target_pairs={{0,11},{1,12},{2,13},{3,14},{4,15},{5,8},{6,9},{7,10},{8,19},{9,20... | collective-permute-start | bytes 196616 | tf_op jit(solution)/shard_map/ppermute | solution.py:360
  66.5 1.9 %collective-permute-start.13 = (bf16[256,128]{1,0:T(8,128)(2,1)S(1)}, bf16[256,128]{1,0:T(8,128)(2,1)S(1)}, u32[]{:S(2)}, u32[]{:S(2)}) collective-permute-start(bf16[256,128]{1,0:T(8,128)(2,1)S(1)} %get-tuple-element.37), channel_id=1, source_target_pairs={{0,10},{1,11},{2,12},{3,13},{4,14},{5,15},{6,8},{7,9},{8,18},{9,19... | collective-permute-start | bytes 196616 | tf_op jit(solution)/shard_map/ppermute | solution.py:360
  68.4 0.9 %collective-permute-start.14 = (bf16[256,128]{1,0:T(8,128)(2,1)S(1)}, bf16[256,128]{1,0:T(8,128)(2,1)S(1)}, u32[]{:S(2)}, u32[]{:S(2)}) collective-permute-start(bf16[256,128]{1,0:T(8,128)(2,1)S(1)} %get-tuple-element.38), channel_id=1, source_target_pairs={{0,9},{1,10},{2,11},{3,12},{4,13},{5,14},{6,15},{7,8},{8,17},{9,18... | collective-permute-start | bytes 196616 | tf_op jit(solution)/shard_map/ppermute | solution.py:360
  69.3 6.2 %collective-permute-done.11.refs_4_ = bf16[256,128]{1,0:T(8,128)(2,1)S(1)} collective-permute-done((bf16[256,128]{1,0:T(8,128)(2,1)S(1)}, bf16[256,128]{1,0:T(8,128)(2,1)S(1)}, u32[]{:S(2)}, u32[]{:S(2)}) %collective-permute-start.11) | collective-permute-done | bytes 65568 | tf_op jit(solution)/shard_map/ppermute | solution.py:360
  75.6 2.3 %collective-permute-done.12.refs_5_ = bf16[256,128]{1,0:T(8,128)(2,1)S(1)} collective-permute-done((bf16[256,128]{1,0:T(8,128)(2,1)S(1)}, bf16[256,128]{1,0:T(8,128)(2,1)S(1)}, u32[]{:S(2)}, u32[]{:S(2)}) %collective-permute-start.12) | collective-permute-done | bytes 65568 | tf_op jit(solution)/shard_map/ppermute | solution.py:360
  77.9 1.0 %shard_map.77 = bf16[512,512]{1,0:T(8,128)(2,1)} custom-call(s32[1]{0:T(128)} %bitcast.index_ref, bf16[256,128]{1,0:T(8,128)(2,1)S(1)} %collective-permute-done.7.refs_0_, bf16[256,128]{1,0:T(8,128)(2,1)S(1)} %collective-permute-done.8.refs_1_, bf16[256,128]{1,0:T(8,128)(2,1)S(1)} %collective-permute-done.9.refs_2_, ...), custom_call_target="tpu_custom_call" | custom-call | tf_op jit(solution)/shard_map/pallas_call | solution.py:421
  (25 shorter events, 0.1 us)
Async XLA Ops:
  0.0 37.4 %copy-start = (f32[1,512]{1,0:T(1,128)S(1)}, f32[1,512]{1,0:T(1,128)}, u32[]{:S(2)}) copy-start(f32[1,512]{1,0:T(1,128)} %param.11) | copy-start | bytes 6148
  3.1 11.0 %collective-permute-start = (bf16[528,128]{1,0:T(8,128)(2,1)}, bf16[528,128]{1,0:T(8,128)(2,1)S(1)}, u32[]{:S(2)}, u32[]{:S(2)}) collective-permute-start(bf16[528,128]{1,0:T(8,128)(2,1)} %get-tuple-element.23), channel_id=1, source_target_pairs={{0,1},{1,2},{2,3},{3,4},{4,5},{5,6},{6,7},{7,0},{8,9},{9,10},{10,1... | collective-permute-start | bytes 405512 | tf_op jit(solution)/shard_map/ppermute | solution.py:360
  6.1 9.7 %collective-permute-start.1 = (bf16[528,128]{1,0:T(8,128)(2,1)}, bf16[528,128]{1,0:T(8,128)(2,1)S(1)}, u32[]{:S(2)}, u32[]{:S(2)}) collective-permute-start(bf16[528,128]{1,0:T(8,128)(2,1)} %get-tuple-element.24), channel_id=1, source_target_pairs={{0,2},{1,3},{2,4},{3,5},{4,6},{5,7},{6,0},{7,1},{8,10},{9,11},{10,... | collective-permute-start | bytes 405512 | tf_op jit(solution)/shard_map/ppermute | solution.py:360
  7.7 16.9 %collective-permute-start.2 = (bf16[528,128]{1,0:T(8,128)(2,1)}, bf16[528,128]{1,0:T(8,128)(2,1)S(1)}, u32[]{:S(2)}, u32[]{:S(2)}) collective-permute-start(bf16[528,128]{1,0:T(8,128)(2,1)} %get-tuple-element.25), channel_id=1, source_target_pairs={{0,3},{1,4},{2,5},{3,6},{4,7},{5,0},{6,1},{7,2},{8,11},{9,12},{10,... | collective-permute-start | bytes 405512 | tf_op jit(solution)/shard_map/ppermute | solution.py:360
  10.2 14.8 %collective-permute-start.3 = (bf16[528,128]{1,0:T(8,128)(2,1)}, bf16[528,128]{1,0:T(8,128)(2,1)S(1)}, u32[]{:S(2)}, u32[]{:S(2)}) collective-permute-start(bf16[528,128]{1,0:T(8,128)(2,1)} %get-tuple-element.26), channel_id=1, source_target_pairs={{0,4},{1,5},{2,6},{3,7},{4,0},{5,1},{6,2},{7,3},{8,12},{9,13},{10,... | collective-permute-start | bytes 405512 | tf_op jit(solution)/shard_map/ppermute | solution.py:360
  11.5 13.6 %collective-permute-start.4 = (bf16[528,128]{1,0:T(8,128)(2,1)}, bf16[528,128]{1,0:T(8,128)(2,1)S(1)}, u32[]{:S(2)}, u32[]{:S(2)}) collective-permute-start(bf16[528,128]{1,0:T(8,128)(2,1)} %get-tuple-element.27), channel_id=1, source_target_pairs={{0,5},{1,6},{2,7},{3,0},{4,1},{5,2},{6,3},{7,4},{8,13},{9,14},{10,... | collective-permute-start | bytes 405512 | tf_op jit(solution)/shard_map/ppermute | solution.py:360
  14.1 24.0 %copy-start.2 = (bf16[528,128]{1,0:T(8,128)(2,1)}, bf16[528,128]{1,0:T(8,128)(2,1)S(1)}, u32[]{:S(2)}) copy-start(bf16[528,128]{1,0:T(8,128)(2,1)S(1)} %collective-permute-done.refs_1_) | copy-start | bytes 405508
  14.1 10.9 %collective-permute-start.5 = (bf16[528,128]{1,0:T(8,128)(2,1)}, bf16[528,128]{1,0:T(8,128)(2,1)S(1)}, u32[]{:S(2)}, u32[]{:S(2)}) collective-permute-start(bf16[528,128]{1,0:T(8,128)(2,1)} %get-tuple-element.28), channel_id=1, source_target_pairs={{0,6},{1,7},{2,0},{3,1},{4,2},{5,3},{6,4},{7,5},{8,14},{9,15},{10,... | collective-permute-start | bytes 405512 | tf_op jit(solution)/shard_map/ppermute | solution.py:360
  15.8 22.3 %copy-start.3 = (bf16[528,128]{1,0:T(8,128)(2,1)}, bf16[528,128]{1,0:T(8,128)(2,1)S(1)}, u32[]{:S(2)}) copy-start(bf16[528,128]{1,0:T(8,128)(2,1)S(1)} %collective-permute-done.1.refs_2_) | copy-start | bytes 405508
  15.8 9.3 %collective-permute-start.6 = (bf16[528,128]{1,0:T(8,128)(2,1)}, bf16[528,128]{1,0:T(8,128)(2,1)S(1)}, u32[]{:S(2)}, u32[]{:S(2)}) collective-permute-start(bf16[528,128]{1,0:T(8,128)(2,1)} %get-tuple-element.29), channel_id=1, source_target_pairs={{0,7},{1,0},{2,1},{3,2},{4,3},{5,4},{6,5},{7,6},{8,15},{9,8},{10,9... | collective-permute-start | bytes 405512 | tf_op jit(solution)/shard_map/ppermute | solution.py:360
  24.6 13.5 %copy-start.4 = (bf16[528,128]{1,0:T(8,128)(2,1)}, bf16[528,128]{1,0:T(8,128)(2,1)S(1)}, u32[]{:S(2)}) copy-start(bf16[528,128]{1,0:T(8,128)(2,1)S(1)} %collective-permute-done.2.refs_3_) | copy-start | bytes 405508
  25.0 13.1 %copy-start.5 = (bf16[528,128]{1,0:T(8,128)(2,1)}, bf16[528,128]{1,0:T(8,128)(2,1)S(1)}, u32[]{:S(2)}) copy-start(bf16[528,128]{1,0:T(8,128)(2,1)S(1)} %collective-permute-done.3.refs_4_) | copy-start | bytes 405508
  25.0 13.1 %copy-start.6 = (bf16[528,128]{1,0:T(8,128)(2,1)}, bf16[528,128]{1,0:T(8,128)(2,1)S(1)}, u32[]{:S(2)}) copy-start(bf16[528,128]{1,0:T(8,128)(2,1)S(1)} %collective-permute-done.4.refs_5_) | copy-start | bytes 405508
  25.0 13.1 %copy-start.7 = (bf16[528,128]{1,0:T(8,128)(2,1)}, bf16[528,128]{1,0:T(8,128)(2,1)S(1)}, u32[]{:S(2)}) copy-start(bf16[528,128]{1,0:T(8,128)(2,1)S(1)} %collective-permute-done.5.refs_6_) | copy-start | bytes 405508
  25.1 13.0 %copy-start.8 = (bf16[528,128]{1,0:T(8,128)(2,1)}, bf16[528,128]{1,0:T(8,128)(2,1)S(1)}, u32[]{:S(2)}) copy-start(bf16[528,128]{1,0:T(8,128)(2,1)S(1)} %collective-permute-done.6.refs_7_) | copy-start | bytes 405508
  25.1 30.6 %all-to-all-start = ((bf16[8,256,128]{2,1,0:T(8,128)(2,1)}), bf16[8,256,128]{2,1,0:T(8,128)(2,1)S(1)}, u32[]{:S(2)}, u32[]{:S(2)}) async-start(bf16[8,256,128]{2,1,0:T(8,128)(2,1)} %shard_map.75), calls=%async_computation | async-start | bytes 1048576 | tf_op jit(solution)/shard_map/all_to_all | solution.py:396
  55.7 1.2 %copy-start.1 = (f32[8,256,128]{2,1,0:T(8,128)S(1)}, f32[8,256,128]{2,1,0:T(8,128)}, u32[]{:S(2)}) copy-start(f32[8,256,128]{2,1,0:T(8,128)} %shard_map.74.y_ref) | copy-start | bytes 3145732
  57.0 8.7 %collective-permute-start.7 = (bf16[256,128]{1,0:T(8,128)(2,1)S(1)}, bf16[256,128]{1,0:T(8,128)(2,1)S(1)}, u32[]{:S(2)}, u32[]{:S(2)}) collective-permute-start(bf16[256,128]{1,0:T(8,128)(2,1)S(1)} %get-tuple-element.31), channel_id=1, source_target_pairs={{0,8},{1,9},{2,10},{3,11},{4,12},{5,13},{6,14},{7,15},{8,16},{9,17... | collective-permute-start | bytes 196616 | tf_op jit(solution)/shard_map/ppermute | solution.py:360
  57.1 9.4 %collective-permute-start.8 = (bf16[256,128]{1,0:T(8,128)(2,1)S(1)}, bf16[256,128]{1,0:T(8,128)(2,1)S(1)}, u32[]{:S(2)}, u32[]{:S(2)}) collective-permute-start(bf16[256,128]{1,0:T(8,128)(2,1)S(1)} %get-tuple-element.32), channel_id=1, source_target_pairs={{0,15},{1,8},{2,9},{3,10},{4,11},{5,12},{6,13},{7,14},{8,23},{9,16... | collective-permute-start | bytes 196616 | tf_op jit(solution)/shard_map/ppermute | solution.py:360
  63.0 5.4 %collective-permute-start.9 = (bf16[256,128]{1,0:T(8,128)(2,1)S(1)}, bf16[256,128]{1,0:T(8,128)(2,1)S(1)}, u32[]{:S(2)}, u32[]{:S(2)}) collective-permute-start(bf16[256,128]{1,0:T(8,128)(2,1)S(1)} %get-tuple-element.33), channel_id=1, source_target_pairs={{0,14},{1,15},{2,8},{3,9},{4,10},{5,11},{6,12},{7,13},{8,22},{9,23... | collective-permute-start | bytes 196616 | tf_op jit(solution)/shard_map/ppermute | solution.py:360
  63.1 6.2 %collective-permute-start.10 = (bf16[256,128]{1,0:T(8,128)(2,1)S(1)}, bf16[256,128]{1,0:T(8,128)(2,1)S(1)}, u32[]{:S(2)}, u32[]{:S(2)}) collective-permute-start(bf16[256,128]{1,0:T(8,128)(2,1)S(1)} %get-tuple-element.34), channel_id=1, source_target_pairs={{0,13},{1,14},{2,15},{3,8},{4,9},{5,10},{6,11},{7,12},{8,21},{9,22... | collective-permute-start | bytes 196616 | tf_op jit(solution)/shard_map/ppermute | solution.py:360
  63.1 12.5 %collective-permute-start.11 = (bf16[256,128]{1,0:T(8,128)(2,1)S(1)}, bf16[256,128]{1,0:T(8,128)(2,1)S(1)}, u32[]{:S(2)}, u32[]{:S(2)}) collective-permute-start(bf16[256,128]{1,0:T(8,128)(2,1)S(1)} %get-tuple-element.35), channel_id=1, source_target_pairs={{0,12},{1,13},{2,14},{3,15},{4,8},{5,9},{6,10},{7,11},{8,20},{9,21... | collective-permute-start | bytes 196616 | tf_op jit(solution)/shard_map/ppermute | solution.py:360
  65.7 12.2 %collective-permute-start.12 = (bf16[256,128]{1,0:T(8,128)(2,1)S(1)}, bf16[256,128]{1,0:T(8,128)(2,1)S(1)}, u32[]{:S(2)}, u32[]{:S(2)}) collective-permute-start(bf16[256,128]{1,0:T(8,128)(2,1)S(1)} %get-tuple-element.36), channel_id=1, source_target_pairs={{0,11},{1,12},{2,13},{3,14},{4,15},{5,8},{6,9},{7,10},{8,19},{9,20... | collective-permute-start | bytes 196616 | tf_op jit(solution)/shard_map/ppermute | solution.py:360
  66.5 11.4 %collective-permute-start.13 = (bf16[256,128]{1,0:T(8,128)(2,1)S(1)}, bf16[256,128]{1,0:T(8,128)(2,1)S(1)}, u32[]{:S(2)}, u32[]{:S(2)}) collective-permute-start(bf16[256,128]{1,0:T(8,128)(2,1)S(1)} %get-tuple-element.37), channel_id=1, source_target_pairs={{0,10},{1,11},{2,12},{3,13},{4,14},{5,15},{6,8},{7,9},{8,18},{9,19... | collective-permute-start | bytes 196616 | tf_op jit(solution)/shard_map/ppermute | solution.py:360
  68.4 9.5 %collective-permute-start.14 = (bf16[256,128]{1,0:T(8,128)(2,1)S(1)}, bf16[256,128]{1,0:T(8,128)(2,1)S(1)}, u32[]{:S(2)}, u32[]{:S(2)}) collective-permute-start(bf16[256,128]{1,0:T(8,128)(2,1)S(1)} %get-tuple-element.38), channel_id=1, source_target_pairs={{0,9},{1,10},{2,11},{3,12},{4,13},{5,14},{6,15},{7,8},{8,17},{9,18... | collective-permute-start | bytes 196616 | tf_op jit(solution)/shard_map/ppermute | solution.py:360

commit v6 on v5

--- a/solution.py
+++ b/solution.py
@@ -18,6 +18,7 @@
 DOUBLINGS = 4
 SCALE = 215.0
 SMALLEST = 1e-30
+LIMIT = 30
 WIDE = 16
 F32 = jnp.float32
 BF16 = jnp.bfloat16
@@ -167,7 +168,7 @@
         wide = np.stack([np.cos(theta), np.sin(theta)], axis=1).astype(np.float32)
         return np.ascontiguousarray(np.broadcast_to(wide[..., None], wide.shape + (LANES,)))
 
-    return np.concatenate([forward_a, back_a, forward_b, back_b], axis=1), turns(b)
+    return forward_a, forward_b, back_b, back_a, turns(b)
 
 
 def fetched(sources, targets, sems):
@@ -229,17 +230,12 @@
         out_ref[rows:, LANES * e : LANES * (e + 1)] = jnp.where(low, swap_halves(even), odd).astype(BF16)
 
 
-def convolve_kernel(parts, outer, index_ref, *refs):
+def forward_kernel(parts, outer, index_ref, *refs):
     blocks = refs[:parts]
-    skip_ref, sources = refs[parts], refs[parts + 1 : parts + 3]
-    out_ref, x_s, z_s, w_s, y_s, p_s = refs[parts + 3 : parts + 9]
-    matrix_ref, turn_ref = arrived = refs[parts + 9 : parts + 11]
-    copies = fetched(sources, arrived, refs[-1])
-    edges = (0, 3 * outer, 6 * outer, 6 * outer + 6 * INNER, 6 * outer + 9 * INNER)
-    rows = out_ref.shape[1]
+    matrix_ref, turn_ref, z_s, p_s, x_s = refs[parts:]
+    rows = p_s.shape[1]
     per = rows // INNER
     low = lower_half((INNER, LANES))
-    lowc = lower_half((outer, LANES))
 
     def origin(n):
         return lax.rem(index_ref[0] + parts - n, parts)
@@ -257,12 +253,6 @@
             x_s[pl.ds(a, INNER, stride=outer), :] = jnp.where(low, p, swap_halves(h))
             x_s[pl.ds(a + per, INNER, stride=outer), :] = jnp.where(low, swap_halves(p), h)
 
-    for copy in copies:
-        copy.wait()
-
-    def matrix(i):
-        return matrix_ref[:, edges[i] : edges[i + 1]]
-
     def turn(group, n):
         return turn_ref[group * STEP + n, 0], turn_ref[group * STEP + n, 1]
 
@@ -276,7 +266,7 @@
                 ],
                 axis=1,
             )
-            both = jnp.dot(matrix(0), data, preferred_element_type=F32)
+            both = jnp.dot(matrix_ref[...], data, preferred_element_type=F32)
             for j in range(WIDE):
                 re = both[:outer, LANES * j : LANES * (j + 1)]
                 im = both[outer:, LANES * j : LANES * (j + 1)]
@@ -286,6 +276,10 @@
         return carry
 
     lax.fori_loop(0, INNER // STEP, forward_outer, 0)
+
+
+def middle_kernel(outer, z_s, forward_ref, back_ref, w_s):
+    low = lower_half((INNER, LANES))
 
     def middle(group, carry):
         for n in range(0, STEP, WIDE):
@@ -297,7 +291,7 @@
                 ],
                 axis=1,
             )
-            both = jnp.dot(matrix(2), data, preferred_element_type=F32)
+            both = jnp.dot(forward_ref[...], data, preferred_element_type=F32)
             mixed = []
             for j in range(WIDE):
                 re = both[:INNER, LANES * j : LANES * (j + 1)]
@@ -306,7 +300,7 @@
                 mixed.append(
                     stacked(jnp.where(low, re * re_2 - im * im_2, re * im_2 + im * re_2))
                 )
-            both = jnp.dot(matrix(3), jnp.concatenate(mixed, axis=1), preferred_element_type=F32)
+            both = jnp.dot(back_ref[...], jnp.concatenate(mixed, axis=1), preferred_element_type=F32)
             for j in range(WIDE):
                 straight = both[:INNER, LANES * j : LANES * (j + 1)]
                 crossed = swap_halves(both[INNER:, LANES * j : LANES * (j + 1)])
@@ -316,6 +310,18 @@
         return carry
 
     lax.fori_loop(0, outer // STEP, middle, 0)
+
+
+def back_kernel(parts, outer, index_ref, skip_ref, w_s, p_s, *refs):
+    matrix_ref, turn_ref, out_ref, y_s = refs
+    rows = out_ref.shape[1]
+    lowc = lower_half((outer, LANES))
+
+    def origin(n):
+        return lax.rem(index_ref[0] + parts - n, parts)
+
+    def turn(group, n):
+        return turn_ref[group * STEP + n, 0], turn_ref[group * STEP + n, 1]
 
     def back_outer(group, carry):
         for n in range(0, STEP, WIDE):
@@ -327,7 +333,7 @@
                 other = swap_halves(value) * sin
                 straight = value * cos
                 data.append(stacked(jnp.where(lowc, straight - other, straight + other)))
-            both = jnp.dot(matrix(1), jnp.concatenate(data, axis=1), preferred_element_type=F32)
+            both = jnp.dot(matrix_ref[...], jnp.concatenate(data, axis=1), preferred_element_type=F32)
             for j in range(WIDE):
                 re = both[:outer, LANES * j : LANES * (j + 1)]
                 im = both[outer:, LANES * j : LANES * (j + 1)]
@@ -337,11 +343,15 @@
     lax.fori_loop(0, INNER // STEP, back_outer, 0)
 
     lowr = lower_half((rows, LANES))
+    pair = pl.multiple_of(index_ref[0] // 2 * LANES, LANES)
+    wide = skip_ref[:, pl.ds(pair, LANES)]
+    mine = lower_half((1, LANES)) == (index_ref[0] % 2 == 0)
+    skip = jnp.where(mine, wide, swap_halves(wide))
     for n in range(parts):
         at = pl.multiple_of(origin(n) * 2 * rows, 2 * rows)
         early = y_s[pl.ds(at, rows), :]
         late = y_s[pl.ds(at + rows, rows), :]
-        out_ref[n] = jnp.where(lowr, early, swap_halves(late)) + skip_ref[...] * p_s[n]
+        out_ref[n] = jnp.where(lowr, early, swap_halves(late)) + skip * p_s[n]
 
 
 def gate_kernel(parts, index_ref, y_ref, q_ref, *outs):
@@ -360,12 +370,42 @@
     return lax.ppermute(value, ("segment", "ctx"), pairs)
 
 
+def convolved(parts, length, index, slabs, skip_weight):
+    rows = length // 2
+    outer = parts * length // INNER
+    forward_a, forward_b, back_b, back_a, turns = [jnp.asarray(t) for t in tables(outer)]
+    scalar = pl.BlockSpec(memory_space=pltpu.SMEM)
+    whole = pl.BlockSpec(memory_space=pltpu.VMEM)
+
+    def block(*shape):
+        return jax.ShapeDtypeStruct(shape, F32)
+
+    z, p = pl.pallas_call(
+        functools.partial(forward_kernel, parts, outer),
+        out_shape=(block(2 * outer * INNER, LANES), block(parts, rows, LANES)),
+        in_specs=[scalar] + [whole] * (parts + 2),
+        scratch_shapes=[pltpu.VMEM((outer * INNER, LANES), F32)],
+        compiler_params=pltpu.CompilerParams(vmem_limit_bytes=LIMIT * 2**20),
+    )(index, *slabs, forward_a, turns)
+    w = pl.pallas_call(
+        functools.partial(middle_kernel, outer),
+        out_shape=block(outer * INNER, LANES),
+        compiler_params=pltpu.CompilerParams(vmem_limit_bytes=LIMIT * 2**20),
+    )(z, forward_b, back_b)
+    return pl.pallas_call(
+        functools.partial(back_kernel, parts, outer),
+        out_shape=block(parts, rows, LANES),
+        in_specs=[scalar] + [whole] * 5,
+        scratch_shapes=[pltpu.VMEM((outer * INNER, LANES), F32)],
+        compiler_params=pltpu.CompilerParams(vmem_limit_bytes=LIMIT * 2**20),
+    )(index, skip_weight, w, p, back_a, turns)
+
+
 def fast_on_device(query_stream, key_stream, value_stream, filter_taps, skip_weight):
     parts = lax.axis_size("ctx")
     device = lax.axis_index("ctx")
     length, channels = query_stream.shape[1:]
     rows = length // 2
-    outer = parts * length // INNER
     index = jnp.full((1,), device, jnp.int32)
     scalar = pl.BlockSpec(memory_space=pltpu.SMEM)
     whole = pl.BlockSpec(memory_space=pltpu.VMEM)
@@ -392,25 +432,9 @@
         out_shape=block(parts, rows, LANES),
         compiler_params=large,
     )(query_stream[0])
-    q, *_ = lax.optimization_barrier((q, *slabs))
+    q, *_ = lax.optimization_barrier((q, *slabs[: parts - 0]))
     q = lax.all_to_all(q, "ctx", split_axis=0, concat_axis=0, tiled=True)
-    skip = lax.dynamic_slice(skip_weight, (0, device * HALF), (1, HALF))
-    consts = [jnp.asarray(t) for t in tables(outer)]
-    y = pl.pallas_call(
-        functools.partial(convolve_kernel, parts, outer),
-        out_shape=block(parts, rows, LANES, dtype=F32),
-        in_specs=[scalar] + [whole] * (parts + 1) + [far] * len(consts),
-        scratch_shapes=[
-            pltpu.VMEM((outer * INNER, LANES), F32),
-            pltpu.VMEM((2 * outer * INNER, LANES), F32),
-            pltpu.VMEM((outer * INNER, LANES), F32),
-            pltpu.VMEM((outer * INNER, LANES), F32),
-            pltpu.VMEM((parts, rows, LANES), F32),
-        ]
-        + [pltpu.VMEM(t.shape, t.dtype) for t in consts]
-        + [pltpu.SemaphoreType.DMA((len(consts),))],
-        compiler_params=large,
-    )(index, *slabs, jnp.concatenate([skip, skip], axis=1), *consts)
+    y = convolved(parts, length, index, slabs, skip_weight)
     gated = pl.pallas_call(
         functools.partial(gate_kernel, parts),
         out_shape=(block(rows, LANES),) * parts,

time: 79.3 us -> 78.5 us (0.990)
  Pallas kernels: 23.9 us -> 21.1 us
  local copies, waits for them, and re-layouts: 1.32 us -> 3.96 us
    pallas_call x1 -> x3, Pallas kernels: 17.6 us -> 14.7 us  [the longest x1 6.91 us: convolved(): pl.pallas_call(functools.partial(forward_kernel, parts, outer), out_shape...]
    unnamed x18 -> x16, local copies, waits for them, and re-layouts: 1.25 us -> 3.96 us
  transfers between devices with their start and end apart: 16 -> 16, of which waited for: 5 -> 5; matrix products, arithmetic and copies ran while one was open for 1% -> 0% of each run, Pallas kernels for 25% -> 21%
where the time goes in v6:
time: 78.5 us; the launch traced here: 78.2 us
  starting transfers between devices  39.3 us (50%)
  Pallas kernels  21.1 us (27%)
  waiting for transfers between devices  13.7 us (17%)
  local copies, waits for them, and re-layouts  3.96 us (5%)
    ppermute x15, starting transfers between devices, joint_shift(): return lax.ppermute(value, ('segment', 'ctx'), pairs)  27 us
    ppermute x15, waiting for transfers between devices, joint_shift(): return lax.ppermute(value, ('segment', 'ctx'), pairs)  13.7 us
    all_to_all x1, starting transfers between devices, fast_on_device(): q = lax.all_to_all(q, 'ctx', split_axis=0, concat_axis=0, tiled=True)  12.2 us
    pallas_call x1, Pallas kernels, convolved(): pl.pallas_call(functools.partial(forward_kernel, parts, outer), out_shape...  6.91 us
    pallas_call x1, Pallas kernels, convolved(): pl.pallas_call(functools.partial(middle_kernel, outer), out_shape=block(o...  4.37 us
    unnamed x16, local copies, waits for them, and re-layouts  3.96 us
    pallas_call x1, Pallas kernels, convolved(): pl.pallas_call(functools.partial(back_kernel, parts, outer), out_shape=bl...  3.46 us
    pallas_call x1, Pallas kernels, fast_on_device(): pl.pallas_call(functools.partial(pack_kernel, parts), out_shape=(block(si...  3.12 us
  transfers between devices with their start and end apart: 16, of which 5 were waited for; matrix products, arithmetic and copies ran while one was open for 0% of the time, Pallas kernels for 21%

profile of v6, /device:TPU:0, one launch (start us, length us, event | category | flops | bytes accessed | tf_op | source)
XLA Modules:
  0.0 78.2 jit_solution(2936435341745402970)
XLA Ops:
  0.0 3.1 %shard_map.100 = (bf16[528,128]{1,0:T(8,128)(2,1)}, bf16[528,128]{1,0:T(8,128)(2,1)}, bf16[528,128]{1,0:T(8,128)(2,1)}, bf16[528,128]{1,0:T(8,128)(2,1)}, bf16[5...) custom-call(s32[1]{0:T(128)} %bitcast.index_ref, ...), custom_call_target="tpu_custom_call" | custom-call | tf_op jit(solution)/shard_map/pallas_call | solution.py:420
  3.1 3.0 %collective-permute-start = (bf16[528,128]{1,0:T(8,128)(2,1)}, bf16[528,128]{1,0:T(8,128)(2,1)S(1)}, u32[]{:S(2)}, u32[]{:S(2)}) collective-permute-start(bf16[528,128]{1,0:T(8,128)(2,1)} %get-tuple-element.25), channel_id=1, source_target_pairs={{0,1},{1,2},{2,3},{3,4},{4,5},{5,6},{6,7},{7,0},{8,9},{9,10},{10,1... | collective-permute-start | bytes 405512 | tf_op jit(solution)/shard_map/ppermute | solution.py:370
  6.2 1.6 %collective-permute-start.1 = (bf16[528,128]{1,0:T(8,128)(2,1)}, bf16[528,128]{1,0:T(8,128)(2,1)S(1)}, u32[]{:S(2)}, u32[]{:S(2)}) collective-permute-start(bf16[528,128]{1,0:T(8,128)(2,1)} %get-tuple-element.26), channel_id=1, source_target_pairs={{0,2},{1,3},{2,4},{3,5},{4,6},{5,7},{6,0},{7,1},{8,10},{9,11},{10,... | collective-permute-start | bytes 405512 | tf_op jit(solution)/shard_map/ppermute | solution.py:370
  7.7 2.5 %collective-permute-start.2 = (bf16[528,128]{1,0:T(8,128)(2,1)}, bf16[528,128]{1,0:T(8,128)(2,1)S(1)}, u32[]{:S(2)}, u32[]{:S(2)}) collective-permute-start(bf16[528,128]{1,0:T(8,128)(2,1)} %get-tuple-element.27), channel_id=1, source_target_pairs={{0,3},{1,4},{2,5},{3,6},{4,7},{5,0},{6,1},{7,2},{8,11},{9,12},{10,... | collective-permute-start | bytes 405512 | tf_op jit(solution)/shard_map/ppermute | solution.py:370
  10.3 1.2 %collective-permute-start.3 = (bf16[528,128]{1,0:T(8,128)(2,1)}, bf16[528,128]{1,0:T(8,128)(2,1)S(1)}, u32[]{:S(2)}, u32[]{:S(2)}) collective-permute-start(bf16[528,128]{1,0:T(8,128)(2,1)} %get-tuple-element.28), channel_id=1, source_target_pairs={{0,4},{1,5},{2,6},{3,7},{4,0},{5,1},{6,2},{7,3},{8,12},{9,13},{10,... | collective-permute-start | bytes 405512 | tf_op jit(solution)/shard_map/ppermute | solution.py:370
  11.5 2.6 %collective-permute-start.4 = (bf16[528,128]{1,0:T(8,128)(2,1)}, bf16[528,128]{1,0:T(8,128)(2,1)S(1)}, u32[]{:S(2)}, u32[]{:S(2)}) collective-permute-start(bf16[528,128]{1,0:T(8,128)(2,1)} %get-tuple-element.29), channel_id=1, source_target_pairs={{0,5},{1,6},{2,7},{3,0},{4,1},{5,2},{6,3},{7,4},{8,13},{9,14},{10,... | collective-permute-start | bytes 405512 | tf_op jit(solution)/shard_map/ppermute | solution.py:370
  14.2 1.7 %collective-permute-start.5 = (bf16[528,128]{1,0:T(8,128)(2,1)}, bf16[528,128]{1,0:T(8,128)(2,1)S(1)}, u32[]{:S(2)}, u32[]{:S(2)}) collective-permute-start(bf16[528,128]{1,0:T(8,128)(2,1)} %get-tuple-element.30), channel_id=1, source_target_pairs={{0,6},{1,7},{2,0},{3,1},{4,2},{5,3},{6,4},{7,5},{8,14},{9,15},{10,... | collective-permute-start | bytes 405512 | tf_op jit(solution)/shard_map/ppermute | solution.py:370
  15.8 2.1 %collective-permute-start.6 = (bf16[528,128]{1,0:T(8,128)(2,1)}, bf16[528,128]{1,0:T(8,128)(2,1)S(1)}, u32[]{:S(2)}, u32[]{:S(2)}) collective-permute-start(bf16[528,128]{1,0:T(8,128)(2,1)} %get-tuple-element.31), channel_id=1, source_target_pairs={{0,7},{1,0},{2,1},{3,2},{4,3},{5,4},{6,5},{7,6},{8,15},{9,8},{10,9... | collective-permute-start | bytes 405512 | tf_op jit(solution)/shard_map/ppermute | solution.py:370
  18.0 2.1 %shard_map.104 = bf16[8,256,128]{2,1,0:T(8,128)(2,1)} custom-call(bf16[512,512]{1,0:T(8,128)(2,1)} %bitcast.9), custom_call_target="tpu_custom_call" | custom-call | tf_op jit(solution)/shard_map/pallas_call | solution.py:430
  20.0 4.7 %collective-permute-done.2.refs_3_ = bf16[528,128]{1,0:T(8,128)(2,1)S(1)} collective-permute-done((bf16[528,128]{1,0:T(8,128)(2,1)}, bf16[528,128]{1,0:T(8,128)(2,1)S(1)}, u32[]{:S(2)}, u32[]{:S(2)}) %collective-permute-start.2) | collective-permute-done | bytes 135200 | tf_op jit(solution)/shard_map/ppermute | solution.py:370
  24.7 0.4 collective-permute-done.3.refs_4_
  25.1 0.1 collective-permute-done.6.refs_7_
  25.1 12.2 %all-to-all-start = ((bf16[8,256,128]{2,1,0:T(8,128)(2,1)}), bf16[8,256,128]{2,1,0:T(8,128)(2,1)S(1)}, u32[]{:S(2)}, u32[]{:S(2)}) async-start(bf16[8,256,128]{2,1,0:T(8,128)(2,1)} %shard_map.104), calls=%async_computation | async-start | bytes 1048576 | tf_op jit(solution)/shard_map/all_to_all | solution.py:436
  37.4 2.2 %copy-done = f32[64,2,64,128]{3,2,1,0:T(8,128)S(1)} copy-done((f32[64,2,64,128]{3,2,1,0:T(8,128)S(1)}, f32[64,2,64,128]{3,2,1,0:T(8,128)}, u32[]{:S(2)}) %copy-start) | copy-done | bytes 4194328
  39.6 0.9 %copy-done.2 = bf16[528,128]{1,0:T(8,128)(2,1)S(1)} copy-done((bf16[528,128]{1,0:T(8,128)(2,1)S(1)}, bf16[528,128]{1,0:T(8,128)(2,1)}, u32[]{:S(2)}) %copy-start.2) | copy-done | bytes 135192
  40.5 0.8 %copy-done.6 = bf16[128,192]{1,0:T(8,128)(2,1)S(1)} copy-done((bf16[128,192]{1,0:T(8,128)(2,1)S(1)}, bf16[128,192]{1,0:T(8,128)(2,1)}, u32[]{:S(2)}) %copy-start.6) | copy-done | bytes 49176
  41.3 6.9 %shard_map.101 = (f32[8192,128]{1,0:T(8,128)S(1)}, f32[8,256,128]{2,1,0:T(8,128)S(1)}) custom-call(s32[1]{0:T(128)} %bitcast.index_ref, bf16[528,128]{1,0:T(8,128)(2,1)S(1)} %copy-done.2, bf16[528,128]{1,0:T(8,128)(2,1)S(1)} %collective-permute-done.refs_1_, bf16[528,128]{1,0:T(8,128)(2,1)S(1)} %collective-permute-done.1.refs_2_, ...), custom_call_target="tpu_custom_call" | custom-call | tf_op jit(solution)/shard_map/pallas_call | solution.py:383
  48.2 0.0 copy-start.1
  48.2 0.0 copy-start.4
  48.3 4.4 %shard_map.102.w_s = f32[4096,128]{1,0:T(8,128)S(1)} custom-call(f32[8192,128]{1,0:T(8,128)S(1)} %get-tuple-element.32.z_s, bf16[128,384]{1,0:T(8,128)(2,1)S(1)} %copy-done.3, bf16[128,192]{1,0:T(8,128)(2,1)S(1)} %copy-done.5), custom_call_target="tpu_custom_call" | custom-call | tf_op jit(solution)/shard_map/pallas_call | solution.py:390
  52.7 3.5 %shard_map.103.y_ref = f32[8,256,128]{2,1,0:T(8,128)S(1)} custom-call(s32[1]{0:T(128)} %bitcast.index_ref, f32[1,512]{1,0:T(1,128)S(1)} %copy-done.7, f32[4096,128]{1,0:T(8,128)S(1)} %shard_map.102.w_s, f32[8,256,128]{2,1,0:T(8,128)S(1)} %get-tuple-element.33.p_s, bf16[128,192]{1,0:T(8,128)(2,1)S(1)} %copy-done.4, f32[64,2,64,128]{3,2,1,0:T(8,128)S(1)} %copy-done.1), custom_call_target="tpu_custom_call" | custom-call | tf_op jit(solution)/shard_map/pallas_call | solution.py:395
  56.2 0.1 shard_map.105
  56.3 0.1 collective-permute-start.7
  56.3 5.9 %collective-permute-start.8 = (bf16[256,128]{1,0:T(8,128)(2,1)S(1)}, bf16[256,128]{1,0:T(8,128)(2,1)S(1)}, u32[]{:S(2)}, u32[]{:S(2)}) collective-permute-start(bf16[256,128]{1,0:T(8,128)(2,1)S(1)} %get-tuple-element.36), channel_id=1, source_target_pairs={{0,15},{1,8},{2,9},{3,10},{4,11},{5,12},{6,13},{7,14},{8,23},{9,16... | collective-permute-start | bytes 196616 | tf_op jit(solution)/shard_map/ppermute | solution.py:370
  62.2 0.1 collective-permute-start.9
  62.3 2.6 %collective-permute-start.11 = (bf16[256,128]{1,0:T(8,128)(2,1)S(1)}, bf16[256,128]{1,0:T(8,128)(2,1)S(1)}, u32[]{:S(2)}, u32[]{:S(2)}) collective-permute-start(bf16[256,128]{1,0:T(8,128)(2,1)S(1)} %get-tuple-element.39), channel_id=1, source_target_pairs={{0,12},{1,13},{2,14},{3,15},{4,8},{5,9},{6,10},{7,11},{8,20},{9,21... | collective-permute-start | bytes 196616 | tf_op jit(solution)/shard_map/ppermute | solution.py:370
  64.9 0.8 %collective-permute-start.12 = (bf16[256,128]{1,0:T(8,128)(2,1)S(1)}, bf16[256,128]{1,0:T(8,128)(2,1)S(1)}, u32[]{:S(2)}, u32[]{:S(2)}) collective-permute-start(bf16[256,128]{1,0:T(8,128)(2,1)S(1)} %get-tuple-element.40), channel_id=1, source_target_pairs={{0,11},{1,12},{2,13},{3,14},{4,15},{5,8},{6,9},{7,10},{8,19},{9,20... | collective-permute-start | bytes 196616 | tf_op jit(solution)/shard_map/ppermute | solution.py:370
  65.7 1.9 %collective-permute-start.13 = (bf16[256,128]{1,0:T(8,128)(2,1)S(1)}, bf16[256,128]{1,0:T(8,128)(2,1)S(1)}, u32[]{:S(2)}, u32[]{:S(2)}) collective-permute-start(bf16[256,128]{1,0:T(8,128)(2,1)S(1)} %get-tuple-element.41), channel_id=1, source_target_pairs={{0,10},{1,11},{2,12},{3,13},{4,14},{5,15},{6,8},{7,9},{8,18},{9,19... | collective-permute-start | bytes 196616 | tf_op jit(solution)/shard_map/ppermute | solution.py:370
  67.6 0.9 %collective-permute-start.14 = (bf16[256,128]{1,0:T(8,128)(2,1)S(1)}, bf16[256,128]{1,0:T(8,128)(2,1)S(1)}, u32[]{:S(2)}, u32[]{:S(2)}) collective-permute-start(bf16[256,128]{1,0:T(8,128)(2,1)S(1)} %get-tuple-element.42), channel_id=1, source_target_pairs={{0,9},{1,10},{2,11},{3,12},{4,13},{5,14},{6,15},{7,8},{8,17},{9,18... | collective-permute-start | bytes 196616 | tf_op jit(solution)/shard_map/ppermute | solution.py:370
  68.5 6.2 %collective-permute-done.11.refs_4_ = bf16[256,128]{1,0:T(8,128)(2,1)S(1)} collective-permute-done((bf16[256,128]{1,0:T(8,128)(2,1)S(1)}, bf16[256,128]{1,0:T(8,128)(2,1)S(1)}, u32[]{:S(2)}, u32[]{:S(2)}) %collective-permute-start.11) | collective-permute-done | bytes 65568 | tf_op jit(solution)/shard_map/ppermute | solution.py:370
  74.8 2.3 %collective-permute-done.12.refs_5_ = bf16[256,128]{1,0:T(8,128)(2,1)S(1)} collective-permute-done((bf16[256,128]{1,0:T(8,128)(2,1)S(1)}, bf16[256,128]{1,0:T(8,128)(2,1)S(1)}, u32[]{:S(2)}, u32[]{:S(2)}) %collective-permute-start.12) | collective-permute-done | bytes 65568 | tf_op jit(solution)/shard_map/ppermute | solution.py:370
  77.1 1.0 %shard_map.106 = bf16[512,512]{1,0:T(8,128)(2,1)} custom-call(s32[1]{0:T(128)} %bitcast.index_ref, bf16[256,128]{1,0:T(8,128)(2,1)S(1)} %collective-permute-done.7.refs_0_, bf16[256,128]{1,0:T(8,128)(2,1)S(1)} %collective-permute-done.8.refs_1_, bf16[256,128]{1,0:T(8,128)(2,1)S(1)} %collective-permute-done.9.refs_2_, ...), custom_call_target="tpu_custom_call" | custom-call | tf_op jit(solution)/shard_map/pallas_call | solution.py:445
  (23 shorter events, 0.1 us)
Async XLA Ops:
  0.0 48.3 %copy-start.3 = (bf16[128,384]{1,0:T(8,128)(2,1)S(1)}, bf16[128,384]{1,0:T(8,128)(2,1)}, u32[]{:S(2)}) copy-start(bf16[128,384]{1,0:T(8,128)(2,1)} %constant.15.clone.forward_ref) | copy-start | bytes 294916
  0.0 48.3 %copy-start.5 = (bf16[128,192]{1,0:T(8,128)(2,1)S(1)}, bf16[128,192]{1,0:T(8,128)(2,1)}, u32[]{:S(2)}) copy-start(bf16[128,192]{1,0:T(8,128)(2,1)} %constant.16.clone.back_ref) | copy-start | bytes 147460
  3.1 11.0 %collective-permute-start = (bf16[528,128]{1,0:T(8,128)(2,1)}, bf16[528,128]{1,0:T(8,128)(2,1)S(1)}, u32[]{:S(2)}, u32[]{:S(2)}) collective-permute-start(bf16[528,128]{1,0:T(8,128)(2,1)} %get-tuple-element.25), channel_id=1, source_target_pairs={{0,1},{1,2},{2,3},{3,4},{4,5},{5,6},{6,7},{7,0},{8,9},{9,10},{10,1... | collective-permute-start | bytes 405512 | tf_op jit(solution)/shard_map/ppermute | solution.py:370
  6.2 9.7 %collective-permute-start.1 = (bf16[528,128]{1,0:T(8,128)(2,1)}, bf16[528,128]{1,0:T(8,128)(2,1)S(1)}, u32[]{:S(2)}, u32[]{:S(2)}) collective-permute-start(bf16[528,128]{1,0:T(8,128)(2,1)} %get-tuple-element.26), channel_id=1, source_target_pairs={{0,2},{1,3},{2,4},{3,5},{4,6},{5,7},{6,0},{7,1},{8,10},{9,11},{10,... | collective-permute-start | bytes 405512 | tf_op jit(solution)/shard_map/ppermute | solution.py:370
  7.7 16.9 %collective-permute-start.2 = (bf16[528,128]{1,0:T(8,128)(2,1)}, bf16[528,128]{1,0:T(8,128)(2,1)S(1)}, u32[]{:S(2)}, u32[]{:S(2)}) collective-permute-start(bf16[528,128]{1,0:T(8,128)(2,1)} %get-tuple-element.27), channel_id=1, source_target_pairs={{0,3},{1,4},{2,5},{3,6},{4,7},{5,0},{6,1},{7,2},{8,11},{9,12},{10,... | collective-permute-start | bytes 405512 | tf_op jit(solution)/shard_map/ppermute | solution.py:370
  10.3 14.8 %collective-permute-start.3 = (bf16[528,128]{1,0:T(8,128)(2,1)}, bf16[528,128]{1,0:T(8,128)(2,1)S(1)}, u32[]{:S(2)}, u32[]{:S(2)}) collective-permute-start(bf16[528,128]{1,0:T(8,128)(2,1)} %get-tuple-element.28), channel_id=1, source_target_pairs={{0,4},{1,5},{2,6},{3,7},{4,0},{5,1},{6,2},{7,3},{8,12},{9,13},{10,... | collective-permute-start | bytes 405512 | tf_op jit(solution)/shard_map/ppermute | solution.py:370
  11.5 13.6 %collective-permute-start.4 = (bf16[528,128]{1,0:T(8,128)(2,1)}, bf16[528,128]{1,0:T(8,128)(2,1)S(1)}, u32[]{:S(2)}, u32[]{:S(2)}) collective-permute-start(bf16[528,128]{1,0:T(8,128)(2,1)} %get-tuple-element.29), channel_id=1, source_target_pairs={{0,5},{1,6},{2,7},{3,0},{4,1},{5,2},{6,3},{7,4},{8,13},{9,14},{10,... | collective-permute-start | bytes 405512 | tf_op jit(solution)/shard_map/ppermute | solution.py:370
  14.2 10.9 %collective-permute-start.5 = (bf16[528,128]{1,0:T(8,128)(2,1)}, bf16[528,128]{1,0:T(8,128)(2,1)S(1)}, u32[]{:S(2)}, u32[]{:S(2)}) collective-permute-start(bf16[528,128]{1,0:T(8,128)(2,1)} %get-tuple-element.30), channel_id=1, source_target_pairs={{0,6},{1,7},{2,0},{3,1},{4,2},{5,3},{6,4},{7,5},{8,14},{9,15},{10,... | collective-permute-start | bytes 405512 | tf_op jit(solution)/shard_map/ppermute | solution.py:370
  15.8 9.3 %collective-permute-start.6 = (bf16[528,128]{1,0:T(8,128)(2,1)}, bf16[528,128]{1,0:T(8,128)(2,1)S(1)}, u32[]{:S(2)}, u32[]{:S(2)}) collective-permute-start(bf16[528,128]{1,0:T(8,128)(2,1)} %get-tuple-element.31), channel_id=1, source_target_pairs={{0,7},{1,0},{2,1},{3,2},{4,3},{5,4},{6,5},{7,6},{8,15},{9,8},{10,9... | collective-permute-start | bytes 405512 | tf_op jit(solution)/shard_map/ppermute | solution.py:370
  25.1 31.0 %all-to-all-start = ((bf16[8,256,128]{2,1,0:T(8,128)(2,1)}), bf16[8,256,128]{2,1,0:T(8,128)(2,1)S(1)}, u32[]{:S(2)}, u32[]{:S(2)}) async-start(bf16[8,256,128]{2,1,0:T(8,128)(2,1)} %shard_map.104), calls=%async_computation | async-start | bytes 1048576 | tf_op jit(solution)/shard_map/all_to_all | solution.py:436
  37.4 2.2 %copy-start = (f32[64,2,64,128]{3,2,1,0:T(8,128)S(1)}, f32[64,2,64,128]{3,2,1,0:T(8,128)}, u32[]{:S(2)}) copy-start(f32[64,2,64,128]{3,2,1,0:T(8,128)} %constant.18.clone.refs_9_.refs_1_) | copy-start | bytes 12582916
  39.5 0.9 %copy-start.2 = (bf16[528,128]{1,0:T(8,128)(2,1)S(1)}, bf16[528,128]{1,0:T(8,128)(2,1)}, u32[]{:S(2)}) copy-start(bf16[528,128]{1,0:T(8,128)(2,1)} %get-tuple-element.24.refs_0_) | copy-start | bytes 405508
  40.5 0.8 %copy-start.6 = (bf16[128,192]{1,0:T(8,128)(2,1)S(1)}, bf16[128,192]{1,0:T(8,128)(2,1)}, u32[]{:S(2)}) copy-start(bf16[128,192]{1,0:T(8,128)(2,1)} %constant.14.clone.refs_8_) | copy-start | bytes 147460
  48.2 4.4 %copy-start.1 = (f32[64,2,64,128]{3,2,1,0:T(8,128)S(1)}, f32[64,2,64,128]{3,2,1,0:T(8,128)}, u32[]{:S(2)}) copy-start(f32[64,2,64,128]{3,2,1,0:T(8,128)} %constant.18.clone.refs_9_.refs_1_) | copy-start | bytes 12582916
  48.2 4.4 %copy-start.4 = (bf16[128,192]{1,0:T(8,128)(2,1)S(1)}, bf16[128,192]{1,0:T(8,128)(2,1)}, u32[]{:S(2)}) copy-start(bf16[128,192]{1,0:T(8,128)(2,1)} %constant.17.clone.refs_0_) | copy-start | bytes 147460
  48.2 4.4 %copy-start.7 = (f32[1,512]{1,0:T(1,128)S(1)}, f32[1,512]{1,0:T(1,128)}, u32[]{:S(2)}) copy-start(f32[1,512]{1,0:T(1,128)} %skip_ref.1) | copy-start | bytes 6148
  56.3 8.7 %collective-permute-start.7 = (bf16[256,128]{1,0:T(8,128)(2,1)S(1)}, bf16[256,128]{1,0:T(8,128)(2,1)S(1)}, u32[]{:S(2)}, u32[]{:S(2)}) collective-permute-start(bf16[256,128]{1,0:T(8,128)(2,1)S(1)} %get-tuple-element.35), channel_id=1, source_target_pairs={{0,8},{1,9},{2,10},{3,11},{4,12},{5,13},{6,14},{7,15},{8,16},{9,17... | collective-permute-start | bytes 196616 | tf_op jit(solution)/shard_map/ppermute | solution.py:370
  56.3 9.4 %collective-permute-start.8 = (bf16[256,128]{1,0:T(8,128)(2,1)S(1)}, bf16[256,128]{1,0:T(8,128)(2,1)S(1)}, u32[]{:S(2)}, u32[]{:S(2)}) collective-permute-start(bf16[256,128]{1,0:T(8,128)(2,1)S(1)} %get-tuple-element.36), channel_id=1, source_target_pairs={{0,15},{1,8},{2,9},{3,10},{4,11},{5,12},{6,13},{7,14},{8,23},{9,16... | collective-permute-start | bytes 196616 | tf_op jit(solution)/shard_map/ppermute | solution.py:370
  62.2 5.4 %collective-permute-start.9 = (bf16[256,128]{1,0:T(8,128)(2,1)S(1)}, bf16[256,128]{1,0:T(8,128)(2,1)S(1)}, u32[]{:S(2)}, u32[]{:S(2)}) collective-permute-start(bf16[256,128]{1,0:T(8,128)(2,1)S(1)} %get-tuple-element.37), channel_id=1, source_target_pairs={{0,14},{1,15},{2,8},{3,9},{4,10},{5,11},{6,12},{7,13},{8,22},{9,23... | collective-permute-start | bytes 196616 | tf_op jit(solution)/shard_map/ppermute | solution.py:370
  62.3 6.2 %collective-permute-start.10 = (bf16[256,128]{1,0:T(8,128)(2,1)S(1)}, bf16[256,128]{1,0:T(8,128)(2,1)S(1)}, u32[]{:S(2)}, u32[]{:S(2)}) collective-permute-start(bf16[256,128]{1,0:T(8,128)(2,1)S(1)} %get-tuple-element.38), channel_id=1, source_target_pairs={{0,13},{1,14},{2,15},{3,8},{4,9},{5,10},{6,11},{7,12},{8,21},{9,22... | collective-permute-start | bytes 196616 | tf_op jit(solution)/shard_map/ppermute | solution.py:370
  62.3 12.5 %collective-permute-start.11 = (bf16[256,128]{1,0:T(8,128)(2,1)S(1)}, bf16[256,128]{1,0:T(8,128)(2,1)S(1)}, u32[]{:S(2)}, u32[]{:S(2)}) collective-permute-start(bf16[256,128]{1,0:T(8,128)(2,1)S(1)} %get-tuple-element.39), channel_id=1, source_target_pairs={{0,12},{1,13},{2,14},{3,15},{4,8},{5,9},{6,10},{7,11},{8,20},{9,21... | collective-permute-start | bytes 196616 | tf_op jit(solution)/shard_map/ppermute | solution.py:370
  64.9 12.2 %collective-permute-start.12 = (bf16[256,128]{1,0:T(8,128)(2,1)S(1)}, bf16[256,128]{1,0:T(8,128)(2,1)S(1)}, u32[]{:S(2)}, u32[]{:S(2)}) collective-permute-start(bf16[256,128]{1,0:T(8,128)(2,1)S(1)} %get-tuple-element.40), channel_id=1, source_target_pairs={{0,11},{1,12},{2,13},{3,14},{4,15},{5,8},{6,9},{7,10},{8,19},{9,20... | collective-permute-start | bytes 196616 | tf_op jit(solution)/shard_map/ppermute | solution.py:370
  65.7 11.4 %collective-permute-start.13 = (bf16[256,128]{1,0:T(8,128)(2,1)S(1)}, bf16[256,128]{1,0:T(8,128)(2,1)S(1)}, u32[]{:S(2)}, u32[]{:S(2)}) collective-permute-start(bf16[256,128]{1,0:T(8,128)(2,1)S(1)} %get-tuple-element.41), channel_id=1, source_target_pairs={{0,10},{1,11},{2,12},{3,13},{4,14},{5,15},{6,8},{7,9},{8,18},{9,19... | collective-permute-start | bytes 196616 | tf_op jit(solution)/shard_map/ppermute | solution.py:370
  67.6 9.5 %collective-permute-start.14 = (bf16[256,128]{1,0:T(8,128)(2,1)S(1)}, bf16[256,128]{1,0:T(8,128)(2,1)S(1)}, u32[]{:S(2)}, u32[]{:S(2)}) collective-permute-start(bf16[256,128]{1,0:T(8,128)(2,1)S(1)} %get-tuple-element.42), channel_id=1, source_target_pairs={{0,9},{1,10},{2,11},{3,12},{4,13},{5,14},{6,15},{7,8},{8,17},{9,18... | collective-permute-start | bytes 196616 | tf_op jit(solution)/shard_map/ppermute | solution.py:370

commit v7 on v6

--- a/solution.py
+++ b/solution.py
@@ -168,7 +168,7 @@
         wide = np.stack([np.cos(theta), np.sin(theta)], axis=1).astype(np.float32)
         return np.ascontiguousarray(np.broadcast_to(wide[..., None], wide.shape + (LANES,)))
 
-    return forward_a, forward_b, back_b, back_a, turns(b)
+    return forward_a, forward_b, back_b, back_a, turns(b), turns(np.concatenate([b[:STEP], b[::STEP]]))
 
 
 def fetched(sources, targets, sems):
@@ -218,6 +218,12 @@
         out_ref[2 * e + 1] = jnp.where(low, swap_halves(early), late).astype(BF16)
 
 
+def hold_kernel(*refs):
+    half = len(refs) // 2
+    for source, target in zip(refs[:half], refs[half:]):
+        target[...] = source[...]
+
+
 def unpack_kernel(parts, index_ref, *refs):
     blocks, out_ref, held = refs[:parts], refs[parts], refs[parts + 1]
     rows = held.shape[1]
@@ -254,7 +260,11 @@
             x_s[pl.ds(a + per, INNER, stride=outer), :] = jnp.where(low, swap_halves(p), h)
 
     def turn(group, n):
-        return turn_ref[group * STEP + n, 0], turn_ref[group * STEP + n, 1]
+        cos_1, sin_1 = turn_ref[STEP + group, 0], turn_ref[STEP + group, 1]
+        if n == 0:
+            return cos_1, sin_1
+        cos_2, sin_2 = turn_ref[n, 0], turn_ref[n, 1]
+        return cos_1 * cos_2 - sin_1 * sin_2, sin_1 * cos_2 + cos_1 * sin_2
 
     def forward_outer(group, carry):
         for n in range(0, STEP, WIDE):
@@ -370,10 +380,10 @@
     return lax.ppermute(value, ("segment", "ctx"), pairs)
 
 
-def convolved(parts, length, index, slabs, skip_weight):
+def convolved(parts, length, index, slabs, skip_weight, consts):
     rows = length // 2
     outer = parts * length // INNER
-    forward_a, forward_b, back_b, back_a, turns = [jnp.asarray(t) for t in tables(outer)]
+    first_turns, forward_a, turns, forward_b, back_b, back_a = consts
     scalar = pl.BlockSpec(memory_space=pltpu.SMEM)
     whole = pl.BlockSpec(memory_space=pltpu.VMEM)
 
@@ -386,7 +396,7 @@
         in_specs=[scalar] + [whole] * (parts + 2),
         scratch_shapes=[pltpu.VMEM((outer * INNER, LANES), F32)],
         compiler_params=pltpu.CompilerParams(vmem_limit_bytes=LIMIT * 2**20),
-    )(index, *slabs, forward_a, turns)
+    )(index, *slabs, forward_a, first_turns)
     w = pl.pallas_call(
         functools.partial(middle_kernel, outer),
         out_shape=block(outer * INNER, LANES),
@@ -432,9 +442,20 @@
         out_shape=block(parts, rows, LANES),
         compiler_params=large,
     )(query_stream[0])
-    q, *_ = lax.optimization_barrier((q, *slabs[: parts - 0]))
+    forward_a, forward_b, back_b, back_a, turns, two_turns = [
+        jnp.asarray(t) for t in tables(parts * length // INNER)
+    ]
+    held = (sent[0], forward_a)
+    held = pl.pallas_call(
+        hold_kernel,
+        out_shape=tuple(jax.ShapeDtypeStruct(x.shape, x.dtype) for x in held),
+        compiler_params=small,
+    )(*held)
+    q, *_ = lax.optimization_barrier((q, *slabs, *held))
+    slabs = [held[0]] + slabs[1:]
+    consts = (two_turns, held[1], turns, forward_b, back_b, back_a)
     q = lax.all_to_all(q, "ctx", split_axis=0, concat_axis=0, tiled=True)
-    y = convolved(parts, length, index, slabs, skip_weight)
+    y = convolved(parts, length, index, slabs, skip_weight, consts)
     gated = pl.pallas_call(
         functools.partial(gate_kernel, parts),
         out_shape=(block(rows, LANES),) * parts,

time: 78.5 us -> 74.9 us (0.954)
  local copies, waits for them, and re-layouts: 3.96 us -> 1.78 us
  waiting for transfers between devices: 13.7 us -> 12 us
    unnamed x16, local copies, waits for them, and re-layouts: 3.96 us -> 1.78 us
    ppermute x15, waiting for transfers between devices: 13.7 us -> 12 us  [joint_shift(): return lax.ppermute(value, ('segment', 'ctx'), pairs)]
  transfers between devices with their start and end apart: 16 -> 16, of which waited for: 5 -> 5; matrix products, arithmetic and copies ran while one was open for 0% -> 0% of each run, Pallas kernels for 21% -> 23%
where the time goes in v7:
time: 74.9 us; the launch traced here: 74.5 us
  starting transfers between devices  39.2 us (52%)
  Pallas kernels  21.4 us (29%)
  waiting for transfers between devices  12 us (16%)
  local copies, waits for them, and re-layouts  1.78 us (2%)
    ppermute x15, starting transfers between devices, joint_shift(): return lax.ppermute(value, ('segment', 'ctx'), pairs)  27 us
    all_to_all x1, starting transfers between devices, fast_on_device(): q = lax.all_to_all(q, 'ctx', split_axis=0, concat_axis=0, tiled=True)  12.2 us
    ppermute x15, waiting for transfers between devices, joint_shift(): return lax.ppermute(value, ('segment', 'ctx'), pairs)  12 us
    pallas_call x1, Pallas kernels, convolved(): pl.pallas_call(functools.partial(forward_kernel, parts, outer), out_shape...  7.04 us
    pallas_call x1, Pallas kernels, convolved(): pl.pallas_call(functools.partial(middle_kernel, outer), out_shape=block(o...  4.4 us
    pallas_call x1, Pallas kernels, convolved(): pl.pallas_call(functools.partial(back_kernel, parts, outer), out_shape=bl...  3.52 us
    pallas_call x1, Pallas kernels, fast_on_device(): pl.pallas_call(functools.partial(pack_kernel, parts), out_shape=(block(si...  3.21 us
    pallas_call x1, Pallas kernels, fast_on_device(): pl.pallas_call(functools.partial(pack_gate_kernel, parts), out_shape=bloc...  2.06 us
  transfers between devices with their start and end apart: 16, of which 5 were waited for; matrix products, arithmetic and copies ran while one was open for 0% of the time, Pallas kernels for 23%

profile of v7, /device:TPU:0, one launch (start us, length us, event | category | flops | bytes accessed | tf_op | source)
XLA Modules:
  0.0 74.5 jit_solution(12842357561721907924)
XLA Ops:
  0.0 3.2 %shard_map.109 = (bf16[528,128]{1,0:T(8,128)(2,1)}, bf16[528,128]{1,0:T(8,128)(2,1)}, bf16[528,128]{1,0:T(8,128)(2,1)}, bf16[528,128]{1,0:T(8,128)(2,1)}, bf16[5...) custom-call(s32[1]{0:T(128)} %bitcast.index_ref, ...), custom_call_target="tpu_custom_call" | custom-call | tf_op jit(solution)/shard_map/pallas_call | solution.py:430
  3.2 3.0 %collective-permute-start = (bf16[528,128]{1,0:T(8,128)(2,1)}, bf16[528,128]{1,0:T(8,128)(2,1)S(1)}, u32[]{:S(2)}, u32[]{:S(2)}) collective-permute-start(bf16[528,128]{1,0:T(8,128)(2,1)} %get-tuple-element.28), channel_id=1, source_target_pairs={{0,1},{1,2},{2,3},{3,4},{4,5},{5,6},{6,7},{7,0},{8,9},{9,10},{10,1... | collective-permute-start | bytes 405512 | tf_op jit(solution)/shard_map/ppermute | solution.py:380
  6.3 1.6 %collective-permute-start.1 = (bf16[528,128]{1,0:T(8,128)(2,1)}, bf16[528,128]{1,0:T(8,128)(2,1)S(1)}, u32[]{:S(2)}, u32[]{:S(2)}) collective-permute-start(bf16[528,128]{1,0:T(8,128)(2,1)} %get-tuple-element.29), channel_id=1, source_target_pairs={{0,2},{1,3},{2,4},{3,5},{4,6},{5,7},{6,0},{7,1},{8,10},{9,11},{10,... | collective-permute-start | bytes 405512 | tf_op jit(solution)/shard_map/ppermute | solution.py:380
  7.8 2.5 %collective-permute-start.2 = (bf16[528,128]{1,0:T(8,128)(2,1)}, bf16[528,128]{1,0:T(8,128)(2,1)S(1)}, u32[]{:S(2)}, u32[]{:S(2)}) collective-permute-start(bf16[528,128]{1,0:T(8,128)(2,1)} %get-tuple-element.30), channel_id=1, source_target_pairs={{0,3},{1,4},{2,5},{3,6},{4,7},{5,0},{6,1},{7,2},{8,11},{9,12},{10,... | collective-permute-start | bytes 405512 | tf_op jit(solution)/shard_map/ppermute | solution.py:380
  10.4 1.2 %collective-permute-start.3 = (bf16[528,128]{1,0:T(8,128)(2,1)}, bf16[528,128]{1,0:T(8,128)(2,1)S(1)}, u32[]{:S(2)}, u32[]{:S(2)}) collective-permute-start(bf16[528,128]{1,0:T(8,128)(2,1)} %get-tuple-element.31), channel_id=1, source_target_pairs={{0,4},{1,5},{2,6},{3,7},{4,0},{5,1},{6,2},{7,3},{8,12},{9,13},{10,... | collective-permute-start | bytes 405512 | tf_op jit(solution)/shard_map/ppermute | solution.py:380
  11.6 2.6 %collective-permute-start.4 = (bf16[528,128]{1,0:T(8,128)(2,1)}, bf16[528,128]{1,0:T(8,128)(2,1)S(1)}, u32[]{:S(2)}, u32[]{:S(2)}) collective-permute-start(bf16[528,128]{1,0:T(8,128)(2,1)} %get-tuple-element.32), channel_id=1, source_target_pairs={{0,5},{1,6},{2,7},{3,0},{4,1},{5,2},{6,3},{7,4},{8,13},{9,14},{10,... | collective-permute-start | bytes 405512 | tf_op jit(solution)/shard_map/ppermute | solution.py:380
  14.2 1.7 %collective-permute-start.5 = (bf16[528,128]{1,0:T(8,128)(2,1)}, bf16[528,128]{1,0:T(8,128)(2,1)S(1)}, u32[]{:S(2)}, u32[]{:S(2)}) collective-permute-start(bf16[528,128]{1,0:T(8,128)(2,1)} %get-tuple-element.33), channel_id=1, source_target_pairs={{0,6},{1,7},{2,0},{3,1},{4,2},{5,3},{6,4},{7,5},{8,14},{9,15},{10,... | collective-permute-start | bytes 405512 | tf_op jit(solution)/shard_map/ppermute | solution.py:380
  15.9 2.1 %collective-permute-start.6 = (bf16[528,128]{1,0:T(8,128)(2,1)}, bf16[528,128]{1,0:T(8,128)(2,1)S(1)}, u32[]{:S(2)}, u32[]{:S(2)}) collective-permute-start(bf16[528,128]{1,0:T(8,128)(2,1)} %get-tuple-element.34), channel_id=1, source_target_pairs={{0,7},{1,0},{2,1},{3,2},{4,3},{5,4},{6,5},{7,6},{8,15},{9,8},{10,9... | collective-permute-start | bytes 405512 | tf_op jit(solution)/shard_map/ppermute | solution.py:380
  18.1 2.1 %shard_map.114 = bf16[8,256,128]{2,1,0:T(8,128)(2,1)} custom-call(bf16[512,512]{1,0:T(8,128)(2,1)} %bitcast.9), custom_call_target="tpu_custom_call" | custom-call | tf_op jit(solution)/shard_map/pallas_call | solution.py:440
  20.1 0.9 %copy-done.2 = bf16[528,128]{1,0:T(8,128)(2,1)S(1)} copy-done((bf16[528,128]{1,0:T(8,128)(2,1)S(1)}, bf16[528,128]{1,0:T(8,128)(2,1)}, u32[]{:S(2)}) %copy-start.2) | copy-done | bytes 135192
  21.0 0.8 %copy-done.6 = bf16[128,192]{1,0:T(8,128)(2,1)S(1)} copy-done((bf16[128,192]{1,0:T(8,128)(2,1)S(1)}, bf16[128,192]{1,0:T(8,128)(2,1)}, u32[]{:S(2)}) %copy-start.6) | copy-done | bytes 49176
  21.9 2.9 %collective-permute-done.2.refs_3_ = bf16[528,128]{1,0:T(8,128)(2,1)S(1)} collective-permute-done((bf16[528,128]{1,0:T(8,128)(2,1)}, bf16[528,128]{1,0:T(8,128)(2,1)S(1)}, u32[]{:S(2)}, u32[]{:S(2)}) %collective-permute-start.2) | collective-permute-done | bytes 135200 | tf_op jit(solution)/shard_map/ppermute | solution.py:380
  24.8 0.4 collective-permute-done.3.refs_4_
  25.2 0.1 collective-permute-done.6.refs_7_
  25.2 12.2 %all-to-all-start = ((bf16[8,256,128]{2,1,0:T(8,128)(2,1)}), bf16[8,256,128]{2,1,0:T(8,128)(2,1)S(1)}, u32[]{:S(2)}, u32[]{:S(2)}) async-start(bf16[8,256,128]{2,1,0:T(8,128)(2,1)} %shard_map.114), calls=%async_computation | async-start | bytes 1048576 | tf_op jit(solution)/shard_map/all_to_all | solution.py:457
  37.5 0.0 copy-start
  37.5 0.0 copy-start.4
  37.5 0.0 copy-start.7
  37.5 7.0 %shard_map.111 = (f32[8192,128]{1,0:T(8,128)S(1)}, f32[8,256,128]{2,1,0:T(8,128)S(1)}) custom-call(s32[1]{0:T(128)} %bitcast.index_ref, bf16[528,128]{1,0:T(8,128)(2,1)S(1)} %get-tuple-element.27.refs_0_, bf16[528,128]{1,0:T(8,128)(2,1)S(1)} %collective-permute-done.refs_1_, bf16[528,128]{1,0:T(8,128)(2,1)S(1)} %collective-permute-done.1.refs_2_, ...), custom_call_target="tpu_custom_call" | custom-call | tf_op jit(solution)/shard_map/pallas_call | solution.py:393
  44.6 4.4 %shard_map.112.w_s = f32[4096,128]{1,0:T(8,128)S(1)} custom-call(f32[8192,128]{1,0:T(8,128)S(1)} %get-tuple-element.36.z_s, bf16[128,384]{1,0:T(8,128)(2,1)S(1)} %copy-done.3, bf16[128,192]{1,0:T(8,128)(2,1)S(1)} %copy-done.5), custom_call_target="tpu_custom_call" | custom-call | tf_op jit(solution)/shard_map/pallas_call | solution.py:400
  49.0 3.5 %shard_map.113.y_ref = f32[8,256,128]{2,1,0:T(8,128)S(1)} custom-call(s32[1]{0:T(128)} %bitcast.index_ref, f32[1,512]{1,0:T(1,128)S(1)} %copy-done.7, f32[4096,128]{1,0:T(8,128)S(1)} %shard_map.112.w_s, f32[8,256,128]{2,1,0:T(8,128)S(1)} %get-tuple-element.37.p_s, bf16[128,192]{1,0:T(8,128)(2,1)S(1)} %copy-done.4, f32[64,2,64,128]{3,2,1,0:T(8,128)S(1)} %copy-done), custom_call_target="tpu_custom_call" | custom-call | tf_op jit(solution)/shard_map/pallas_call | solution.py:405
  52.5 0.1 shard_map.115
  52.6 0.1 collective-permute-start.7
  52.7 5.9 %collective-permute-start.8 = (bf16[256,128]{1,0:T(8,128)(2,1)S(1)}, bf16[256,128]{1,0:T(8,128)(2,1)S(1)}, u32[]{:S(2)}, u32[]{:S(2)}) collective-permute-start(bf16[256,128]{1,0:T(8,128)(2,1)S(1)} %get-tuple-element.40), channel_id=1, source_target_pairs={{0,15},{1,8},{2,9},{3,10},{4,11},{5,12},{6,13},{7,14},{8,23},{9,16... | collective-permute-start | bytes 196616 | tf_op jit(solution)/shard_map/ppermute | solution.py:380
  58.6 0.1 collective-permute-start.9
  58.7 2.6 %collective-permute-start.11 = (bf16[256,128]{1,0:T(8,128)(2,1)S(1)}, bf16[256,128]{1,0:T(8,128)(2,1)S(1)}, u32[]{:S(2)}, u32[]{:S(2)}) collective-permute-start(bf16[256,128]{1,0:T(8,128)(2,1)S(1)} %get-tuple-element.43), channel_id=1, source_target_pairs={{0,12},{1,13},{2,14},{3,15},{4,8},{5,9},{6,10},{7,11},{8,20},{9,21... | collective-permute-start | bytes 196616 | tf_op jit(solution)/shard_map/ppermute | solution.py:380
  61.3 0.8 %collective-permute-start.12 = (bf16[256,128]{1,0:T(8,128)(2,1)S(1)}, bf16[256,128]{1,0:T(8,128)(2,1)S(1)}, u32[]{:S(2)}, u32[]{:S(2)}) collective-permute-start(bf16[256,128]{1,0:T(8,128)(2,1)S(1)} %get-tuple-element.44), channel_id=1, source_target_pairs={{0,11},{1,12},{2,13},{3,14},{4,15},{5,8},{6,9},{7,10},{8,19},{9,20... | collective-permute-start | bytes 196616 | tf_op jit(solution)/shard_map/ppermute | solution.py:380
  62.1 1.9 %collective-permute-start.13 = (bf16[256,128]{1,0:T(8,128)(2,1)S(1)}, bf16[256,128]{1,0:T(8,128)(2,1)S(1)}, u32[]{:S(2)}, u32[]{:S(2)}) collective-permute-start(bf16[256,128]{1,0:T(8,128)(2,1)S(1)} %get-tuple-element.45), channel_id=1, source_target_pairs={{0,10},{1,11},{2,12},{3,13},{4,14},{5,15},{6,8},{7,9},{8,18},{9,19... | collective-permute-start | bytes 196616 | tf_op jit(solution)/shard_map/ppermute | solution.py:380
  64.0 0.9 %collective-permute-start.14 = (bf16[256,128]{1,0:T(8,128)(2,1)S(1)}, bf16[256,128]{1,0:T(8,128)(2,1)S(1)}, u32[]{:S(2)}, u32[]{:S(2)}) collective-permute-start(bf16[256,128]{1,0:T(8,128)(2,1)S(1)} %get-tuple-element.46), channel_id=1, source_target_pairs={{0,9},{1,10},{2,11},{3,12},{4,13},{5,14},{6,15},{7,8},{8,17},{9,18... | collective-permute-start | bytes 196616 | tf_op jit(solution)/shard_map/ppermute | solution.py:380
  64.9 6.3 %collective-permute-done.11.refs_4_ = bf16[256,128]{1,0:T(8,128)(2,1)S(1)} collective-permute-done((bf16[256,128]{1,0:T(8,128)(2,1)S(1)}, bf16[256,128]{1,0:T(8,128)(2,1)S(1)}, u32[]{:S(2)}, u32[]{:S(2)}) %collective-permute-start.11) | collective-permute-done | bytes 65568 | tf_op jit(solution)/shard_map/ppermute | solution.py:380
  71.1 2.3 %collective-permute-done.12.refs_5_ = bf16[256,128]{1,0:T(8,128)(2,1)S(1)} collective-permute-done((bf16[256,128]{1,0:T(8,128)(2,1)S(1)}, bf16[256,128]{1,0:T(8,128)(2,1)S(1)}, u32[]{:S(2)}, u32[]{:S(2)}) %collective-permute-start.12) | collective-permute-done | bytes 65568 | tf_op jit(solution)/shard_map/ppermute | solution.py:380
  73.5 1.0 %shard_map.116 = bf16[512,512]{1,0:T(8,128)(2,1)} custom-call(s32[1]{0:T(128)} %bitcast.index_ref, bf16[256,128]{1,0:T(8,128)(2,1)S(1)} %collective-permute-done.7.refs_0_, bf16[256,128]{1,0:T(8,128)(2,1)S(1)} %collective-permute-done.8.refs_1_, bf16[256,128]{1,0:T(8,128)(2,1)S(1)} %collective-permute-done.9.refs_2_, ...), custom_call_target="tpu_custom_call" | custom-call | tf_op jit(solution)/shard_map/pallas_call | solution.py:466
  (24 shorter events, 0.1 us)
Async XLA Ops:
  0.0 37.5 %copy-start.1 = (f32[20,2,64,128]{3,2,1,0:T(8,128)S(1)}, f32[20,2,64,128]{3,2,1,0:T(8,128)}, u32[]{:S(2)}) copy-start(f32[20,2,64,128]{3,2,1,0:T(8,128)} %constant.21.clone.refs_9_) | copy-start | bytes 3932164
  0.0 44.5 %copy-start.5 = (bf16[128,192]{1,0:T(8,128)(2,1)S(1)}, bf16[128,192]{1,0:T(8,128)(2,1)}, u32[]{:S(2)}) copy-start(bf16[128,192]{1,0:T(8,128)(2,1)} %constant.18.clone.back_ref) | copy-start | bytes 147460
  0.0 44.6 %copy-start.3 = (bf16[128,384]{1,0:T(8,128)(2,1)S(1)}, bf16[128,384]{1,0:T(8,128)(2,1)}, u32[]{:S(2)}) copy-start(bf16[128,384]{1,0:T(8,128)(2,1)} %constant.17.clone.forward_ref) | copy-start | bytes 294916
  3.2 11.0 %collective-permute-start = (bf16[528,128]{1,0:T(8,128)(2,1)}, bf16[528,128]{1,0:T(8,128)(2,1)S(1)}, u32[]{:S(2)}, u32[]{:S(2)}) collective-permute-start(bf16[528,128]{1,0:T(8,128)(2,1)} %get-tuple-element.28), channel_id=1, source_target_pairs={{0,1},{1,2},{2,3},{3,4},{4,5},{5,6},{6,7},{7,0},{8,9},{9,10},{10,1... | collective-permute-start | bytes 405512 | tf_op jit(solution)/shard_map/ppermute | solution.py:380
  6.3 9.7 %collective-permute-start.1 = (bf16[528,128]{1,0:T(8,128)(2,1)}, bf16[528,128]{1,0:T(8,128)(2,1)S(1)}, u32[]{:S(2)}, u32[]{:S(2)}) collective-permute-start(bf16[528,128]{1,0:T(8,128)(2,1)} %get-tuple-element.29), channel_id=1, source_target_pairs={{0,2},{1,3},{2,4},{3,5},{4,6},{5,7},{6,0},{7,1},{8,10},{9,11},{10,... | collective-permute-start | bytes 405512 | tf_op jit(solution)/shard_map/ppermute | solution.py:380
  7.8 16.9 %collective-permute-start.2 = (bf16[528,128]{1,0:T(8,128)(2,1)}, bf16[528,128]{1,0:T(8,128)(2,1)S(1)}, u32[]{:S(2)}, u32[]{:S(2)}) collective-permute-start(bf16[528,128]{1,0:T(8,128)(2,1)} %get-tuple-element.30), channel_id=1, source_target_pairs={{0,3},{1,4},{2,5},{3,6},{4,7},{5,0},{6,1},{7,2},{8,11},{9,12},{10,... | collective-permute-start | bytes 405512 | tf_op jit(solution)/shard_map/ppermute | solution.py:380
  10.4 14.8 %collective-permute-start.3 = (bf16[528,128]{1,0:T(8,128)(2,1)}, bf16[528,128]{1,0:T(8,128)(2,1)S(1)}, u32[]{:S(2)}, u32[]{:S(2)}) collective-permute-start(bf16[528,128]{1,0:T(8,128)(2,1)} %get-tuple-element.31), channel_id=1, source_target_pairs={{0,4},{1,5},{2,6},{3,7},{4,0},{5,1},{6,2},{7,3},{8,12},{9,13},{10,... | collective-permute-start | bytes 405512 | tf_op jit(solution)/shard_map/ppermute | solution.py:380
  11.6 13.6 %collective-permute-start.4 = (bf16[528,128]{1,0:T(8,128)(2,1)}, bf16[528,128]{1,0:T(8,128)(2,1)S(1)}, u32[]{:S(2)}, u32[]{:S(2)}) collective-permute-start(bf16[528,128]{1,0:T(8,128)(2,1)} %get-tuple-element.32), channel_id=1, source_target_pairs={{0,5},{1,6},{2,7},{3,0},{4,1},{5,2},{6,3},{7,4},{8,13},{9,14},{10,... | collective-permute-start | bytes 405512 | tf_op jit(solution)/shard_map/ppermute | solution.py:380
  14.2 10.9 %collective-permute-start.5 = (bf16[528,128]{1,0:T(8,128)(2,1)}, bf16[528,128]{1,0:T(8,128)(2,1)S(1)}, u32[]{:S(2)}, u32[]{:S(2)}) collective-permute-start(bf16[528,128]{1,0:T(8,128)(2,1)} %get-tuple-element.33), channel_id=1, source_target_pairs={{0,6},{1,7},{2,0},{3,1},{4,2},{5,3},{6,4},{7,5},{8,14},{9,15},{10,... | collective-permute-start | bytes 405512 | tf_op jit(solution)/shard_map/ppermute | solution.py:380
  15.9 9.3 %collective-permute-start.6 = (bf16[528,128]{1,0:T(8,128)(2,1)}, bf16[528,128]{1,0:T(8,128)(2,1)S(1)}, u32[]{:S(2)}, u32[]{:S(2)}) collective-permute-start(bf16[528,128]{1,0:T(8,128)(2,1)} %get-tuple-element.34), channel_id=1, source_target_pairs={{0,7},{1,0},{2,1},{3,2},{4,3},{5,4},{6,5},{7,6},{8,15},{9,8},{10,9... | collective-permute-start | bytes 405512 | tf_op jit(solution)/shard_map/ppermute | solution.py:380
  20.1 0.9 %copy-start.2 = (bf16[528,128]{1,0:T(8,128)(2,1)S(1)}, bf16[528,128]{1,0:T(8,128)(2,1)}, u32[]{:S(2)}) copy-start(bf16[528,128]{1,0:T(8,128)(2,1)} %get-tuple-element.26.refs_0_) | copy-start | bytes 405508
  21.0 0.8 %copy-start.6 = (bf16[128,192]{1,0:T(8,128)(2,1)S(1)}, bf16[128,192]{1,0:T(8,128)(2,1)}, u32[]{:S(2)}) copy-start(bf16[128,192]{1,0:T(8,128)(2,1)} %constant.16.clone.refs_1_) | copy-start | bytes 147460
  25.2 27.3 %all-to-all-start = ((bf16[8,256,128]{2,1,0:T(8,128)(2,1)}), bf16[8,256,128]{2,1,0:T(8,128)(2,1)S(1)}, u32[]{:S(2)}, u32[]{:S(2)}) async-start(bf16[8,256,128]{2,1,0:T(8,128)(2,1)} %shard_map.114), calls=%async_computation | async-start | bytes 1048576 | tf_op jit(solution)/shard_map/all_to_all | solution.py:457
  37.5 11.5 %copy-start = (f32[64,2,64,128]{3,2,1,0:T(8,128)S(1)}, f32[64,2,64,128]{3,2,1,0:T(8,128)}, u32[]{:S(2)}) copy-start(f32[64,2,64,128]{3,2,1,0:T(8,128)} %constant.20.clone.refs_1_) | copy-start | bytes 12582916
  37.5 11.5 %copy-start.4 = (bf16[128,192]{1,0:T(8,128)(2,1)S(1)}, bf16[128,192]{1,0:T(8,128)(2,1)}, u32[]{:S(2)}) copy-start(bf16[128,192]{1,0:T(8,128)(2,1)} %constant.19.clone.refs_0_) | copy-start | bytes 147460
  37.5 11.5 %copy-start.7 = (f32[1,512]{1,0:T(1,128)S(1)}, f32[1,512]{1,0:T(1,128)}, u32[]{:S(2)}) copy-start(f32[1,512]{1,0:T(1,128)} %skip_ref.1) | copy-start | bytes 6148
  52.6 8.6 %collective-permute-start.7 = (bf16[256,128]{1,0:T(8,128)(2,1)S(1)}, bf16[256,128]{1,0:T(8,128)(2,1)S(1)}, u32[]{:S(2)}, u32[]{:S(2)}) collective-permute-start(bf16[256,128]{1,0:T(8,128)(2,1)S(1)} %get-tuple-element.39), channel_id=1, source_target_pairs={{0,8},{1,9},{2,10},{3,11},{4,12},{5,13},{6,14},{7,15},{8,16},{9,17... | collective-permute-start | bytes 196616 | tf_op jit(solution)/shard_map/ppermute | solution.py:380
  52.7 9.4 %collective-permute-start.8 = (bf16[256,128]{1,0:T(8,128)(2,1)S(1)}, bf16[256,128]{1,0:T(8,128)(2,1)S(1)}, u32[]{:S(2)}, u32[]{:S(2)}) collective-permute-start(bf16[256,128]{1,0:T(8,128)(2,1)S(1)} %get-tuple-element.40), channel_id=1, source_target_pairs={{0,15},{1,8},{2,9},{3,10},{4,11},{5,12},{6,13},{7,14},{8,23},{9,16... | collective-permute-start | bytes 196616 | tf_op jit(solution)/shard_map/ppermute | solution.py:380
  58.6 5.4 %collective-permute-start.9 = (bf16[256,128]{1,0:T(8,128)(2,1)S(1)}, bf16[256,128]{1,0:T(8,128)(2,1)S(1)}, u32[]{:S(2)}, u32[]{:S(2)}) collective-permute-start(bf16[256,128]{1,0:T(8,128)(2,1)S(1)} %get-tuple-element.41), channel_id=1, source_target_pairs={{0,14},{1,15},{2,8},{3,9},{4,10},{5,11},{6,12},{7,13},{8,22},{9,23... | collective-permute-start | bytes 196616 | tf_op jit(solution)/shard_map/ppermute | solution.py:380
  58.7 6.2 %collective-permute-start.10 = (bf16[256,128]{1,0:T(8,128)(2,1)S(1)}, bf16[256,128]{1,0:T(8,128)(2,1)S(1)}, u32[]{:S(2)}, u32[]{:S(2)}) collective-permute-start(bf16[256,128]{1,0:T(8,128)(2,1)S(1)} %get-tuple-element.42), channel_id=1, source_target_pairs={{0,13},{1,14},{2,15},{3,8},{4,9},{5,10},{6,11},{7,12},{8,21},{9,22... | collective-permute-start | bytes 196616 | tf_op jit(solution)/shard_map/ppermute | solution.py:380
  58.7 12.5 %collective-permute-start.11 = (bf16[256,128]{1,0:T(8,128)(2,1)S(1)}, bf16[256,128]{1,0:T(8,128)(2,1)S(1)}, u32[]{:S(2)}, u32[]{:S(2)}) collective-permute-start(bf16[256,128]{1,0:T(8,128)(2,1)S(1)} %get-tuple-element.43), channel_id=1, source_target_pairs={{0,12},{1,13},{2,14},{3,15},{4,8},{5,9},{6,10},{7,11},{8,20},{9,21... | collective-permute-start | bytes 196616 | tf_op jit(solution)/shard_map/ppermute | solution.py:380
  61.3 12.2 %collective-permute-start.12 = (bf16[256,128]{1,0:T(8,128)(2,1)S(1)}, bf16[256,128]{1,0:T(8,128)(2,1)S(1)}, u32[]{:S(2)}, u32[]{:S(2)}) collective-permute-start(bf16[256,128]{1,0:T(8,128)(2,1)S(1)} %get-tuple-element.44), channel_id=1, source_target_pairs={{0,11},{1,12},{2,13},{3,14},{4,15},{5,8},{6,9},{7,10},{8,19},{9,20... | collective-permute-start | bytes 196616 | tf_op jit(solution)/shard_map/ppermute | solution.py:380
  62.1 11.4 %collective-permute-start.13 = (bf16[256,128]{1,0:T(8,128)(2,1)S(1)}, bf16[256,128]{1,0:T(8,128)(2,1)S(1)}, u32[]{:S(2)}, u32[]{:S(2)}) collective-permute-start(bf16[256,128]{1,0:T(8,128)(2,1)S(1)} %get-tuple-element.45), channel_id=1, source_target_pairs={{0,10},{1,11},{2,12},{3,13},{4,14},{5,15},{6,8},{7,9},{8,18},{9,19... | collective-permute-start | bytes 196616 | tf_op jit(solution)/shard_map/ppermute | solution.py:380
  64.0 9.5 %collective-permute-start.14 = (bf16[256,128]{1,0:T(8,128)(2,1)S(1)}, bf16[256,128]{1,0:T(8,128)(2,1)S(1)}, u32[]{:S(2)}, u32[]{:S(2)}) collective-permute-start(bf16[256,128]{1,0:T(8,128)(2,1)S(1)} %get-tuple-element.46), channel_id=1, source_target_pairs={{0,9},{1,10},{2,11},{3,12},{4,13},{5,14},{6,15},{7,8},{8,17},{9,18... | collective-permute-start | bytes 196616 | tf_op jit(solution)/shard_map/ppermute | solution.py:380

commit v8 on v7

--- a/solution.py
+++ b/solution.py
@@ -19,6 +19,7 @@
 SCALE = 215.0
 SMALLEST = 1e-30
 LIMIT = 30
+PAD = 8
 WIDE = 16
 F32 = jnp.float32
 BF16 = jnp.bfloat16
@@ -256,8 +257,8 @@
             p_s[n, at : at + INNER, :] = p
             h = block[rows + at : rows + at + INNER, :].astype(F32)
             a = origin(n) * (2 * per) + m
-            x_s[pl.ds(a, INNER, stride=outer), :] = jnp.where(low, p, swap_halves(h))
-            x_s[pl.ds(a + per, INNER, stride=outer), :] = jnp.where(low, swap_halves(p), h)
+            x_s[pl.ds(a, INNER, stride=outer + PAD), :] = jnp.where(low, p, swap_halves(h))
+            x_s[pl.ds(a + per, INNER, stride=outer + PAD), :] = jnp.where(low, swap_halves(p), h)
 
     def turn(group, n):
         cos_1, sin_1 = turn_ref[STEP + group, 0], turn_ref[STEP + group, 1]
@@ -271,7 +272,7 @@
             b = group * STEP + n
             data = jnp.concatenate(
                 [
-                    stacked(x_s[pl.ds(pl.multiple_of((b + j) * outer, outer), outer), :])
+                    stacked(x_s[pl.ds(pl.multiple_of((b + j) * (outer + PAD), PAD), outer), :])
                     for j in range(WIDE)
                 ],
                 axis=1,
@@ -281,8 +282,8 @@
                 re = both[:outer, LANES * j : LANES * (j + 1)]
                 im = both[outer:, LANES * j : LANES * (j + 1)]
                 cos, sin = turn(group, n + j)
-                z_s[pl.ds(b + j, outer, stride=2 * INNER), :] = re * cos + im * sin
-                z_s[pl.ds(b + j + INNER, outer, stride=2 * INNER), :] = im * cos - re * sin
+                z_s[pl.ds(b + j, outer, stride=2 * INNER + PAD), :] = re * cos + im * sin
+                z_s[pl.ds(b + j + INNER, outer, stride=2 * INNER + PAD), :] = im * cos - re * sin
         return carry
 
     lax.fori_loop(0, INNER // STEP, forward_outer, 0)
@@ -296,7 +297,7 @@
             c = group * STEP + n
             data = jnp.concatenate(
                 [
-                    stacked(z_s[pl.ds(pl.multiple_of((c + j) * 2 * INNER, 2 * INNER), 2 * INNER), :])
+                    stacked(z_s[pl.ds(pl.multiple_of((c + j) * (2 * INNER + PAD), PAD), 2 * INNER), :])
                     for j in range(WIDE)
                 ],
                 axis=1,
@@ -314,7 +315,7 @@
             for j in range(WIDE):
                 straight = both[:INNER, LANES * j : LANES * (j + 1)]
                 crossed = swap_halves(both[INNER:, LANES * j : LANES * (j + 1)])
-                w_s[pl.ds(c + j, INNER, stride=outer), :] = jnp.where(
+                w_s[pl.ds(c + j, INNER, stride=outer + PAD), :] = jnp.where(
                     low, straight - crossed, straight + crossed
                 )
         return carry
@@ -338,7 +339,7 @@
             b = group * STEP + n
             data = []
             for j in range(WIDE):
-                value = w_s[pl.ds(pl.multiple_of((b + j) * outer, outer), outer), :]
+                value = w_s[pl.ds(pl.multiple_of((b + j) * (outer + PAD), PAD), outer), :]
                 cos, sin = turn(group, n + j)
                 other = swap_halves(value) * sin
                 straight = value * cos
@@ -392,14 +393,14 @@
 
     z, p = pl.pallas_call(
         functools.partial(forward_kernel, parts, outer),
-        out_shape=(block(2 * outer * INNER, LANES), block(parts, rows, LANES)),
+        out_shape=(block(outer * (2 * INNER + PAD), LANES), block(parts, rows, LANES)),
         in_specs=[scalar] + [whole] * (parts + 2),
-        scratch_shapes=[pltpu.VMEM((outer * INNER, LANES), F32)],
+        scratch_shapes=[pltpu.VMEM((INNER * (outer + PAD), LANES), F32)],
         compiler_params=pltpu.CompilerParams(vmem_limit_bytes=LIMIT * 2**20),
     )(index, *slabs, forward_a, first_turns)
     w = pl.pallas_call(
         functools.partial(middle_kernel, outer),
-        out_shape=block(outer * INNER, LANES),
+        out_shape=block(INNER * (outer + PAD), LANES),
         compiler_params=pltpu.CompilerParams(vmem_limit_bytes=LIMIT * 2**20),
     )(z, forward_b, back_b)
     return pl.pallas_call(

time: 74.9 us -> 71.2 us (0.951)
  Pallas kernels: 21.4 us -> 16.2 us
  waiting for transfers between devices: 12 us -> 15.9 us
  starting transfers between devices: 39.2 us -> 37 us
    pallas_call x1, Pallas kernels: 7.04 us -> 2.66 us  [convolved(): pl.pallas_call(functools.partial(forward_kernel, parts, outer), out_shape...]
    all_to_all x1, waiting for transfers between devices: 0.01 us -> 3.81 us  [fast_on_device(): q = lax.all_to_all(q, 'ctx', split_axis=0, concat_axis=0, tiled=True)]
    ppermute x15, starting transfers between devices: 27 us -> 24.7 us  [joint_shift(): return lax.ppermute(value, ('segment', 'ctx'), pairs)]
    pallas_call x1, Pallas kernels: 4.4 us -> 3.57 us  [convolved(): pl.pallas_call(functools.partial(middle_kernel, outer), out_shape=block(I...]
  transfers between devices with their start and end apart: 16 -> 16, of which waited for: 5 -> 6; matrix products, arithmetic and copies ran while one was open for 0% -> 0% of each run, Pallas kernels for 23% -> 17%
where the time goes in v8:
time: 71.2 us; the launch traced here: 70.9 us
  starting transfers between devices  37 us (52%)
  Pallas kernels  16.2 us (23%)
  waiting for transfers between devices  15.9 us (22%)
  local copies, waits for them, and re-layouts  1.78 us (2%)
    ppermute x15, starting transfers between devices, joint_shift(): return lax.ppermute(value, ('segment', 'ctx'), pairs)  24.7 us
    all_to_all x1, starting transfers between devices, fast_on_device(): q = lax.all_to_all(q, 'ctx', split_axis=0, concat_axis=0, tiled=True)  12.2 us
    ppermute x15, waiting for transfers between devices, joint_shift(): return lax.ppermute(value, ('segment', 'ctx'), pairs)  12.1 us
    all_to_all x1, waiting for transfers between devices, fast_on_device(): q = lax.all_to_all(q, 'ctx', split_axis=0, concat_axis=0, tiled=True)  3.81 us
    pallas_call x1, Pallas kernels, convolved(): pl.pallas_call(functools.partial(middle_kernel, outer), out_shape=block(I...  3.57 us
    pallas_call x1, Pallas kernels, convolved(): pl.pallas_call(functools.partial(back_kernel, parts, outer), out_shape=bl...  3.53 us
    pallas_call x1, Pallas kernels, fast_on_device(): pl.pallas_call(functools.partial(pack_kernel, parts), out_shape=(block(si...  3.21 us
    pallas_call x1, Pallas kernels, convolved(): pl.pallas_call(functools.partial(forward_kernel, parts, outer), out_shape...  2.66 us
  transfers between devices with their start and end apart: 16, of which 6 were waited for; matrix products, arithmetic and copies ran while one was open for 0% of the time, Pallas kernels for 17%

profile of v8, /device:TPU:0, one launch (start us, length us, event | category | flops | bytes accessed | tf_op | source)
XLA Modules:
  0.0 70.9 jit_solution(5628662019862925338)
XLA Ops:
  0.0 3.2 %shard_map.109 = (bf16[528,128]{1,0:T(8,128)(2,1)}, bf16[528,128]{1,0:T(8,128)(2,1)}, bf16[528,128]{1,0:T(8,128)(2,1)}, bf16[528,128]{1,0:T(8,128)(2,1)}, bf16[5...) custom-call(s32[1]{0:T(128)} %bitcast.index_ref, ...), custom_call_target="tpu_custom_call" | custom-call | tf_op jit(solution)/shard_map/pallas_call | solution.py:431
  3.2 3.0 %collective-permute-start = (bf16[528,128]{1,0:T(8,128)(2,1)}, bf16[528,128]{1,0:T(8,128)(2,1)S(1)}, u32[]{:S(2)}, u32[]{:S(2)}) collective-permute-start(bf16[528,128]{1,0:T(8,128)(2,1)} %get-tuple-element.28), channel_id=1, source_target_pairs={{0,1},{1,2},{2,3},{3,4},{4,5},{5,6},{6,7},{7,0},{8,9},{9,10},{10,1... | collective-permute-start | bytes 405512 | tf_op jit(solution)/shard_map/ppermute | solution.py:381
  6.3 1.6 %collective-permute-start.1 = (bf16[528,128]{1,0:T(8,128)(2,1)}, bf16[528,128]{1,0:T(8,128)(2,1)S(1)}, u32[]{:S(2)}, u32[]{:S(2)}) collective-permute-start(bf16[528,128]{1,0:T(8,128)(2,1)} %get-tuple-element.29), channel_id=1, source_target_pairs={{0,2},{1,3},{2,4},{3,5},{4,6},{5,7},{6,0},{7,1},{8,10},{9,11},{10,... | collective-permute-start | bytes 405512 | tf_op jit(solution)/shard_map/ppermute | solution.py:381
  7.8 2.5 %collective-permute-start.2 = (bf16[528,128]{1,0:T(8,128)(2,1)}, bf16[528,128]{1,0:T(8,128)(2,1)S(1)}, u32[]{:S(2)}, u32[]{:S(2)}) collective-permute-start(bf16[528,128]{1,0:T(8,128)(2,1)} %get-tuple-element.30), channel_id=1, source_target_pairs={{0,3},{1,4},{2,5},{3,6},{4,7},{5,0},{6,1},{7,2},{8,11},{9,12},{10,... | collective-permute-start | bytes 405512 | tf_op jit(solution)/shard_map/ppermute | solution.py:381
  10.4 1.2 %collective-permute-start.3 = (bf16[528,128]{1,0:T(8,128)(2,1)}, bf16[528,128]{1,0:T(8,128)(2,1)S(1)}, u32[]{:S(2)}, u32[]{:S(2)}) collective-permute-start(bf16[528,128]{1,0:T(8,128)(2,1)} %get-tuple-element.31), channel_id=1, source_target_pairs={{0,4},{1,5},{2,6},{3,7},{4,0},{5,1},{6,2},{7,3},{8,12},{9,13},{10,... | collective-permute-start | bytes 405512 | tf_op jit(solution)/shard_map/ppermute | solution.py:381
  11.6 2.6 %collective-permute-start.4 = (bf16[528,128]{1,0:T(8,128)(2,1)}, bf16[528,128]{1,0:T(8,128)(2,1)S(1)}, u32[]{:S(2)}, u32[]{:S(2)}) collective-permute-start(bf16[528,128]{1,0:T(8,128)(2,1)} %get-tuple-element.32), channel_id=1, source_target_pairs={{0,5},{1,6},{2,7},{3,0},{4,1},{5,2},{6,3},{7,4},{8,13},{9,14},{10,... | collective-permute-start | bytes 405512 | tf_op jit(solution)/shard_map/ppermute | solution.py:381
  14.2 1.7 %collective-permute-start.5 = (bf16[528,128]{1,0:T(8,128)(2,1)}, bf16[528,128]{1,0:T(8,128)(2,1)S(1)}, u32[]{:S(2)}, u32[]{:S(2)}) collective-permute-start(bf16[528,128]{1,0:T(8,128)(2,1)} %get-tuple-element.33), channel_id=1, source_target_pairs={{0,6},{1,7},{2,0},{3,1},{4,2},{5,3},{6,4},{7,5},{8,14},{9,15},{10,... | collective-permute-start | bytes 405512 | tf_op jit(solution)/shard_map/ppermute | solution.py:381
  15.9 2.1 %collective-permute-start.6 = (bf16[528,128]{1,0:T(8,128)(2,1)}, bf16[528,128]{1,0:T(8,128)(2,1)S(1)}, u32[]{:S(2)}, u32[]{:S(2)}) collective-permute-start(bf16[528,128]{1,0:T(8,128)(2,1)} %get-tuple-element.34), channel_id=1, source_target_pairs={{0,7},{1,0},{2,1},{3,2},{4,3},{5,4},{6,5},{7,6},{8,15},{9,8},{10,9... | collective-permute-start | bytes 405512 | tf_op jit(solution)/shard_map/ppermute | solution.py:381
  18.1 2.1 %shard_map.114 = bf16[8,256,128]{2,1,0:T(8,128)(2,1)} custom-call(bf16[512,512]{1,0:T(8,128)(2,1)} %bitcast.9), custom_call_target="tpu_custom_call" | custom-call | tf_op jit(solution)/shard_map/pallas_call | solution.py:441
  20.1 0.9 %copy-done.2 = bf16[528,128]{1,0:T(8,128)(2,1)S(1)} copy-done((bf16[528,128]{1,0:T(8,128)(2,1)S(1)}, bf16[528,128]{1,0:T(8,128)(2,1)}, u32[]{:S(2)}) %copy-start.2) | copy-done | bytes 135192
  21.0 0.8 %copy-done.6 = bf16[128,192]{1,0:T(8,128)(2,1)S(1)} copy-done((bf16[128,192]{1,0:T(8,128)(2,1)S(1)}, bf16[128,192]{1,0:T(8,128)(2,1)}, u32[]{:S(2)}) %copy-start.6) | copy-done | bytes 49176
  21.9 2.9 %collective-permute-done.2.refs_3_ = bf16[528,128]{1,0:T(8,128)(2,1)S(1)} collective-permute-done((bf16[528,128]{1,0:T(8,128)(2,1)}, bf16[528,128]{1,0:T(8,128)(2,1)S(1)}, u32[]{:S(2)}, u32[]{:S(2)}) %collective-permute-start.2) | collective-permute-done | bytes 135200 | tf_op jit(solution)/shard_map/ppermute | solution.py:381
  24.8 0.4 collective-permute-done.3.refs_4_
  25.2 0.1 collective-permute-done.6.refs_7_
  25.2 12.2 %all-to-all-start = ((bf16[8,256,128]{2,1,0:T(8,128)(2,1)}), bf16[8,256,128]{2,1,0:T(8,128)(2,1)S(1)}, u32[]{:S(2)}, u32[]{:S(2)}) async-start(bf16[8,256,128]{2,1,0:T(8,128)(2,1)} %shard_map.114), calls=%async_computation | async-start | bytes 1048576 | tf_op jit(solution)/shard_map/all_to_all | solution.py:458
  37.5 0.0 copy-start
  37.5 0.0 copy-start.4
  37.5 2.7 %shard_map.111 = (f32[8704,128]{1,0:T(8,128)S(1)}, f32[8,256,128]{2,1,0:T(8,128)S(1)}) custom-call(s32[1]{0:T(128)} %bitcast.index_ref, bf16[528,128]{1,0:T(8,128)(2,1)S(1)} %get-tuple-element.27.refs_0_, bf16[528,128]{1,0:T(8,128)(2,1)S(1)} %collective-permute-done.refs_1_, bf16[528,128]{1,0:T(8,128)(2,1)S(1)} %collective-permute-done.1.refs_2_, ...), custom_call_target="tpu_custom_call" | custom-call | tf_op jit(solution)/shard_map/pallas_call | solution.py:394
  40.2 3.6 %shard_map.112.w_s = f32[4608,128]{1,0:T(8,128)S(1)} custom-call(f32[8704,128]{1,0:T(8,128)S(1)} %get-tuple-element.36.z_s, bf16[128,384]{1,0:T(8,128)(2,1)S(1)} %copy-done.3, bf16[128,192]{1,0:T(8,128)(2,1)S(1)} %copy-done.5), custom_call_target="tpu_custom_call" | custom-call | tf_op jit(solution)/shard_map/pallas_call | solution.py:401
  43.8 3.5 %shard_map.113.y_ref = f32[8,256,128]{2,1,0:T(8,128)S(1)} custom-call(s32[1]{0:T(128)} %bitcast.index_ref, f32[1,512]{1,0:T(1,128)S(1)} %copy-done.7, f32[4608,128]{1,0:T(8,128)S(1)} %shard_map.112.w_s, f32[8,256,128]{2,1,0:T(8,128)S(1)} %get-tuple-element.37.p_s, bf16[128,192]{1,0:T(8,128)(2,1)S(1)} %copy-done.4, f32[64,2,64,128]{3,2,1,0:T(8,128)S(1)} %copy-done), custom_call_target="tpu_custom_call" | custom-call | tf_op jit(solution)/shard_map/pallas_call | solution.py:406
  47.3 3.8 %all-to-all-done.q_ref = bf16[8,256,128]{2,1,0:T(8,128)(2,1)S(1)} async-done(((bf16[8,256,128]{2,1,0:T(8,128)(2,1)}), bf16[8,256,128]{2,1,0:T(8,128)(2,1)S(1)}, u32[]{:S(2)}, u32[]{:S(2)}) %all-to-all-start) | async-done | bytes 524320 | tf_op jit(solution)/shard_map/all_to_all | solution.py:458
  51.1 0.1 shard_map.115
  51.2 0.1 collective-permute-start.7
  51.3 3.6 %collective-permute-start.8 = (bf16[256,128]{1,0:T(8,128)(2,1)S(1)}, bf16[256,128]{1,0:T(8,128)(2,1)S(1)}, u32[]{:S(2)}, u32[]{:S(2)}) collective-permute-start(bf16[256,128]{1,0:T(8,128)(2,1)S(1)} %get-tuple-element.40), channel_id=1, source_target_pairs={{0,15},{1,8},{2,9},{3,10},{4,11},{5,12},{6,13},{7,14},{8,23},{9,16... | collective-permute-start | bytes 196616 | tf_op jit(solution)/shard_map/ppermute | solution.py:381
  54.9 1.0 %collective-permute-start.10 = (bf16[256,128]{1,0:T(8,128)(2,1)S(1)}, bf16[256,128]{1,0:T(8,128)(2,1)S(1)}, u32[]{:S(2)}, u32[]{:S(2)}) collective-permute-start(bf16[256,128]{1,0:T(8,128)(2,1)S(1)} %get-tuple-element.42), channel_id=1, source_target_pairs={{0,13},{1,14},{2,15},{3,8},{4,9},{5,10},{6,11},{7,12},{8,21},{9,22... | collective-permute-start | bytes 196616 | tf_op jit(solution)/shard_map/ppermute | solution.py:381
  55.8 1.6 %collective-permute-start.11 = (bf16[256,128]{1,0:T(8,128)(2,1)S(1)}, bf16[256,128]{1,0:T(8,128)(2,1)S(1)}, u32[]{:S(2)}, u32[]{:S(2)}) collective-permute-start(bf16[256,128]{1,0:T(8,128)(2,1)S(1)} %get-tuple-element.43), channel_id=1, source_target_pairs={{0,12},{1,13},{2,14},{3,15},{4,8},{5,9},{6,10},{7,11},{8,20},{9,21... | collective-permute-start | bytes 196616 | tf_op jit(solution)/shard_map/ppermute | solution.py:381
  57.5 2.6 %collective-permute-start.12 = (bf16[256,128]{1,0:T(8,128)(2,1)S(1)}, bf16[256,128]{1,0:T(8,128)(2,1)S(1)}, u32[]{:S(2)}, u32[]{:S(2)}) collective-permute-start(bf16[256,128]{1,0:T(8,128)(2,1)S(1)} %get-tuple-element.44), channel_id=1, source_target_pairs={{0,11},{1,12},{2,13},{3,14},{4,15},{5,8},{6,9},{7,10},{8,19},{9,20... | collective-permute-start | bytes 196616 | tf_op jit(solution)/shard_map/ppermute | solution.py:381
  60.1 0.0 collective-permute-start.13
  60.2 1.0 %collective-permute-start.14 = (bf16[256,128]{1,0:T(8,128)(2,1)S(1)}, bf16[256,128]{1,0:T(8,128)(2,1)S(1)}, u32[]{:S(2)}, u32[]{:S(2)}) collective-permute-start(bf16[256,128]{1,0:T(8,128)(2,1)S(1)} %get-tuple-element.46), channel_id=1, source_target_pairs={{0,9},{1,10},{2,11},{3,12},{4,13},{5,14},{6,15},{7,8},{8,17},{9,18... | collective-permute-start | bytes 196616 | tf_op jit(solution)/shard_map/ppermute | solution.py:381
  61.2 6.7 %collective-permute-done.11.refs_4_ = bf16[256,128]{1,0:T(8,128)(2,1)S(1)} collective-permute-done((bf16[256,128]{1,0:T(8,128)(2,1)S(1)}, bf16[256,128]{1,0:T(8,128)(2,1)S(1)}, u32[]{:S(2)}, u32[]{:S(2)}) %collective-permute-start.11) | collective-permute-done | bytes 65568 | tf_op jit(solution)/shard_map/ppermute | solution.py:381
  67.9 1.9 %collective-permute-done.12.refs_5_ = bf16[256,128]{1,0:T(8,128)(2,1)S(1)} collective-permute-done((bf16[256,128]{1,0:T(8,128)(2,1)S(1)}, bf16[256,128]{1,0:T(8,128)(2,1)S(1)}, u32[]{:S(2)}, u32[]{:S(2)}) %collective-permute-start.12) | collective-permute-done | bytes 65568 | tf_op jit(solution)/shard_map/ppermute | solution.py:381
  69.9 1.0 %shard_map.116 = bf16[512,512]{1,0:T(8,128)(2,1)} custom-call(s32[1]{0:T(128)} %bitcast.index_ref, bf16[256,128]{1,0:T(8,128)(2,1)S(1)} %collective-permute-done.7.refs_0_, bf16[256,128]{1,0:T(8,128)(2,1)S(1)} %collective-permute-done.8.refs_1_, bf16[256,128]{1,0:T(8,128)(2,1)S(1)} %collective-permute-done.9.refs_2_, ...), custom_call_target="tpu_custom_call" | custom-call | tf_op jit(solution)/shard_map/pallas_call | solution.py:467
  (24 shorter events, 0.1 us)
Async XLA Ops:
  0.0 37.5 %copy-start.1 = (f32[20,2,64,128]{3,2,1,0:T(8,128)S(1)}, f32[20,2,64,128]{3,2,1,0:T(8,128)}, u32[]{:S(2)}) copy-start(f32[20,2,64,128]{3,2,1,0:T(8,128)} %constant.21.clone.refs_9_) | copy-start | bytes 3932164
  0.0 40.2 %copy-start.5 = (bf16[128,192]{1,0:T(8,128)(2,1)S(1)}, bf16[128,192]{1,0:T(8,128)(2,1)}, u32[]{:S(2)}) copy-start(bf16[128,192]{1,0:T(8,128)(2,1)} %constant.18.clone.back_ref) | copy-start | bytes 147460
  0.0 40.2 %copy-start.3 = (bf16[128,384]{1,0:T(8,128)(2,1)S(1)}, bf16[128,384]{1,0:T(8,128)(2,1)}, u32[]{:S(2)}) copy-start(bf16[128,384]{1,0:T(8,128)(2,1)} %constant.17.clone.forward_ref) | copy-start | bytes 294916
  3.2 11.0 %collective-permute-start = (bf16[528,128]{1,0:T(8,128)(2,1)}, bf16[528,128]{1,0:T(8,128)(2,1)S(1)}, u32[]{:S(2)}, u32[]{:S(2)}) collective-permute-start(bf16[528,128]{1,0:T(8,128)(2,1)} %get-tuple-element.28), channel_id=1, source_target_pairs={{0,1},{1,2},{2,3},{3,4},{4,5},{5,6},{6,7},{7,0},{8,9},{9,10},{10,1... | collective-permute-start | bytes 405512 | tf_op jit(solution)/shard_map/ppermute | solution.py:381
  6.3 9.7 %collective-permute-start.1 = (bf16[528,128]{1,0:T(8,128)(2,1)}, bf16[528,128]{1,0:T(8,128)(2,1)S(1)}, u32[]{:S(2)}, u32[]{:S(2)}) collective-permute-start(bf16[528,128]{1,0:T(8,128)(2,1)} %get-tuple-element.29), channel_id=1, source_target_pairs={{0,2},{1,3},{2,4},{3,5},{4,6},{5,7},{6,0},{7,1},{8,10},{9,11},{10,... | collective-permute-start | bytes 405512 | tf_op jit(solution)/shard_map/ppermute | solution.py:381
  7.8 16.9 %collective-permute-start.2 = (bf16[528,128]{1,0:T(8,128)(2,1)}, bf16[528,128]{1,0:T(8,128)(2,1)S(1)}, u32[]{:S(2)}, u32[]{:S(2)}) collective-permute-start(bf16[528,128]{1,0:T(8,128)(2,1)} %get-tuple-element.30), channel_id=1, source_target_pairs={{0,3},{1,4},{2,5},{3,6},{4,7},{5,0},{6,1},{7,2},{8,11},{9,12},{10,... | collective-permute-start | bytes 405512 | tf_op jit(solution)/shard_map/ppermute | solution.py:381
  10.4 14.8 %collective-permute-start.3 = (bf16[528,128]{1,0:T(8,128)(2,1)}, bf16[528,128]{1,0:T(8,128)(2,1)S(1)}, u32[]{:S(2)}, u32[]{:S(2)}) collective-permute-start(bf16[528,128]{1,0:T(8,128)(2,1)} %get-tuple-element.31), channel_id=1, source_target_pairs={{0,4},{1,5},{2,6},{3,7},{4,0},{5,1},{6,2},{7,3},{8,12},{9,13},{10,... | collective-permute-start | bytes 405512 | tf_op jit(solution)/shard_map/ppermute | solution.py:381
  11.6 13.6 %collective-permute-start.4 = (bf16[528,128]{1,0:T(8,128)(2,1)}, bf16[528,128]{1,0:T(8,128)(2,1)S(1)}, u32[]{:S(2)}, u32[]{:S(2)}) collective-permute-start(bf16[528,128]{1,0:T(8,128)(2,1)} %get-tuple-element.32), channel_id=1, source_target_pairs={{0,5},{1,6},{2,7},{3,0},{4,1},{5,2},{6,3},{7,4},{8,13},{9,14},{10,... | collective-permute-start | bytes 405512 | tf_op jit(solution)/shard_map/ppermute | solution.py:381
  14.2 10.9 %collective-permute-start.5 = (bf16[528,128]{1,0:T(8,128)(2,1)}, bf16[528,128]{1,0:T(8,128)(2,1)S(1)}, u32[]{:S(2)}, u32[]{:S(2)}) collective-permute-start(bf16[528,128]{1,0:T(8,128)(2,1)} %get-tuple-element.33), channel_id=1, source_target_pairs={{0,6},{1,7},{2,0},{3,1},{4,2},{5,3},{6,4},{7,5},{8,14},{9,15},{10,... | collective-permute-start | bytes 405512 | tf_op jit(solution)/shard_map/ppermute | solution.py:381
  15.9 9.3 %collective-permute-start.6 = (bf16[528,128]{1,0:T(8,128)(2,1)}, bf16[528,128]{1,0:T(8,128)(2,1)S(1)}, u32[]{:S(2)}, u32[]{:S(2)}) collective-permute-start(bf16[528,128]{1,0:T(8,128)(2,1)} %get-tuple-element.34), channel_id=1, source_target_pairs={{0,7},{1,0},{2,1},{3,2},{4,3},{5,4},{6,5},{7,6},{8,15},{9,8},{10,9... | collective-permute-start | bytes 405512 | tf_op jit(solution)/shard_map/ppermute | solution.py:381
  20.1 0.9 %copy-start.2 = (bf16[528,128]{1,0:T(8,128)(2,1)S(1)}, bf16[528,128]{1,0:T(8,128)(2,1)}, u32[]{:S(2)}) copy-start(bf16[528,128]{1,0:T(8,128)(2,1)} %get-tuple-element.26.refs_0_) | copy-start | bytes 405508
  21.0 0.8 %copy-start.6 = (bf16[128,192]{1,0:T(8,128)(2,1)S(1)}, bf16[128,192]{1,0:T(8,128)(2,1)}, u32[]{:S(2)}) copy-start(bf16[128,192]{1,0:T(8,128)(2,1)} %constant.16.clone.refs_1_) | copy-start | bytes 147460
  25.2 25.9 %all-to-all-start = ((bf16[8,256,128]{2,1,0:T(8,128)(2,1)}), bf16[8,256,128]{2,1,0:T(8,128)(2,1)S(1)}, u32[]{:S(2)}, u32[]{:S(2)}) async-start(bf16[8,256,128]{2,1,0:T(8,128)(2,1)} %shard_map.114), calls=%async_computation | async-start | bytes 1048576 | tf_op jit(solution)/shard_map/all_to_all | solution.py:458
  37.5 6.3 %copy-start = (f32[64,2,64,128]{3,2,1,0:T(8,128)S(1)}, f32[64,2,64,128]{3,2,1,0:T(8,128)}, u32[]{:S(2)}) copy-start(f32[64,2,64,128]{3,2,1,0:T(8,128)} %constant.20.clone.refs_1_) | copy-start | bytes 12582916
  37.5 6.3 %copy-start.4 = (bf16[128,192]{1,0:T(8,128)(2,1)S(1)}, bf16[128,192]{1,0:T(8,128)(2,1)}, u32[]{:S(2)}) copy-start(bf16[128,192]{1,0:T(8,128)(2,1)} %constant.19.clone.refs_0_) | copy-start | bytes 147460
  37.5 6.3 %copy-start.7 = (f32[1,512]{1,0:T(1,128)S(1)}, f32[1,512]{1,0:T(1,128)}, u32[]{:S(2)}) copy-start(f32[1,512]{1,0:T(1,128)} %skip_ref.1) | copy-start | bytes 6148
  51.2 6.2 %collective-permute-start.7 = (bf16[256,128]{1,0:T(8,128)(2,1)S(1)}, bf16[256,128]{1,0:T(8,128)(2,1)S(1)}, u32[]{:S(2)}, u32[]{:S(2)}) collective-permute-start(bf16[256,128]{1,0:T(8,128)(2,1)S(1)} %get-tuple-element.39), channel_id=1, source_target_pairs={{0,8},{1,9},{2,10},{3,11},{4,12},{5,13},{6,14},{7,15},{8,16},{9,17... | collective-permute-start | bytes 196616 | tf_op jit(solution)/shard_map/ppermute | solution.py:381
  51.3 8.8 %collective-permute-start.8 = (bf16[256,128]{1,0:T(8,128)(2,1)S(1)}, bf16[256,128]{1,0:T(8,128)(2,1)S(1)}, u32[]{:S(2)}, u32[]{:S(2)}) collective-permute-start(bf16[256,128]{1,0:T(8,128)(2,1)S(1)} %get-tuple-element.40), channel_id=1, source_target_pairs={{0,15},{1,8},{2,9},{3,10},{4,11},{5,12},{6,13},{7,14},{8,23},{9,16... | collective-permute-start | bytes 196616 | tf_op jit(solution)/shard_map/ppermute | solution.py:381
  54.9 5.3 %collective-permute-start.9 = (bf16[256,128]{1,0:T(8,128)(2,1)S(1)}, bf16[256,128]{1,0:T(8,128)(2,1)S(1)}, u32[]{:S(2)}, u32[]{:S(2)}) collective-permute-start(bf16[256,128]{1,0:T(8,128)(2,1)S(1)} %get-tuple-element.41), channel_id=1, source_target_pairs={{0,14},{1,15},{2,8},{3,9},{4,10},{5,11},{6,12},{7,13},{8,22},{9,23... | collective-permute-start | bytes 196616 | tf_op jit(solution)/shard_map/ppermute | solution.py:381
  54.9 6.3 %collective-permute-start.10 = (bf16[256,128]{1,0:T(8,128)(2,1)S(1)}, bf16[256,128]{1,0:T(8,128)(2,1)S(1)}, u32[]{:S(2)}, u32[]{:S(2)}) collective-permute-start(bf16[256,128]{1,0:T(8,128)(2,1)S(1)} %get-tuple-element.42), channel_id=1, source_target_pairs={{0,13},{1,14},{2,15},{3,8},{4,9},{5,10},{6,11},{7,12},{8,21},{9,22... | collective-permute-start | bytes 196616 | tf_op jit(solution)/shard_map/ppermute | solution.py:381
  55.8 12.1 %collective-permute-start.11 = (bf16[256,128]{1,0:T(8,128)(2,1)S(1)}, bf16[256,128]{1,0:T(8,128)(2,1)S(1)}, u32[]{:S(2)}, u32[]{:S(2)}) collective-permute-start(bf16[256,128]{1,0:T(8,128)(2,1)S(1)} %get-tuple-element.43), channel_id=1, source_target_pairs={{0,12},{1,13},{2,14},{3,15},{4,8},{5,9},{6,10},{7,11},{8,20},{9,21... | collective-permute-start | bytes 196616 | tf_op jit(solution)/shard_map/ppermute | solution.py:381
  57.5 12.4 %collective-permute-start.12 = (bf16[256,128]{1,0:T(8,128)(2,1)S(1)}, bf16[256,128]{1,0:T(8,128)(2,1)S(1)}, u32[]{:S(2)}, u32[]{:S(2)}) collective-permute-start(bf16[256,128]{1,0:T(8,128)(2,1)S(1)} %get-tuple-element.44), channel_id=1, source_target_pairs={{0,11},{1,12},{2,13},{3,14},{4,15},{5,8},{6,9},{7,10},{8,19},{9,20... | collective-permute-start | bytes 196616 | tf_op jit(solution)/shard_map/ppermute | solution.py:381
  60.1 9.8 %collective-permute-start.13 = (bf16[256,128]{1,0:T(8,128)(2,1)S(1)}, bf16[256,128]{1,0:T(8,128)(2,1)S(1)}, u32[]{:S(2)}, u32[]{:S(2)}) collective-permute-start(bf16[256,128]{1,0:T(8,128)(2,1)S(1)} %get-tuple-element.45), channel_id=1, source_target_pairs={{0,10},{1,11},{2,12},{3,13},{4,14},{5,15},{6,8},{7,9},{8,18},{9,19... | collective-permute-start | bytes 196616 | tf_op jit(solution)/shard_map/ppermute | solution.py:381
  60.2 9.7 %collective-permute-start.14 = (bf16[256,128]{1,0:T(8,128)(2,1)S(1)}, bf16[256,128]{1,0:T(8,128)(2,1)S(1)}, u32[]{:S(2)}, u32[]{:S(2)}) collective-permute-start(bf16[256,128]{1,0:T(8,128)(2,1)S(1)} %get-tuple-element.46), channel_id=1, source_target_pairs={{0,9},{1,10},{2,11},{3,12},{4,13},{5,14},{6,15},{7,8},{8,17},{9,18... | collective-permute-start | bytes 196616 | tf_op jit(solution)/shard_map/ppermute | solution.py:381

commit v9 on v8

--- a/solution.py
+++ b/solution.py
@@ -180,12 +180,14 @@
 
 
 def pack_kernel(parts, index_ref, *refs):
-    sources, outs, held, arrived, sems = refs[:3], refs[3 : 3 + parts], refs[-5], refs[-4:-1], refs[-1]
+    sources, outs, held, arrived, sems = refs[:3], refs[3 : 3 + parts], refs[-6], refs[-5:-2], refs[-2]
+    out_sems = refs[-1]
     k_ref, v_ref, h_ref = arrived
     rows = k_ref.shape[0] // 2
     low = lower_half((rows, LANES))
-    for copy in fetched(sources, arrived, sems):
-        copy.wait()
+    k_copy, v_copy, h_copy = fetched(sources, arrived, sems)
+    k_copy.wait()
+    v_copy.wait()
 
     def place(e, at, tile, low):
         half = tile.shape[0] // 2
@@ -203,10 +205,13 @@
         for _ in range(DOUBLINGS - 1):
             power = power * power
         place(e, 0, jnp.where(code < 0.0, -power, power), low)
-        place(e, rows, h_ref[:, lanes].astype(F32), low)
         place(e, 2 * rows, jnp.broadcast_to(largest, (2 * EXTRA, LANES)), low[:EXTRA])
-    for n, out in enumerate(outs):
-        out[...] = held[lax.rem(index_ref[0] + n, parts)]
+    h_copy.wait()
+    for e in range(parts // 2):
+        place(e, rows, h_ref[:, LANES * e : LANES * (e + 1)].astype(F32), low)
+    ready = [held.at[lax.rem(index_ref[0] + n, parts)] for n in range(parts)]
+    for copy in fetched(ready, outs, out_sems):
+        copy.wait()
 
 
 def pack_gate_kernel(parts, q_ref, out_ref):
@@ -432,9 +437,10 @@
         functools.partial(pack_kernel, parts),
         out_shape=(block(size, LANES),) * parts,
         in_specs=[scalar] + [far] * 3,
+        out_specs=(far,) * parts,
         scratch_shapes=[pltpu.VMEM((parts, size, LANES), BF16)]
         + [pltpu.VMEM((length, channels), BF16)] * 3
-        + [pltpu.SemaphoreType.DMA((3,))],
+        + [pltpu.SemaphoreType.DMA((3,)), pltpu.SemaphoreType.DMA((parts,))],
         compiler_params=large,
     )(index, key_stream[0], value_stream[0], filter_taps[0])
     slabs = [sent[0]] + [joint_shift(sent[n], 0, n) for n in range(1, parts)]

time: 71.2 us -> 71.2 us (level)
  no operation moved by 1% of the time
where the time goes in v9:
time: 71.2 us; the launch traced here: 70.9 us
  starting transfers between devices  37 us (52%)
  Pallas kernels  16.2 us (23%)
  waiting for transfers between devices  15.8 us (22%)
  local copies, waits for them, and re-layouts  1.78 us (2%)
    ppermute x15, starting transfers between devices, joint_shift(): return lax.ppermute(value, ('segment', 'ctx'), pairs)  24.7 us
    all_to_all x1, starting transfers between devices, fast_on_device(): q = lax.all_to_all(q, 'ctx', split_axis=0, concat_axis=0, tiled=True)  12.2 us
    ppermute x15, waiting for transfers between devices, joint_shift(): return lax.ppermute(value, ('segment', 'ctx'), pairs)  12.1 us
    all_to_all x1, waiting for transfers between devices, fast_on_device(): q = lax.all_to_all(q, 'ctx', split_axis=0, concat_axis=0, tiled=True)  3.77 us
    pallas_call x1, Pallas kernels, convolved(): pl.pallas_call(functools.partial(middle_kernel, outer), out_shape=block(I...  3.57 us
    pallas_call x1, Pallas kernels, convolved(): pl.pallas_call(functools.partial(back_kernel, parts, outer), out_shape=bl...  3.53 us
    pallas_call x1, Pallas kernels, fast_on_device(): pl.pallas_call(functools.partial(pack_kernel, parts), out_shape=(block(si...  3.18 us
    pallas_call x1, Pallas kernels, convolved(): pl.pallas_call(functools.partial(forward_kernel, parts, outer), out_shape...  2.69 us
  transfers between devices with their start and end apart: 16, of which 6 were waited for; matrix products, arithmetic and copies ran while one was open for 0% of the time, Pallas kernels for 17%

profile of v9, /device:TPU:0, one launch (start us, length us, event | category | flops | bytes accessed | tf_op | source)
XLA Modules:
  0.0 70.9 jit_solution(17265446018537660582)
XLA Ops:
  0.0 3.2 %shard_map.109 = (bf16[528,128]{1,0:T(8,128)(2,1)}, bf16[528,128]{1,0:T(8,128)(2,1)}, bf16[528,128]{1,0:T(8,128)(2,1)}, bf16[528,128]{1,0:T(8,128)(2,1)}, bf16[5...) custom-call(s32[1]{0:T(128)} %bitcast.index_ref, ...), custom_call_target="tpu_custom_call" | custom-call | tf_op jit(solution)/shard_map/pallas_call | solution.py:436
  3.2 3.0 %collective-permute-start = (bf16[528,128]{1,0:T(8,128)(2,1)}, bf16[528,128]{1,0:T(8,128)(2,1)S(1)}, u32[]{:S(2)}, u32[]{:S(2)}) collective-permute-start(bf16[528,128]{1,0:T(8,128)(2,1)} %get-tuple-element.28), channel_id=1, source_target_pairs={{0,1},{1,2},{2,3},{3,4},{4,5},{5,6},{6,7},{7,0},{8,9},{9,10},{10,1... | collective-permute-start | bytes 405512 | tf_op jit(solution)/shard_map/ppermute | solution.py:386
  6.2 1.6 %collective-permute-start.1 = (bf16[528,128]{1,0:T(8,128)(2,1)}, bf16[528,128]{1,0:T(8,128)(2,1)S(1)}, u32[]{:S(2)}, u32[]{:S(2)}) collective-permute-start(bf16[528,128]{1,0:T(8,128)(2,1)} %get-tuple-element.29), channel_id=1, source_target_pairs={{0,2},{1,3},{2,4},{3,5},{4,6},{5,7},{6,0},{7,1},{8,10},{9,11},{10,... | collective-permute-start | bytes 405512 | tf_op jit(solution)/shard_map/ppermute | solution.py:386
  7.8 2.5 %collective-permute-start.2 = (bf16[528,128]{1,0:T(8,128)(2,1)}, bf16[528,128]{1,0:T(8,128)(2,1)S(1)}, u32[]{:S(2)}, u32[]{:S(2)}) collective-permute-start(bf16[528,128]{1,0:T(8,128)(2,1)} %get-tuple-element.30), channel_id=1, source_target_pairs={{0,3},{1,4},{2,5},{3,6},{4,7},{5,0},{6,1},{7,2},{8,11},{9,12},{10,... | collective-permute-start | bytes 405512 | tf_op jit(solution)/shard_map/ppermute | solution.py:386
  10.3 1.2 %collective-permute-start.3 = (bf16[528,128]{1,0:T(8,128)(2,1)}, bf16[528,128]{1,0:T(8,128)(2,1)S(1)}, u32[]{:S(2)}, u32[]{:S(2)}) collective-permute-start(bf16[528,128]{1,0:T(8,128)(2,1)} %get-tuple-element.31), channel_id=1, source_target_pairs={{0,4},{1,5},{2,6},{3,7},{4,0},{5,1},{6,2},{7,3},{8,12},{9,13},{10,... | collective-permute-start | bytes 405512 | tf_op jit(solution)/shard_map/ppermute | solution.py:386
  11.6 2.6 %collective-permute-start.4 = (bf16[528,128]{1,0:T(8,128)(2,1)}, bf16[528,128]{1,0:T(8,128)(2,1)S(1)}, u32[]{:S(2)}, u32[]{:S(2)}) collective-permute-start(bf16[528,128]{1,0:T(8,128)(2,1)} %get-tuple-element.32), channel_id=1, source_target_pairs={{0,5},{1,6},{2,7},{3,0},{4,1},{5,2},{6,3},{7,4},{8,13},{9,14},{10,... | collective-permute-start | bytes 405512 | tf_op jit(solution)/shard_map/ppermute | solution.py:386
  14.2 1.7 %collective-permute-start.5 = (bf16[528,128]{1,0:T(8,128)(2,1)}, bf16[528,128]{1,0:T(8,128)(2,1)S(1)}, u32[]{:S(2)}, u32[]{:S(2)}) collective-permute-start(bf16[528,128]{1,0:T(8,128)(2,1)} %get-tuple-element.33), channel_id=1, source_target_pairs={{0,6},{1,7},{2,0},{3,1},{4,2},{5,3},{6,4},{7,5},{8,14},{9,15},{10,... | collective-permute-start | bytes 405512 | tf_op jit(solution)/shard_map/ppermute | solution.py:386
  15.9 2.1 %collective-permute-start.6 = (bf16[528,128]{1,0:T(8,128)(2,1)}, bf16[528,128]{1,0:T(8,128)(2,1)S(1)}, u32[]{:S(2)}, u32[]{:S(2)}) collective-permute-start(bf16[528,128]{1,0:T(8,128)(2,1)} %get-tuple-element.34), channel_id=1, source_target_pairs={{0,7},{1,0},{2,1},{3,2},{4,3},{5,4},{6,5},{7,6},{8,15},{9,8},{10,9... | collective-permute-start | bytes 405512 | tf_op jit(solution)/shard_map/ppermute | solution.py:386
  18.0 2.1 %shard_map.114 = bf16[8,256,128]{2,1,0:T(8,128)(2,1)} custom-call(bf16[512,512]{1,0:T(8,128)(2,1)} %bitcast.9), custom_call_target="tpu_custom_call" | custom-call | tf_op jit(solution)/shard_map/pallas_call | solution.py:447
  20.1 0.9 %copy-done.2 = bf16[528,128]{1,0:T(8,128)(2,1)S(1)} copy-done((bf16[528,128]{1,0:T(8,128)(2,1)S(1)}, bf16[528,128]{1,0:T(8,128)(2,1)}, u32[]{:S(2)}) %copy-start.2) | copy-done | bytes 135192
  21.0 0.8 %copy-done.6 = bf16[128,192]{1,0:T(8,128)(2,1)S(1)} copy-done((bf16[128,192]{1,0:T(8,128)(2,1)S(1)}, bf16[128,192]{1,0:T(8,128)(2,1)}, u32[]{:S(2)}) %copy-start.6) | copy-done | bytes 49176
  21.8 2.9 %collective-permute-done.2.refs_3_ = bf16[528,128]{1,0:T(8,128)(2,1)S(1)} collective-permute-done((bf16[528,128]{1,0:T(8,128)(2,1)}, bf16[528,128]{1,0:T(8,128)(2,1)S(1)}, u32[]{:S(2)}, u32[]{:S(2)}) %collective-permute-start.2) | collective-permute-done | bytes 135200 | tf_op jit(solution)/shard_map/ppermute | solution.py:386
  24.7 0.4 collective-permute-done.3.refs_4_
  25.1 0.1 collective-permute-done.6.refs_7_
  25.2 12.2 %all-to-all-start = ((bf16[8,256,128]{2,1,0:T(8,128)(2,1)}), bf16[8,256,128]{2,1,0:T(8,128)(2,1)S(1)}, u32[]{:S(2)}, u32[]{:S(2)}) async-start(bf16[8,256,128]{2,1,0:T(8,128)(2,1)} %shard_map.114), calls=%async_computation | async-start | bytes 1048576 | tf_op jit(solution)/shard_map/all_to_all | solution.py:464
  37.4 0.0 copy-start
  37.4 0.0 copy-start.4
  37.5 2.7 %shard_map.111 = (f32[8704,128]{1,0:T(8,128)S(1)}, f32[8,256,128]{2,1,0:T(8,128)S(1)}) custom-call(s32[1]{0:T(128)} %bitcast.index_ref, bf16[528,128]{1,0:T(8,128)(2,1)S(1)} %get-tuple-element.27.refs_0_, bf16[528,128]{1,0:T(8,128)(2,1)S(1)} %collective-permute-done.refs_1_, bf16[528,128]{1,0:T(8,128)(2,1)S(1)} %collective-permute-done.1.refs_2_, ...), custom_call_target="tpu_custom_call" | custom-call | tf_op jit(solution)/shard_map/pallas_call | solution.py:399
  40.2 3.6 %shard_map.112.w_s = f32[4608,128]{1,0:T(8,128)S(1)} custom-call(f32[8704,128]{1,0:T(8,128)S(1)} %get-tuple-element.36.z_s, bf16[128,384]{1,0:T(8,128)(2,1)S(1)} %copy-done.3, bf16[128,192]{1,0:T(8,128)(2,1)S(1)} %copy-done.5), custom_call_target="tpu_custom_call" | custom-call | tf_op jit(solution)/shard_map/pallas_call | solution.py:406
  43.8 3.5 %shard_map.113.y_ref = f32[8,256,128]{2,1,0:T(8,128)S(1)} custom-call(s32[1]{0:T(128)} %bitcast.index_ref, f32[1,512]{1,0:T(1,128)S(1)} %copy-done.7, f32[4608,128]{1,0:T(8,128)S(1)} %shard_map.112.w_s, f32[8,256,128]{2,1,0:T(8,128)S(1)} %get-tuple-element.37.p_s, bf16[128,192]{1,0:T(8,128)(2,1)S(1)} %copy-done.4, f32[64,2,64,128]{3,2,1,0:T(8,128)S(1)} %copy-done), custom_call_target="tpu_custom_call" | custom-call | tf_op jit(solution)/shard_map/pallas_call | solution.py:411
  47.3 3.8 %all-to-all-done.q_ref = bf16[8,256,128]{2,1,0:T(8,128)(2,1)S(1)} async-done(((bf16[8,256,128]{2,1,0:T(8,128)(2,1)}), bf16[8,256,128]{2,1,0:T(8,128)(2,1)S(1)}, u32[]{:S(2)}, u32[]{:S(2)}) %all-to-all-start) | async-done | bytes 524320 | tf_op jit(solution)/shard_map/all_to_all | solution.py:464
  51.1 0.1 shard_map.115
  51.2 0.1 collective-permute-start.7
  51.3 3.6 %collective-permute-start.8 = (bf16[256,128]{1,0:T(8,128)(2,1)S(1)}, bf16[256,128]{1,0:T(8,128)(2,1)S(1)}, u32[]{:S(2)}, u32[]{:S(2)}) collective-permute-start(bf16[256,128]{1,0:T(8,128)(2,1)S(1)} %get-tuple-element.40), channel_id=1, source_target_pairs={{0,15},{1,8},{2,9},{3,10},{4,11},{5,12},{6,13},{7,14},{8,23},{9,16... | collective-permute-start | bytes 196616 | tf_op jit(solution)/shard_map/ppermute | solution.py:386
  54.8 1.0 %collective-permute-start.10 = (bf16[256,128]{1,0:T(8,128)(2,1)S(1)}, bf16[256,128]{1,0:T(8,128)(2,1)S(1)}, u32[]{:S(2)}, u32[]{:S(2)}) collective-permute-start(bf16[256,128]{1,0:T(8,128)(2,1)S(1)} %get-tuple-element.42), channel_id=1, source_target_pairs={{0,13},{1,14},{2,15},{3,8},{4,9},{5,10},{6,11},{7,12},{8,21},{9,22... | collective-permute-start | bytes 196616 | tf_op jit(solution)/shard_map/ppermute | solution.py:386
  55.8 1.6 %collective-permute-start.11 = (bf16[256,128]{1,0:T(8,128)(2,1)S(1)}, bf16[256,128]{1,0:T(8,128)(2,1)S(1)}, u32[]{:S(2)}, u32[]{:S(2)}) collective-permute-start(bf16[256,128]{1,0:T(8,128)(2,1)S(1)} %get-tuple-element.43), channel_id=1, source_target_pairs={{0,12},{1,13},{2,14},{3,15},{4,8},{5,9},{6,10},{7,11},{8,20},{9,21... | collective-permute-start | bytes 196616 | tf_op jit(solution)/shard_map/ppermute | solution.py:386
  57.5 2.6 %collective-permute-start.12 = (bf16[256,128]{1,0:T(8,128)(2,1)S(1)}, bf16[256,128]{1,0:T(8,128)(2,1)S(1)}, u32[]{:S(2)}, u32[]{:S(2)}) collective-permute-start(bf16[256,128]{1,0:T(8,128)(2,1)S(1)} %get-tuple-element.44), channel_id=1, source_target_pairs={{0,11},{1,12},{2,13},{3,14},{4,15},{5,8},{6,9},{7,10},{8,19},{9,20... | collective-permute-start | bytes 196616 | tf_op jit(solution)/shard_map/ppermute | solution.py:386
  60.1 0.0 collective-permute-start.13
  60.1 1.0 %collective-permute-start.14 = (bf16[256,128]{1,0:T(8,128)(2,1)S(1)}, bf16[256,128]{1,0:T(8,128)(2,1)S(1)}, u32[]{:S(2)}, u32[]{:S(2)}) collective-permute-start(bf16[256,128]{1,0:T(8,128)(2,1)S(1)} %get-tuple-element.46), channel_id=1, source_target_pairs={{0,9},{1,10},{2,11},{3,12},{4,13},{5,14},{6,15},{7,8},{8,17},{9,18... | collective-permute-start | bytes 196616 | tf_op jit(solution)/shard_map/ppermute | solution.py:386
  61.2 6.7 %collective-permute-done.11.refs_4_ = bf16[256,128]{1,0:T(8,128)(2,1)S(1)} collective-permute-done((bf16[256,128]{1,0:T(8,128)(2,1)S(1)}, bf16[256,128]{1,0:T(8,128)(2,1)S(1)}, u32[]{:S(2)}, u32[]{:S(2)}) %collective-permute-start.11) | collective-permute-done | bytes 65568 | tf_op jit(solution)/shard_map/ppermute | solution.py:386
  67.9 1.9 %collective-permute-done.12.refs_5_ = bf16[256,128]{1,0:T(8,128)(2,1)S(1)} collective-permute-done((bf16[256,128]{1,0:T(8,128)(2,1)S(1)}, bf16[256,128]{1,0:T(8,128)(2,1)S(1)}, u32[]{:S(2)}, u32[]{:S(2)}) %collective-permute-start.12) | collective-permute-done | bytes 65568 | tf_op jit(solution)/shard_map/ppermute | solution.py:386
  69.8 1.0 %shard_map.116 = bf16[512,512]{1,0:T(8,128)(2,1)} custom-call(s32[1]{0:T(128)} %bitcast.index_ref, bf16[256,128]{1,0:T(8,128)(2,1)S(1)} %collective-permute-done.7.refs_0_, bf16[256,128]{1,0:T(8,128)(2,1)S(1)} %collective-permute-done.8.refs_1_, bf16[256,128]{1,0:T(8,128)(2,1)S(1)} %collective-permute-done.9.refs_2_, ...), custom_call_target="tpu_custom_call" | custom-call | tf_op jit(solution)/shard_map/pallas_call | solution.py:473
  (24 shorter events, 0.1 us)
Async XLA Ops:
  0.0 37.4 %copy-start.1 = (f32[20,2,64,128]{3,2,1,0:T(8,128)S(1)}, f32[20,2,64,128]{3,2,1,0:T(8,128)}, u32[]{:S(2)}) copy-start(f32[20,2,64,128]{3,2,1,0:T(8,128)} %constant.21.clone.refs_9_) | copy-start | bytes 3932164
  0.0 40.2 %copy-start.5 = (bf16[128,192]{1,0:T(8,128)(2,1)S(1)}, bf16[128,192]{1,0:T(8,128)(2,1)}, u32[]{:S(2)}) copy-start(bf16[128,192]{1,0:T(8,128)(2,1)} %constant.18.clone.back_ref) | copy-start | bytes 147460
  0.0 40.2 %copy-start.3 = (bf16[128,384]{1,0:T(8,128)(2,1)S(1)}, bf16[128,384]{1,0:T(8,128)(2,1)}, u32[]{:S(2)}) copy-start(bf16[128,384]{1,0:T(8,128)(2,1)} %constant.17.clone.forward_ref) | copy-start | bytes 294916
  3.2 11.0 %collective-permute-start = (bf16[528,128]{1,0:T(8,128)(2,1)}, bf16[528,128]{1,0:T(8,128)(2,1)S(1)}, u32[]{:S(2)}, u32[]{:S(2)}) collective-permute-start(bf16[528,128]{1,0:T(8,128)(2,1)} %get-tuple-element.28), channel_id=1, source_target_pairs={{0,1},{1,2},{2,3},{3,4},{4,5},{5,6},{6,7},{7,0},{8,9},{9,10},{10,1... | collective-permute-start | bytes 405512 | tf_op jit(solution)/shard_map/ppermute | solution.py:386
  6.2 9.7 %collective-permute-start.1 = (bf16[528,128]{1,0:T(8,128)(2,1)}, bf16[528,128]{1,0:T(8,128)(2,1)S(1)}, u32[]{:S(2)}, u32[]{:S(2)}) collective-permute-start(bf16[528,128]{1,0:T(8,128)(2,1)} %get-tuple-element.29), channel_id=1, source_target_pairs={{0,2},{1,3},{2,4},{3,5},{4,6},{5,7},{6,0},{7,1},{8,10},{9,11},{10,... | collective-permute-start | bytes 405512 | tf_op jit(solution)/shard_map/ppermute | solution.py:386
  7.8 16.9 %collective-permute-start.2 = (bf16[528,128]{1,0:T(8,128)(2,1)}, bf16[528,128]{1,0:T(8,128)(2,1)S(1)}, u32[]{:S(2)}, u32[]{:S(2)}) collective-permute-start(bf16[528,128]{1,0:T(8,128)(2,1)} %get-tuple-element.30), channel_id=1, source_target_pairs={{0,3},{1,4},{2,5},{3,6},{4,7},{5,0},{6,1},{7,2},{8,11},{9,12},{10,... | collective-permute-start | bytes 405512 | tf_op jit(solution)/shard_map/ppermute | solution.py:386
  10.3 14.8 %collective-permute-start.3 = (bf16[528,128]{1,0:T(8,128)(2,1)}, bf16[528,128]{1,0:T(8,128)(2,1)S(1)}, u32[]{:S(2)}, u32[]{:S(2)}) collective-permute-start(bf16[528,128]{1,0:T(8,128)(2,1)} %get-tuple-element.31), channel_id=1, source_target_pairs={{0,4},{1,5},{2,6},{3,7},{4,0},{5,1},{6,2},{7,3},{8,12},{9,13},{10,... | collective-permute-start | bytes 405512 | tf_op jit(solution)/shard_map/ppermute | solution.py:386
  11.6 13.6 %collective-permute-start.4 = (bf16[528,128]{1,0:T(8,128)(2,1)}, bf16[528,128]{1,0:T(8,128)(2,1)S(1)}, u32[]{:S(2)}, u32[]{:S(2)}) collective-permute-start(bf16[528,128]{1,0:T(8,128)(2,1)} %get-tuple-element.32), channel_id=1, source_target_pairs={{0,5},{1,6},{2,7},{3,0},{4,1},{5,2},{6,3},{7,4},{8,13},{9,14},{10,... | collective-permute-start | bytes 405512 | tf_op jit(solution)/shard_map/ppermute | solution.py:386
  14.2 10.9 %collective-permute-start.5 = (bf16[528,128]{1,0:T(8,128)(2,1)}, bf16[528,128]{1,0:T(8,128)(2,1)S(1)}, u32[]{:S(2)}, u32[]{:S(2)}) collective-permute-start(bf16[528,128]{1,0:T(8,128)(2,1)} %get-tuple-element.33), channel_id=1, source_target_pairs={{0,6},{1,7},{2,0},{3,1},{4,2},{5,3},{6,4},{7,5},{8,14},{9,15},{10,... | collective-permute-start | bytes 405512 | tf_op jit(solution)/shard_map/ppermute | solution.py:386
  15.9 9.3 %collective-permute-start.6 = (bf16[528,128]{1,0:T(8,128)(2,1)}, bf16[528,128]{1,0:T(8,128)(2,1)S(1)}, u32[]{:S(2)}, u32[]{:S(2)}) collective-permute-start(bf16[528,128]{1,0:T(8,128)(2,1)} %get-tuple-element.34), channel_id=1, source_target_pairs={{0,7},{1,0},{2,1},{3,2},{4,3},{5,4},{6,5},{7,6},{8,15},{9,8},{10,9... | collective-permute-start | bytes 405512 | tf_op jit(solution)/shard_map/ppermute | solution.py:386
  20.1 0.9 %copy-start.2 = (bf16[528,128]{1,0:T(8,128)(2,1)S(1)}, bf16[528,128]{1,0:T(8,128)(2,1)}, u32[]{:S(2)}) copy-start(bf16[528,128]{1,0:T(8,128)(2,1)} %get-tuple-element.26.refs_0_) | copy-start | bytes 405508
  21.0 0.8 %copy-start.6 = (bf16[128,192]{1,0:T(8,128)(2,1)S(1)}, bf16[128,192]{1,0:T(8,128)(2,1)}, u32[]{:S(2)}) copy-start(bf16[128,192]{1,0:T(8,128)(2,1)} %constant.16.clone.refs_1_) | copy-start | bytes 147460
  25.2 25.9 %all-to-all-start = ((bf16[8,256,128]{2,1,0:T(8,128)(2,1)}), bf16[8,256,128]{2,1,0:T(8,128)(2,1)S(1)}, u32[]{:S(2)}, u32[]{:S(2)}) async-start(bf16[8,256,128]{2,1,0:T(8,128)(2,1)} %shard_map.114), calls=%async_computation | async-start | bytes 1048576 | tf_op jit(solution)/shard_map/all_to_all | solution.py:464
  37.4 6.3 %copy-start = (f32[64,2,64,128]{3,2,1,0:T(8,128)S(1)}, f32[64,2,64,128]{3,2,1,0:T(8,128)}, u32[]{:S(2)}) copy-start(f32[64,2,64,128]{3,2,1,0:T(8,128)} %constant.20.clone.refs_1_) | copy-start | bytes 12582916
  37.4 6.3 %copy-start.4 = (bf16[128,192]{1,0:T(8,128)(2,1)S(1)}, bf16[128,192]{1,0:T(8,128)(2,1)}, u32[]{:S(2)}) copy-start(bf16[128,192]{1,0:T(8,128)(2,1)} %constant.19.clone.refs_0_) | copy-start | bytes 147460
  37.5 6.3 %copy-start.7 = (f32[1,512]{1,0:T(1,128)S(1)}, f32[1,512]{1,0:T(1,128)}, u32[]{:S(2)}) copy-start(f32[1,512]{1,0:T(1,128)} %skip_ref.1) | copy-start | bytes 6148
  51.2 6.2 %collective-permute-start.7 = (bf16[256,128]{1,0:T(8,128)(2,1)S(1)}, bf16[256,128]{1,0:T(8,128)(2,1)S(1)}, u32[]{:S(2)}, u32[]{:S(2)}) collective-permute-start(bf16[256,128]{1,0:T(8,128)(2,1)S(1)} %get-tuple-element.39), channel_id=1, source_target_pairs={{0,8},{1,9},{2,10},{3,11},{4,12},{5,13},{6,14},{7,15},{8,16},{9,17... | collective-permute-start | bytes 196616 | tf_op jit(solution)/shard_map/ppermute | solution.py:386
  51.3 8.8 %collective-permute-start.8 = (bf16[256,128]{1,0:T(8,128)(2,1)S(1)}, bf16[256,128]{1,0:T(8,128)(2,1)S(1)}, u32[]{:S(2)}, u32[]{:S(2)}) collective-permute-start(bf16[256,128]{1,0:T(8,128)(2,1)S(1)} %get-tuple-element.40), channel_id=1, source_target_pairs={{0,15},{1,8},{2,9},{3,10},{4,11},{5,12},{6,13},{7,14},{8,23},{9,16... | collective-permute-start | bytes 196616 | tf_op jit(solution)/shard_map/ppermute | solution.py:386
  54.8 5.3 %collective-permute-start.9 = (bf16[256,128]{1,0:T(8,128)(2,1)S(1)}, bf16[256,128]{1,0:T(8,128)(2,1)S(1)}, u32[]{:S(2)}, u32[]{:S(2)}) collective-permute-start(bf16[256,128]{1,0:T(8,128)(2,1)S(1)} %get-tuple-element.41), channel_id=1, source_target_pairs={{0,14},{1,15},{2,8},{3,9},{4,10},{5,11},{6,12},{7,13},{8,22},{9,23... | collective-permute-start | bytes 196616 | tf_op jit(solution)/shard_map/ppermute | solution.py:386
  54.8 6.3 %collective-permute-start.10 = (bf16[256,128]{1,0:T(8,128)(2,1)S(1)}, bf16[256,128]{1,0:T(8,128)(2,1)S(1)}, u32[]{:S(2)}, u32[]{:S(2)}) collective-permute-start(bf16[256,128]{1,0:T(8,128)(2,1)S(1)} %get-tuple-element.42), channel_id=1, source_target_pairs={{0,13},{1,14},{2,15},{3,8},{4,9},{5,10},{6,11},{7,12},{8,21},{9,22... | collective-permute-start | bytes 196616 | tf_op jit(solution)/shard_map/ppermute | solution.py:386
  55.8 12.1 %collective-permute-start.11 = (bf16[256,128]{1,0:T(8,128)(2,1)S(1)}, bf16[256,128]{1,0:T(8,128)(2,1)S(1)}, u32[]{:S(2)}, u32[]{:S(2)}) collective-permute-start(bf16[256,128]{1,0:T(8,128)(2,1)S(1)} %get-tuple-element.43), channel_id=1, source_target_pairs={{0,12},{1,13},{2,14},{3,15},{4,8},{5,9},{6,10},{7,11},{8,20},{9,21... | collective-permute-start | bytes 196616 | tf_op jit(solution)/shard_map/ppermute | solution.py:386
  57.5 12.4 %collective-permute-start.12 = (bf16[256,128]{1,0:T(8,128)(2,1)S(1)}, bf16[256,128]{1,0:T(8,128)(2,1)S(1)}, u32[]{:S(2)}, u32[]{:S(2)}) collective-permute-start(bf16[256,128]{1,0:T(8,128)(2,1)S(1)} %get-tuple-element.44), channel_id=1, source_target_pairs={{0,11},{1,12},{2,13},{3,14},{4,15},{5,8},{6,9},{7,10},{8,19},{9,20... | collective-permute-start | bytes 196616 | tf_op jit(solution)/shard_map/ppermute | solution.py:386
  60.1 9.8 %collective-permute-start.13 = (bf16[256,128]{1,0:T(8,128)(2,1)S(1)}, bf16[256,128]{1,0:T(8,128)(2,1)S(1)}, u32[]{:S(2)}, u32[]{:S(2)}) collective-permute-start(bf16[256,128]{1,0:T(8,128)(2,1)S(1)} %get-tuple-element.45), channel_id=1, source_target_pairs={{0,10},{1,11},{2,12},{3,13},{4,14},{5,15},{6,8},{7,9},{8,18},{9,19... | collective-permute-start | bytes 196616 | tf_op jit(solution)/shard_map/ppermute | solution.py:386
  60.1 9.7 %collective-permute-start.14 = (bf16[256,128]{1,0:T(8,128)(2,1)S(1)}, bf16[256,128]{1,0:T(8,128)(2,1)S(1)}, u32[]{:S(2)}, u32[]{:S(2)}) collective-permute-start(bf16[256,128]{1,0:T(8,128)(2,1)S(1)} %get-tuple-element.46), channel_id=1, source_target_pairs={{0,9},{1,10},{2,11},{3,12},{4,13},{5,14},{6,15},{7,8},{8,17},{9,18... | collective-permute-start | bytes 196616 | tf_op jit(solution)/shard_map/ppermute | solution.py:386

commit v10 on v8

--- a/solution.py
+++ b/solution.py
@@ -225,11 +225,15 @@
         target[...] = source[...]
 
 
+def longest_first(parts):
+    return sorted(range(parts), key=lambda n: abs(n - parts // 2))
+
+
 def unpack_kernel(parts, index_ref, *refs):
     blocks, out_ref, held = refs[:parts], refs[parts], refs[parts + 1]
     rows = held.shape[1]
     low = lower_half((rows, LANES))
-    for n, block in enumerate(blocks):
+    for n, block in zip(longest_first(parts), blocks):
         held[lax.rem(index_ref[0] + n, parts)] = block[...]
     for e in range(parts // 2):
         even, odd = held[2 * e].astype(F32), held[2 * e + 1].astype(F32)
@@ -247,7 +251,7 @@
     def origin(n):
         return lax.rem(index_ref[0] + parts - n, parts)
 
-    for n, block in enumerate(blocks):
+    for n, block in zip(longest_first(parts), blocks):
         scale = block[2 * rows : 2 * rows + EXTRA, :].astype(F32)[:1] * (1.0 / SCALE)
         for m in range(per):
             at = m * INNER
@@ -397,7 +401,7 @@
         in_specs=[scalar] + [whole] * (parts + 2),
         scratch_shapes=[pltpu.VMEM((INNER * (outer + PAD), LANES), F32)],
         compiler_params=pltpu.CompilerParams(vmem_limit_bytes=LIMIT * 2**20),
-    )(index, *slabs, forward_a, first_turns)
+    )(index, *[slabs[n] for n in longest_first(parts)], forward_a, first_turns)
     w = pl.pallas_call(
         functools.partial(middle_kernel, outer),
         out_shape=block(INNER * (outer + PAD), LANES),
@@ -437,7 +441,7 @@
         + [pltpu.SemaphoreType.DMA((3,))],
         compiler_params=large,
     )(index, key_stream[0], value_stream[0], filter_taps[0])
-    slabs = [sent[0]] + [joint_shift(sent[n], 0, n) for n in range(1, parts)]
+    slabs = {n: joint_shift(sent[n], 0, n) for n in longest_first(parts) if n}
     q = pl.pallas_call(
         functools.partial(pack_gate_kernel, parts),
         out_shape=block(parts, rows, LANES),
@@ -452,8 +456,8 @@
         out_shape=tuple(jax.ShapeDtypeStruct(x.shape, x.dtype) for x in held),
         compiler_params=small,
     )(*held)
-    q, *_ = lax.optimization_barrier((q, *slabs, *held))
-    slabs = [held[0]] + slabs[1:]
+    q, *_ = lax.optimization_barrier((q, *slabs.values(), *held))
+    slabs[0] = held[0]
     consts = (two_turns, held[1], turns, forward_b, back_b, back_a)
     q = lax.all_to_all(q, "ctx", split_axis=0, concat_axis=0, tiled=True)
     y = convolved(parts, length, index, slabs, skip_weight, consts)
@@ -463,7 +467,7 @@
         in_specs=[scalar, whole, whole],
         compiler_params=small,
     )(index, y, q)
-    gated = [joint_shift(gated[n], 1, -n) for n in range(parts)]
+    gated = [joint_shift(gated[n], 1, -n) for n in longest_first(parts)]
     out = pl.pallas_call(
         functools.partial(unpack_kernel, parts),
         out_shape=block(length, channels),

time: 71.2 us -> 71.5 us (level)
  waiting for transfers between devices: 15.9 us -> 19.2 us
  starting transfers between devices: 37 us -> 33.9 us
    all_to_all x1, starting transfers between devices: 12.2 us -> 5.32 us  [fast_on_device(): q = lax.all_to_all(q, 'ctx', split_axis=0, concat_axis=0, tiled=True)]
    ppermute x15, starting transfers between devices: 24.7 us -> 28.5 us  [joint_shift(): return lax.ppermute(value, ('segment', 'ctx'), pairs)]
    ppermute x15, waiting for transfers between devices: 12.1 us -> 15.4 us  [joint_shift(): return lax.ppermute(value, ('segment', 'ctx'), pairs)]
  transfers between devices with their start and end apart: 16 -> 16, of which waited for: 6 -> 5; matrix products, arithmetic and copies ran while one was open for 0% -> 0% of each run, Pallas kernels for 17% -> 17%
where the time goes in v10:
time: 71.5 us; the launch traced here: 71.2 us
  starting transfers between devices  33.9 us (47%)
  waiting for transfers between devices  19.2 us (27%)
  Pallas kernels  16.2 us (23%)
  local copies, waits for them, and re-layouts  1.78 us (2%)
    ppermute x15, starting transfers between devices, joint_shift(): return lax.ppermute(value, ('segment', 'ctx'), pairs)  28.5 us
    ppermute x15, waiting for transfers between devices, joint_shift(): return lax.ppermute(value, ('segment', 'ctx'), pairs)  15.4 us
    all_to_all x1, starting transfers between devices, fast_on_device(): q = lax.all_to_all(q, 'ctx', split_axis=0, concat_axis=0, tiled=True)  5.32 us
    all_to_all x1, waiting for transfers between devices, fast_on_device(): q = lax.all_to_all(q, 'ctx', split_axis=0, concat_axis=0, tiled=True)  3.76 us
    pallas_call x1, Pallas kernels, convolved(): pl.pallas_call(functools.partial(middle_kernel, outer), out_shape=block(I...  3.57 us
    pallas_call x1, Pallas kernels, convolved(): pl.pallas_call(functools.partial(back_kernel, parts, outer), out_shape=bl...  3.53 us
    pallas_call x1, Pallas kernels, fast_on_device(): pl.pallas_call(functools.partial(pack_kernel, parts), out_shape=(block(si...  3.21 us
    pallas_call x1, Pallas kernels, convolved(): pl.pallas_call(functools.partial(forward_kernel, parts, outer), out_shape...  2.71 us
  transfers between devices with their start and end apart: 16, of which 5 were waited for; matrix products, arithmetic and copies ran while one was open for 0% of the time, Pallas kernels for 17%

profile of v10, /device:TPU:0, one launch (start us, length us, event | category | flops | bytes accessed | tf_op | source)
XLA Modules:
  0.0 71.2 jit_solution(11622900411311661093)
XLA Ops:
  0.0 3.2 %shard_map.109 = (bf16[528,128]{1,0:T(8,128)(2,1)}, bf16[528,128]{1,0:T(8,128)(2,1)}, bf16[528,128]{1,0:T(8,128)(2,1)}, bf16[528,128]{1,0:T(8,128)(2,1)}, bf16[5...) custom-call(s32[1]{0:T(128)} %bitcast.index_ref, ...), custom_call_target="tpu_custom_call" | custom-call | tf_op jit(solution)/shard_map/pallas_call | solution.py:435
  3.2 4.1 %collective-permute-start = (bf16[528,128]{1,0:T(8,128)(2,1)}, bf16[528,128]{1,0:T(8,128)(2,1)S(1)}, u32[]{:S(2)}, u32[]{:S(2)}) collective-permute-start(bf16[528,128]{1,0:T(8,128)(2,1)} %get-tuple-element.26), channel_id=1, source_target_pairs={{0,4},{1,5},{2,6},{3,7},{4,0},{5,1},{6,2},{7,3},{8,12},{9,13},{10,... | collective-permute-start | bytes 405512 | tf_op jit(solution)/shard_map/ppermute | solution.py:385
  7.3 2.5 %collective-permute-start.1 = (bf16[528,128]{1,0:T(8,128)(2,1)}, bf16[528,128]{1,0:T(8,128)(2,1)S(1)}, u32[]{:S(2)}, u32[]{:S(2)}) collective-permute-start(bf16[528,128]{1,0:T(8,128)(2,1)} %get-tuple-element.27), channel_id=1, source_target_pairs={{0,3},{1,4},{2,5},{3,6},{4,7},{5,0},{6,1},{7,2},{8,11},{9,12},{10,... | collective-permute-start | bytes 405512 | tf_op jit(solution)/shard_map/ppermute | solution.py:385
  9.9 1.3 %collective-permute-start.2 = (bf16[528,128]{1,0:T(8,128)(2,1)}, bf16[528,128]{1,0:T(8,128)(2,1)S(1)}, u32[]{:S(2)}, u32[]{:S(2)}) collective-permute-start(bf16[528,128]{1,0:T(8,128)(2,1)} %get-tuple-element.28), channel_id=1, source_target_pairs={{0,5},{1,6},{2,7},{3,0},{4,1},{5,2},{6,3},{7,4},{8,13},{9,14},{10,... | collective-permute-start | bytes 405512 | tf_op jit(solution)/shard_map/ppermute | solution.py:385
  11.2 1.6 %collective-permute-start.3 = (bf16[528,128]{1,0:T(8,128)(2,1)}, bf16[528,128]{1,0:T(8,128)(2,1)S(1)}, u32[]{:S(2)}, u32[]{:S(2)}) collective-permute-start(bf16[528,128]{1,0:T(8,128)(2,1)} %get-tuple-element.29), channel_id=1, source_target_pairs={{0,2},{1,3},{2,4},{3,5},{4,6},{5,7},{6,0},{7,1},{8,10},{9,11},{10,... | collective-permute-start | bytes 405512 | tf_op jit(solution)/shard_map/ppermute | solution.py:385
  12.7 2.2 %collective-permute-start.4 = (bf16[528,128]{1,0:T(8,128)(2,1)}, bf16[528,128]{1,0:T(8,128)(2,1)S(1)}, u32[]{:S(2)}, u32[]{:S(2)}) collective-permute-start(bf16[528,128]{1,0:T(8,128)(2,1)} %get-tuple-element.30), channel_id=1, source_target_pairs={{0,6},{1,7},{2,0},{3,1},{4,2},{5,3},{6,4},{7,5},{8,14},{9,15},{10,... | collective-permute-start | bytes 405512 | tf_op jit(solution)/shard_map/ppermute | solution.py:385
  15.0 8.6 %collective-permute-done.refs_0_ = bf16[528,128]{1,0:T(8,128)(2,1)S(1)} collective-permute-done((bf16[528,128]{1,0:T(8,128)(2,1)}, bf16[528,128]{1,0:T(8,128)(2,1)S(1)}, u32[]{:S(2)}, u32[]{:S(2)}) %collective-permute-start) | collective-permute-done | bytes 135200 | tf_op jit(solution)/shard_map/ppermute | solution.py:385
  23.6 0.0 collective-permute-start.5
  23.6 1.3 %collective-permute-done.1.refs_1_ = bf16[528,128]{1,0:T(8,128)(2,1)S(1)} collective-permute-done((bf16[528,128]{1,0:T(8,128)(2,1)}, bf16[528,128]{1,0:T(8,128)(2,1)S(1)}, u32[]{:S(2)}, u32[]{:S(2)}) %collective-permute-start.1) | collective-permute-done | bytes 135200 | tf_op jit(solution)/shard_map/ppermute | solution.py:385
  24.9 3.4 %collective-permute-start.6 = (bf16[528,128]{1,0:T(8,128)(2,1)}, bf16[528,128]{1,0:T(8,128)(2,1)S(1)}, u32[]{:S(2)}, u32[]{:S(2)}) collective-permute-start(bf16[528,128]{1,0:T(8,128)(2,1)} %get-tuple-element.32), channel_id=1, source_target_pairs={{0,7},{1,0},{2,1},{3,2},{4,3},{5,4},{6,5},{7,6},{8,15},{9,8},{10,9... | collective-permute-start | bytes 405512 | tf_op jit(solution)/shard_map/ppermute | solution.py:385
  28.3 2.1 %shard_map.114 = bf16[8,256,128]{2,1,0:T(8,128)(2,1)} custom-call(bf16[512,512]{1,0:T(8,128)(2,1)} %bitcast.9), custom_call_target="tpu_custom_call" | custom-call | tf_op jit(solution)/shard_map/pallas_call | solution.py:445
  30.4 0.9 %copy-done.2 = bf16[528,128]{1,0:T(8,128)(2,1)S(1)} copy-done((bf16[528,128]{1,0:T(8,128)(2,1)S(1)}, bf16[528,128]{1,0:T(8,128)(2,1)}, u32[]{:S(2)}) %copy-start.2) | copy-done | bytes 135192
  31.3 0.8 %copy-done.6 = bf16[128,192]{1,0:T(8,128)(2,1)S(1)} copy-done((bf16[128,192]{1,0:T(8,128)(2,1)S(1)}, bf16[128,192]{1,0:T(8,128)(2,1)}, u32[]{:S(2)}) %copy-start.6) | copy-done | bytes 49176
  32.2 0.0 collective-permute-done.2.refs_2_
  32.2 0.0 collective-permute-done.4.refs_4_
  32.2 5.3 %all-to-all-start = ((bf16[8,256,128]{2,1,0:T(8,128)(2,1)}), bf16[8,256,128]{2,1,0:T(8,128)(2,1)S(1)}, u32[]{:S(2)}, u32[]{:S(2)}) async-start(bf16[8,256,128]{2,1,0:T(8,128)(2,1)} %shard_map.114), calls=%async_computation | async-start | bytes 1048576 | tf_op jit(solution)/shard_map/all_to_all | solution.py:462
  37.5 0.0 copy-start
  37.5 0.0 copy-start.4
  37.6 0.0 copy-start.7
  37.6 2.7 %shard_map.111 = (f32[8704,128]{1,0:T(8,128)S(1)}, f32[8,256,128]{2,1,0:T(8,128)S(1)}) custom-call(s32[1]{0:T(128)} %bitcast.index_ref, bf16[528,128]{1,0:T(8,128)(2,1)S(1)} %collective-permute-done.refs_0_, bf16[528,128]{1,0:T(8,128)(2,1)S(1)} %collective-permute-done.1.refs_1_, bf16[528,128]{1,0:T(8,128)(2,1)S(1)} %collective-permute-done.2.refs_2_, ...), custom_call_target="tpu_custom_call" | custom-call | tf_op jit(solution)/shard_map/pallas_call | solution.py:398
  40.3 3.6 %shard_map.112.w_s = f32[4608,128]{1,0:T(8,128)S(1)} custom-call(f32[8704,128]{1,0:T(8,128)S(1)} %get-tuple-element.36.z_s, bf16[128,384]{1,0:T(8,128)(2,1)S(1)} %copy-done.3, bf16[128,192]{1,0:T(8,128)(2,1)S(1)} %copy-done.5), custom_call_target="tpu_custom_call" | custom-call | tf_op jit(solution)/shard_map/pallas_call | solution.py:405
  43.9 3.5 %shard_map.113.y_ref = f32[8,256,128]{2,1,0:T(8,128)S(1)} custom-call(s32[1]{0:T(128)} %bitcast.index_ref, f32[1,512]{1,0:T(1,128)S(1)} %copy-done.7, f32[4608,128]{1,0:T(8,128)S(1)} %shard_map.112.w_s, f32[8,256,128]{2,1,0:T(8,128)S(1)} %get-tuple-element.37.p_s, bf16[128,192]{1,0:T(8,128)(2,1)S(1)} %copy-done.4, f32[64,2,64,128]{3,2,1,0:T(8,128)S(1)} %copy-done), custom_call_target="tpu_custom_call" | custom-call | tf_op jit(solution)/shard_map/pallas_call | solution.py:410
  47.5 3.8 %all-to-all-done.q_ref = bf16[8,256,128]{2,1,0:T(8,128)(2,1)S(1)} async-done(((bf16[8,256,128]{2,1,0:T(8,128)(2,1)}), bf16[8,256,128]{2,1,0:T(8,128)(2,1)S(1)}, u32[]{:S(2)}, u32[]{:S(2)}) %all-to-all-start) | async-done | bytes 524320 | tf_op jit(solution)/shard_map/all_to_all | solution.py:462
  51.2 0.1 shard_map.115
  51.3 0.1 collective-permute-start.7
  51.4 4.4 %collective-permute-start.8 = (bf16[256,128]{1,0:T(8,128)(2,1)S(1)}, bf16[256,128]{1,0:T(8,128)(2,1)S(1)}, u32[]{:S(2)}, u32[]{:S(2)}) collective-permute-start(bf16[256,128]{1,0:T(8,128)(2,1)S(1)} %get-tuple-element.40), channel_id=1, source_target_pairs={{0,13},{1,14},{2,15},{3,8},{4,9},{5,10},{6,11},{7,12},{8,21},{9,22... | collective-permute-start | bytes 196616 | tf_op jit(solution)/shard_map/ppermute | solution.py:385
  55.8 3.7 %collective-permute-start.10 = (bf16[256,128]{1,0:T(8,128)(2,1)S(1)}, bf16[256,128]{1,0:T(8,128)(2,1)S(1)}, u32[]{:S(2)}, u32[]{:S(2)}) collective-permute-start(bf16[256,128]{1,0:T(8,128)(2,1)S(1)} %get-tuple-element.42), channel_id=1, source_target_pairs={{0,14},{1,15},{2,8},{3,9},{4,10},{5,11},{6,12},{7,13},{8,22},{9,23... | collective-permute-start | bytes 196616 | tf_op jit(solution)/shard_map/ppermute | solution.py:385
  59.5 2.9 %collective-permute-start.12 = (bf16[256,128]{1,0:T(8,128)(2,1)S(1)}, bf16[256,128]{1,0:T(8,128)(2,1)S(1)}, u32[]{:S(2)}, u32[]{:S(2)}) collective-permute-start(bf16[256,128]{1,0:T(8,128)(2,1)S(1)} %get-tuple-element.44), channel_id=1, source_target_pairs={{0,15},{1,8},{2,9},{3,10},{4,11},{5,12},{6,13},{7,14},{8,23},{9,16... | collective-permute-start | bytes 196616 | tf_op jit(solution)/shard_map/ppermute | solution.py:385
  62.4 2.3 %collective-permute-start.14 = (bf16[256,128]{1,0:T(8,128)(2,1)S(1)}, bf16[256,128]{1,0:T(8,128)(2,1)S(1)}, u32[]{:S(2)}, u32[]{:S(2)}) collective-permute-start(bf16[256,128]{1,0:T(8,128)(2,1)S(1)} %get-tuple-element.46), channel_id=1, source_target_pairs={{0,8},{1,9},{2,10},{3,11},{4,12},{5,13},{6,14},{7,15},{8,16},{9,17... | collective-permute-start | bytes 196616 | tf_op jit(solution)/shard_map/ppermute | solution.py:385
  64.7 1.8 %collective-permute-done.11.refs_4_ = bf16[256,128]{1,0:T(8,128)(2,1)S(1)} collective-permute-done((bf16[256,128]{1,0:T(8,128)(2,1)S(1)}, bf16[256,128]{1,0:T(8,128)(2,1)S(1)}, u32[]{:S(2)}, u32[]{:S(2)}) %collective-permute-start.11) | collective-permute-done | bytes 65568 | tf_op jit(solution)/shard_map/ppermute | solution.py:385
  66.5 3.7 %collective-permute-done.13.refs_6_ = bf16[256,128]{1,0:T(8,128)(2,1)S(1)} collective-permute-done((bf16[256,128]{1,0:T(8,128)(2,1)S(1)}, bf16[256,128]{1,0:T(8,128)(2,1)S(1)}, u32[]{:S(2)}, u32[]{:S(2)}) %collective-permute-start.13) | collective-permute-done | bytes 65568 | tf_op jit(solution)/shard_map/ppermute | solution.py:385
  70.1 1.0 %shard_map.116 = bf16[512,512]{1,0:T(8,128)(2,1)} custom-call(s32[1]{0:T(128)} %bitcast.index_ref, bf16[256,128]{1,0:T(8,128)(2,1)S(1)} %collective-permute-done.7.refs_0_, bf16[256,128]{1,0:T(8,128)(2,1)S(1)} %collective-permute-done.8.refs_1_, bf16[256,128]{1,0:T(8,128)(2,1)S(1)} %collective-permute-done.9.refs_2_, ...), custom_call_target="tpu_custom_call" | custom-call | tf_op jit(solution)/shard_map/pallas_call | solution.py:471
  (24 shorter events, 0.1 us)
Async XLA Ops:
  0.0 37.5 %copy-start.1 = (f32[20,2,64,128]{3,2,1,0:T(8,128)S(1)}, f32[20,2,64,128]{3,2,1,0:T(8,128)}, u32[]{:S(2)}) copy-start(f32[20,2,64,128]{3,2,1,0:T(8,128)} %constant.21.clone.refs_9_) | copy-start | bytes 3932164
  0.0 40.3 %copy-start.5 = (bf16[128,192]{1,0:T(8,128)(2,1)S(1)}, bf16[128,192]{1,0:T(8,128)(2,1)}, u32[]{:S(2)}) copy-start(bf16[128,192]{1,0:T(8,128)(2,1)} %constant.18.clone.back_ref) | copy-start | bytes 147460
  0.0 40.3 %copy-start.3 = (bf16[128,384]{1,0:T(8,128)(2,1)S(1)}, bf16[128,384]{1,0:T(8,128)(2,1)}, u32[]{:S(2)}) copy-start(bf16[128,384]{1,0:T(8,128)(2,1)} %constant.17.clone.forward_ref) | copy-start | bytes 294916
  3.2 20.4 %collective-permute-start = (bf16[528,128]{1,0:T(8,128)(2,1)}, bf16[528,128]{1,0:T(8,128)(2,1)S(1)}, u32[]{:S(2)}, u32[]{:S(2)}) collective-permute-start(bf16[528,128]{1,0:T(8,128)(2,1)} %get-tuple-element.26), channel_id=1, source_target_pairs={{0,4},{1,5},{2,6},{3,7},{4,0},{5,1},{6,2},{7,3},{8,12},{9,13},{10,... | collective-permute-start | bytes 405512 | tf_op jit(solution)/shard_map/ppermute | solution.py:385
  7.3 17.6 %collective-permute-start.1 = (bf16[528,128]{1,0:T(8,128)(2,1)}, bf16[528,128]{1,0:T(8,128)(2,1)S(1)}, u32[]{:S(2)}, u32[]{:S(2)}) collective-permute-start(bf16[528,128]{1,0:T(8,128)(2,1)} %get-tuple-element.27), channel_id=1, source_target_pairs={{0,3},{1,4},{2,5},{3,6},{4,7},{5,0},{6,1},{7,2},{8,11},{9,12},{10,... | collective-permute-start | bytes 405512 | tf_op jit(solution)/shard_map/ppermute | solution.py:385
  9.9 22.3 %collective-permute-start.2 = (bf16[528,128]{1,0:T(8,128)(2,1)}, bf16[528,128]{1,0:T(8,128)(2,1)S(1)}, u32[]{:S(2)}, u32[]{:S(2)}) collective-permute-start(bf16[528,128]{1,0:T(8,128)(2,1)} %get-tuple-element.28), channel_id=1, source_target_pairs={{0,5},{1,6},{2,7},{3,0},{4,1},{5,2},{6,3},{7,4},{8,13},{9,14},{10,... | collective-permute-start | bytes 405512 | tf_op jit(solution)/shard_map/ppermute | solution.py:385
  11.2 21.0 %collective-permute-start.3 = (bf16[528,128]{1,0:T(8,128)(2,1)}, bf16[528,128]{1,0:T(8,128)(2,1)S(1)}, u32[]{:S(2)}, u32[]{:S(2)}) collective-permute-start(bf16[528,128]{1,0:T(8,128)(2,1)} %get-tuple-element.29), channel_id=1, source_target_pairs={{0,2},{1,3},{2,4},{3,5},{4,6},{5,7},{6,0},{7,1},{8,10},{9,11},{10,... | collective-permute-start | bytes 405512 | tf_op jit(solution)/shard_map/ppermute | solution.py:385
  12.7 19.4 %collective-permute-start.4 = (bf16[528,128]{1,0:T(8,128)(2,1)}, bf16[528,128]{1,0:T(8,128)(2,1)S(1)}, u32[]{:S(2)}, u32[]{:S(2)}) collective-permute-start(bf16[528,128]{1,0:T(8,128)(2,1)} %get-tuple-element.30), channel_id=1, source_target_pairs={{0,6},{1,7},{2,0},{3,1},{4,2},{5,3},{6,4},{7,5},{8,14},{9,15},{10,... | collective-permute-start | bytes 405512 | tf_op jit(solution)/shard_map/ppermute | solution.py:385
  23.6 8.6 %collective-permute-start.5 = (bf16[528,128]{1,0:T(8,128)(2,1)}, bf16[528,128]{1,0:T(8,128)(2,1)S(1)}, u32[]{:S(2)}, u32[]{:S(2)}) collective-permute-start(bf16[528,128]{1,0:T(8,128)(2,1)} %get-tuple-element.31), channel_id=1, source_target_pairs={{0,1},{1,2},{2,3},{3,4},{4,5},{5,6},{6,7},{7,0},{8,9},{9,10},{10,1... | collective-permute-start | bytes 405512 | tf_op jit(solution)/shard_map/ppermute | solution.py:385
  24.9 7.3 %collective-permute-start.6 = (bf16[528,128]{1,0:T(8,128)(2,1)}, bf16[528,128]{1,0:T(8,128)(2,1)S(1)}, u32[]{:S(2)}, u32[]{:S(2)}) collective-permute-start(bf16[528,128]{1,0:T(8,128)(2,1)} %get-tuple-element.32), channel_id=1, source_target_pairs={{0,7},{1,0},{2,1},{3,2},{4,3},{5,4},{6,5},{7,6},{8,15},{9,8},{10,9... | collective-permute-start | bytes 405512 | tf_op jit(solution)/shard_map/ppermute | solution.py:385
  30.4 0.9 %copy-start.2 = (bf16[528,128]{1,0:T(8,128)(2,1)S(1)}, bf16[528,128]{1,0:T(8,128)(2,1)}, u32[]{:S(2)}) copy-start(bf16[528,128]{1,0:T(8,128)(2,1)} %get-tuple-element.33.refs_0_) | copy-start | bytes 405508
  31.3 0.8 %copy-start.6 = (bf16[128,192]{1,0:T(8,128)(2,1)S(1)}, bf16[128,192]{1,0:T(8,128)(2,1)}, u32[]{:S(2)}) copy-start(bf16[128,192]{1,0:T(8,128)(2,1)} %constant.16.clone.refs_1_) | copy-start | bytes 147460
  32.2 19.0 %all-to-all-start = ((bf16[8,256,128]{2,1,0:T(8,128)(2,1)}), bf16[8,256,128]{2,1,0:T(8,128)(2,1)S(1)}, u32[]{:S(2)}, u32[]{:S(2)}) async-start(bf16[8,256,128]{2,1,0:T(8,128)(2,1)} %shard_map.114), calls=%async_computation | async-start | bytes 1048576 | tf_op jit(solution)/shard_map/all_to_all | solution.py:462
  37.5 6.4 %copy-start = (f32[64,2,64,128]{3,2,1,0:T(8,128)S(1)}, f32[64,2,64,128]{3,2,1,0:T(8,128)}, u32[]{:S(2)}) copy-start(f32[64,2,64,128]{3,2,1,0:T(8,128)} %constant.20.clone.refs_1_) | copy-start | bytes 12582916
  37.5 6.4 %copy-start.4 = (bf16[128,192]{1,0:T(8,128)(2,1)S(1)}, bf16[128,192]{1,0:T(8,128)(2,1)}, u32[]{:S(2)}) copy-start(bf16[128,192]{1,0:T(8,128)(2,1)} %constant.19.clone.refs_0_) | copy-start | bytes 147460
  37.6 6.4 %copy-start.7 = (f32[1,512]{1,0:T(1,128)S(1)}, f32[1,512]{1,0:T(1,128)}, u32[]{:S(2)}) copy-start(f32[1,512]{1,0:T(1,128)} %skip_ref.1) | copy-start | bytes 6148
  51.3 8.2 %collective-permute-start.7 = (bf16[256,128]{1,0:T(8,128)(2,1)S(1)}, bf16[256,128]{1,0:T(8,128)(2,1)S(1)}, u32[]{:S(2)}, u32[]{:S(2)}) collective-permute-start(bf16[256,128]{1,0:T(8,128)(2,1)S(1)} %get-tuple-element.39), channel_id=1, source_target_pairs={{0,12},{1,13},{2,14},{3,15},{4,8},{5,9},{6,10},{7,11},{8,20},{9,21... | collective-permute-start | bytes 196616 | tf_op jit(solution)/shard_map/ppermute | solution.py:385
  51.4 11.0 %collective-permute-start.8 = (bf16[256,128]{1,0:T(8,128)(2,1)S(1)}, bf16[256,128]{1,0:T(8,128)(2,1)S(1)}, u32[]{:S(2)}, u32[]{:S(2)}) collective-permute-start(bf16[256,128]{1,0:T(8,128)(2,1)S(1)} %get-tuple-element.40), channel_id=1, source_target_pairs={{0,13},{1,14},{2,15},{3,8},{4,9},{5,10},{6,11},{7,12},{8,21},{9,22... | collective-permute-start | bytes 196616 | tf_op jit(solution)/shard_map/ppermute | solution.py:385
  55.8 6.6 %collective-permute-start.9 = (bf16[256,128]{1,0:T(8,128)(2,1)S(1)}, bf16[256,128]{1,0:T(8,128)(2,1)S(1)}, u32[]{:S(2)}, u32[]{:S(2)}) collective-permute-start(bf16[256,128]{1,0:T(8,128)(2,1)S(1)} %get-tuple-element.41), channel_id=1, source_target_pairs={{0,11},{1,12},{2,13},{3,14},{4,15},{5,8},{6,9},{7,10},{8,19},{9,20... | collective-permute-start | bytes 196616 | tf_op jit(solution)/shard_map/ppermute | solution.py:385
  55.8 8.9 %collective-permute-start.10 = (bf16[256,128]{1,0:T(8,128)(2,1)S(1)}, bf16[256,128]{1,0:T(8,128)(2,1)S(1)}, u32[]{:S(2)}, u32[]{:S(2)}) collective-permute-start(bf16[256,128]{1,0:T(8,128)(2,1)S(1)} %get-tuple-element.42), channel_id=1, source_target_pairs={{0,14},{1,15},{2,8},{3,9},{4,10},{5,11},{6,12},{7,13},{8,22},{9,23... | collective-permute-start | bytes 196616 | tf_op jit(solution)/shard_map/ppermute | solution.py:385
  59.5 7.0 %collective-permute-start.11 = (bf16[256,128]{1,0:T(8,128)(2,1)S(1)}, bf16[256,128]{1,0:T(8,128)(2,1)S(1)}, u32[]{:S(2)}, u32[]{:S(2)}) collective-permute-start(bf16[256,128]{1,0:T(8,128)(2,1)S(1)} %get-tuple-element.43), channel_id=1, source_target_pairs={{0,10},{1,11},{2,12},{3,13},{4,14},{5,15},{6,8},{7,9},{8,18},{9,19... | collective-permute-start | bytes 196616 | tf_op jit(solution)/shard_map/ppermute | solution.py:385
  59.5 7.0 %collective-permute-start.12 = (bf16[256,128]{1,0:T(8,128)(2,1)S(1)}, bf16[256,128]{1,0:T(8,128)(2,1)S(1)}, u32[]{:S(2)}, u32[]{:S(2)}) collective-permute-start(bf16[256,128]{1,0:T(8,128)(2,1)S(1)} %get-tuple-element.44), channel_id=1, source_target_pairs={{0,15},{1,8},{2,9},{3,10},{4,11},{5,12},{6,13},{7,14},{8,23},{9,16... | collective-permute-start | bytes 196616 | tf_op jit(solution)/shard_map/ppermute | solution.py:385
  62.4 7.8 %collective-permute-start.13 = (bf16[256,128]{1,0:T(8,128)(2,1)S(1)}, bf16[256,128]{1,0:T(8,128)(2,1)S(1)}, u32[]{:S(2)}, u32[]{:S(2)}) collective-permute-start(bf16[256,128]{1,0:T(8,128)(2,1)S(1)} %get-tuple-element.45), channel_id=1, source_target_pairs={{0,9},{1,10},{2,11},{3,12},{4,13},{5,14},{6,15},{7,8},{8,17},{9,18... | collective-permute-start | bytes 196616 | tf_op jit(solution)/shard_map/ppermute | solution.py:385
  62.4 7.8 %collective-permute-start.14 = (bf16[256,128]{1,0:T(8,128)(2,1)S(1)}, bf16[256,128]{1,0:T(8,128)(2,1)S(1)}, u32[]{:S(2)}, u32[]{:S(2)}) collective-permute-start(bf16[256,128]{1,0:T(8,128)(2,1)S(1)} %get-tuple-element.46), channel_id=1, source_target_pairs={{0,8},{1,9},{2,10},{3,11},{4,12},{5,13},{6,14},{7,15},{8,16},{9,17... | collective-permute-start | bytes 196616 | tf_op jit(solution)/shard_map/ppermute | solution.py:385

commit v11 on v8

--- a/solution.py
+++ b/solution.py
@@ -184,8 +184,10 @@
     k_ref, v_ref, h_ref = arrived
     rows = k_ref.shape[0] // 2
     low = lower_half((rows, LANES))
-    for copy in fetched(sources, arrived, sems):
-        copy.wait()
+    tiles = [slice(LANES * e, LANES * (e + 1)) for e in range(parts // 2)]
+    copies = fetched(
+        [x.at[:, t] for t in tiles for x in sources], [x.at[:, t] for t in tiles for x in arrived], sems
+    )
 
     def place(e, at, tile, low):
         half = tile.shape[0] // 2
@@ -194,7 +196,9 @@
         held[2 * e + 1, at : at + half, :] = jnp.where(low, swap_halves(early), late).astype(BF16)
 
     for e in range(parts // 2):
-        lanes = slice(LANES * e, LANES * (e + 1))
+        lanes = tiles[e]
+        for copy in copies[3 * e : 3 * e + 3]:
+            copy.wait()
         product = k_ref[:, lanes].astype(F32) * v_ref[:, lanes].astype(F32)
         largest = jnp.max(jnp.abs(product), axis=0, keepdims=True)
         largest = jnp.maximum(largest * 1.01, SMALLEST).astype(BF16).astype(F32)
@@ -348,21 +352,24 @@
             for j in range(WIDE):
                 re = both[:outer, LANES * j : LANES * (j + 1)]
                 im = both[outer:, LANES * j : LANES * (j + 1)]
-                y_s[pl.ds(b + j, outer, stride=INNER), :] = re + swap_halves(im)
+                y_s[pl.ds(b + j, outer, stride=INNER + PAD), :] = re + swap_halves(im)
         return carry
 
     lax.fori_loop(0, INNER // STEP, back_outer, 0)
 
-    lowr = lower_half((rows, LANES))
+    lowr = lower_half((INNER, LANES))
     pair = pl.multiple_of(index_ref[0] // 2 * LANES, LANES)
     wide = skip_ref[:, pl.ds(pair, LANES)]
     mine = lower_half((1, LANES)) == (index_ref[0] % 2 == 0)
     skip = jnp.where(mine, wide, swap_halves(wide))
+    per = rows // INNER
     for n in range(parts):
-        at = pl.multiple_of(origin(n) * 2 * rows, 2 * rows)
-        early = y_s[pl.ds(at, rows), :]
-        late = y_s[pl.ds(at + rows, rows), :]
-        out_ref[n] = jnp.where(lowr, early, swap_halves(late)) + skip * p_s[n]
+        for m in range(per):
+            a = origin(n) * 2 * per + m
+            early = y_s[pl.ds(pl.multiple_of(a * (INNER + PAD), PAD), INNER), :]
+            late = y_s[pl.ds(pl.multiple_of((a + per) * (INNER + PAD), PAD), INNER), :]
+            span = slice(m * INNER, (m + 1) * INNER)
+            out_ref[n, span, :] = jnp.where(lowr, early, swap_halves(late)) + skip * p_s[n, span, :]
 
 
 def gate_kernel(parts, index_ref, y_ref, q_ref, *outs):
@@ -407,7 +414,7 @@
         functools.partial(back_kernel, parts, outer),
         out_shape=block(parts, rows, LANES),
         in_specs=[scalar] + [whole] * 5,
-        scratch_shapes=[pltpu.VMEM((outer * INNER, LANES), F32)],
+        scratch_shapes=[pltpu.VMEM((outer * (INNER + PAD), LANES), F32)],
         compiler_params=pltpu.CompilerParams(vmem_limit_bytes=LIMIT * 2**20),
     )(index, skip_weight, w, p, back_a, turns)
 
@@ -434,7 +441,7 @@
         in_specs=[scalar] + [far] * 3,
         scratch_shapes=[pltpu.VMEM((parts, size, LANES), BF16)]
         + [pltpu.VMEM((length, channels), BF16)] * 3
-        + [pltpu.SemaphoreType.DMA((3,))],
+        + [pltpu.SemaphoreType.DMA((3 * parts // 2,))],
         compiler_params=large,
     )(index, key_stream[0], value_stream[0], filter_taps[0])
     slabs = [sent[0]] + [joint_shift(sent[n], 0, n) for n in range(1, parts)]

time: 71.2 us -> 71.2 us (level)
  Pallas kernels: 16.2 us -> 15 us
  waiting for transfers between devices: 15.9 us -> 17 us
    pallas_call x1, Pallas kernels: 3.53 us -> 2.35 us  [convolved(): pl.pallas_call(functools.partial(back_kernel, parts, outer), out_shape=bl...]
    all_to_all x1, waiting for transfers between devices: 3.81 us -> 4.95 us  [fast_on_device(): q = lax.all_to_all(q, 'ctx', split_axis=0, concat_axis=0, tiled=True)]
  transfers between devices with their start and end apart: 16 -> 16, of which waited for: 6 -> 6; matrix products, arithmetic and copies ran while one was open for 0% -> 0% of each run, Pallas kernels for 17% -> 15%
where the time goes in v11:
time: 71.2 us; the launch traced here: 70.9 us
  starting transfers between devices  37 us (52%)
  waiting for transfers between devices  17 us (24%)
  Pallas kernels  15 us (21%)
  local copies, waits for them, and re-layouts  1.78 us (2%)
    ppermute x15, starting transfers between devices, joint_shift(): return lax.ppermute(value, ('segment', 'ctx'), pairs)  24.7 us
    all_to_all x1, starting transfers between devices, fast_on_device(): q = lax.all_to_all(q, 'ctx', split_axis=0, concat_axis=0, tiled=True)  12.2 us
    ppermute x15, waiting for transfers between devices, joint_shift(): return lax.ppermute(value, ('segment', 'ctx'), pairs)  12.1 us
    all_to_all x1, waiting for transfers between devices, fast_on_device(): q = lax.all_to_all(q, 'ctx', split_axis=0, concat_axis=0, tiled=True)  4.95 us
    pallas_call x1, Pallas kernels, convolved(): pl.pallas_call(functools.partial(middle_kernel, outer), out_shape=block(I...  3.57 us
    pallas_call x1, Pallas kernels, fast_on_device(): pl.pallas_call(functools.partial(pack_kernel, parts), out_shape=(block(si...  3.15 us
    pallas_call x1, Pallas kernels, convolved(): pl.pallas_call(functools.partial(forward_kernel, parts, outer), out_shape...  2.7 us
    pallas_call x1, Pallas kernels, convolved(): pl.pallas_call(functools.partial(back_kernel, parts, outer), out_shape=bl...  2.35 us
  transfers between devices with their start and end apart: 16, of which 6 were waited for; matrix products, arithmetic and copies ran while one was open for 0% of the time, Pallas kernels for 15%

profile of v11, /device:TPU:0, one launch (start us, length us, event | category | flops | bytes accessed | tf_op | source)
XLA Modules:
  0.0 70.9 jit_solution(5219017586312820430)
XLA Ops:
  0.0 3.1 %shard_map.109 = (bf16[528,128]{1,0:T(8,128)(2,1)}, bf16[528,128]{1,0:T(8,128)(2,1)}, bf16[528,128]{1,0:T(8,128)(2,1)}, bf16[528,128]{1,0:T(8,128)(2,1)}, bf16[5...) custom-call(s32[1]{0:T(128)} %bitcast.index_ref, ...), custom_call_target="tpu_custom_call" | custom-call | tf_op jit(solution)/shard_map/pallas_call | solution.py:438
  3.2 3.0 %collective-permute-start = (bf16[528,128]{1,0:T(8,128)(2,1)}, bf16[528,128]{1,0:T(8,128)(2,1)S(1)}, u32[]{:S(2)}, u32[]{:S(2)}) collective-permute-start(bf16[528,128]{1,0:T(8,128)(2,1)} %get-tuple-element.28), channel_id=1, source_target_pairs={{0,1},{1,2},{2,3},{3,4},{4,5},{5,6},{6,7},{7,0},{8,9},{9,10},{10,1... | collective-permute-start | bytes 405512 | tf_op jit(solution)/shard_map/ppermute | solution.py:388
  6.2 1.6 %collective-permute-start.1 = (bf16[528,128]{1,0:T(8,128)(2,1)}, bf16[528,128]{1,0:T(8,128)(2,1)S(1)}, u32[]{:S(2)}, u32[]{:S(2)}) collective-permute-start(bf16[528,128]{1,0:T(8,128)(2,1)} %get-tuple-element.29), channel_id=1, source_target_pairs={{0,2},{1,3},{2,4},{3,5},{4,6},{5,7},{6,0},{7,1},{8,10},{9,11},{10,... | collective-permute-start | bytes 405512 | tf_op jit(solution)/shard_map/ppermute | solution.py:388
  7.8 2.5 %collective-permute-start.2 = (bf16[528,128]{1,0:T(8,128)(2,1)}, bf16[528,128]{1,0:T(8,128)(2,1)S(1)}, u32[]{:S(2)}, u32[]{:S(2)}) collective-permute-start(bf16[528,128]{1,0:T(8,128)(2,1)} %get-tuple-element.30), channel_id=1, source_target_pairs={{0,3},{1,4},{2,5},{3,6},{4,7},{5,0},{6,1},{7,2},{8,11},{9,12},{10,... | collective-permute-start | bytes 405512 | tf_op jit(solution)/shard_map/ppermute | solution.py:388
  10.3 1.2 %collective-permute-start.3 = (bf16[528,128]{1,0:T(8,128)(2,1)}, bf16[528,128]{1,0:T(8,128)(2,1)S(1)}, u32[]{:S(2)}, u32[]{:S(2)}) collective-permute-start(bf16[528,128]{1,0:T(8,128)(2,1)} %get-tuple-element.31), channel_id=1, source_target_pairs={{0,4},{1,5},{2,6},{3,7},{4,0},{5,1},{6,2},{7,3},{8,12},{9,13},{10,... | collective-permute-start | bytes 405512 | tf_op jit(solution)/shard_map/ppermute | solution.py:388
  11.5 2.6 %collective-permute-start.4 = (bf16[528,128]{1,0:T(8,128)(2,1)}, bf16[528,128]{1,0:T(8,128)(2,1)S(1)}, u32[]{:S(2)}, u32[]{:S(2)}) collective-permute-start(bf16[528,128]{1,0:T(8,128)(2,1)} %get-tuple-element.32), channel_id=1, source_target_pairs={{0,5},{1,6},{2,7},{3,0},{4,1},{5,2},{6,3},{7,4},{8,13},{9,14},{10,... | collective-permute-start | bytes 405512 | tf_op jit(solution)/shard_map/ppermute | solution.py:388
  14.2 1.7 %collective-permute-start.5 = (bf16[528,128]{1,0:T(8,128)(2,1)}, bf16[528,128]{1,0:T(8,128)(2,1)S(1)}, u32[]{:S(2)}, u32[]{:S(2)}) collective-permute-start(bf16[528,128]{1,0:T(8,128)(2,1)} %get-tuple-element.33), channel_id=1, source_target_pairs={{0,6},{1,7},{2,0},{3,1},{4,2},{5,3},{6,4},{7,5},{8,14},{9,15},{10,... | collective-permute-start | bytes 405512 | tf_op jit(solution)/shard_map/ppermute | solution.py:388
  15.9 2.1 %collective-permute-start.6 = (bf16[528,128]{1,0:T(8,128)(2,1)}, bf16[528,128]{1,0:T(8,128)(2,1)S(1)}, u32[]{:S(2)}, u32[]{:S(2)}) collective-permute-start(bf16[528,128]{1,0:T(8,128)(2,1)} %get-tuple-element.34), channel_id=1, source_target_pairs={{0,7},{1,0},{2,1},{3,2},{4,3},{5,4},{6,5},{7,6},{8,15},{9,8},{10,9... | collective-permute-start | bytes 405512 | tf_op jit(solution)/shard_map/ppermute | solution.py:388
  18.0 2.1 %shard_map.114 = bf16[8,256,128]{2,1,0:T(8,128)(2,1)} custom-call(bf16[512,512]{1,0:T(8,128)(2,1)} %bitcast.9), custom_call_target="tpu_custom_call" | custom-call | tf_op jit(solution)/shard_map/pallas_call | solution.py:448
  20.0 0.9 %copy-done.2 = bf16[528,128]{1,0:T(8,128)(2,1)S(1)} copy-done((bf16[528,128]{1,0:T(8,128)(2,1)S(1)}, bf16[528,128]{1,0:T(8,128)(2,1)}, u32[]{:S(2)}) %copy-start.2) | copy-done | bytes 135192
  21.0 0.8 %copy-done.6 = bf16[128,192]{1,0:T(8,128)(2,1)S(1)} copy-done((bf16[128,192]{1,0:T(8,128)(2,1)S(1)}, bf16[128,192]{1,0:T(8,128)(2,1)}, u32[]{:S(2)}) %copy-start.6) | copy-done | bytes 49176
  21.8 2.9 %collective-permute-done.2.refs_3_ = bf16[528,128]{1,0:T(8,128)(2,1)S(1)} collective-permute-done((bf16[528,128]{1,0:T(8,128)(2,1)}, bf16[528,128]{1,0:T(8,128)(2,1)S(1)}, u32[]{:S(2)}, u32[]{:S(2)}) %collective-permute-start.2) | collective-permute-done | bytes 135200 | tf_op jit(solution)/shard_map/ppermute | solution.py:388
  24.7 0.4 collective-permute-done.3.refs_4_
  25.1 0.1 collective-permute-done.6.refs_7_
  25.2 12.2 %all-to-all-start = ((bf16[8,256,128]{2,1,0:T(8,128)(2,1)}), bf16[8,256,128]{2,1,0:T(8,128)(2,1)S(1)}, u32[]{:S(2)}, u32[]{:S(2)}) async-start(bf16[8,256,128]{2,1,0:T(8,128)(2,1)} %shard_map.114), calls=%async_computation | async-start | bytes 1048576 | tf_op jit(solution)/shard_map/all_to_all | solution.py:465
  37.4 0.0 copy-start
  37.4 0.0 copy-start.4
  37.4 2.7 %shard_map.111 = (f32[8704,128]{1,0:T(8,128)S(1)}, f32[8,256,128]{2,1,0:T(8,128)S(1)}) custom-call(s32[1]{0:T(128)} %bitcast.index_ref, bf16[528,128]{1,0:T(8,128)(2,1)S(1)} %get-tuple-element.27.refs_0_, bf16[528,128]{1,0:T(8,128)(2,1)S(1)} %collective-permute-done.refs_1_, bf16[528,128]{1,0:T(8,128)(2,1)S(1)} %collective-permute-done.1.refs_2_, ...), custom_call_target="tpu_custom_call" | custom-call | tf_op jit(solution)/shard_map/pallas_call | solution.py:401
  40.2 3.6 %shard_map.112.w_s = f32[4608,128]{1,0:T(8,128)S(1)} custom-call(f32[8704,128]{1,0:T(8,128)S(1)} %get-tuple-element.36.z_s, bf16[128,384]{1,0:T(8,128)(2,1)S(1)} %copy-done.3, bf16[128,192]{1,0:T(8,128)(2,1)S(1)} %copy-done.5), custom_call_target="tpu_custom_call" | custom-call | tf_op jit(solution)/shard_map/pallas_call | solution.py:408
  43.8 2.4 %shard_map.113.y_ref = f32[8,256,128]{2,1,0:T(8,128)S(1)} custom-call(s32[1]{0:T(128)} %bitcast.index_ref, f32[1,512]{1,0:T(1,128)S(1)} %copy-done.7, f32[4608,128]{1,0:T(8,128)S(1)} %shard_map.112.w_s, f32[8,256,128]{2,1,0:T(8,128)S(1)} %get-tuple-element.37.p_s, bf16[128,192]{1,0:T(8,128)(2,1)S(1)} %copy-done.4, f32[64,2,64,128]{3,2,1,0:T(8,128)S(1)} %copy-done), custom_call_target="tpu_custom_call" | custom-call | tf_op jit(solution)/shard_map/pallas_call | solution.py:413
  46.1 5.0 %all-to-all-done.q_ref = bf16[8,256,128]{2,1,0:T(8,128)(2,1)S(1)} async-done(((bf16[8,256,128]{2,1,0:T(8,128)(2,1)}), bf16[8,256,128]{2,1,0:T(8,128)(2,1)S(1)}, u32[]{:S(2)}, u32[]{:S(2)}) %all-to-all-start) | async-done | bytes 524320 | tf_op jit(solution)/shard_map/all_to_all | solution.py:465
  51.1 0.1 shard_map.115
  51.2 0.1 collective-permute-start.7
  51.2 3.6 %collective-permute-start.8 = (bf16[256,128]{1,0:T(8,128)(2,1)S(1)}, bf16[256,128]{1,0:T(8,128)(2,1)S(1)}, u32[]{:S(2)}, u32[]{:S(2)}) collective-permute-start(bf16[256,128]{1,0:T(8,128)(2,1)S(1)} %get-tuple-element.40), channel_id=1, source_target_pairs={{0,15},{1,8},{2,9},{3,10},{4,11},{5,12},{6,13},{7,14},{8,23},{9,16... | collective-permute-start | bytes 196616 | tf_op jit(solution)/shard_map/ppermute | solution.py:388
  54.8 1.0 %collective-permute-start.10 = (bf16[256,128]{1,0:T(8,128)(2,1)S(1)}, bf16[256,128]{1,0:T(8,128)(2,1)S(1)}, u32[]{:S(2)}, u32[]{:S(2)}) collective-permute-start(bf16[256,128]{1,0:T(8,128)(2,1)S(1)} %get-tuple-element.42), channel_id=1, source_target_pairs={{0,13},{1,14},{2,15},{3,8},{4,9},{5,10},{6,11},{7,12},{8,21},{9,22... | collective-permute-start | bytes 196616 | tf_op jit(solution)/shard_map/ppermute | solution.py:388
  55.8 1.6 %collective-permute-start.11 = (bf16[256,128]{1,0:T(8,128)(2,1)S(1)}, bf16[256,128]{1,0:T(8,128)(2,1)S(1)}, u32[]{:S(2)}, u32[]{:S(2)}) collective-permute-start(bf16[256,128]{1,0:T(8,128)(2,1)S(1)} %get-tuple-element.43), channel_id=1, source_target_pairs={{0,12},{1,13},{2,14},{3,15},{4,8},{5,9},{6,10},{7,11},{8,20},{9,21... | collective-permute-start | bytes 196616 | tf_op jit(solution)/shard_map/ppermute | solution.py:388
  57.4 2.6 %collective-permute-start.12 = (bf16[256,128]{1,0:T(8,128)(2,1)S(1)}, bf16[256,128]{1,0:T(8,128)(2,1)S(1)}, u32[]{:S(2)}, u32[]{:S(2)}) collective-permute-start(bf16[256,128]{1,0:T(8,128)(2,1)S(1)} %get-tuple-element.44), channel_id=1, source_target_pairs={{0,11},{1,12},{2,13},{3,14},{4,15},{5,8},{6,9},{7,10},{8,19},{9,20... | collective-permute-start | bytes 196616 | tf_op jit(solution)/shard_map/ppermute | solution.py:388
  60.1 0.0 collective-permute-start.13
  60.1 1.0 %collective-permute-start.14 = (bf16[256,128]{1,0:T(8,128)(2,1)S(1)}, bf16[256,128]{1,0:T(8,128)(2,1)S(1)}, u32[]{:S(2)}, u32[]{:S(2)}) collective-permute-start(bf16[256,128]{1,0:T(8,128)(2,1)S(1)} %get-tuple-element.46), channel_id=1, source_target_pairs={{0,9},{1,10},{2,11},{3,12},{4,13},{5,14},{6,15},{7,8},{8,17},{9,18... | collective-permute-start | bytes 196616 | tf_op jit(solution)/shard_map/ppermute | solution.py:388
  61.1 6.7 %collective-permute-done.11.refs_4_ = bf16[256,128]{1,0:T(8,128)(2,1)S(1)} collective-permute-done((bf16[256,128]{1,0:T(8,128)(2,1)S(1)}, bf16[256,128]{1,0:T(8,128)(2,1)S(1)}, u32[]{:S(2)}, u32[]{:S(2)}) %collective-permute-start.11) | collective-permute-done | bytes 65568 | tf_op jit(solution)/shard_map/ppermute | solution.py:388
  67.9 1.9 %collective-permute-done.12.refs_5_ = bf16[256,128]{1,0:T(8,128)(2,1)S(1)} collective-permute-done((bf16[256,128]{1,0:T(8,128)(2,1)S(1)}, bf16[256,128]{1,0:T(8,128)(2,1)S(1)}, u32[]{:S(2)}, u32[]{:S(2)}) %collective-permute-start.12) | collective-permute-done | bytes 65568 | tf_op jit(solution)/shard_map/ppermute | solution.py:388
  69.8 1.0 %shard_map.116 = bf16[512,512]{1,0:T(8,128)(2,1)} custom-call(s32[1]{0:T(128)} %bitcast.index_ref, bf16[256,128]{1,0:T(8,128)(2,1)S(1)} %collective-permute-done.7.refs_0_, bf16[256,128]{1,0:T(8,128)(2,1)S(1)} %collective-permute-done.8.refs_1_, bf16[256,128]{1,0:T(8,128)(2,1)S(1)} %collective-permute-done.9.refs_2_, ...), custom_call_target="tpu_custom_call" | custom-call | tf_op jit(solution)/shard_map/pallas_call | solution.py:474
  (24 shorter events, 0.1 us)
Async XLA Ops:
  0.0 37.4 %copy-start.1 = (f32[20,2,64,128]{3,2,1,0:T(8,128)S(1)}, f32[20,2,64,128]{3,2,1,0:T(8,128)}, u32[]{:S(2)}) copy-start(f32[20,2,64,128]{3,2,1,0:T(8,128)} %constant.21.clone.refs_9_) | copy-start | bytes 3932164
  0.0 40.1 %copy-start.5 = (bf16[128,192]{1,0:T(8,128)(2,1)S(1)}, bf16[128,192]{1,0:T(8,128)(2,1)}, u32[]{:S(2)}) copy-start(bf16[128,192]{1,0:T(8,128)(2,1)} %constant.18.clone.back_ref) | copy-start | bytes 147460
  0.0 40.1 %copy-start.3 = (bf16[128,384]{1,0:T(8,128)(2,1)S(1)}, bf16[128,384]{1,0:T(8,128)(2,1)}, u32[]{:S(2)}) copy-start(bf16[128,384]{1,0:T(8,128)(2,1)} %constant.17.clone.forward_ref) | copy-start | bytes 294916
  3.2 11.0 %collective-permute-start = (bf16[528,128]{1,0:T(8,128)(2,1)}, bf16[528,128]{1,0:T(8,128)(2,1)S(1)}, u32[]{:S(2)}, u32[]{:S(2)}) collective-permute-start(bf16[528,128]{1,0:T(8,128)(2,1)} %get-tuple-element.28), channel_id=1, source_target_pairs={{0,1},{1,2},{2,3},{3,4},{4,5},{5,6},{6,7},{7,0},{8,9},{9,10},{10,1... | collective-permute-start | bytes 405512 | tf_op jit(solution)/shard_map/ppermute | solution.py:388
  6.2 9.7 %collective-permute-start.1 = (bf16[528,128]{1,0:T(8,128)(2,1)}, bf16[528,128]{1,0:T(8,128)(2,1)S(1)}, u32[]{:S(2)}, u32[]{:S(2)}) collective-permute-start(bf16[528,128]{1,0:T(8,128)(2,1)} %get-tuple-element.29), channel_id=1, source_target_pairs={{0,2},{1,3},{2,4},{3,5},{4,6},{5,7},{6,0},{7,1},{8,10},{9,11},{10,... | collective-permute-start | bytes 405512 | tf_op jit(solution)/shard_map/ppermute | solution.py:388
  7.8 16.9 %collective-permute-start.2 = (bf16[528,128]{1,0:T(8,128)(2,1)}, bf16[528,128]{1,0:T(8,128)(2,1)S(1)}, u32[]{:S(2)}, u32[]{:S(2)}) collective-permute-start(bf16[528,128]{1,0:T(8,128)(2,1)} %get-tuple-element.30), channel_id=1, source_target_pairs={{0,3},{1,4},{2,5},{3,6},{4,7},{5,0},{6,1},{7,2},{8,11},{9,12},{10,... | collective-permute-start | bytes 405512 | tf_op jit(solution)/shard_map/ppermute | solution.py:388
  10.3 14.8 %collective-permute-start.3 = (bf16[528,128]{1,0:T(8,128)(2,1)}, bf16[528,128]{1,0:T(8,128)(2,1)S(1)}, u32[]{:S(2)}, u32[]{:S(2)}) collective-permute-start(bf16[528,128]{1,0:T(8,128)(2,1)} %get-tuple-element.31), channel_id=1, source_target_pairs={{0,4},{1,5},{2,6},{3,7},{4,0},{5,1},{6,2},{7,3},{8,12},{9,13},{10,... | collective-permute-start | bytes 405512 | tf_op jit(solution)/shard_map/ppermute | solution.py:388
  11.5 13.6 %collective-permute-start.4 = (bf16[528,128]{1,0:T(8,128)(2,1)}, bf16[528,128]{1,0:T(8,128)(2,1)S(1)}, u32[]{:S(2)}, u32[]{:S(2)}) collective-permute-start(bf16[528,128]{1,0:T(8,128)(2,1)} %get-tuple-element.32), channel_id=1, source_target_pairs={{0,5},{1,6},{2,7},{3,0},{4,1},{5,2},{6,3},{7,4},{8,13},{9,14},{10,... | collective-permute-start | bytes 405512 | tf_op jit(solution)/shard_map/ppermute | solution.py:388
  14.2 10.9 %collective-permute-start.5 = (bf16[528,128]{1,0:T(8,128)(2,1)}, bf16[528,128]{1,0:T(8,128)(2,1)S(1)}, u32[]{:S(2)}, u32[]{:S(2)}) collective-permute-start(bf16[528,128]{1,0:T(8,128)(2,1)} %get-tuple-element.33), channel_id=1, source_target_pairs={{0,6},{1,7},{2,0},{3,1},{4,2},{5,3},{6,4},{7,5},{8,14},{9,15},{10,... | collective-permute-start | bytes 405512 | tf_op jit(solution)/shard_map/ppermute | solution.py:388
  15.9 9.3 %collective-permute-start.6 = (bf16[528,128]{1,0:T(8,128)(2,1)}, bf16[528,128]{1,0:T(8,128)(2,1)S(1)}, u32[]{:S(2)}, u32[]{:S(2)}) collective-permute-start(bf16[528,128]{1,0:T(8,128)(2,1)} %get-tuple-element.34), channel_id=1, source_target_pairs={{0,7},{1,0},{2,1},{3,2},{4,3},{5,4},{6,5},{7,6},{8,15},{9,8},{10,9... | collective-permute-start | bytes 405512 | tf_op jit(solution)/shard_map/ppermute | solution.py:388
  20.0 0.9 %copy-start.2 = (bf16[528,128]{1,0:T(8,128)(2,1)S(1)}, bf16[528,128]{1,0:T(8,128)(2,1)}, u32[]{:S(2)}) copy-start(bf16[528,128]{1,0:T(8,128)(2,1)} %get-tuple-element.26.refs_0_) | copy-start | bytes 405508
  21.0 0.8 %copy-start.6 = (bf16[128,192]{1,0:T(8,128)(2,1)S(1)}, bf16[128,192]{1,0:T(8,128)(2,1)}, u32[]{:S(2)}) copy-start(bf16[128,192]{1,0:T(8,128)(2,1)} %constant.16.clone.refs_1_) | copy-start | bytes 147460
  25.2 25.9 %all-to-all-start = ((bf16[8,256,128]{2,1,0:T(8,128)(2,1)}), bf16[8,256,128]{2,1,0:T(8,128)(2,1)S(1)}, u32[]{:S(2)}, u32[]{:S(2)}) async-start(bf16[8,256,128]{2,1,0:T(8,128)(2,1)} %shard_map.114), calls=%async_computation | async-start | bytes 1048576 | tf_op jit(solution)/shard_map/all_to_all | solution.py:465
  37.4 6.3 %copy-start = (f32[64,2,64,128]{3,2,1,0:T(8,128)S(1)}, f32[64,2,64,128]{3,2,1,0:T(8,128)}, u32[]{:S(2)}) copy-start(f32[64,2,64,128]{3,2,1,0:T(8,128)} %constant.20.clone.refs_1_) | copy-start | bytes 12582916
  37.4 6.3 %copy-start.4 = (bf16[128,192]{1,0:T(8,128)(2,1)S(1)}, bf16[128,192]{1,0:T(8,128)(2,1)}, u32[]{:S(2)}) copy-start(bf16[128,192]{1,0:T(8,128)(2,1)} %constant.19.clone.refs_0_) | copy-start | bytes 147460
  37.4 6.3 %copy-start.7 = (f32[1,512]{1,0:T(1,128)S(1)}, f32[1,512]{1,0:T(1,128)}, u32[]{:S(2)}) copy-start(f32[1,512]{1,0:T(1,128)} %skip_ref.1) | copy-start | bytes 6148
  51.2 6.2 %collective-permute-start.7 = (bf16[256,128]{1,0:T(8,128)(2,1)S(1)}, bf16[256,128]{1,0:T(8,128)(2,1)S(1)}, u32[]{:S(2)}, u32[]{:S(2)}) collective-permute-start(bf16[256,128]{1,0:T(8,128)(2,1)S(1)} %get-tuple-element.39), channel_id=1, source_target_pairs={{0,8},{1,9},{2,10},{3,11},{4,12},{5,13},{6,14},{7,15},{8,16},{9,17... | collective-permute-start | bytes 196616 | tf_op jit(solution)/shard_map/ppermute | solution.py:388
  51.2 8.8 %collective-permute-start.8 = (bf16[256,128]{1,0:T(8,128)(2,1)S(1)}, bf16[256,128]{1,0:T(8,128)(2,1)S(1)}, u32[]{:S(2)}, u32[]{:S(2)}) collective-permute-start(bf16[256,128]{1,0:T(8,128)(2,1)S(1)} %get-tuple-element.40), channel_id=1, source_target_pairs={{0,15},{1,8},{2,9},{3,10},{4,11},{5,12},{6,13},{7,14},{8,23},{9,16... | collective-permute-start | bytes 196616 | tf_op jit(solution)/shard_map/ppermute | solution.py:388
  54.8 5.3 %collective-permute-start.9 = (bf16[256,128]{1,0:T(8,128)(2,1)S(1)}, bf16[256,128]{1,0:T(8,128)(2,1)S(1)}, u32[]{:S(2)}, u32[]{:S(2)}) collective-permute-start(bf16[256,128]{1,0:T(8,128)(2,1)S(1)} %get-tuple-element.41), channel_id=1, source_target_pairs={{0,14},{1,15},{2,8},{3,9},{4,10},{5,11},{6,12},{7,13},{8,22},{9,23... | collective-permute-start | bytes 196616 | tf_op jit(solution)/shard_map/ppermute | solution.py:388
  54.8 6.3 %collective-permute-start.10 = (bf16[256,128]{1,0:T(8,128)(2,1)S(1)}, bf16[256,128]{1,0:T(8,128)(2,1)S(1)}, u32[]{:S(2)}, u32[]{:S(2)}) collective-permute-start(bf16[256,128]{1,0:T(8,128)(2,1)S(1)} %get-tuple-element.42), channel_id=1, source_target_pairs={{0,13},{1,14},{2,15},{3,8},{4,9},{5,10},{6,11},{7,12},{8,21},{9,22... | collective-permute-start | bytes 196616 | tf_op jit(solution)/shard_map/ppermute | solution.py:388
  55.8 12.1 %collective-permute-start.11 = (bf16[256,128]{1,0:T(8,128)(2,1)S(1)}, bf16[256,128]{1,0:T(8,128)(2,1)S(1)}, u32[]{:S(2)}, u32[]{:S(2)}) collective-permute-start(bf16[256,128]{1,0:T(8,128)(2,1)S(1)} %get-tuple-element.43), channel_id=1, source_target_pairs={{0,12},{1,13},{2,14},{3,15},{4,8},{5,9},{6,10},{7,11},{8,20},{9,21... | collective-permute-start | bytes 196616 | tf_op jit(solution)/shard_map/ppermute | solution.py:388
  57.4 12.4 %collective-permute-start.12 = (bf16[256,128]{1,0:T(8,128)(2,1)S(1)}, bf16[256,128]{1,0:T(8,128)(2,1)S(1)}, u32[]{:S(2)}, u32[]{:S(2)}) collective-permute-start(bf16[256,128]{1,0:T(8,128)(2,1)S(1)} %get-tuple-element.44), channel_id=1, source_target_pairs={{0,11},{1,12},{2,13},{3,14},{4,15},{5,8},{6,9},{7,10},{8,19},{9,20... | collective-permute-start | bytes 196616 | tf_op jit(solution)/shard_map/ppermute | solution.py:388
  60.1 9.8 %collective-permute-start.13 = (bf16[256,128]{1,0:T(8,128)(2,1)S(1)}, bf16[256,128]{1,0:T(8,128)(2,1)S(1)}, u32[]{:S(2)}, u32[]{:S(2)}) collective-permute-start(bf16[256,128]{1,0:T(8,128)(2,1)S(1)} %get-tuple-element.45), channel_id=1, source_target_pairs={{0,10},{1,11},{2,12},{3,13},{4,14},{5,15},{6,8},{7,9},{8,18},{9,19... | collective-permute-start | bytes 196616 | tf_op jit(solution)/shard_map/ppermute | solution.py:388
  60.1 9.7 %collective-permute-start.14 = (bf16[256,128]{1,0:T(8,128)(2,1)S(1)}, bf16[256,128]{1,0:T(8,128)(2,1)S(1)}, u32[]{:S(2)}, u32[]{:S(2)}) collective-permute-start(bf16[256,128]{1,0:T(8,128)(2,1)S(1)} %get-tuple-element.46), channel_id=1, source_target_pairs={{0,9},{1,10},{2,11},{3,12},{4,13},{5,14},{6,15},{7,8},{8,17},{9,18... | collective-permute-start | bytes 196616 | tf_op jit(solution)/shard_map/ppermute | solution.py:388

commit v12 on v11

--- a/solution.py
+++ b/solution.py
@@ -229,11 +229,15 @@
         target[...] = source[...]
 
 
+def longest_first(parts):
+    return sorted(range(parts), key=lambda n: abs(n - parts // 2))
+
+
 def unpack_kernel(parts, index_ref, *refs):
     blocks, out_ref, held = refs[:parts], refs[parts], refs[parts + 1]
     rows = held.shape[1]
     low = lower_half((rows, LANES))
-    for n, block in enumerate(blocks):
+    for n, block in zip(longest_first(parts), blocks):
         held[lax.rem(index_ref[0] + n, parts)] = block[...]
     for e in range(parts // 2):
         even, odd = held[2 * e].astype(F32), held[2 * e + 1].astype(F32)
@@ -470,7 +474,7 @@
         in_specs=[scalar, whole, whole],
         compiler_params=small,
     )(index, y, q)
-    gated = [joint_shift(gated[n], 1, -n) for n in range(parts)]
+    gated = [joint_shift(gated[n], 1, -n) for n in longest_first(parts)]
     out = pl.pallas_call(
         functools.partial(unpack_kernel, parts),
         out_shape=block(length, channels),

time: 71.2 us -> 71.4 us (level)
  starting transfers between devices: 37 us -> 40.2 us
  waiting for transfers between devices: 17 us -> 13.9 us
    ppermute x15, starting transfers between devices: 24.7 us -> 28 us  [joint_shift(): return lax.ppermute(value, ('segment', 'ctx'), pairs)]
    ppermute x15, waiting for transfers between devices: 12.1 us -> 8.99 us  [joint_shift(): return lax.ppermute(value, ('segment', 'ctx'), pairs)]
  transfers between devices with their start and end apart: 16 -> 16, of which waited for: 6 -> 7; matrix products, arithmetic and copies ran while one was open for 0% -> 0% of each run, Pallas kernels for 15% -> 15%
where the time goes in v12:
time: 71.4 us; the launch traced here: 71.1 us
  starting transfers between devices  40.2 us (56%)
  Pallas kernels  15 us (21%)
  waiting for transfers between devices  13.9 us (19%)
  local copies, waits for them, and re-layouts  1.78 us (2%)
    ppermute x15, starting transfers between devices, joint_shift(): return lax.ppermute(value, ('segment', 'ctx'), pairs)  28 us
    all_to_all x1, starting transfers between devices, fast_on_device(): q = lax.all_to_all(q, 'ctx', split_axis=0, concat_axis=0, tiled=True)  12.2 us
    ppermute x15, waiting for transfers between devices, joint_shift(): return lax.ppermute(value, ('segment', 'ctx'), pairs)  8.99 us
    all_to_all x1, waiting for transfers between devices, fast_on_device(): q = lax.all_to_all(q, 'ctx', split_axis=0, concat_axis=0, tiled=True)  4.95 us
    pallas_call x1, Pallas kernels, convolved(): pl.pallas_call(functools.partial(middle_kernel, outer), out_shape=block(I...  3.57 us
    pallas_call x1, Pallas kernels, fast_on_device(): pl.pallas_call(functools.partial(pack_kernel, parts), out_shape=(block(si...  3.15 us
    pallas_call x1, Pallas kernels, convolved(): pl.pallas_call(functools.partial(forward_kernel, parts, outer), out_shape...  2.7 us
    pallas_call x1, Pallas kernels, convolved(): pl.pallas_call(functools.partial(back_kernel, parts, outer), out_shape=bl...  2.35 us
  transfers between devices with their start and end apart: 16, of which 7 were waited for; matrix products, arithmetic and copies ran while one was open for 0% of the time, Pallas kernels for 15%

profile of v12, /device:TPU:0, one launch (start us, length us, event | category | flops | bytes accessed | tf_op | source)
XLA Modules:
  0.0 71.1 jit_solution(3932343480325543796)
XLA Ops:
  0.0 3.1 %shard_map.109 = (bf16[528,128]{1,0:T(8,128)(2,1)}, bf16[528,128]{1,0:T(8,128)(2,1)}, bf16[528,128]{1,0:T(8,128)(2,1)}, bf16[528,128]{1,0:T(8,128)(2,1)}, bf16[5...) custom-call(s32[1]{0:T(128)} %bitcast.index_ref, ...), custom_call_target="tpu_custom_call" | custom-call | tf_op jit(solution)/shard_map/pallas_call | solution.py:442
  3.2 3.0 %collective-permute-start = (bf16[528,128]{1,0:T(8,128)(2,1)}, bf16[528,128]{1,0:T(8,128)(2,1)S(1)}, u32[]{:S(2)}, u32[]{:S(2)}) collective-permute-start(bf16[528,128]{1,0:T(8,128)(2,1)} %get-tuple-element.28), channel_id=1, source_target_pairs={{0,1},{1,2},{2,3},{3,4},{4,5},{5,6},{6,7},{7,0},{8,9},{9,10},{10,1... | collective-permute-start | bytes 405512 | tf_op jit(solution)/shard_map/ppermute | solution.py:392
  6.2 1.6 %collective-permute-start.1 = (bf16[528,128]{1,0:T(8,128)(2,1)}, bf16[528,128]{1,0:T(8,128)(2,1)S(1)}, u32[]{:S(2)}, u32[]{:S(2)}) collective-permute-start(bf16[528,128]{1,0:T(8,128)(2,1)} %get-tuple-element.29), channel_id=1, source_target_pairs={{0,2},{1,3},{2,4},{3,5},{4,6},{5,7},{6,0},{7,1},{8,10},{9,11},{10,... | collective-permute-start | bytes 405512 | tf_op jit(solution)/shard_map/ppermute | solution.py:392
  7.8 2.5 %collective-permute-start.2 = (bf16[528,128]{1,0:T(8,128)(2,1)}, bf16[528,128]{1,0:T(8,128)(2,1)S(1)}, u32[]{:S(2)}, u32[]{:S(2)}) collective-permute-start(bf16[528,128]{1,0:T(8,128)(2,1)} %get-tuple-element.30), channel_id=1, source_target_pairs={{0,3},{1,4},{2,5},{3,6},{4,7},{5,0},{6,1},{7,2},{8,11},{9,12},{10,... | collective-permute-start | bytes 405512 | tf_op jit(solution)/shard_map/ppermute | solution.py:392
  10.3 1.2 %collective-permute-start.3 = (bf16[528,128]{1,0:T(8,128)(2,1)}, bf16[528,128]{1,0:T(8,128)(2,1)S(1)}, u32[]{:S(2)}, u32[]{:S(2)}) collective-permute-start(bf16[528,128]{1,0:T(8,128)(2,1)} %get-tuple-element.31), channel_id=1, source_target_pairs={{0,4},{1,5},{2,6},{3,7},{4,0},{5,1},{6,2},{7,3},{8,12},{9,13},{10,... | collective-permute-start | bytes 405512 | tf_op jit(solution)/shard_map/ppermute | solution.py:392
  11.5 2.6 %collective-permute-start.4 = (bf16[528,128]{1,0:T(8,128)(2,1)}, bf16[528,128]{1,0:T(8,128)(2,1)S(1)}, u32[]{:S(2)}, u32[]{:S(2)}) collective-permute-start(bf16[528,128]{1,0:T(8,128)(2,1)} %get-tuple-element.32), channel_id=1, source_target_pairs={{0,5},{1,6},{2,7},{3,0},{4,1},{5,2},{6,3},{7,4},{8,13},{9,14},{10,... | collective-permute-start | bytes 405512 | tf_op jit(solution)/shard_map/ppermute | solution.py:392
  14.2 1.7 %collective-permute-start.5 = (bf16[528,128]{1,0:T(8,128)(2,1)}, bf16[528,128]{1,0:T(8,128)(2,1)S(1)}, u32[]{:S(2)}, u32[]{:S(2)}) collective-permute-start(bf16[528,128]{1,0:T(8,128)(2,1)} %get-tuple-element.33), channel_id=1, source_target_pairs={{0,6},{1,7},{2,0},{3,1},{4,2},{5,3},{6,4},{7,5},{8,14},{9,15},{10,... | collective-permute-start | bytes 405512 | tf_op jit(solution)/shard_map/ppermute | solution.py:392
  15.9 2.1 %collective-permute-start.6 = (bf16[528,128]{1,0:T(8,128)(2,1)}, bf16[528,128]{1,0:T(8,128)(2,1)S(1)}, u32[]{:S(2)}, u32[]{:S(2)}) collective-permute-start(bf16[528,128]{1,0:T(8,128)(2,1)} %get-tuple-element.34), channel_id=1, source_target_pairs={{0,7},{1,0},{2,1},{3,2},{4,3},{5,4},{6,5},{7,6},{8,15},{9,8},{10,9... | collective-permute-start | bytes 405512 | tf_op jit(solution)/shard_map/ppermute | solution.py:392
  18.0 2.1 %shard_map.114 = bf16[8,256,128]{2,1,0:T(8,128)(2,1)} custom-call(bf16[512,512]{1,0:T(8,128)(2,1)} %bitcast.9), custom_call_target="tpu_custom_call" | custom-call | tf_op jit(solution)/shard_map/pallas_call | solution.py:452
  20.0 0.9 %copy-done.2 = bf16[528,128]{1,0:T(8,128)(2,1)S(1)} copy-done((bf16[528,128]{1,0:T(8,128)(2,1)S(1)}, bf16[528,128]{1,0:T(8,128)(2,1)}, u32[]{:S(2)}) %copy-start.2) | copy-done | bytes 135192
  21.0 0.8 %copy-done.6 = bf16[128,192]{1,0:T(8,128)(2,1)S(1)} copy-done((bf16[128,192]{1,0:T(8,128)(2,1)S(1)}, bf16[128,192]{1,0:T(8,128)(2,1)}, u32[]{:S(2)}) %copy-start.6) | copy-done | bytes 49176
  21.8 2.9 %collective-permute-done.2.refs_3_ = bf16[528,128]{1,0:T(8,128)(2,1)S(1)} collective-permute-done((bf16[528,128]{1,0:T(8,128)(2,1)}, bf16[528,128]{1,0:T(8,128)(2,1)S(1)}, u32[]{:S(2)}, u32[]{:S(2)}) %collective-permute-start.2) | collective-permute-done | bytes 135200 | tf_op jit(solution)/shard_map/ppermute | solution.py:392
  24.7 0.4 collective-permute-done.3.refs_4_
  25.1 0.1 collective-permute-done.6.refs_7_
  25.2 12.2 %all-to-all-start = ((bf16[8,256,128]{2,1,0:T(8,128)(2,1)}), bf16[8,256,128]{2,1,0:T(8,128)(2,1)S(1)}, u32[]{:S(2)}, u32[]{:S(2)}) async-start(bf16[8,256,128]{2,1,0:T(8,128)(2,1)} %shard_map.114), calls=%async_computation | async-start | bytes 1048576 | tf_op jit(solution)/shard_map/all_to_all | solution.py:469
  37.4 0.0 copy-start
  37.4 0.0 copy-start.4
  37.4 0.0 copy-start.7
  37.4 2.7 %shard_map.111 = (f32[8704,128]{1,0:T(8,128)S(1)}, f32[8,256,128]{2,1,0:T(8,128)S(1)}) custom-call(s32[1]{0:T(128)} %bitcast.index_ref, bf16[528,128]{1,0:T(8,128)(2,1)S(1)} %get-tuple-element.27.refs_0_, bf16[528,128]{1,0:T(8,128)(2,1)S(1)} %collective-permute-done.refs_1_, bf16[528,128]{1,0:T(8,128)(2,1)S(1)} %collective-permute-done.1.refs_2_, ...), custom_call_target="tpu_custom_call" | custom-call | tf_op jit(solution)/shard_map/pallas_call | solution.py:405
  40.2 3.6 %shard_map.112.w_s = f32[4608,128]{1,0:T(8,128)S(1)} custom-call(f32[8704,128]{1,0:T(8,128)S(1)} %get-tuple-element.36.z_s, bf16[128,384]{1,0:T(8,128)(2,1)S(1)} %copy-done.3, bf16[128,192]{1,0:T(8,128)(2,1)S(1)} %copy-done.5), custom_call_target="tpu_custom_call" | custom-call | tf_op jit(solution)/shard_map/pallas_call | solution.py:412
  43.8 2.4 %shard_map.113.y_ref = f32[8,256,128]{2,1,0:T(8,128)S(1)} custom-call(s32[1]{0:T(128)} %bitcast.index_ref, f32[1,512]{1,0:T(1,128)S(1)} %copy-done.7, f32[4608,128]{1,0:T(8,128)S(1)} %shard_map.112.w_s, f32[8,256,128]{2,1,0:T(8,128)S(1)} %get-tuple-element.37.p_s, bf16[128,192]{1,0:T(8,128)(2,1)S(1)} %copy-done.4, f32[64,2,64,128]{3,2,1,0:T(8,128)S(1)} %copy-done), custom_call_target="tpu_custom_call" | custom-call | tf_op jit(solution)/shard_map/pallas_call | solution.py:417
  46.1 5.0 %all-to-all-done.q_ref = bf16[8,256,128]{2,1,0:T(8,128)(2,1)S(1)} async-done(((bf16[8,256,128]{2,1,0:T(8,128)(2,1)}), bf16[8,256,128]{2,1,0:T(8,128)(2,1)S(1)}, u32[]{:S(2)}, u32[]{:S(2)}) %all-to-all-start) | async-done | bytes 524320 | tf_op jit(solution)/shard_map/all_to_all | solution.py:469
  51.1 0.1 shard_map.115
  51.2 0.1 collective-permute-start.7
  51.2 4.4 %collective-permute-start.8 = (bf16[256,128]{1,0:T(8,128)(2,1)S(1)}, bf16[256,128]{1,0:T(8,128)(2,1)S(1)}, u32[]{:S(2)}, u32[]{:S(2)}) collective-permute-start(bf16[256,128]{1,0:T(8,128)(2,1)S(1)} %get-tuple-element.40), channel_id=1, source_target_pairs={{0,13},{1,14},{2,15},{3,8},{4,9},{5,10},{6,11},{7,12},{8,21},{9,22... | collective-permute-start | bytes 196616 | tf_op jit(solution)/shard_map/ppermute | solution.py:392
  55.7 3.7 %collective-permute-start.10 = (bf16[256,128]{1,0:T(8,128)(2,1)S(1)}, bf16[256,128]{1,0:T(8,128)(2,1)S(1)}, u32[]{:S(2)}, u32[]{:S(2)}) collective-permute-start(bf16[256,128]{1,0:T(8,128)(2,1)S(1)} %get-tuple-element.42), channel_id=1, source_target_pairs={{0,14},{1,15},{2,8},{3,9},{4,10},{5,11},{6,12},{7,13},{8,22},{9,23... | collective-permute-start | bytes 196616 | tf_op jit(solution)/shard_map/ppermute | solution.py:392
  59.4 2.9 %collective-permute-start.12 = (bf16[256,128]{1,0:T(8,128)(2,1)S(1)}, bf16[256,128]{1,0:T(8,128)(2,1)S(1)}, u32[]{:S(2)}, u32[]{:S(2)}) collective-permute-start(bf16[256,128]{1,0:T(8,128)(2,1)S(1)} %get-tuple-element.44), channel_id=1, source_target_pairs={{0,15},{1,8},{2,9},{3,10},{4,11},{5,12},{6,13},{7,14},{8,23},{9,16... | collective-permute-start | bytes 196616 | tf_op jit(solution)/shard_map/ppermute | solution.py:392
  62.2 0.3 collective-permute-done.9.refs_2_
  62.5 2.1 %collective-permute-start.14 = (bf16[256,128]{1,0:T(8,128)(2,1)S(1)}, bf16[256,128]{1,0:T(8,128)(2,1)S(1)}, u32[]{:S(2)}, u32[]{:S(2)}) collective-permute-start(bf16[256,128]{1,0:T(8,128)(2,1)S(1)} %get-tuple-element.46), channel_id=1, source_target_pairs={{0,8},{1,9},{2,10},{3,11},{4,12},{5,13},{6,14},{7,15},{8,16},{9,17... | collective-permute-start | bytes 196616 | tf_op jit(solution)/shard_map/ppermute | solution.py:392
  64.6 1.7 %collective-permute-done.11.refs_4_ = bf16[256,128]{1,0:T(8,128)(2,1)S(1)} collective-permute-done((bf16[256,128]{1,0:T(8,128)(2,1)S(1)}, bf16[256,128]{1,0:T(8,128)(2,1)S(1)}, u32[]{:S(2)}, u32[]{:S(2)}) %collective-permute-start.11) | collective-permute-done | bytes 65568 | tf_op jit(solution)/shard_map/ppermute | solution.py:392
  66.3 3.7 %collective-permute-done.13.refs_6_ = bf16[256,128]{1,0:T(8,128)(2,1)S(1)} collective-permute-done((bf16[256,128]{1,0:T(8,128)(2,1)S(1)}, bf16[256,128]{1,0:T(8,128)(2,1)S(1)}, u32[]{:S(2)}, u32[]{:S(2)}) %collective-permute-start.13) | collective-permute-done | bytes 65568 | tf_op jit(solution)/shard_map/ppermute | solution.py:392
  70.0 1.0 %shard_map.116 = bf16[512,512]{1,0:T(8,128)(2,1)} custom-call(s32[1]{0:T(128)} %bitcast.index_ref, bf16[256,128]{1,0:T(8,128)(2,1)S(1)} %collective-permute-done.7.refs_0_, bf16[256,128]{1,0:T(8,128)(2,1)S(1)} %collective-permute-done.8.refs_1_, bf16[256,128]{1,0:T(8,128)(2,1)S(1)} %collective-permute-done.9.refs_2_, ...), custom_call_target="tpu_custom_call" | custom-call | tf_op jit(solution)/shard_map/pallas_call | solution.py:478
  (24 shorter events, 0.1 us)
Async XLA Ops:
  0.0 37.4 %copy-start.1 = (f32[20,2,64,128]{3,2,1,0:T(8,128)S(1)}, f32[20,2,64,128]{3,2,1,0:T(8,128)}, u32[]{:S(2)}) copy-start(f32[20,2,64,128]{3,2,1,0:T(8,128)} %constant.21.clone.refs_9_) | copy-start | bytes 3932164
  0.0 40.1 %copy-start.5 = (bf16[128,192]{1,0:T(8,128)(2,1)S(1)}, bf16[128,192]{1,0:T(8,128)(2,1)}, u32[]{:S(2)}) copy-start(bf16[128,192]{1,0:T(8,128)(2,1)} %constant.18.clone.back_ref) | copy-start | bytes 147460
  0.0 40.1 %copy-start.3 = (bf16[128,384]{1,0:T(8,128)(2,1)S(1)}, bf16[128,384]{1,0:T(8,128)(2,1)}, u32[]{:S(2)}) copy-start(bf16[128,384]{1,0:T(8,128)(2,1)} %constant.17.clone.forward_ref) | copy-start | bytes 294916
  3.2 11.0 %collective-permute-start = (bf16[528,128]{1,0:T(8,128)(2,1)}, bf16[528,128]{1,0:T(8,128)(2,1)S(1)}, u32[]{:S(2)}, u32[]{:S(2)}) collective-permute-start(bf16[528,128]{1,0:T(8,128)(2,1)} %get-tuple-element.28), channel_id=1, source_target_pairs={{0,1},{1,2},{2,3},{3,4},{4,5},{5,6},{6,7},{7,0},{8,9},{9,10},{10,1... | collective-permute-start | bytes 405512 | tf_op jit(solution)/shard_map/ppermute | solution.py:392
  6.2 9.7 %collective-permute-start.1 = (bf16[528,128]{1,0:T(8,128)(2,1)}, bf16[528,128]{1,0:T(8,128)(2,1)S(1)}, u32[]{:S(2)}, u32[]{:S(2)}) collective-permute-start(bf16[528,128]{1,0:T(8,128)(2,1)} %get-tuple-element.29), channel_id=1, source_target_pairs={{0,2},{1,3},{2,4},{3,5},{4,6},{5,7},{6,0},{7,1},{8,10},{9,11},{10,... | collective-permute-start | bytes 405512 | tf_op jit(solution)/shard_map/ppermute | solution.py:392
  7.8 16.9 %collective-permute-start.2 = (bf16[528,128]{1,0:T(8,128)(2,1)}, bf16[528,128]{1,0:T(8,128)(2,1)S(1)}, u32[]{:S(2)}, u32[]{:S(2)}) collective-permute-start(bf16[528,128]{1,0:T(8,128)(2,1)} %get-tuple-element.30), channel_id=1, source_target_pairs={{0,3},{1,4},{2,5},{3,6},{4,7},{5,0},{6,1},{7,2},{8,11},{9,12},{10,... | collective-permute-start | bytes 405512 | tf_op jit(solution)/shard_map/ppermute | solution.py:392
  10.3 14.8 %collective-permute-start.3 = (bf16[528,128]{1,0:T(8,128)(2,1)}, bf16[528,128]{1,0:T(8,128)(2,1)S(1)}, u32[]{:S(2)}, u32[]{:S(2)}) collective-permute-start(bf16[528,128]{1,0:T(8,128)(2,1)} %get-tuple-element.31), channel_id=1, source_target_pairs={{0,4},{1,5},{2,6},{3,7},{4,0},{5,1},{6,2},{7,3},{8,12},{9,13},{10,... | collective-permute-start | bytes 405512 | tf_op jit(solution)/shard_map/ppermute | solution.py:392
  11.5 13.6 %collective-permute-start.4 = (bf16[528,128]{1,0:T(8,128)(2,1)}, bf16[528,128]{1,0:T(8,128)(2,1)S(1)}, u32[]{:S(2)}, u32[]{:S(2)}) collective-permute-start(bf16[528,128]{1,0:T(8,128)(2,1)} %get-tuple-element.32), channel_id=1, source_target_pairs={{0,5},{1,6},{2,7},{3,0},{4,1},{5,2},{6,3},{7,4},{8,13},{9,14},{10,... | collective-permute-start | bytes 405512 | tf_op jit(solution)/shard_map/ppermute | solution.py:392
  14.2 10.9 %collective-permute-start.5 = (bf16[528,128]{1,0:T(8,128)(2,1)}, bf16[528,128]{1,0:T(8,128)(2,1)S(1)}, u32[]{:S(2)}, u32[]{:S(2)}) collective-permute-start(bf16[528,128]{1,0:T(8,128)(2,1)} %get-tuple-element.33), channel_id=1, source_target_pairs={{0,6},{1,7},{2,0},{3,1},{4,2},{5,3},{6,4},{7,5},{8,14},{9,15},{10,... | collective-permute-start | bytes 405512 | tf_op jit(solution)/shard_map/ppermute | solution.py:392
  15.9 9.3 %collective-permute-start.6 = (bf16[528,128]{1,0:T(8,128)(2,1)}, bf16[528,128]{1,0:T(8,128)(2,1)S(1)}, u32[]{:S(2)}, u32[]{:S(2)}) collective-permute-start(bf16[528,128]{1,0:T(8,128)(2,1)} %get-tuple-element.34), channel_id=1, source_target_pairs={{0,7},{1,0},{2,1},{3,2},{4,3},{5,4},{6,5},{7,6},{8,15},{9,8},{10,9... | collective-permute-start | bytes 405512 | tf_op jit(solution)/shard_map/ppermute | solution.py:392
  20.0 0.9 %copy-start.2 = (bf16[528,128]{1,0:T(8,128)(2,1)S(1)}, bf16[528,128]{1,0:T(8,128)(2,1)}, u32[]{:S(2)}) copy-start(bf16[528,128]{1,0:T(8,128)(2,1)} %get-tuple-element.26.refs_0_) | copy-start | bytes 405508
  21.0 0.8 %copy-start.6 = (bf16[128,192]{1,0:T(8,128)(2,1)S(1)}, bf16[128,192]{1,0:T(8,128)(2,1)}, u32[]{:S(2)}) copy-start(bf16[128,192]{1,0:T(8,128)(2,1)} %constant.16.clone.refs_1_) | copy-start | bytes 147460
  25.2 25.9 %all-to-all-start = ((bf16[8,256,128]{2,1,0:T(8,128)(2,1)}), bf16[8,256,128]{2,1,0:T(8,128)(2,1)S(1)}, u32[]{:S(2)}, u32[]{:S(2)}) async-start(bf16[8,256,128]{2,1,0:T(8,128)(2,1)} %shard_map.114), calls=%async_computation | async-start | bytes 1048576 | tf_op jit(solution)/shard_map/all_to_all | solution.py:469
  37.4 6.3 %copy-start = (f32[64,2,64,128]{3,2,1,0:T(8,128)S(1)}, f32[64,2,64,128]{3,2,1,0:T(8,128)}, u32[]{:S(2)}) copy-start(f32[64,2,64,128]{3,2,1,0:T(8,128)} %constant.20.clone.refs_1_) | copy-start | bytes 12582916
  37.4 6.3 %copy-start.4 = (bf16[128,192]{1,0:T(8,128)(2,1)S(1)}, bf16[128,192]{1,0:T(8,128)(2,1)}, u32[]{:S(2)}) copy-start(bf16[128,192]{1,0:T(8,128)(2,1)} %constant.19.clone.refs_0_) | copy-start | bytes 147460
  37.4 6.3 %copy-start.7 = (f32[1,512]{1,0:T(1,128)S(1)}, f32[1,512]{1,0:T(1,128)}, u32[]{:S(2)}) copy-start(f32[1,512]{1,0:T(1,128)} %skip_ref.1) | copy-start | bytes 6148
  51.2 8.2 %collective-permute-start.7 = (bf16[256,128]{1,0:T(8,128)(2,1)S(1)}, bf16[256,128]{1,0:T(8,128)(2,1)S(1)}, u32[]{:S(2)}, u32[]{:S(2)}) collective-permute-start(bf16[256,128]{1,0:T(8,128)(2,1)S(1)} %get-tuple-element.39), channel_id=1, source_target_pairs={{0,12},{1,13},{2,14},{3,15},{4,8},{5,9},{6,10},{7,11},{8,20},{9,21... | collective-permute-start | bytes 196616 | tf_op jit(solution)/shard_map/ppermute | solution.py:392
  51.2 11.0 %collective-permute-start.8 = (bf16[256,128]{1,0:T(8,128)(2,1)S(1)}, bf16[256,128]{1,0:T(8,128)(2,1)S(1)}, u32[]{:S(2)}, u32[]{:S(2)}) collective-permute-start(bf16[256,128]{1,0:T(8,128)(2,1)S(1)} %get-tuple-element.40), channel_id=1, source_target_pairs={{0,13},{1,14},{2,15},{3,8},{4,9},{5,10},{6,11},{7,12},{8,21},{9,22... | collective-permute-start | bytes 196616 | tf_op jit(solution)/shard_map/ppermute | solution.py:392
  55.7 6.8 %collective-permute-start.9 = (bf16[256,128]{1,0:T(8,128)(2,1)S(1)}, bf16[256,128]{1,0:T(8,128)(2,1)S(1)}, u32[]{:S(2)}, u32[]{:S(2)}) collective-permute-start(bf16[256,128]{1,0:T(8,128)(2,1)S(1)} %get-tuple-element.41), channel_id=1, source_target_pairs={{0,11},{1,12},{2,13},{3,14},{4,15},{5,8},{6,9},{7,10},{8,19},{9,20... | collective-permute-start | bytes 196616 | tf_op jit(solution)/shard_map/ppermute | solution.py:392
  55.7 9.0 %collective-permute-start.10 = (bf16[256,128]{1,0:T(8,128)(2,1)S(1)}, bf16[256,128]{1,0:T(8,128)(2,1)S(1)}, u32[]{:S(2)}, u32[]{:S(2)}) collective-permute-start(bf16[256,128]{1,0:T(8,128)(2,1)S(1)} %get-tuple-element.42), channel_id=1, source_target_pairs={{0,14},{1,15},{2,8},{3,9},{4,10},{5,11},{6,12},{7,13},{8,22},{9,23... | collective-permute-start | bytes 196616 | tf_op jit(solution)/shard_map/ppermute | solution.py:392
  59.4 7.0 %collective-permute-start.11 = (bf16[256,128]{1,0:T(8,128)(2,1)S(1)}, bf16[256,128]{1,0:T(8,128)(2,1)S(1)}, u32[]{:S(2)}, u32[]{:S(2)}) collective-permute-start(bf16[256,128]{1,0:T(8,128)(2,1)S(1)} %get-tuple-element.43), channel_id=1, source_target_pairs={{0,10},{1,11},{2,12},{3,13},{4,14},{5,15},{6,8},{7,9},{8,18},{9,19... | collective-permute-start | bytes 196616 | tf_op jit(solution)/shard_map/ppermute | solution.py:392
  59.4 7.0 %collective-permute-start.12 = (bf16[256,128]{1,0:T(8,128)(2,1)S(1)}, bf16[256,128]{1,0:T(8,128)(2,1)S(1)}, u32[]{:S(2)}, u32[]{:S(2)}) collective-permute-start(bf16[256,128]{1,0:T(8,128)(2,1)S(1)} %get-tuple-element.44), channel_id=1, source_target_pairs={{0,15},{1,8},{2,9},{3,10},{4,11},{5,12},{6,13},{7,14},{8,23},{9,16... | collective-permute-start | bytes 196616 | tf_op jit(solution)/shard_map/ppermute | solution.py:392
  62.2 7.8 %collective-permute-start.13 = (bf16[256,128]{1,0:T(8,128)(2,1)S(1)}, bf16[256,128]{1,0:T(8,128)(2,1)S(1)}, u32[]{:S(2)}, u32[]{:S(2)}) collective-permute-start(bf16[256,128]{1,0:T(8,128)(2,1)S(1)} %get-tuple-element.45), channel_id=1, source_target_pairs={{0,9},{1,10},{2,11},{3,12},{4,13},{5,14},{6,15},{7,8},{8,17},{9,18... | collective-permute-start | bytes 196616 | tf_op jit(solution)/shard_map/ppermute | solution.py:392
  62.5 7.5 %collective-permute-start.14 = (bf16[256,128]{1,0:T(8,128)(2,1)S(1)}, bf16[256,128]{1,0:T(8,128)(2,1)S(1)}, u32[]{:S(2)}, u32[]{:S(2)}) collective-permute-start(bf16[256,128]{1,0:T(8,128)(2,1)S(1)} %get-tuple-element.46), channel_id=1, source_target_pairs={{0,8},{1,9},{2,10},{3,11},{4,12},{5,13},{6,14},{7,15},{8,16},{9,17... | collective-permute-start | bytes 196616 | tf_op jit(solution)/shard_map/ppermute | solution.py:392
